TPU v7x, 32 devices: a whole 2x2x4 slice. The times are simulated.
32 devices in a mesh: dp: 8 (over y, x, core), shard: 4 (over z).
Axes of the slice: x: 2, y: 2, z: 4, core: 2. Of those that a mesh axis runs over, the one named last changes fastest.
Arguments:
- partials: bfloat16 [8, 32, 256, 256], P('dp', 'shard'), may hold values from -4 to 4
- params: float32 [32, 256, 256], P('shard', 'dp'), may hold values from -0.75 to 0.75
- left_basis: float32 [8, 4, 1, 256, 256], P('dp', 'shard'), may hold values from -0.375 to 0.375
- right_basis: float32 [8, 4, 1, 256, 256], P('dp', 'shard'), may hold values from -0.375 to 0.375
- first_moment: float32 [8, 4, 1, 256, 256], P('dp', 'shard'), may hold values from -4 to 4
- second_moment: float32 [8, 4, 1, 256, 256], P('dp', 'shard'), may hold values from 0.1 to 10
- owner_list: int32 [32], replicated, may hold values from 0 to 31, as said below
Outputs:
- updated: float32 [32, 256, 256], P('shard')
- first_out: float32 [8, 4, 1, 256, 256], P('dp', 'shard')
- second_out: float32 [8, 4, 1, 256, 256], P('dp', 'shard')
Inputs may be any that keep to these rules, and one draw needn't show every extreme that they name: `owner_list`: each owner device is named by at most 1 block, and some device by exactly 1.
All inputs are finite; a program needn't handle non-finite values.
Results may differ from a plain program's by a relative error of at most 0.0003.
Values sent between devices are 32-bit elements; how exact they have to be, the bound alone decides.
No kernel may reach another device: no remote copies, remote signals or barrier semaphores. Data moves between devices by JAX's collectives and lax.ppermute only.
A program may use at most 64 MiB of HBM per device.

v0:
```python
import jax
import jax.numpy as jnp
from jax import lax
from jax.sharding import PartitionSpec as P

beta_one = 0.9
beta_two = 0.95
epsilon = 1e-08
learn_rate = 0.2
decay_rate = 0.1
step_count = 10


def local(partials, params, left_basis, right_basis, first_moment, second_moment, owner_list):
    highest = lax.Precision.HIGHEST
    shard_here = lax.axis_index("shard")
    data_here = lax.axis_index("dp")
    shard_count = lax.axis_size("shard")
    data_count = lax.axis_size("dp")
    home_count = params.shape[0]
    row_count = params.shape[1]
    width = params.shape[2]
    slot_count = first_moment.shape[2]
    block_total = owner_list.shape[0]
    summed = lax.psum_scatter(
        partials[0].astype(jnp.float32), "dp", scatter_dimension=1, tiled=True
    )
    home_owner = lax.dynamic_slice_in_dim(owner_list, shard_here * home_count, home_count)
    column_ids = jnp.arange(shard_count, dtype=jnp.int32)
    column_mask = (home_owner[None, :] % shard_count == column_ids[:, None]).astype(jnp.float32)
    outgoing = column_mask[:, :, None, None] * summed[None]
    arrived = lax.all_to_all(outgoing, "shard", split_axis=0, concat_axis=0, tiled=True).reshape(
        block_total, row_count, width
    )
    dest_ids = jnp.arange(data_count, dtype=jnp.int32)
    slot_ids = jnp.arange(slot_count, dtype=jnp.int32)
    owner_match = owner_list[None, None, :] == dest_ids[None, :, None] * shard_count + shard_here
    slot_match = slot_ids[:, None, None] == 0
    picker = (owner_match & slot_match).astype(jnp.float32)
    outgoing_rows = jnp.einsum("kob,brj->korj", picker, arrived, precision=highest)
    whole = lax.all_to_all(outgoing_rows, "dp", split_axis=1, concat_axis=1, tiled=True).reshape(
        slot_count, width, width
    )
    left_mats = left_basis[0, 0]
    right_mats = right_basis[0, 0]
    first_old = first_moment[0, 0]
    second_old = second_moment[0, 0]
    partway = jnp.einsum("cia,cij->caj", left_mats, whole, precision=highest)
    rotated = jnp.einsum("caj,cjb->cab", partway, right_mats, precision=highest)
    first_new = beta_one * first_old + (1.0 - beta_one) * rotated
    second_new = beta_two * second_old + (1.0 - beta_two) * rotated * rotated
    correct_one = 1.0 - beta_one**step_count
    correct_two = 1.0 - beta_two**step_count
    scaled = first_new / correct_one / (jnp.sqrt(second_new / correct_two) + epsilon)
    back_rot = jnp.einsum("cab,cjb->caj", scaled, right_mats, precision=highest)
    change = jnp.einsum("cia,caj->cij", left_mats, back_rot, precision=highest)
    leaving = change.reshape(slot_count, data_count, row_count, width)
    coming = lax.all_to_all(leaving, "dp", split_axis=1, concat_axis=1, tiled=True)
    back_rows = jnp.einsum("kob,korj->brj", picker, coming, precision=highest)
    sending = back_rows.reshape(shard_count, home_count, row_count, width)
    returned = jnp.sum(
        lax.all_to_all(sending, "shard", split_axis=0, concat_axis=0, tiled=True), axis=0
    )
    new_home = params - learn_rate * (returned + decay_rate * params)
    updated = lax.all_gather(new_home, "dp", axis=1, tiled=True)
    my_id = data_here * shard_count + shard_here
    my_count = jnp.sum((owner_list == my_id).astype(jnp.int32))
    live_slot = (slot_ids < my_count)[:, None, None]
    first_keep = jnp.where(live_slot, first_new, first_old)
    second_keep = jnp.where(live_slot, second_new, second_old)
    return (updated, first_keep[None, None], second_keep[None, None])


def solution(mesh):
    return jax.shard_map(
        local,
        mesh=mesh,
        in_specs=(
            P("dp", "shard", None, None),
            P("shard", "dp", None),
            P("dp", "shard", None, None, None),
            P("dp", "shard", None, None, None),
            P("dp", "shard", None, None, None),
            P("dp", "shard", None, None, None),
            P(),
        ),
        out_specs=(
            P("shard", None, None),
            P("dp", "shard", None, None, None),
            P("dp", "shard", None, None, None),
        ),
        check_vma=False,
    )
```

profile of v0, /device:TPU:0, one launch (start us, length us, event | category | flops | bytes accessed | tf_op | source)
XLA Modules:
  0.0 177.4 jit_solution(7258017166070272111)
XLA Ops:
  7.2 0.0 copy-start
  7.2 0.0 reduce-scatter.2.cloned.1.call-start
  7.2 2.8 %bitcast_convert_fusion = f32[8,256,256]{2,1,0:T(8,128)} fusion(bf16[1,8,256,256]{3,2,1,0:T(8,128)(2,1)} %param.7), kind=kLoop, calls=%fused_computation.3 | loop fusion | flops 524288 | bytes 3145728 | tf_op jit(solution)/shard_map/convert_element_type | solution.py:26
  10.0 0.0 reduce-scatter.2.cloned.1.call-update
  10.0 0.1 and_select_fusion
  10.1 45.7 %reduce-scatter.2.cloned.1.call-done = f32[8,32,256]{2,1,0:T(8,128)} async-done(((f32[8,256,256]{2,1,0:T(8,128)}), f32[8,32,256]{2,1,0:T(8,128)}) %reduce-scatter.2.cloned.1.call-update) | async-done | bytes 262160 | tf_op jit(solution)/shard_map/reduce_scatter | solution.py:25
  55.8 1.1 copy.23
  56.9 1.1 broadcast_multiply_fusion
  58.0 4.6 %all-to-all-start = ((f32[4,8,32,256]{3,1,2,0:T(8,128)}), f32[4,8,32,256]{3,1,2,0:T(8,128)S(1)}, u32[]{:S(2)}, u32[]{:S(2)}) async-start(f32[4,8,32,256]{3,1,2,0:T(8,128)} %broadcast_multiply_fusion), calls=%async_computation.1 | async-start | bytes 2097152 | tf_op jit(solution)/shard_map/all_to_all | solution.py:32
  62.7 25.7 %all-to-all-done = f32[4,8,32,256]{3,1,2,0:T(8,128)S(1)} async-done(((f32[4,8,32,256]{3,1,2,0:T(8,128)}), f32[4,8,32,256]{3,1,2,0:T(8,128)S(1)}, u32[]{:S(2)}, u32[]{:S(2)}) %all-to-all-start) | async-done | bytes 1048608 | tf_op jit(solution)/shard_map/all_to_all | solution.py:32
  88.4 0.5 convolution_bitcast_fusion.2
  88.8 0.1 copy.25
  88.9 9.5 %all_to_all.20 = f32[1,8,32,256]{3,2,0,1:T(8,128)S(1)} all-to-all(f32[1,8,32,256]{3,2,0,1:T(8,128)S(1)} %copy.25), channel_id=1, replica_groups=mesh['dp'=8,'shard'=4] {'dp'}, dimensions={1} | all-to-all | bytes 524288 | tf_op jit(solution)/shard_map/all_to_all | solution.py:41
  98.4 0.6 fusion.9
  99.0 0.0 copy-done.1
  99.0 0.6 fusion.7
  99.6 0.6 convolution_bitcast_fusion.1
  100.2 1.1 convolution_bitcast_fusion
  101.3 3.4 %all-to-all-start.2 = ((f32[1,8,32,256]{3,2,0,1:T(8,128)}), f32[1,8,32,256]{3,2,0,1:T(8,128)S(1)}, u32[]{:S(2)}, u32[]{:S(2)}) async-start(f32[1,8,32,256]{3,2,0,1:T(8,128)} %convolution_bitcast_fusion), calls=%async_computation.3 | async-start | bytes 524288 | tf_op jit(solution)/shard_map/all_to_all | solution.py:58
  104.7 0.0 all-gather.2.cloned.1.call-start
  104.8 0.1 eq.57
  104.9 6.7 %all-to-all-done.2 = f32[1,8,32,256]{3,2,0,1:T(8,128)S(1)} async-done(((f32[1,8,32,256]{3,2,0,1:T(8,128)}), f32[1,8,32,256]{3,2,0,1:T(8,128)S(1)}, u32[]{:S(2)}, u32[]{:S(2)}) %all-to-all-start.2) | async-done | bytes 262176 | tf_op jit(solution)/shard_map/all_to_all | solution.py:58
  111.6 0.6 fusion.3
  112.2 27.8 %all_to_all.21 = f32[4,8,32,256]{3,1,2,0:T(8,128)S(1)} all-to-all(f32[4,8,32,256]{3,1,2,0:T(8,128)S(1)} %fusion.3), channel_id=1, replica_groups=mesh['dp'=8,'shard'=4] {'shard'}, dimensions={0} | all-to-all | bytes 2097152 | tf_op jit(solution)/shard_map/all_to_all | solution.py:62
  140.0 0.1 reduce_sum.18
  140.1 0.0 copy-done.2
  140.1 0.9 multiply_subtract_fusion
  141.0 0.0 all-gather.2.cloned.1.call-update
  141.0 0.6 fusion.37
  142.3 0.9 fusion.5
  143.2 23.8 %all-gather.2.cloned.1.call-done = f32[8,256,256]{2,0,1:T(8,128)} async-done(((f32[8,32,256]{2,0,1:T(8,128)}), f32[8,256,256]{2,0,1:T(8,128)}) %all-gather.2.cloned.1.call-update) | async-done | bytes 2097168 | tf_op jit(solution)/shard_map/all_gather | solution.py:65
  167.0 3.6 %copy.30 = f32[8,256,256]{2,1,0:T(8,128)} copy(f32[8,256,256]{2,0,1:T(8,128)} %all-gather.2.cloned.1.call-done) | data formatting | bytes 4194304
  (11 shorter events, 0.0 us)
Async XLA Ops:
  7.2 91.2 %copy-start = (f32[1,1,1,256,256]{4,3,2,1,0:T(8,128)S(1)}, f32[1,1,1,256,256]{4,3,2,1,0:T(8,128)}, u32[]{:S(2)}) copy-start(f32[1,1,1,256,256]{4,3,2,1,0:T(8,128)} %param.9) | copy-start | bytes 786436
  7.2 2.9 %copy-start.5 = (s32[32]{0:T(128)S(1)}, s32[32]{0:T(128)}, u32[]{:S(2)}) copy-start(s32[32]{0:T(128)} %param.13) | copy-start | bytes 388
  7.2 48.6 %reduce-scatter.2.cloned.1.call-start = ((), (), s32[]{:S(2)}) async-start(), calls=%async_computation.5 | async-start | bytes 2359296 | tf_op jit(solution)/shard_map/reduce_scatter | solution.py:25
  58.0 30.3 %all-to-all-start = ((f32[4,8,32,256]{3,1,2,0:T(8,128)}), f32[4,8,32,256]{3,1,2,0:T(8,128)S(1)}, u32[]{:S(2)}, u32[]{:S(2)}) async-start(f32[4,8,32,256]{3,1,2,0:T(8,128)} %broadcast_multiply_fusion), calls=%async_computation.1 | async-start | bytes 2097152 | tf_op jit(solution)/shard_map/all_to_all | solution.py:32
  62.7 36.3 %copy-start.1 = (f32[1,1,1,256,256]{4,3,2,1,0:T(8,128)S(1)}, f32[1,1,1,256,256]{4,3,2,1,0:T(8,128)}, u32[]{:S(2)}) copy-start(f32[1,1,1,256,256]{4,3,2,1,0:T(8,128)} %param.10) | copy-start | bytes 786436
  62.7 37.0 %copy-start.3 = (f32[1,1,1,256,256]{4,3,2,1,0:T(8,128)S(1)}, f32[1,1,1,256,256]{4,3,2,1,0:T(8,128)}, u32[]{:S(2)}) copy-start(f32[1,1,1,256,256]{4,3,2,1,0:T(8,128)} %param.11) | copy-start | bytes 786436
  62.7 37.0 %copy-start.4 = (f32[1,1,1,256,256]{4,3,2,1,0:T(8,128)S(1)}, f32[1,1,1,256,256]{4,3,2,1,0:T(8,128)}, u32[]{:S(2)}) copy-start(f32[1,1,1,256,256]{4,3,2,1,0:T(8,128)} %param.12) | copy-start | bytes 786436
  101.3 10.3 %all-to-all-start.2 = ((f32[1,8,32,256]{3,2,0,1:T(8,128)}), f32[1,8,32,256]{3,2,0,1:T(8,128)S(1)}, u32[]{:S(2)}, u32[]{:S(2)}) async-start(f32[1,8,32,256]{3,2,0,1:T(8,128)} %convolution_bitcast_fusion), calls=%async_computation.3 | async-start | bytes 524288 | tf_op jit(solution)/shard_map/all_to_all | solution.py:58
  104.7 62.3 %all-gather.2.cloned.1.call-start = ((), (), s32[]{:S(2)}) async-start(), calls=%async_computation.6 | async-start | bytes 2359296 | tf_op jit(solution)/shard_map/all_gather | solution.py:65
  104.9 35.2 %copy-start.2 = (f32[8,32,256]{2,1,0:T(8,128)S(1)}, f32[8,32,256]{2,1,0:T(8,128)}, u32[]{:S(2)}) copy-start(f32[8,32,256]{2,1,0:T(8,128)} %param.8) | copy-start | bytes 786436
Sparse Core Ops, SparseCore 0:
  11.9 43.8 reduce-scatter.1
  141.1 25.8 all-gather.1
where the time goes:
time: 178 us; the launch traced here: 177 us
  waiting for transfers between devices  102 us (57%)
  blocking collectives  37.2 us (21%)
  between operations  14.8 us (8%)
  starting transfers between devices  8.1 us (5%)
  other arithmetic  6.46 us (4%)
  local copies, waits for them, and re-layouts  4.89 us (3%)
  matrix products  3.94 us (2%)
    reduce_scatter x1, waiting for transfers between devices, local(): lax.psum_scatter(partials[0].astype(jnp.float32), 'dp', scatter_dimension...  45.7 us
    all_to_all x1, blocking collectives, local(): lax.all_to_all(sending, 'shard', split_axis=0, concat_axis=0, tiled=True)  27.8 us
    all_to_all x1, waiting for transfers between devices, local(): lax.all_to_all(outgoing, 'shard', split_axis=0, concat_axis=0, tiled=True)  25.7 us
    all_gather x1, waiting for transfers between devices, local(): updated = lax.all_gather(new_home, 'dp', axis=1, tiled=True)  23.8 us
    all_to_all x1, blocking collectives, local(): lax.all_to_all(outgoing_rows, 'dp', split_axis=1, concat_axis=1, tiled=True)  9.45 us
    all_to_all x1, waiting for transfers between devices, local(): lax.all_to_all(leaving, 'dp', split_axis=1, concat_axis=1, tiled=True)  6.73 us
    all_to_all x1, starting transfers between devices, local(): lax.all_to_all(outgoing, 'shard', split_axis=0, concat_axis=0, tiled=True)  4.61 us
    unnamed x13, local copies, waits for them, and re-layouts  3.61 us
  transfers between devices with their start and end apart: 4, of which 4 were waited for; matrix products, arithmetic and copies ran while one was open for 1% of the time, Pallas kernels for 0%

commit v1 on v0

v1 whole, which is shorter than its diff:
```python
import jax
import jax.numpy as jnp
from jax import lax
from jax.sharding import PartitionSpec as P

beta_one = 0.9
beta_two = 0.95
epsilon = 1e-08
learn_rate = 0.2
decay_rate = 0.1
step_count = 10


def swap(values, axis_size, bit):
    return lax.ppermute(values, "dp", [(i, i ^ (1 << bit)) for i in range(axis_size)])


def take(values, axis, index):
    return lax.dynamic_index_in_dim(values, index, axis, keepdims=False)


def halve(values, axes, bits, me, count):
    for bit in bits:
        axis = 1 + axes.index(bit)
        mine = (me >> bit) & 1
        away = take(values, axis, 1 - mine).astype(jnp.float32)
        here = take(values, axis, mine).astype(jnp.float32)
        values = here + swap(away, count, bit)
        axes = [a for a in axes if a != bit]
    return values


def spread(values, bits, me, count):
    axes = []
    for bit in bits:
        mine = (me >> bit) & 1
        other = swap(values, count, bit)
        low = jnp.where(mine == 0, values, other)
        high = jnp.where(mine == 0, other, values)
        place = sum(1 for a in axes if a > bit)
        values = jnp.stack([low, high], axis=1 + place)
        axes = sorted(axes + [bit], reverse=True)
    return values


def local(partials, params, left_basis, right_basis, first_moment, second_moment, owner_list):
    highest = lax.Precision.HIGHEST
    shard_here = lax.axis_index("shard")
    data_here = lax.axis_index("dp")
    shard_count = lax.axis_size("shard")
    data_count = lax.axis_size("dp")
    device_total = shard_count * data_count
    home_count, row_count, width = params.shape
    block_total = owner_list.shape[0]
    bit_count = data_count.bit_length() - 1
    high_low = list(range(bit_count))[::-1]
    middle = home_count // 2

    grid = partials[0].reshape((home_count,) + (2,) * bit_count + (row_count, width))
    low_first = halve(grid[:middle], high_low, list(range(bit_count)), data_here, data_count)
    high_first = halve(
        grid[middle:], high_low, [0] + list(range(1, bit_count))[::-1], data_here, data_count
    )
    summed = jnp.concatenate([low_first, high_first], axis=0)

    piece = row_count * width // shard_count
    cut = summed.reshape(home_count, shard_count, piece).swapaxes(0, 1)
    pieces = lax.all_to_all(cut, "shard", split_axis=0, concat_axis=0, tiled=True).reshape(
        block_total, piece
    )
    device_ids = jnp.arange(device_total, dtype=jnp.int32)
    picker = (owner_list[None, :] == device_ids[:, None]).astype(jnp.float32)
    leaving = jnp.einsum("eb,bn->en", picker, pieces, precision=highest)
    whole = lax.all_to_all(
        leaving, ("dp", "shard"), split_axis=0, concat_axis=0, tiled=True
    ).reshape(width, width)

    left_mat = left_basis[0, 0, 0]
    right_mat = right_basis[0, 0, 0]
    first_old = first_moment[0, 0, 0]
    second_old = second_moment[0, 0, 0]
    partway = jnp.einsum("ia,ij->aj", left_mat, whole, precision=highest)
    rotated = jnp.einsum("aj,jb->ab", partway, right_mat, precision=highest)
    first_new = beta_one * first_old + (1.0 - beta_one) * rotated
    second_new = beta_two * second_old + (1.0 - beta_two) * rotated * rotated
    correct_one = 1.0 - beta_one**step_count
    correct_two = 1.0 - beta_two**step_count
    scaled = first_new / correct_one / (jnp.sqrt(second_new / correct_two) + epsilon)
    back_rot = jnp.einsum("ab,jb->aj", scaled, right_mat, precision=highest)
    change = jnp.einsum("ia,aj->ij", left_mat, back_rot, precision=highest)

    coming = lax.all_to_all(
        change.reshape(device_total, piece), ("dp", "shard"), split_axis=0, concat_axis=0, tiled=True
    )
    back = jnp.einsum("eb,en->bn", picker, coming, precision=highest)
    returned = lax.all_to_all(
        back.reshape(shard_count, home_count, piece), "shard", split_axis=0, concat_axis=0, tiled=True
    )
    returned = returned.swapaxes(0, 1).reshape(home_count, row_count, width)
    new_home = params - learn_rate * (returned + decay_rate * params)
    updated = jnp.concatenate(
        [
            spread(new_home[:middle], high_low, data_here, data_count),
            spread(new_home[middle:], list(range(1, bit_count)) + [0], data_here, data_count),
        ],
        axis=0,
    ).reshape(home_count, width, width)

    my_id = data_here * shard_count + shard_here
    live = jnp.any(owner_list == my_id)
    first_keep = jnp.where(live, first_new, first_old)
    second_keep = jnp.where(live, second_new, second_old)
    return (updated, first_keep[None, None, None], second_keep[None, None, None])


def solution(mesh):
    return jax.shard_map(
        local,
        mesh=mesh,
        in_specs=(
            P("dp", "shard", None, None),
            P("shard", "dp", None),
            P("dp", "shard", None, None, None),
            P("dp", "shard", None, None, None),
            P("dp", "shard", None, None, None),
            P("dp", "shard", None, None, None),
            P(),
        ),
        out_specs=(
            P("shard", None, None),
            P("dp", "shard", None, None, None),
            P("dp", "shard", None, None, None),
        ),
        check_vma=False,
    )
```

time: 178 us -> 97.3 us (0.55)
  waiting for transfers between devices: 102 us -> 30.1 us
  between operations: 14.8 us -> 1.02 us
  starting transfers between devices: 8.1 us -> 15 us
    reduce_scatter x1 -> x0, waiting for transfers between devices: 45.7 us -> none  [local(): lax.psum_scatter(partials[0].astype(jnp.float32), 'dp', scatter_dimension...]
    all_gather x1 -> x0, waiting for transfers between devices: 23.8 us -> none  [local(): updated = lax.all_gather(new_home, 'dp', axis=1, tiled=True)]
    all_to_all x2 -> x1, waiting for transfers between devices: 32.4 us -> 10.1 us  [local(): lax.all_to_all(change.reshape(device_total, piece), ('dp', 'shard'), spli...]
    ppermute x0 -> x12, waiting for transfers between devices: none -> 20 us  [swap(): lax.ppermute(values, 'dp', [(i, i ^ 1 << bit) for i in range(axis_size)])]
    ppermute x0 -> x12, starting transfers between devices: none -> 12.3 us  [swap(): lax.ppermute(values, 'dp', [(i, i ^ 1 << bit) for i in range(axis_size)])]
    all_to_all x2 -> x1, starting transfers between devices: 8.02 us -> 2.72 us  [local(): lax.all_to_all(change.reshape(device_total, piece), ('dp', 'shard'), spli...]
    unnamed x13 -> x12, local copies, waits for them, and re-layouts: 3.61 us -> 0.04 us
    convert_element_type x2, other arithmetic: 2.77 us -> 0.09 us  [halve(): away = take(values, axis, 1 - mine).astype(jnp.float32)]
  transfers between devices with their start and end apart: 4 -> 13, of which waited for: 4 -> 9; matrix products, arithmetic and copies ran while one was open for 1% -> 5% of each run, Pallas kernels for 0% -> 0%
where the time goes in v1:
time: 97.3 us; the launch traced here: 97 us
  blocking collectives  37 us (38%)
  waiting for transfers between devices  30.1 us (31%)
  starting transfers between devices  15 us (15%)
  other arithmetic  5.72 us (6%)
  local copies, waits for them, and re-layouts  5.12 us (5%)
  matrix products  2.96 us (3%)
  between operations  1.02 us (1%)
    ppermute x12, waiting for transfers between devices, swap(): lax.ppermute(values, 'dp', [(i, i ^ 1 << bit) for i in range(axis_size)])  20 us
    all_to_all x1, blocking collectives, local(): lax.all_to_all(leaving, ('dp', 'shard'), split_axis=0, concat_axis=0, til...  13.2 us
    ppermute x12, starting transfers between devices, swap(): lax.ppermute(values, 'dp', [(i, i ^ 1 << bit) for i in range(axis_size)])  12.3 us
    all_to_all x1, blocking collectives, local(): lax.all_to_all(back.reshape(shard_count, home_count, piece), 'shard', spl...  12.1 us
    all_to_all x1, blocking collectives, local(): lax.all_to_all(cut, 'shard', split_axis=0, concat_axis=0, tiled=True)  11.8 us
    all_to_all x1, waiting for transfers between devices, local(): lax.all_to_all(change.reshape(device_total, piece), ('dp', 'shard'), spli...  10.1 us
    all_to_all x1, starting transfers between devices, local(): lax.all_to_all(change.reshape(device_total, piece), ('dp', 'shard'), spli...  2.72 us
    broadcast_in_dim x1, other arithmetic, local(): second_keep[None, None, None]  2.53 us
  transfers between devices with their start and end apart: 13, of which 9 were waited for; matrix products, arithmetic and copies ran while one was open for 5% of the time, Pallas kernels for 0%

profile of v1, /device:TPU:0, one launch (start us, length us, event | category | flops | bytes accessed | tf_op | source)
XLA Modules:
  0.0 97.0 jit_solution(14567465793776499104)
XLA Ops:
  0.7 1.3 %fusion.40 = (bf16[1,4,256,256]{3,2,1,0:T(8,128)(2,1)S(1)}, bf16[1,4,256,256]{3,2,1,0:T(8,128)(2,1)S(1)}) fusion(bf16[1,8,256,256]{3,2,1,0:T(8,128)(2,1)} %param.7), kind=kLoop, calls=%fused_computation.78 | loop fusion | bytes 2097152 | tf_op jit(solution)/shard_map/slice | solution.py:60
  2.0 0.5 collective-permute-start
  2.7 1.4 %collective-permute-done = f32[4,2,2,32,256]{4,3,2,1,0:T(8,128)S(1)} collective-permute-done((f32[4,2,2,32,256]{4,3,2,1,0:T(8,128)S(1)}, f32[4,2,2,32,256]{4,3,2,1,0:T(8,128)S(1)}, u32[]{:S(2)}, u32[]{:S(2)}) %collective-permute-start) | collective-permute-done | bytes 524320 | tf_op jit(solution)/shard_map/ppermute | solution.py:15
  4.2 2.9 %collective-permute-start.1 = (f32[4,2,32,256]{3,2,1,0:T(8,128)S(1)}, f32[4,2,32,256]{3,2,1,0:T(8,128)S(1)}, u32[]{:S(2)}, u32[]{:S(2)}) collective-permute-start(f32[4,2,32,256]{3,2,1,0:T(8,128)S(1)} %dynamic-slice_bitcast_fusion.1), channel_id=1, source_target_pairs={{0,8},{4,12},{8,0},{12,4},{16,24},{20,28},{24,16},{28,20},{1,9},{5... | collective-permute-start | bytes 786440 | tf_op jit(solution)/shard_map/ppermute | solution.py:15
  7.2 1.6 %collective-permute-start.4 = (f32[4,2,32,256]{3,2,1,0:T(8,128)S(1)}, f32[4,2,32,256]{3,2,1,0:T(8,128)S(1)}, u32[]{:S(2)}, u32[]{:S(2)}) collective-permute-start(f32[4,2,32,256]{3,2,1,0:T(8,128)S(1)} %dynamic-slice_bitcast_fusion), channel_id=1, source_target_pairs={{0,16},{4,20},{8,24},{12,28},{16,0},{20,4},{24,8},{28,12},{1,17},{... | collective-permute-start | bytes 786440 | tf_op jit(solution)/shard_map/ppermute | solution.py:15
  8.8 4.9 %collective-permute-done.1 = f32[4,2,32,256]{3,2,1,0:T(8,128)S(1)} collective-permute-done((f32[4,2,32,256]{3,2,1,0:T(8,128)S(1)}, f32[4,2,32,256]{3,2,1,0:T(8,128)S(1)}, u32[]{:S(2)}, u32[]{:S(2)}) %collective-permute-start.1) | collective-permute-done | bytes 262176 | tf_op jit(solution)/shard_map/ppermute | solution.py:15
  13.8 1.8 %collective-permute-start.2 = (f32[4,32,256]{2,1,0:T(8,128)S(1)}, f32[4,32,256]{2,1,0:T(8,128)S(1)}, u32[]{:S(2)}, u32[]{:S(2)}) collective-permute-start(f32[4,32,256]{2,1,0:T(8,128)S(1)} %dynamic-slice_bitcast_fusion.3), channel_id=1, source_target_pairs={{0,16},{4,20},{8,24},{12,28},{16,0},{20,4},{24,8},{28,12},{1,17},{... | collective-permute-start | bytes 393224 | tf_op jit(solution)/shard_map/ppermute | solution.py:15
  15.7 1.6 %collective-permute-start.5 = (f32[4,32,256]{2,1,0:T(8,128)S(1)}, f32[4,32,256]{2,1,0:T(8,128)S(1)}, u32[]{:S(2)}, u32[]{:S(2)}) collective-permute-start(f32[4,32,256]{2,1,0:T(8,128)S(1)} %dynamic-slice_bitcast_fusion.2), channel_id=1, source_target_pairs={{0,8},{4,12},{8,0},{12,4},{16,24},{20,28},{24,16},{28,20},{1,9},{5... | collective-permute-start | bytes 393224 | tf_op jit(solution)/shard_map/ppermute | solution.py:15
  17.3 1.6 %collective-permute-done.2 = f32[4,32,256]{2,1,0:T(8,128)S(1)} collective-permute-done((f32[4,32,256]{2,1,0:T(8,128)S(1)}, f32[4,32,256]{2,1,0:T(8,128)S(1)}, u32[]{:S(2)}, u32[]{:S(2)}) %collective-permute-start.2) | collective-permute-done | bytes 131104 | tf_op jit(solution)/shard_map/ppermute | solution.py:15
  18.9 1.8 %collective-permute-done.5 = f32[4,32,256]{2,1,0:T(8,128)S(1)} collective-permute-done((f32[4,32,256]{2,1,0:T(8,128)S(1)}, f32[4,32,256]{2,1,0:T(8,128)S(1)}, u32[]{:S(2)}, u32[]{:S(2)}) %collective-permute-start.5) | collective-permute-done | bytes 131104 | tf_op jit(solution)/shard_map/ppermute | solution.py:15
  21.1 11.8 %all_to_all.32 = f32[4,8,2048]{2,1,0:T(8,128)S(1)} all-to-all(f32[4,8,2048]{2,1,0:T(8,128)S(1)} %copy.40), channel_id=1, replica_groups=mesh['dp'=8,'shard'=4] {'shard'}, dimensions={0} | all-to-all | bytes 524288 | tf_op jit(solution)/shard_map/all_to_all | solution.py:68
  33.4 13.2 %all_to_all.33 = f32[32,1,2048]{2,1,0:T(1,128)S(1)} all-to-all(f32[32,1,2048]{2,1,0:T(1,128)S(1)} %copy.41), channel_id=1, replica_groups=mesh['dp'=8,'shard'=4] {'dp','shard'}, dimensions={0} | all-to-all | bytes 524288 | tf_op jit(solution)/shard_map/all_to_all | solution.py:74
  46.6 0.6 reduce
  47.3 0.6 fusion.10
  47.9 0.6 fusion.7
  48.5 0.6 fusion.5
  49.1 0.6 convolution_bitcast_fusion.1
  49.9 1.0 all_to_all.27
  50.8 2.7 %all-to-all-start.2 = ((f32[32,1,2048]{2,1,0:T(1,128)}), f32[32,1,2048]{2,1,0:T(1,128)S(1)}, u32[]{:S(2)}, u32[]{:S(2)}) async-start(f32[32,1,2048]{2,1,0:T(1,128)} %all_to_all.27), calls=%async_computation.2 | async-start | bytes 524288 | tf_op jit(solution)/shard_map/all_to_all | solution.py:92
  53.6 10.1 %all-to-all-done.2 = f32[32,1,2048]{2,1,0:T(1,128)S(1)} async-done(((f32[32,1,2048]{2,1,0:T(1,128)}), f32[32,1,2048]{2,1,0:T(1,128)S(1)}, u32[]{:S(2)}, u32[]{:S(2)}) %all-to-all-start.2) | async-done | bytes 262176 | tf_op jit(solution)/shard_map/all_to_all | solution.py:92
  64.1 12.1 %all_to_all.34 = f32[4,8,2048]{2,1,0:T(8,128)S(1)} all-to-all(f32[4,8,2048]{2,1,0:T(8,128)S(1)} %fusion.1), channel_id=1, replica_groups=mesh['dp'=8,'shard'=4] {'shard'}, dimensions={0} | all-to-all | bytes 524288 | tf_op jit(solution)/shard_map/all_to_all | solution.py:96
  76.6 1.0 %collective-permute-start.6 = (f32[4,32,256]{2,1,0:T(8,128)S(1)}, f32[4,32,256]{2,1,0:T(8,128)S(1)}, u32[]{:S(2)}, u32[]{:S(2)}) collective-permute-start(f32[4,32,256]{2,1,0:T(8,128)S(1)} %get-tuple-element.21), channel_id=1, source_target_pairs={{0,16},{4,20},{8,24},{12,28},{16,0},{20,4},{24,8},{28,12},{1,17},{... | collective-permute-start | bytes 393224 | tf_op jit(solution)/shard_map/ppermute | solution.py:15
  77.6 0.5 collective-permute-start.9
  78.1 3.5 %collective-permute-done.6 = f32[4,32,256]{2,1,0:T(8,128)S(1)} collective-permute-done((f32[4,32,256]{2,1,0:T(8,128)S(1)}, f32[4,32,256]{2,1,0:T(8,128)S(1)}, u32[]{:S(2)}, u32[]{:S(2)}) %collective-permute-start.6) | collective-permute-done | bytes 131104 | tf_op jit(solution)/shard_map/ppermute | solution.py:15
  81.6 2.0 %collective-permute-done.9 = f32[4,32,256]{2,1,0:T(8,128)S(1)} collective-permute-done((f32[4,32,256]{2,1,0:T(8,128)S(1)}, f32[4,32,256]{2,1,0:T(8,128)S(1)}, u32[]{:S(2)}, u32[]{:S(2)}) %collective-permute-start.9) | collective-permute-done | bytes 131104 | tf_op jit(solution)/shard_map/ppermute | solution.py:15
  83.7 0.6 collective-permute-start.7
  84.3 1.5 %collective-permute-start.10 = (f32[4,2,32,256]{3,2,0,1:T(8,128)S(1)}, f32[4,2,32,256]{3,2,0,1:T(8,128)S(1)}, u32[]{:S(2)}, u32[]{:S(2)}) collective-permute-start(f32[4,2,32,256]{3,2,0,1:T(8,128)S(1)} %pad_maximum_fusion.4), channel_id=1, source_target_pairs={{0,16},{4,20},{8,24},{12,28},{16,0},{20,4},{24,8},{28,12},{1,17},{... | collective-permute-start | bytes 786440 | tf_op jit(solution)/shard_map/ppermute | solution.py:15
  85.8 4.3 %collective-permute-done.7 = f32[4,2,32,256]{3,2,0,1:T(8,128)S(1)} collective-permute-done((f32[4,2,32,256]{3,2,0,1:T(8,128)S(1)}, f32[4,2,32,256]{3,2,0,1:T(8,128)S(1)}, u32[]{:S(2)}, u32[]{:S(2)}) %collective-permute-start.7) | collective-permute-done | bytes 262176 | tf_op jit(solution)/shard_map/ppermute | solution.py:15
  90.8 0.8 pad_maximum_fusion.1
  91.7 0.7 compare_reduce_fusion
  92.3 2.5 %fusion.4 = (f32[1,1,1,256,256]{4,3,2,1,0:T(8,128)}, f32[1,1,1,256,256]{4,3,2,1,0:T(8,128)}) fusion(f32[1,1,1,256,256]{4,3,2,1,0:T(8,128)} %param.12, f32[256,256]{1,0:T(8,128)S(1)} %fusion.7, pred[]{:T(512)} %compare_reduce_fusion, f32[1,1,1,256,256]{4,3,2,1,0:T(8,128)} %param.11), kind=kLoop, calls=%fused_computation.23 | loop fusion | flops 589824 | bytes 1310721 | tf_op jit(solution)/shard_map/broadcast_in_dim | solution.py:113
  95.4 1.6 %copy.46 = f32[8,2,2,2,32,256]{5,4,3,2,1,0:T(8,128)} copy(f32[8,2,2,2,32,256]{5,4,0,2,1,3:T(8,128)S(1)} %maximum_maximum_fusion) | data formatting | bytes 4194304 | tf_op jit(solution)/shard_map/concatenate | solution.py:101
  (54 shorter events, 3.6 us)
Async XLA Ops:
  0.6 47.3 %copy-start = (f32[1,1,1,256,256]{4,3,2,1,0:T(8,128)S(1)}, f32[1,1,1,256,256]{4,3,2,1,0:T(8,128)}, u32[]{:S(2)}) copy-start(f32[1,1,1,256,256]{4,3,2,1,0:T(8,128)} %param.10) | copy-start | bytes 786436
  2.0 2.1 %collective-permute-start = (f32[4,2,2,32,256]{4,3,2,1,0:T(8,128)S(1)}, f32[4,2,2,32,256]{4,3,2,1,0:T(8,128)S(1)}, u32[]{:S(2)}, u32[]{:S(2)}) collective-permute-start(f32[4,2,2,32,256]{4,3,2,1,0:T(8,128)S(1)} %bitcast_convert_fusion.1), channel_id=1, source_target_pairs={{0,4},{4,0},{8,12},{12,8},{16,20},{20,16},{24,28},{28,24},{1,5},{5... | collective-permute-start | bytes 1572872 | tf_op jit(solution)/shard_map/ppermute | solution.py:15
  2.6 4.5 %collective-permute-start.3 = (f32[4,2,2,32,256]{4,3,2,1,0:T(8,128)S(1)}, f32[4,2,2,32,256]{4,3,2,1,0:T(8,128)S(1)}, u32[]{:S(2)}, u32[]{:S(2)}) collective-permute-start(f32[4,2,2,32,256]{4,3,2,1,0:T(8,128)S(1)} %bitcast_convert_fusion), channel_id=1, source_target_pairs={{0,4},{4,0},{8,12},{12,8},{16,20},{20,16},{24,28},{28,24},{1,5},{5... | collective-permute-start | bytes 1572872 | tf_op jit(solution)/shard_map/ppermute | solution.py:15
  4.2 9.5 %collective-permute-start.1 = (f32[4,2,32,256]{3,2,1,0:T(8,128)S(1)}, f32[4,2,32,256]{3,2,1,0:T(8,128)S(1)}, u32[]{:S(2)}, u32[]{:S(2)}) collective-permute-start(f32[4,2,32,256]{3,2,1,0:T(8,128)S(1)} %dynamic-slice_bitcast_fusion.1), channel_id=1, source_target_pairs={{0,8},{4,12},{8,0},{12,4},{16,24},{20,28},{24,16},{28,20},{1,9},{5... | collective-permute-start | bytes 786440 | tf_op jit(solution)/shard_map/ppermute | solution.py:15
  7.2 8.4 %collective-permute-start.4 = (f32[4,2,32,256]{3,2,1,0:T(8,128)S(1)}, f32[4,2,32,256]{3,2,1,0:T(8,128)S(1)}, u32[]{:S(2)}, u32[]{:S(2)}) collective-permute-start(f32[4,2,32,256]{3,2,1,0:T(8,128)S(1)} %dynamic-slice_bitcast_fusion), channel_id=1, source_target_pairs={{0,16},{4,20},{8,24},{12,28},{16,0},{20,4},{24,8},{28,12},{1,17},{... | collective-permute-start | bytes 786440 | tf_op jit(solution)/shard_map/ppermute | solution.py:15
  13.8 19.1 %copy-start.5 = (s32[32]{0:T(128)S(1)}, s32[32]{0:T(128)}, u32[]{:S(2)}) copy-start(s32[32]{0:T(128)} %param.13) | copy-start | bytes 388
  13.8 5.1 %collective-permute-start.2 = (f32[4,32,256]{2,1,0:T(8,128)S(1)}, f32[4,32,256]{2,1,0:T(8,128)S(1)}, u32[]{:S(2)}, u32[]{:S(2)}) collective-permute-start(f32[4,32,256]{2,1,0:T(8,128)S(1)} %dynamic-slice_bitcast_fusion.3), channel_id=1, source_target_pairs={{0,16},{4,20},{8,24},{12,28},{16,0},{20,4},{24,8},{28,12},{1,17},{... | collective-permute-start | bytes 393224 | tf_op jit(solution)/shard_map/ppermute | solution.py:15
  15.7 5.0 %collective-permute-start.5 = (f32[4,32,256]{2,1,0:T(8,128)S(1)}, f32[4,32,256]{2,1,0:T(8,128)S(1)}, u32[]{:S(2)}, u32[]{:S(2)}) collective-permute-start(f32[4,32,256]{2,1,0:T(8,128)S(1)} %dynamic-slice_bitcast_fusion.2), channel_id=1, source_target_pairs={{0,8},{4,12},{8,0},{12,4},{16,24},{20,28},{24,16},{28,20},{1,9},{5... | collective-permute-start | bytes 393224 | tf_op jit(solution)/shard_map/ppermute | solution.py:15
  20.8 26.5 %copy-start.1 = (f32[1,1,1,256,256]{4,3,2,1,0:T(8,128)S(1)}, f32[1,1,1,256,256]{4,3,2,1,0:T(8,128)}, u32[]{:S(2)}) copy-start(f32[1,1,1,256,256]{4,3,2,1,0:T(8,128)} %param.9) | copy-start | bytes 786436
  32.9 15.6 %copy-start.3 = (f32[1,1,1,256,256]{4,3,2,1,0:T(8,128)S(1)}, f32[1,1,1,256,256]{4,3,2,1,0:T(8,128)}, u32[]{:S(2)}) copy-start(f32[1,1,1,256,256]{4,3,2,1,0:T(8,128)} %param.11) | copy-start | bytes 786436
  32.9 15.6 %copy-start.4 = (f32[1,1,1,256,256]{4,3,2,1,0:T(8,128)S(1)}, f32[1,1,1,256,256]{4,3,2,1,0:T(8,128)}, u32[]{:S(2)}) copy-start(f32[1,1,1,256,256]{4,3,2,1,0:T(8,128)} %param.12) | copy-start | bytes 786436
  49.1 27.4 %copy-start.2 = (f32[8,32,256]{2,1,0:T(8,128)S(1)}, f32[8,32,256]{2,1,0:T(8,128)}, u32[]{:S(2)}) copy-start(f32[8,32,256]{2,1,0:T(8,128)} %param.8) | copy-start | bytes 786436
  50.8 12.9 %all-to-all-start.2 = ((f32[32,1,2048]{2,1,0:T(1,128)}), f32[32,1,2048]{2,1,0:T(1,128)S(1)}, u32[]{:S(2)}, u32[]{:S(2)}) async-start(f32[32,1,2048]{2,1,0:T(1,128)} %all_to_all.27), calls=%async_computation.2 | async-start | bytes 524288 | tf_op jit(solution)/shard_map/all_to_all | solution.py:92
  76.6 5.0 %collective-permute-start.6 = (f32[4,32,256]{2,1,0:T(8,128)S(1)}, f32[4,32,256]{2,1,0:T(8,128)S(1)}, u32[]{:S(2)}, u32[]{:S(2)}) collective-permute-start(f32[4,32,256]{2,1,0:T(8,128)S(1)} %get-tuple-element.21), channel_id=1, source_target_pairs={{0,16},{4,20},{8,24},{12,28},{16,0},{20,4},{24,8},{28,12},{1,17},{... | collective-permute-start | bytes 393224 | tf_op jit(solution)/shard_map/ppermute | solution.py:15
  77.6 6.0 %collective-permute-start.9 = (f32[4,32,256]{2,1,0:T(8,128)S(1)}, f32[4,32,256]{2,1,0:T(8,128)S(1)}, u32[]{:S(2)}, u32[]{:S(2)}) collective-permute-start(f32[4,32,256]{2,1,0:T(8,128)S(1)} %get-tuple-element.22), channel_id=1, source_target_pairs={{0,8},{4,12},{8,0},{12,4},{16,24},{20,28},{24,16},{28,20},{1,9},{5... | collective-permute-start | bytes 393224 | tf_op jit(solution)/shard_map/ppermute | solution.py:15
  83.7 6.4 %collective-permute-start.7 = (f32[4,2,32,256]{3,2,0,1:T(8,128)S(1)}, f32[4,2,32,256]{3,2,0,1:T(8,128)S(1)}, u32[]{:S(2)}, u32[]{:S(2)}) collective-permute-start(f32[4,2,32,256]{3,2,0,1:T(8,128)S(1)} %pad_maximum_fusion.3), channel_id=1, source_target_pairs={{0,8},{4,12},{8,0},{12,4},{16,24},{20,28},{24,16},{28,20},{1,9},{5... | collective-permute-start | bytes 786440 | tf_op jit(solution)/shard_map/ppermute | solution.py:15
  84.3 6.4 %collective-permute-start.10 = (f32[4,2,32,256]{3,2,0,1:T(8,128)S(1)}, f32[4,2,32,256]{3,2,0,1:T(8,128)S(1)}, u32[]{:S(2)}, u32[]{:S(2)}) collective-permute-start(f32[4,2,32,256]{3,2,0,1:T(8,128)S(1)} %pad_maximum_fusion.4), channel_id=1, source_target_pairs={{0,16},{4,20},{8,24},{12,28},{16,0},{20,4},{24,8},{28,12},{1,17},{... | collective-permute-start | bytes 786440 | tf_op jit(solution)/shard_map/ppermute | solution.py:15
  90.2 4.7 %collective-permute-start.8 = (f32[4,2,2,32,256]{4,3,0,2,1:T(8,128)S(1)}, f32[4,2,2,32,256]{4,3,0,2,1:T(8,128)S(1)}, u32[]{:S(2)}, u32[]{:S(2)}) collective-permute-start(f32[4,2,2,32,256]{4,3,0,2,1:T(8,128)S(1)} %pad_maximum_fusion), channel_id=1, source_target_pairs={{0,4},{4,0},{8,12},{12,8},{16,20},{20,16},{24,28},{28,24},{1,5},{5... | collective-permute-start | bytes 1572872 | tf_op jit(solution)/shard_map/ppermute | solution.py:15
  91.7 3.3 %collective-permute-start.11 = (f32[4,2,2,32,256]{4,3,0,2,1:T(8,128)}, f32[4,2,2,32,256]{4,3,0,2,1:T(8,128)S(1)}, u32[]{:S(2)}, u32[]{:S(2)}) collective-permute-start(f32[4,2,2,32,256]{4,3,0,2,1:T(8,128)} %pad_maximum_fusion.1), channel_id=1, source_target_pairs={{0,4},{4,0},{8,12},{12,8},{16,20},{20,16},{24,28},{28,24},{1,5},{5... | collective-permute-start | bytes 1572872 | tf_op jit(solution)/shard_map/ppermute | solution.py:15

commit v2 on v1

--- a/solution.py
+++ b/solution.py
@@ -11,30 +11,31 @@
 step_count = 10
 
 
-def swap(values, axis_size, bit):
-    return lax.ppermute(values, "dp", [(i, i ^ (1 << bit)) for i in range(axis_size)])
+def swap(values, name, mask, what="swap"):
+    with jax.named_scope(what):
+        return lax.ppermute(values, name, [(i, i ^ mask) for i in range(lax.axis_size(name))])
 
 
 def take(values, axis, index):
     return lax.dynamic_index_in_dim(values, index, axis, keepdims=False)
 
 
-def halve(values, axes, bits, me, count):
+def halve(values, axes, bits, me):
     for bit in bits:
         axis = 1 + axes.index(bit)
         mine = (me >> bit) & 1
         away = take(values, axis, 1 - mine).astype(jnp.float32)
         here = take(values, axis, mine).astype(jnp.float32)
-        values = here + swap(away, count, bit)
+        values = here + swap(away, "dp", 1 << bit)
         axes = [a for a in axes if a != bit]
     return values
 
 
-def spread(values, bits, me, count):
+def spread(values, bits, me):
     axes = []
     for bit in bits:
         mine = (me >> bit) & 1
-        other = swap(values, count, bit)
+        other = swap(values, "dp", 1 << bit)
         low = jnp.where(mine == 0, values, other)
         high = jnp.where(mine == 0, other, values)
         place = sum(1 for a in axes if a > bit)
@@ -43,7 +44,150 @@
     return values
 
 
-def local(partials, params, left_basis, right_basis, first_moment, second_moment, owner_list):
+def unmix(values, index, axis=0):
+    count = values.shape[axis]
+    lead, tail = values.shape[:axis], values.shape[axis + 1 :]
+    bits = count.bit_length() - 1
+    values = values.reshape(lead + (2,) * bits + tail)
+    for place in range(bits):
+        bit = bits - 1 - place
+        flipped = jnp.flip(values, axis + place)
+        values = jnp.where((index >> bit) & 1 == 1, flipped, values)
+    return values.reshape(lead + (count,) + tail)
+
+
+def adam(left_mat, right_mat, first_old, second_old, whole, precision):
+    partway = jnp.einsum("ia,ij->aj", left_mat, whole, precision=precision)
+    rotated = jnp.einsum("aj,jb->ab", partway, right_mat, precision=precision)
+    first_new = beta_one * first_old + (1.0 - beta_one) * rotated
+    second_new = beta_two * second_old + (1.0 - beta_two) * rotated * rotated
+    correct_one = 1.0 - beta_one**step_count
+    correct_two = 1.0 - beta_two**step_count
+    scaled = first_new / correct_one / (jnp.sqrt(second_new / correct_two) + epsilon)
+    back_rot = jnp.einsum("ab,jb->aj", scaled, right_mat, precision=precision)
+    change = jnp.einsum("ia,aj->ij", left_mat, back_rot, precision=precision)
+    return first_new, second_new, change
+
+
+def shard_exchange(parts):
+    arrived = {k: swap(parts[k], "shard", k, f"shard_{k}") for k in (2, 3, 1)}
+    return [parts[0]] + [arrived[k] for k in (1, 2, 3)]
+
+
+def routed(partials, params, left_basis, right_basis, first_moment, second_moment, owner_list):
+    high = lax.Precision.HIGH
+    core, along_x, along_y, across = 1, 2, 4, 6
+    shard_here = lax.axis_index("shard")
+    data_here = lax.axis_index("dp")
+    shard_count = lax.axis_size("shard")
+    data_count = lax.axis_size("dp")
+    device_total = shard_count * data_count
+    home_count, row_count, width = params.shape
+    half = home_count // 2
+    piece = (row_count // shard_count, width)
+
+    owners = unmix(owner_list.reshape(shard_count, home_count), shard_here).reshape(1, -1)
+    device_ids = jnp.arange(device_total, dtype=jnp.int32)
+    picker = (owners == device_ids[:, None]).astype(jnp.float32)
+
+    chips = data_count // 2
+    grid = partials[0].reshape((home_count, chips, 2, row_count, width))
+    away_rows = take(grid, 2, 1 - (data_here & core))
+    own_rows = take(grid, 2, data_here & core)
+    away_rows, own_rows = lax.optimization_barrier((away_rows, own_rows))
+
+    def rows_of(values, mask):
+        return take(values, 1, (data_here ^ mask) // 2).astype(jnp.float32)
+
+    part = {}
+    for mask in (across, along_x, along_y, 0):
+        total = rows_of(own_rows, mask) + swap(
+            rows_of(away_rows, mask), "dp", core, f"sum_core_{mask}"
+        )
+        part[mask] = lax.optimization_barrier((total[:half], total[half:]))
+        if mask == across:
+            own_rows, part[mask] = lax.optimization_barrier((own_rows, part[mask]))
+    near_y = part[along_y][0] + swap(part[across][0], "dp", along_x, "sum_far_low")
+    near_x = part[along_x][1] + swap(part[across][1], "dp", along_y, "sum_far_top")
+    low = part[0][0] + swap(part[along_x][0], "dp", along_x, "sum_x_low")
+    top = part[0][1] + swap(part[along_y][1], "dp", along_y, "sum_y_top")
+    low, top = lax.optimization_barrier((low, top))
+    low = low + swap(near_y, "dp", along_y, "sum_relay_low")
+    top = top + swap(near_x, "dp", along_x, "sum_relay_top")
+
+    summed = jnp.concatenate([low, top], axis=0)
+    summed = summed.reshape((home_count, shard_count) + piece)
+    mixed = shard_exchange([take(summed, 1, shard_here ^ k) for k in range(shard_count)])
+    pieces = jnp.concatenate(mixed, axis=0).reshape(device_total, -1)
+    leaving = jnp.einsum("eb,bn->en", picker, pieces, precision=high)
+    whole = lax.all_to_all(
+        leaving.reshape((device_total,) + piece),
+        ("dp", "shard"),
+        split_axis=0,
+        concat_axis=0,
+        tiled=True,
+    ).reshape(width, width)
+
+    first_new, second_new, change = adam(
+        left_basis[0, 0, 0],
+        right_basis[0, 0, 0],
+        first_moment[0, 0, 0],
+        second_moment[0, 0, 0],
+        whole,
+        high,
+    )
+
+    coming = lax.all_to_all(
+        change.reshape((device_total,) + piece),
+        ("dp", "shard"),
+        split_axis=0,
+        concat_axis=0,
+        tiled=True,
+    ).reshape(device_total, -1)
+    back = jnp.einsum("eb,en->bn", picker, coming, precision=high)
+    back = back.reshape((shard_count, home_count) + piece)
+    new_home = params
+    returned = shard_exchange([back[k] for k in range(shard_count)])
+    for k in (0, 3, 2, 1):
+        start = (shard_here ^ k) * piece[0]
+        home = lax.dynamic_slice_in_dim(params, start, piece[0], axis=1)
+        home = home - learn_rate * (returned[k] + decay_rate * home)
+        new_home = lax.dynamic_update_slice_in_dim(new_home, home, start, axis=1)
+
+    low, top = new_home[:half], new_home[half:]
+    x_top = swap(top, "dp", along_x, "rows_x_top")
+    y_low = swap(low, "dp", along_y, "rows_y_low")
+    other = swap(new_home, "dp", core, "rows_core_own")
+    x_low = swap(low, "dp", along_x, "rows_x_low")
+    y_top = swap(top, "dp", along_y, "rows_y_top")
+    far_top = swap(x_top, "dp", along_y, "rows_relay_top")
+    far_low = swap(y_low, "dp", along_x, "rows_relay_low")
+    x_rows = jnp.concatenate([x_low, x_top], axis=0)
+    y_rows = jnp.concatenate([y_top, y_low], axis=0)
+    x_rows, y_rows, first_new, second_new = lax.optimization_barrier(
+        (x_rows, y_rows, first_new, second_new)
+    )
+    far_rows = jnp.concatenate([far_low, far_top], axis=0)
+    y_other = swap(y_rows, "dp", core, "rows_core_y")
+    updated = jnp.zeros((home_count, width, width), jnp.float32)
+    for mask, block, values in (
+        (0, 0, new_home),
+        (core, 0, other),
+        (along_x, 0, x_rows),
+        (along_y, half, y_rows[:half]),
+        (along_y, 0, y_rows[half:]),
+        (along_x ^ core, 0, swap(x_rows, "dp", core, "rows_core_x")),
+        (along_y ^ core, half, y_other[:half]),
+        (along_y ^ core, 0, y_other[half:]),
+        (across, 0, far_rows),
+        (across ^ core, 0, swap(far_rows, "dp", core, "rows_core_far")),
+    ):
+        start = (data_here ^ mask) * row_count
+        updated = lax.dynamic_update_slice(updated, values, (block, start, 0))
+    return updated, first_new[None, None, None], second_new[None, None, None]
+
+
+def gathered(partials, params, left_basis, right_basis, first_moment, second_moment, owner_list):
     highest = lax.Precision.HIGHEST
     shard_here = lax.axis_index("shard")
     data_here = lax.axis_index("dp")
@@ -57,9 +201,9 @@
     middle = home_count // 2
 
     grid = partials[0].reshape((home_count,) + (2,) * bit_count + (row_count, width))
-    low_first = halve(grid[:middle], high_low, list(range(bit_count)), data_here, data_count)
+    low_first = halve(grid[:middle], high_low, list(range(bit_count)), data_here)
     high_first = halve(
-        grid[middle:], high_low, [0] + list(range(1, bit_count))[::-1], data_here, data_count
+        grid[middle:], high_low, [0] + list(range(1, bit_count))[::-1], data_here
     )
     summed = jnp.concatenate([low_first, high_first], axis=0)
 
@@ -79,15 +223,9 @@
     right_mat = right_basis[0, 0, 0]
     first_old = first_moment[0, 0, 0]
     second_old = second_moment[0, 0, 0]
-    partway = jnp.einsum("ia,ij->aj", left_mat, whole, precision=highest)
-    rotated = jnp.einsum("aj,jb->ab", partway, right_mat, precision=highest)
-    first_new = beta_one * first_old + (1.0 - beta_one) * rotated
-    second_new = beta_two * second_old + (1.0 - beta_two) * rotated * rotated
-    correct_one = 1.0 - beta_one**step_count
-    correct_two = 1.0 - beta_two**step_count
-    scaled = first_new / correct_one / (jnp.sqrt(second_new / correct_two) + epsilon)
-    back_rot = jnp.einsum("ab,jb->aj", scaled, right_mat, precision=highest)
-    change = jnp.einsum("ia,aj->ij", left_mat, back_rot, precision=highest)
+    first_new, second_new, change = adam(
+        left_mat, right_mat, first_old, second_old, whole, highest
+    )
 
     coming = lax.all_to_all(
         change.reshape(device_total, piece), ("dp", "shard"), split_axis=0, concat_axis=0, tiled=True
@@ -100,8 +238,8 @@
     new_home = params - learn_rate * (returned + decay_rate * params)
     updated = jnp.concatenate(
         [
-            spread(new_home[:middle], high_low, data_here, data_count),
-            spread(new_home[middle:], list(range(1, bit_count)) + [0], data_here, data_count),
+            spread(new_home[:middle], high_low, data_here),
+            spread(new_home[middle:], list(range(1, bit_count)) + [0], data_here),
         ],
         axis=0,
     ).reshape(home_count, width, width)
@@ -111,6 +249,16 @@
     first_keep = jnp.where(live, first_new, first_old)
     second_keep = jnp.where(live, second_new, second_old)
     return (updated, first_keep[None, None, None], second_keep[None, None, None])
+
+
+def local(partials, params, left_basis, right_basis, first_moment, second_moment, owner_list):
+    shard_count, data_count = lax.axis_size("shard"), lax.axis_size("dp")
+    plain = (data_count, shard_count) != (8, 4) or params.shape[1] % (8 * shard_count) != 0
+    plain = plain or owner_list.shape[0] != shard_count * data_count or params.shape[0] % 2 != 0
+    form = gathered if plain else routed
+    return form(
+        partials, params, left_basis, right_basis, first_moment, second_moment, owner_list
+    )
 
 
 def solution(mesh):

time: 97.3 us -> 86.5 us (0.89)
  blocking collectives: 37 us -> 13.3 us
  starting transfers between devices: 15 us -> 28 us
  waiting for transfers between devices: 30.1 us -> 36.7 us
  other arithmetic: 5.72 us -> 0.52 us
  local copies, waits for them, and re-layouts: 5.12 us -> 3.82 us
    all_to_all x3 -> x1, blocking collectives: 37 us -> 13.3 us  [routed(): lax.all_to_all(leaving.reshape((device_total,) + piece), ('dp', 'shard'),...]
    ppermute x12 -> x26, starting transfers between devices: 12.3 us -> 25.3 us  [swap(): lax.ppermute(values, name, [(i, i ^ mask) for i in range(lax.axis_size(na...]
    ppermute x12 -> x26, waiting for transfers between devices: 20 us -> 26.5 us  [swap(): lax.ppermute(values, name, [(i, i ^ mask) for i in range(lax.axis_size(na...]
    broadcast_in_dim x1 -> x0, other arithmetic: 2.53 us -> none  [local(): second_keep[None, None, None]]
    concatenate x1, local copies, waits for them, and re-layouts: 1.57 us -> 0.01 us  [routed(): far_rows = jnp.concatenate([far_low, far_top], axis=0)]
    unnamed x12 -> x27, local copies, waits for them, and re-layouts: 0.04 us -> 1.59 us
    another operation x9 -> x0, other arithmetic: 1.26 us -> none  [spread(): values = jnp.stack([low, high], axis=1 + place)]
    all_to_all x2 -> x0, local copies, waits for them, and re-layouts: 1.24 us -> none  [the longest x1 0.97 us: local(): lax.all_to_all(change.reshape(device_total, piece), ('dp', 'shard'), spli...]
  transfers between devices with their start and end apart: 13 -> 27, of which waited for: 9 -> 18; matrix products, arithmetic and copies ran while one was open for 5% -> 1% of each run, Pallas kernels for 0% -> 0%
where the time goes in v2:
time: 86.5 us; the launch traced here: 86.3 us
  waiting for transfers between devices  36.7 us (42%)
  starting transfers between devices  28 us (32%)
  blocking collectives  13.3 us (15%)
  local copies, waits for them, and re-layouts  3.82 us (4%)
  matrix products  2.64 us (3%)
  between operations  1.26 us (1%)
    ppermute x26, waiting for transfers between devices, swap(): lax.ppermute(values, name, [(i, i ^ mask) for i in range(lax.axis_size(na...  26.5 us
    ppermute x26, starting transfers between devices, swap(): lax.ppermute(values, name, [(i, i ^ mask) for i in range(lax.axis_size(na...  25.3 us
    all_to_all x1, blocking collectives, routed(): lax.all_to_all(leaving.reshape((device_total,) + piece), ('dp', 'shard'),...  13.3 us
    all_to_all x1, waiting for transfers between devices, routed(): lax.all_to_all(change.reshape((device_total,) + piece), ('dp', 'shard'),...  10.2 us
    all_to_all x1, starting transfers between devices, routed(): lax.all_to_all(change.reshape((device_total,) + piece), ('dp', 'shard'),...  2.72 us
  transfers between devices with their start and end apart: 27, of which 18 were waited for; matrix products, arithmetic and copies ran while one was open for 1% of the time, Pallas kernels for 0%

profile of v2, /device:TPU:0, one launch (start us, length us, event | category | flops | bytes accessed | tf_op | source)
XLA Modules:
  0.0 86.3 jit_solution(8276255379956394592)
XLA Ops:
  0.7 1.3 %dynamic-slice_bitcast_fusion = (bf16[8,4,32,256]{3,2,1,0:T(8,128)(2,1)S(1)}, bf16[8,4,32,256]{3,2,1,0:T(8,128)(2,1)S(1)}) fusion(bf16[8,4,2,32,256]{4,3,2,1,0:T(8,128)(2,1)} %bitcast.98, s32[]{:T(128)S(6)} %select_n.117, s32[]{:T(128)S(6)} %select_n.116), kind=kLoop, calls=%fused_computation.1 | loop fusion | bytes 2097160 | tf_op jit(solution)/shard_map/jit(dynamic_index_in_dim)/squeeze | solution.py:20
  3.9 3.0 %collective-permute-start.8 = (f32[4,32,256]{2,1,0:T(8,128)S(1)}, f32[4,32,256]{2,1,0:T(8,128)S(1)}, u32[]{:S(2)}, u32[]{:S(2)}) collective-permute-start(f32[4,32,256]{2,1,0:T(8,128)S(1)} %get-tuple-element.36), channel_id=1, source_target_pairs={{0,16},{4,20},{8,24},{12,28},{16,0},{20,4},{24,8},{28,12},{1,17},{... | collective-permute-start | bytes 393224 | tf_op jit(solution)/shard_map/sum_far_top/ppermute | solution.py:16
  6.8 1.5 %collective-permute-start.6 = (f32[4,32,256]{2,1,0:T(8,128)S(1)}, f32[4,32,256]{2,1,0:T(8,128)S(1)}, u32[]{:S(2)}, u32[]{:S(2)}) collective-permute-start(f32[4,32,256]{2,1,0:T(8,128)S(1)} %get-tuple-element.33), channel_id=1, source_target_pairs={{0,8},{4,12},{8,0},{12,4},{16,24},{20,28},{24,16},{28,20},{1,9},{5... | collective-permute-start | bytes 393224 | tf_op jit(solution)/shard_map/sum_far_low/ppermute | solution.py:16
  9.6 1.1 %collective-permute-done.8 = f32[4,32,256]{2,1,0:T(8,128)S(1)} collective-permute-done((f32[4,32,256]{2,1,0:T(8,128)S(1)}, f32[4,32,256]{2,1,0:T(8,128)S(1)}, u32[]{:S(2)}, u32[]{:S(2)}) %collective-permute-start.8) | collective-permute-done | bytes 131104 | tf_op jit(solution)/shard_map/sum_far_top/ppermute | solution.py:16
  10.7 1.8 %collective-permute-start.9 = (f32[4,32,256]{2,1,0:T(8,128)S(1)}, f32[4,32,256]{2,1,0:T(8,128)S(1)}, u32[]{:S(2)}, u32[]{:S(2)}) collective-permute-start(f32[4,32,256]{2,1,0:T(8,128)S(1)} %add.153), channel_id=1, source_target_pairs={{0,8},{4,12},{8,0},{12,4},{16,24},{20,28},{24,16},{28,20},{1,9},{5... | collective-permute-start | bytes 393224 | tf_op jit(solution)/shard_map/sum_relay_top/ppermute | solution.py:16
  13.2 1.6 %collective-permute-start.7 = (f32[4,32,256]{2,1,0:T(8,128)S(1)}, f32[4,32,256]{2,1,0:T(8,128)S(1)}, u32[]{:S(2)}, u32[]{:S(2)}) collective-permute-start(f32[4,32,256]{2,1,0:T(8,128)S(1)} %add.151), channel_id=1, source_target_pairs={{0,16},{4,20},{8,24},{12,28},{16,0},{20,4},{24,8},{28,12},{1,17},{... | collective-permute-start | bytes 393224 | tf_op jit(solution)/shard_map/sum_relay_low/ppermute | solution.py:16
  14.9 1.2 %collective-permute-done.3 = f32[4,32,256]{2,1,0:T(8,128)S(1)} collective-permute-done((f32[4,32,256]{2,1,0:T(8,128)S(1)}, f32[4,32,256]{2,1,0:T(8,128)S(1)}, u32[]{:S(2)}, u32[]{:S(2)}) %collective-permute-start.3) | collective-permute-done | bytes 131104 | tf_op jit(solution)/shard_map/sum_x_low/ppermute | solution.py:16
  16.1 1.6 %collective-permute-done.9 = f32[4,32,256]{2,1,0:T(8,128)S(1)} collective-permute-done((f32[4,32,256]{2,1,0:T(8,128)S(1)}, f32[4,32,256]{2,1,0:T(8,128)S(1)}, u32[]{:S(2)}, u32[]{:S(2)}) %collective-permute-start.9) | collective-permute-done | bytes 131104 | tf_op jit(solution)/shard_map/sum_relay_top/ppermute | solution.py:16
  18.4 3.7 %collective-permute-start.12 = (f32[8,8,256]{2,1,0:T(8,128)S(1)}, f32[8,8,256]{2,1,0:T(8,128)S(1)}, u32[]{:S(2)}, u32[]{:S(2)}) collective-permute-start(f32[8,8,256]{2,1,0:T(8,128)S(1)} %get-tuple-element.60), channel_id=1, source_target_pairs={{0,3},{1,2},{2,1},{3,0},{4,7},{5,6},{6,5},{7,4},{8,11},{9,10},{10,... | collective-permute-start | bytes 196616 | tf_op jit(solution)/shard_map/shard_3/ppermute | solution.py:16
  22.1 0.8 collective-permute-start.10
  23.0 1.6 %collective-permute-done.12 = f32[8,8,256]{2,1,0:T(8,128)S(1)} collective-permute-done((f32[8,8,256]{2,1,0:T(8,128)S(1)}, f32[8,8,256]{2,1,0:T(8,128)S(1)}, u32[]{:S(2)}, u32[]{:S(2)}) %collective-permute-start.12) | collective-permute-done | bytes 65568 | tf_op jit(solution)/shard_map/shard_3/ppermute | solution.py:16
  24.5 2.7 %collective-permute-done.11 = f32[8,8,256]{2,1,0:T(8,128)S(1)} collective-permute-done((f32[8,8,256]{2,1,0:T(8,128)S(1)}, f32[8,8,256]{2,1,0:T(8,128)S(1)}, u32[]{:S(2)}, u32[]{:S(2)}) %collective-permute-start.11) | collective-permute-done | bytes 65568 | tf_op jit(solution)/shard_map/shard_2/ppermute | solution.py:16
  27.7 13.3 %all_to_all.10 = f32[32,8,256]{2,1,0:T(8,128)S(1)} all-to-all(f32[32,8,256]{2,1,0:T(8,128)S(1)} %copy.55), channel_id=1, replica_groups=mesh['dp'=8,'shard'=4] {'dp','shard'}, dimensions={0} | all-to-all | bytes 524288 | tf_op jit(solution)/shard_map/all_to_all | solution.py:123
  42.3 1.0 %convolution_bitcast_fusion = f32[32,8,256]{2,1,0:T(8,128)} fusion(f32[256,256]{1,0:T(8,128)S(1)} %fusion.4, f32[1,1,1,256,256]{4,3,2,1,0:T(8,128)S(1)} %copy-done.4), kind=kOutput, calls=%fused_computation | convolution fusion | flops 100663296 | bytes 786432 | tf_op jit(solution)/shard_map/ia,aj->ij/dot_general | solution.py:68
  43.3 2.7 %all-to-all-start.1 = ((f32[32,8,256]{2,1,0:T(8,128)}), f32[32,8,256]{2,1,0:T(8,128)S(1)}, u32[]{:S(2)}, u32[]{:S(2)}) async-start(f32[32,8,256]{2,1,0:T(8,128)} %convolution_bitcast_fusion), calls=%async_computation.1 | async-start | bytes 524288 | tf_op jit(solution)/shard_map/all_to_all | solution.py:140
  46.0 10.2 %all-to-all-done.1 = f32[32,8,256]{2,1,0:T(8,128)S(1)} async-done(((f32[32,8,256]{2,1,0:T(8,128)}), f32[32,8,256]{2,1,0:T(8,128)S(1)}, u32[]{:S(2)}, u32[]{:S(2)}) %all-to-all-start.1) | async-done | bytes 262176 | tf_op jit(solution)/shard_map/all_to_all | solution.py:140
  56.7 1.8 %collective-permute-start.13 = (f32[8,8,256]{2,1,0:T(8,128)S(1)}, f32[8,8,256]{2,1,0:T(8,128)S(1)}, u32[]{:S(2)}, u32[]{:S(2)}) collective-permute-start(f32[8,8,256]{2,1,0:T(8,128)S(1)} %copy.57), channel_id=1, source_target_pairs={{0,3},{1,2},{2,1},{3,0},{4,7},{5,6},{6,5},{7,4},{8,11},{9,10},{10,... | collective-permute-start | bytes 196616 | tf_op jit(solution)/shard_map/shard_3/ppermute | solution.py:16
  58.5 0.9 %collective-permute-start.14 = (f32[8,8,256]{2,1,0:T(8,128)S(1)}, f32[8,8,256]{2,1,0:T(8,128)S(1)}, u32[]{:S(2)}, u32[]{:S(2)}) collective-permute-start(f32[8,8,256]{2,1,0:T(8,128)S(1)} %copy.58), channel_id=1, source_target_pairs={{0,2},{1,3},{2,0},{3,1},{4,6},{5,7},{6,4},{7,5},{8,10},{9,11},{10,... | collective-permute-start | bytes 196616 | tf_op jit(solution)/shard_map/shard_2/ppermute | solution.py:16
  59.4 1.9 %collective-permute-start.15 = (f32[8,8,256]{2,1,0:T(8,128)S(1)}, f32[8,8,256]{2,1,0:T(8,128)S(1)}, u32[]{:S(2)}, u32[]{:S(2)}) collective-permute-start(f32[8,8,256]{2,1,0:T(8,128)S(1)} %copy.59), channel_id=1, source_target_pairs={{0,1},{1,0},{2,3},{3,2},{4,5},{5,4},{6,7},{7,6},{8,9},{9,8},{10,11... | collective-permute-start | bytes 196616 | tf_op jit(solution)/shard_map/shard_1/ppermute | solution.py:16
  61.4 2.2 %collective-permute-done.13 = f32[8,8,256]{2,1,0:T(8,128)S(1)} collective-permute-done((f32[8,8,256]{2,1,0:T(8,128)S(1)}, f32[8,8,256]{2,1,0:T(8,128)S(1)}, u32[]{:S(2)}, u32[]{:S(2)}) %collective-permute-start.13) | collective-permute-done | bytes 65568 | tf_op jit(solution)/shard_map/shard_3/ppermute | solution.py:16
  63.6 2.2 %collective-permute-done.14 = f32[8,8,256]{2,1,0:T(8,128)S(1)} collective-permute-done((f32[8,8,256]{2,1,0:T(8,128)S(1)}, f32[8,8,256]{2,1,0:T(8,128)S(1)}, u32[]{:S(2)}, u32[]{:S(2)}) %collective-permute-start.14) | collective-permute-done | bytes 65568 | tf_op jit(solution)/shard_map/shard_2/ppermute | solution.py:16
  65.8 0.9 %collective-permute-start.18 = (f32[4,32,256]{2,1,0:T(8,128)S(1)}, f32[4,32,256]{2,1,0:T(8,128)S(1)}, u32[]{:S(2)}, u32[]{:S(2)}) collective-permute-start(f32[4,32,256]{2,1,0:T(8,128)S(1)} %get-tuple-element.50), channel_id=1, source_target_pairs={{0,8},{4,12},{8,0},{12,4},{16,24},{20,28},{24,16},{28,20},{1,9},{5... | collective-permute-start | bytes 393224 | tf_op jit(solution)/shard_map/rows_x_top/ppermute | solution.py:16
  66.8 1.1 %collective-permute-start.17 = (f32[4,32,256]{2,1,0:T(8,128)S(1)}, f32[4,32,256]{2,1,0:T(8,128)S(1)}, u32[]{:S(2)}, u32[]{:S(2)}) collective-permute-start(f32[4,32,256]{2,1,0:T(8,128)S(1)} %get-tuple-element.49), channel_id=1, source_target_pairs={{0,8},{4,12},{8,0},{12,4},{16,24},{20,28},{24,16},{28,20},{1,9},{5... | collective-permute-start | bytes 393224 | tf_op jit(solution)/shard_map/rows_x_low/ppermute | solution.py:16
  67.9 0.9 %collective-permute-start.20 = (f32[4,32,256]{2,1,0:T(8,128)S(1)}, f32[4,32,256]{2,1,0:T(8,128)S(1)}, u32[]{:S(2)}, u32[]{:S(2)}) collective-permute-start(f32[4,32,256]{2,1,0:T(8,128)S(1)} %get-tuple-element.49), channel_id=1, source_target_pairs={{0,16},{4,20},{8,24},{12,28},{16,0},{20,4},{24,8},{28,12},{1,17},{... | collective-permute-start | bytes 393224 | tf_op jit(solution)/shard_map/rows_y_low/ppermute | solution.py:16
  68.8 1.1 %collective-permute-start.19 = (f32[4,32,256]{2,1,0:T(8,128)S(1)}, f32[4,32,256]{2,1,0:T(8,128)S(1)}, u32[]{:S(2)}, u32[]{:S(2)}) collective-permute-start(f32[4,32,256]{2,1,0:T(8,128)S(1)} %get-tuple-element.50), channel_id=1, source_target_pairs={{0,16},{4,20},{8,24},{12,28},{16,0},{20,4},{24,8},{28,12},{1,17},{... | collective-permute-start | bytes 393224 | tf_op jit(solution)/shard_map/rows_y_top/ppermute | solution.py:16
  70.2 2.1 %collective-permute-done.18 = f32[4,32,256]{2,1,0:T(8,128)S(1)} collective-permute-done((f32[4,32,256]{2,1,0:T(8,128)S(1)}, f32[4,32,256]{2,1,0:T(8,128)S(1)}, u32[]{:S(2)}, u32[]{:S(2)}) %collective-permute-start.18) | collective-permute-done | bytes 131104 | tf_op jit(solution)/shard_map/rows_x_top/ppermute | solution.py:16
  72.3 1.7 %collective-permute-done.17 = f32[4,32,256]{2,1,0:T(8,128)S(1)} collective-permute-done((f32[4,32,256]{2,1,0:T(8,128)S(1)}, f32[4,32,256]{2,1,0:T(8,128)S(1)}, u32[]{:S(2)}, u32[]{:S(2)}) %collective-permute-start.17) | collective-permute-done | bytes 131104 | tf_op jit(solution)/shard_map/rows_x_low/ppermute | solution.py:16
  74.2 2.4 %collective-permute-done.19 = f32[4,32,256]{2,1,0:T(8,128)S(1)} collective-permute-done((f32[4,32,256]{2,1,0:T(8,128)S(1)}, f32[4,32,256]{2,1,0:T(8,128)S(1)}, u32[]{:S(2)}, u32[]{:S(2)}) %collective-permute-start.19) | collective-permute-done | bytes 131104 | tf_op jit(solution)/shard_map/rows_y_top/ppermute | solution.py:16
  77.2 0.9 %collective-permute-start.23 = (f32[4,32,256]{2,1,0:T(8,128)S(1)}, f32[4,32,256]{2,1,0:T(8,128)S(1)}, u32[]{:S(2)}, u32[]{:S(2)}) collective-permute-start(f32[4,32,256]{2,1,0:T(8,128)S(1)} %collective-permute-done.20), channel_id=1, source_target_pairs={{0,8},{4,12},{8,0},{12,4},{16,24},{20,28},{24,16},{28,20},{1,9},{5... | collective-permute-start | bytes 393224 | tf_op jit(solution)/shard_map/rows_relay_low/ppermute | solution.py:16
  78.8 3.9 %collective-permute-done.23 = f32[4,32,256]{2,1,0:T(8,128)S(1)} collective-permute-done((f32[4,32,256]{2,1,0:T(8,128)S(1)}, f32[4,32,256]{2,1,0:T(8,128)S(1)}, u32[]{:S(2)}, u32[]{:S(2)}) %collective-permute-start.23) | collective-permute-done | bytes 131104 | tf_op jit(solution)/shard_map/rows_relay_low/ppermute | solution.py:16
  83.5 1.4 %collective-permute-done.25 = f32[8,32,256]{2,1,0:T(8,128)S(1)} collective-permute-done((f32[8,32,256]{2,1,0:T(8,128)S(1)}, f32[8,32,256]{2,1,0:T(8,128)S(1)}, u32[]{:S(2)}, u32[]{:S(2)}) %collective-permute-start.25) | collective-permute-done | bytes 262176 | tf_op jit(solution)/shard_map/rows_core_far/ppermute | solution.py:16
  85.0 1.3 %copy-done.3 = f32[8,256,256]{2,1,0:T(8,128)} copy-done((f32[8,256,256]{2,1,0:T(8,128)}, f32[8,256,256]{2,1,0:T(8,128)S(1)}, u32[]{:S(2)}) %copy-start.3) | copy-done | bytes 2097176
  (101 shorter events, 9.3 us)
Async XLA Ops:
  0.6 40.8 %copy-start = (f32[1,1,1,256,256]{4,3,2,1,0:T(8,128)S(1)}, f32[1,1,1,256,256]{4,3,2,1,0:T(8,128)}, u32[]{:S(2)}) copy-start(f32[1,1,1,256,256]{4,3,2,1,0:T(8,128)} %param.10) | copy-start | bytes 786436
  2.1 1.7 %collective-permute-start = (f32[8,32,256]{2,1,0:T(8,128)S(1)}, f32[8,32,256]{2,1,0:T(8,128)S(1)}, u32[]{:S(2)}, u32[]{:S(2)}) collective-permute-start(f32[8,32,256]{2,1,0:T(8,128)S(1)} %get-tuple-element.48), channel_id=1, source_target_pairs={{0,4},{4,0},{8,12},{12,8},{16,20},{20,16},{24,28},{28,24},{1,5},{5... | collective-permute-start | bytes 786440 | tf_op jit(solution)/shard_map/sum_core_6/ppermute | solution.py:16
  2.7 5.7 %collective-permute-start.4 = (f32[8,32,256]{2,1,0:T(8,128)S(1)}, f32[8,32,256]{2,1,0:T(8,128)S(1)}, u32[]{:S(2)}, u32[]{:S(2)}) collective-permute-start(f32[8,32,256]{2,1,0:T(8,128)S(1)} %bitcast_convert_fusion), channel_id=1, source_target_pairs={{0,4},{4,0},{8,12},{12,8},{16,20},{20,16},{24,28},{28,24},{1,5},{5... | collective-permute-start | bytes 786440 | tf_op jit(solution)/shard_map/sum_core_4/ppermute | solution.py:16
  2.8 5.5 %collective-permute-start.2 = (f32[8,32,256]{2,1,0:T(8,128)S(1)}, f32[8,32,256]{2,1,0:T(8,128)S(1)}, u32[]{:S(2)}, u32[]{:S(2)}) collective-permute-start(f32[8,32,256]{2,1,0:T(8,128)S(1)} %get-tuple-element.46), channel_id=1, source_target_pairs={{0,4},{4,0},{8,12},{12,8},{16,20},{20,16},{24,28},{28,24},{1,5},{5... | collective-permute-start | bytes 786440 | tf_op jit(solution)/shard_map/sum_core_2/ppermute | solution.py:16
  3.3 5.1 %collective-permute-start.1 = (f32[8,32,256]{2,1,0:T(8,128)S(1)}, f32[8,32,256]{2,1,0:T(8,128)S(1)}, u32[]{:S(2)}, u32[]{:S(2)}) collective-permute-start(f32[8,32,256]{2,1,0:T(8,128)S(1)} %get-tuple-element.47), channel_id=1, source_target_pairs={{0,4},{4,0},{8,12},{12,8},{16,20},{20,16},{24,28},{28,24},{1,5},{5... | collective-permute-start | bytes 786440 | tf_op jit(solution)/shard_map/sum_core_0/ppermute | solution.py:16
  3.9 6.8 %collective-permute-start.8 = (f32[4,32,256]{2,1,0:T(8,128)S(1)}, f32[4,32,256]{2,1,0:T(8,128)S(1)}, u32[]{:S(2)}, u32[]{:S(2)}) collective-permute-start(f32[4,32,256]{2,1,0:T(8,128)S(1)} %get-tuple-element.36), channel_id=1, source_target_pairs={{0,16},{4,20},{8,24},{12,28},{16,0},{20,4},{24,8},{28,12},{1,17},{... | collective-permute-start | bytes 393224 | tf_op jit(solution)/shard_map/sum_far_top/ppermute | solution.py:16
  6.8 6.4 %collective-permute-start.6 = (f32[4,32,256]{2,1,0:T(8,128)S(1)}, f32[4,32,256]{2,1,0:T(8,128)S(1)}, u32[]{:S(2)}, u32[]{:S(2)}) collective-permute-start(f32[4,32,256]{2,1,0:T(8,128)S(1)} %get-tuple-element.33), channel_id=1, source_target_pairs={{0,8},{4,12},{8,0},{12,4},{16,24},{20,28},{24,16},{28,20},{1,9},{5... | collective-permute-start | bytes 393224 | tf_op jit(solution)/shard_map/sum_far_low/ppermute | solution.py:16
  8.5 7.5 %collective-permute-start.3 = (f32[4,32,256]{2,1,0:T(8,128)S(1)}, f32[4,32,256]{2,1,0:T(8,128)S(1)}, u32[]{:S(2)}, u32[]{:S(2)}) collective-permute-start(f32[4,32,256]{2,1,0:T(8,128)S(1)} %get-tuple-element.28), channel_id=1, source_target_pairs={{0,8},{4,12},{8,0},{12,4},{16,24},{20,28},{24,16},{28,20},{1,9},{5... | collective-permute-start | bytes 393224 | tf_op jit(solution)/shard_map/sum_x_low/ppermute | solution.py:16
  9.1 6.9 %collective-permute-start.5 = (f32[4,32,256]{2,1,0:T(8,128)S(1)}, f32[4,32,256]{2,1,0:T(8,128)S(1)}, u32[]{:S(2)}, u32[]{:S(2)}) collective-permute-start(f32[4,32,256]{2,1,0:T(8,128)S(1)} %get-tuple-element.30), channel_id=1, source_target_pairs={{0,16},{4,20},{8,24},{12,28},{16,0},{20,4},{24,8},{28,12},{1,17},{... | collective-permute-start | bytes 393224 | tf_op jit(solution)/shard_map/sum_y_top/ppermute | solution.py:16
  10.7 7.1 %collective-permute-start.9 = (f32[4,32,256]{2,1,0:T(8,128)S(1)}, f32[4,32,256]{2,1,0:T(8,128)S(1)}, u32[]{:S(2)}, u32[]{:S(2)}) collective-permute-start(f32[4,32,256]{2,1,0:T(8,128)S(1)} %add.153), channel_id=1, source_target_pairs={{0,8},{4,12},{8,0},{12,4},{16,24},{20,28},{24,16},{28,20},{1,9},{5... | collective-permute-start | bytes 393224 | tf_op jit(solution)/shard_map/sum_relay_top/ppermute | solution.py:16
  13.2 5.0 %collective-permute-start.7 = (f32[4,32,256]{2,1,0:T(8,128)S(1)}, f32[4,32,256]{2,1,0:T(8,128)S(1)}, u32[]{:S(2)}, u32[]{:S(2)}) collective-permute-start(f32[4,32,256]{2,1,0:T(8,128)S(1)} %add.151), channel_id=1, source_target_pairs={{0,16},{4,20},{8,24},{12,28},{16,0},{20,4},{24,8},{28,12},{1,17},{... | collective-permute-start | bytes 393224 | tf_op jit(solution)/shard_map/sum_relay_low/ppermute | solution.py:16
  17.7 23.3 %copy-start.4 = (f32[1,1,1,256,256]{4,3,2,1,0:T(8,128)S(1)}, f32[1,1,1,256,256]{4,3,2,1,0:T(8,128)}, u32[]{:S(2)}) copy-start(f32[1,1,1,256,256]{4,3,2,1,0:T(8,128)} %param.9) | copy-start | bytes 786436
  18.3 23.1 %copy-start.5 = (f32[1,1,1,256,256]{4,3,2,1,0:T(8,128)S(1)}, f32[1,1,1,256,256]{4,3,2,1,0:T(8,128)}, u32[]{:S(2)}) copy-start(f32[1,1,1,256,256]{4,3,2,1,0:T(8,128)} %param.11) | copy-start | bytes 786436
  18.3 23.1 %copy-start.6 = (f32[1,1,1,256,256]{4,3,2,1,0:T(8,128)S(1)}, f32[1,1,1,256,256]{4,3,2,1,0:T(8,128)}, u32[]{:S(2)}) copy-start(f32[1,1,1,256,256]{4,3,2,1,0:T(8,128)} %param.12) | copy-start | bytes 786436
  18.4 6.1 %collective-permute-start.12 = (f32[8,8,256]{2,1,0:T(8,128)S(1)}, f32[8,8,256]{2,1,0:T(8,128)S(1)}, u32[]{:S(2)}, u32[]{:S(2)}) collective-permute-start(f32[8,8,256]{2,1,0:T(8,128)S(1)} %get-tuple-element.60), channel_id=1, source_target_pairs={{0,3},{1,2},{2,1},{3,0},{4,7},{5,6},{6,5},{7,4},{8,11},{9,10},{10,... | collective-permute-start | bytes 196616 | tf_op jit(solution)/shard_map/shard_3/ppermute | solution.py:16
  22.0 5.2 %collective-permute-start.11 = (f32[8,8,256]{2,1,0:T(8,128)S(1)}, f32[8,8,256]{2,1,0:T(8,128)S(1)}, u32[]{:S(2)}, u32[]{:S(2)}) collective-permute-start(f32[8,8,256]{2,1,0:T(8,128)S(1)} %get-tuple-element.58), channel_id=1, source_target_pairs={{0,2},{1,3},{2,0},{3,1},{4,6},{5,7},{6,4},{7,5},{8,10},{9,11},{10,... | collective-permute-start | bytes 196616 | tf_op jit(solution)/shard_map/shard_2/ppermute | solution.py:16
  22.1 5.2 %collective-permute-start.10 = (f32[8,8,256]{2,1,0:T(8,128)S(1)}, f32[8,8,256]{2,1,0:T(8,128)S(1)}, u32[]{:S(2)}, u32[]{:S(2)}) collective-permute-start(f32[8,8,256]{2,1,0:T(8,128)S(1)} %get-tuple-element.59), channel_id=1, source_target_pairs={{0,1},{1,0},{2,3},{3,2},{4,5},{5,4},{6,7},{7,6},{8,9},{9,8},{10,11... | collective-permute-start | bytes 196616 | tf_op jit(solution)/shard_map/shard_1/ppermute | solution.py:16
  42.3 21.3 %copy-start.1 = (f32[8,32,256]{2,1,0:T(8,128)S(1)}, f32[8,32,256]{2,1,0:T(8,128)}, u32[]{:S(2)}) copy-start(f32[8,32,256]{2,1,0:T(8,128)} %param.8) | copy-start | bytes 786436
  43.3 12.9 %all-to-all-start.1 = ((f32[32,8,256]{2,1,0:T(8,128)}), f32[32,8,256]{2,1,0:T(8,128)S(1)}, u32[]{:S(2)}, u32[]{:S(2)}) async-start(f32[32,8,256]{2,1,0:T(8,128)} %convolution_bitcast_fusion), calls=%async_computation.1 | async-start | bytes 524288 | tf_op jit(solution)/shard_map/all_to_all | solution.py:140
  56.7 6.9 %collective-permute-start.13 = (f32[8,8,256]{2,1,0:T(8,128)S(1)}, f32[8,8,256]{2,1,0:T(8,128)S(1)}, u32[]{:S(2)}, u32[]{:S(2)}) collective-permute-start(f32[8,8,256]{2,1,0:T(8,128)S(1)} %copy.57), channel_id=1, source_target_pairs={{0,3},{1,2},{2,1},{3,0},{4,7},{5,6},{6,5},{7,4},{8,11},{9,10},{10,... | collective-permute-start | bytes 196616 | tf_op jit(solution)/shard_map/shard_3/ppermute | solution.py:16
  58.5 7.2 %collective-permute-start.14 = (f32[8,8,256]{2,1,0:T(8,128)S(1)}, f32[8,8,256]{2,1,0:T(8,128)S(1)}, u32[]{:S(2)}, u32[]{:S(2)}) collective-permute-start(f32[8,8,256]{2,1,0:T(8,128)S(1)} %copy.58), channel_id=1, source_target_pairs={{0,2},{1,3},{2,0},{3,1},{4,6},{5,7},{6,4},{7,5},{8,10},{9,11},{10,... | collective-permute-start | bytes 196616 | tf_op jit(solution)/shard_map/shard_2/ppermute | solution.py:16
  59.4 6.4 %collective-permute-start.15 = (f32[8,8,256]{2,1,0:T(8,128)S(1)}, f32[8,8,256]{2,1,0:T(8,128)S(1)}, u32[]{:S(2)}, u32[]{:S(2)}) collective-permute-start(f32[8,8,256]{2,1,0:T(8,128)S(1)} %copy.59), channel_id=1, source_target_pairs={{0,1},{1,0},{2,3},{3,2},{4,5},{5,4},{6,7},{7,6},{8,9},{9,8},{10,11... | collective-permute-start | bytes 196616 | tf_op jit(solution)/shard_map/shard_1/ppermute | solution.py:16
  65.8 6.4 %collective-permute-start.18 = (f32[4,32,256]{2,1,0:T(8,128)S(1)}, f32[4,32,256]{2,1,0:T(8,128)S(1)}, u32[]{:S(2)}, u32[]{:S(2)}) collective-permute-start(f32[4,32,256]{2,1,0:T(8,128)S(1)} %get-tuple-element.50), channel_id=1, source_target_pairs={{0,8},{4,12},{8,0},{12,4},{16,24},{20,28},{24,16},{28,20},{1,9},{5... | collective-permute-start | bytes 393224 | tf_op jit(solution)/shard_map/rows_x_top/ppermute | solution.py:16
  66.8 7.2 %collective-permute-start.17 = (f32[4,32,256]{2,1,0:T(8,128)S(1)}, f32[4,32,256]{2,1,0:T(8,128)S(1)}, u32[]{:S(2)}, u32[]{:S(2)}) collective-permute-start(f32[4,32,256]{2,1,0:T(8,128)S(1)} %get-tuple-element.49), channel_id=1, source_target_pairs={{0,8},{4,12},{8,0},{12,4},{16,24},{20,28},{24,16},{28,20},{1,9},{5... | collective-permute-start | bytes 393224 | tf_op jit(solution)/shard_map/rows_x_low/ppermute | solution.py:16
  67.9 10.8 %collective-permute-start.16 = (f32[8,32,256]{2,1,0:T(8,128)S(1)}, f32[8,32,256]{2,1,0:T(8,128)S(1)}, u32[]{:S(2)}, u32[]{:S(2)}) collective-permute-start(f32[8,32,256]{2,1,0:T(8,128)S(1)} %subtract_dynamic-update-slice_fusion), channel_id=1, source_target_pairs={{0,4},{4,0},{8,12},{12,8},{16,20},{20,16},{24,28},{28,24},{1,5},{5... | collective-permute-start | bytes 786440 | tf_op jit(solution)/shard_map/rows_core_own/ppermute | solution.py:16
  67.9 6.3 %collective-permute-start.20 = (f32[4,32,256]{2,1,0:T(8,128)S(1)}, f32[4,32,256]{2,1,0:T(8,128)S(1)}, u32[]{:S(2)}, u32[]{:S(2)}) collective-permute-start(f32[4,32,256]{2,1,0:T(8,128)S(1)} %get-tuple-element.49), channel_id=1, source_target_pairs={{0,16},{4,20},{8,24},{12,28},{16,0},{20,4},{24,8},{28,12},{1,17},{... | collective-permute-start | bytes 393224 | tf_op jit(solution)/shard_map/rows_y_low/ppermute | solution.py:16
  68.8 7.8 %collective-permute-start.19 = (f32[4,32,256]{2,1,0:T(8,128)S(1)}, f32[4,32,256]{2,1,0:T(8,128)S(1)}, u32[]{:S(2)}, u32[]{:S(2)}) collective-permute-start(f32[4,32,256]{2,1,0:T(8,128)S(1)} %get-tuple-element.50), channel_id=1, source_target_pairs={{0,16},{4,20},{8,24},{12,28},{16,0},{20,4},{24,8},{28,12},{1,17},{... | collective-permute-start | bytes 393224 | tf_op jit(solution)/shard_map/rows_y_top/ppermute | solution.py:16
  76.7 6.8 %collective-permute-start.21 = (f32[8,32,256]{2,1,0:T(8,128)S(1)}, f32[8,32,256]{2,1,0:T(8,128)S(1)}, u32[]{:S(2)}, u32[]{:S(2)}) collective-permute-start(f32[8,32,256]{2,1,0:T(8,128)S(1)} %pad_maximum_fusion.1), channel_id=1, source_target_pairs={{0,4},{4,0},{8,12},{12,8},{16,20},{20,16},{24,28},{28,24},{1,5},{5... | collective-permute-start | bytes 786440 | tf_op jit(solution)/shard_map/rows_core_x/ppermute | solution.py:16
  76.7 6.7 %collective-permute-start.22 = (f32[8,32,256]{2,1,0:T(8,128)S(1)}, f32[8,32,256]{2,1,0:T(8,128)S(1)}, u32[]{:S(2)}, u32[]{:S(2)}) collective-permute-start(f32[8,32,256]{2,1,0:T(8,128)S(1)} %pad_maximum_fusion.2), channel_id=1, source_target_pairs={{0,4},{4,0},{8,12},{12,8},{16,20},{20,16},{24,28},{28,24},{1,5},{5... | collective-permute-start | bytes 786440 | tf_op jit(solution)/shard_map/rows_core_y/ppermute | solution.py:16
  77.2 5.5 %collective-permute-start.23 = (f32[4,32,256]{2,1,0:T(8,128)S(1)}, f32[4,32,256]{2,1,0:T(8,128)S(1)}, u32[]{:S(2)}, u32[]{:S(2)}) collective-permute-start(f32[4,32,256]{2,1,0:T(8,128)S(1)} %collective-permute-done.20), channel_id=1, source_target_pairs={{0,8},{4,12},{8,0},{12,4},{16,24},{20,28},{24,16},{28,20},{1,9},{5... | collective-permute-start | bytes 393224 | tf_op jit(solution)/shard_map/rows_relay_low/ppermute | solution.py:16
  78.1 5.2 %collective-permute-start.24 = (f32[4,32,256]{2,1,0:T(8,128)S(1)}, f32[4,32,256]{2,1,0:T(8,128)S(1)}, u32[]{:S(2)}, u32[]{:S(2)}) collective-permute-start(f32[4,32,256]{2,1,0:T(8,128)S(1)} %collective-permute-done.18), channel_id=1, source_target_pairs={{0,16},{4,20},{8,24},{12,28},{16,0},{20,4},{24,8},{28,12},{1,17},{... | collective-permute-start | bytes 393224 | tf_op jit(solution)/shard_map/rows_relay_top/ppermute | solution.py:16
  83.3 1.6 %collective-permute-start.25 = (f32[8,32,256]{2,1,0:T(8,128)S(1)}, f32[8,32,256]{2,1,0:T(8,128)S(1)}, u32[]{:S(2)}, u32[]{:S(2)}) collective-permute-start(f32[8,32,256]{2,1,0:T(8,128)S(1)} %constant_dynamic-update-slice_fusion.6), channel_id=1, source_target_pairs={{0,4},{4,0},{8,12},{12,8},{16,20},{20,16},{24,28},{28,24},{1,5},{5... | collective-permute-start | bytes 786440 | tf_op jit(solution)/shard_map/rows_core_far/ppermute | solution.py:16
  (5 other events, 52.5 us)

commit v3 on v2

--- a/solution.py
+++ b/solution.py
@@ -164,8 +164,8 @@
     far_low = swap(y_low, "dp", along_x, "rows_relay_low")
     x_rows = jnp.concatenate([x_low, x_top], axis=0)
     y_rows = jnp.concatenate([y_top, y_low], axis=0)
-    x_rows, y_rows, first_new, second_new = lax.optimization_barrier(
-        (x_rows, y_rows, first_new, second_new)
+    x_rows, y_rows, far_top, first_new, second_new = lax.optimization_barrier(
+        (x_rows, y_rows, far_top, first_new, second_new)
     )
     far_rows = jnp.concatenate([far_low, far_top], axis=0)
     y_other = swap(y_rows, "dp", core, "rows_core_y")

time: 86.5 us -> 81.4 us (0.941)
  waiting for transfers between devices: 36.7 us -> 31.7 us
    ppermute x26, waiting for transfers between devices: 26.5 us -> 21.5 us  [swap(): lax.ppermute(values, name, [(i, i ^ mask) for i in range(lax.axis_size(na...]
  transfers between devices with their start and end apart: 27 -> 27, of which waited for: 18 -> 19; matrix products, arithmetic and copies ran while one was open for 1% -> 1% of each run, Pallas kernels for 0% -> 0%
where the time goes in v3:
time: 81.4 us; the launch traced here: 81.2 us
  waiting for transfers between devices  31.7 us (39%)
  starting transfers between devices  28 us (34%)
  blocking collectives  13.3 us (16%)
  local copies, waits for them, and re-layouts  3.81 us (5%)
  matrix products  2.64 us (3%)
  between operations  1.24 us (2%)
    ppermute x26, starting transfers between devices, swap(): lax.ppermute(values, name, [(i, i ^ mask) for i in range(lax.axis_size(na...  25.2 us
    ppermute x26, waiting for transfers between devices, swap(): lax.ppermute(values, name, [(i, i ^ mask) for i in range(lax.axis_size(na...  21.5 us
    all_to_all x1, blocking collectives, routed(): lax.all_to_all(leaving.reshape((device_total,) + piece), ('dp', 'shard'),...  13.3 us
    all_to_all x1, waiting for transfers between devices, routed(): lax.all_to_all(change.reshape((device_total,) + piece), ('dp', 'shard'),...  10.2 us
    all_to_all x1, starting transfers between devices, routed(): lax.all_to_all(change.reshape((device_total,) + piece), ('dp', 'shard'),...  2.72 us
  transfers between devices with their start and end apart: 27, of which 19 were waited for; matrix products, arithmetic and copies ran while one was open for 1% of the time, Pallas kernels for 0%

profile of v3, /device:TPU:0, one launch (start us, length us, event | category | flops | bytes accessed | tf_op | source)
XLA Modules:
  0.0 81.2 jit_solution(17848583029370716359)
XLA Ops:
  0.7 1.3 %dynamic-slice_bitcast_fusion = (bf16[8,4,32,256]{3,2,1,0:T(8,128)(2,1)S(1)}, bf16[8,4,32,256]{3,2,1,0:T(8,128)(2,1)S(1)}) fusion(bf16[8,4,2,32,256]{4,3,2,1,0:T(8,128)(2,1)} %bitcast.98, s32[]{:T(128)S(6)} %select_n.117, s32[]{:T(128)S(6)} %select_n.116), kind=kLoop, calls=%fused_computation.1 | loop fusion | bytes 2097160 | tf_op jit(solution)/shard_map/jit(dynamic_index_in_dim)/squeeze | solution.py:20
  3.9 3.0 %collective-permute-start.8 = (f32[4,32,256]{2,1,0:T(8,128)S(1)}, f32[4,32,256]{2,1,0:T(8,128)S(1)}, u32[]{:S(2)}, u32[]{:S(2)}) collective-permute-start(f32[4,32,256]{2,1,0:T(8,128)S(1)} %get-tuple-element.37), channel_id=1, source_target_pairs={{0,16},{4,20},{8,24},{12,28},{16,0},{20,4},{24,8},{28,12},{1,17},{... | collective-permute-start | bytes 393224 | tf_op jit(solution)/shard_map/sum_far_top/ppermute | solution.py:16
  6.8 1.5 %collective-permute-start.6 = (f32[4,32,256]{2,1,0:T(8,128)S(1)}, f32[4,32,256]{2,1,0:T(8,128)S(1)}, u32[]{:S(2)}, u32[]{:S(2)}) collective-permute-start(f32[4,32,256]{2,1,0:T(8,128)S(1)} %get-tuple-element.34), channel_id=1, source_target_pairs={{0,8},{4,12},{8,0},{12,4},{16,24},{20,28},{24,16},{28,20},{1,9},{5... | collective-permute-start | bytes 393224 | tf_op jit(solution)/shard_map/sum_far_low/ppermute | solution.py:16
  8.5 0.6 collective-permute-start.3
  9.6 1.1 %collective-permute-done.8 = f32[4,32,256]{2,1,0:T(8,128)S(1)} collective-permute-done((f32[4,32,256]{2,1,0:T(8,128)S(1)}, f32[4,32,256]{2,1,0:T(8,128)S(1)}, u32[]{:S(2)}, u32[]{:S(2)}) %collective-permute-start.8) | collective-permute-done | bytes 131104 | tf_op jit(solution)/shard_map/sum_far_top/ppermute | solution.py:16
  10.7 1.8 %collective-permute-start.9 = (f32[4,32,256]{2,1,0:T(8,128)S(1)}, f32[4,32,256]{2,1,0:T(8,128)S(1)}, u32[]{:S(2)}, u32[]{:S(2)}) collective-permute-start(f32[4,32,256]{2,1,0:T(8,128)S(1)} %add.153), channel_id=1, source_target_pairs={{0,8},{4,12},{8,0},{12,4},{16,24},{20,28},{24,16},{28,20},{1,9},{5... | collective-permute-start | bytes 393224 | tf_op jit(solution)/shard_map/sum_relay_top/ppermute | solution.py:16
  12.4 0.8 collective-permute-done.6
  13.2 1.6 %collective-permute-start.7 = (f32[4,32,256]{2,1,0:T(8,128)S(1)}, f32[4,32,256]{2,1,0:T(8,128)S(1)}, u32[]{:S(2)}, u32[]{:S(2)}) collective-permute-start(f32[4,32,256]{2,1,0:T(8,128)S(1)} %add.151), channel_id=1, source_target_pairs={{0,16},{4,20},{8,24},{12,28},{16,0},{20,4},{24,8},{28,12},{1,17},{... | collective-permute-start | bytes 393224 | tf_op jit(solution)/shard_map/sum_relay_low/ppermute | solution.py:16
  14.9 1.2 %collective-permute-done.3 = f32[4,32,256]{2,1,0:T(8,128)S(1)} collective-permute-done((f32[4,32,256]{2,1,0:T(8,128)S(1)}, f32[4,32,256]{2,1,0:T(8,128)S(1)}, u32[]{:S(2)}, u32[]{:S(2)}) %collective-permute-start.3) | collective-permute-done | bytes 131104 | tf_op jit(solution)/shard_map/sum_x_low/ppermute | solution.py:16
  16.1 1.6 %collective-permute-done.9 = f32[4,32,256]{2,1,0:T(8,128)S(1)} collective-permute-done((f32[4,32,256]{2,1,0:T(8,128)S(1)}, f32[4,32,256]{2,1,0:T(8,128)S(1)}, u32[]{:S(2)}, u32[]{:S(2)}) %collective-permute-start.9) | collective-permute-done | bytes 131104 | tf_op jit(solution)/shard_map/sum_relay_top/ppermute | solution.py:16
  18.4 3.7 %collective-permute-start.12 = (f32[8,8,256]{2,1,0:T(8,128)S(1)}, f32[8,8,256]{2,1,0:T(8,128)S(1)}, u32[]{:S(2)}, u32[]{:S(2)}) collective-permute-start(f32[8,8,256]{2,1,0:T(8,128)S(1)} %get-tuple-element.62), channel_id=1, source_target_pairs={{0,3},{1,2},{2,1},{3,0},{4,7},{5,6},{6,5},{7,4},{8,11},{9,10},{10,... | collective-permute-start | bytes 196616 | tf_op jit(solution)/shard_map/shard_3/ppermute | solution.py:16
  22.1 0.8 collective-permute-start.10
  23.0 1.6 %collective-permute-done.12 = f32[8,8,256]{2,1,0:T(8,128)S(1)} collective-permute-done((f32[8,8,256]{2,1,0:T(8,128)S(1)}, f32[8,8,256]{2,1,0:T(8,128)S(1)}, u32[]{:S(2)}, u32[]{:S(2)}) %collective-permute-start.12) | collective-permute-done | bytes 65568 | tf_op jit(solution)/shard_map/shard_3/ppermute | solution.py:16
  24.5 2.7 %collective-permute-done.11 = f32[8,8,256]{2,1,0:T(8,128)S(1)} collective-permute-done((f32[8,8,256]{2,1,0:T(8,128)S(1)}, f32[8,8,256]{2,1,0:T(8,128)S(1)}, u32[]{:S(2)}, u32[]{:S(2)}) %collective-permute-start.11) | collective-permute-done | bytes 65568 | tf_op jit(solution)/shard_map/shard_2/ppermute | solution.py:16
  27.7 13.3 %all_to_all.10 = f32[32,8,256]{2,1,0:T(8,128)S(1)} all-to-all(f32[32,8,256]{2,1,0:T(8,128)S(1)} %copy.55), channel_id=1, replica_groups=mesh['dp'=8,'shard'=4] {'dp','shard'}, dimensions={0} | all-to-all | bytes 524288 | tf_op jit(solution)/shard_map/all_to_all | solution.py:123
  42.3 1.0 %convolution_bitcast_fusion = f32[32,8,256]{2,1,0:T(8,128)} fusion(f32[256,256]{1,0:T(8,128)S(1)} %fusion.4, f32[1,1,1,256,256]{4,3,2,1,0:T(8,128)S(1)} %copy-done.4), kind=kOutput, calls=%fused_computation | convolution fusion | flops 100663296 | bytes 786432 | tf_op jit(solution)/shard_map/ia,aj->ij/dot_general | solution.py:68
  43.3 2.7 %all-to-all-start.1 = ((f32[32,8,256]{2,1,0:T(8,128)}), f32[32,8,256]{2,1,0:T(8,128)S(1)}, u32[]{:S(2)}, u32[]{:S(2)}) async-start(f32[32,8,256]{2,1,0:T(8,128)} %convolution_bitcast_fusion), calls=%async_computation.1 | async-start | bytes 524288 | tf_op jit(solution)/shard_map/all_to_all | solution.py:140
  46.0 10.2 %all-to-all-done.1 = f32[32,8,256]{2,1,0:T(8,128)S(1)} async-done(((f32[32,8,256]{2,1,0:T(8,128)}), f32[32,8,256]{2,1,0:T(8,128)S(1)}, u32[]{:S(2)}, u32[]{:S(2)}) %all-to-all-start.1) | async-done | bytes 262176 | tf_op jit(solution)/shard_map/all_to_all | solution.py:140
  56.7 1.8 %collective-permute-start.13 = (f32[8,8,256]{2,1,0:T(8,128)S(1)}, f32[8,8,256]{2,1,0:T(8,128)S(1)}, u32[]{:S(2)}, u32[]{:S(2)}) collective-permute-start(f32[8,8,256]{2,1,0:T(8,128)S(1)} %copy.57), channel_id=1, source_target_pairs={{0,3},{1,2},{2,1},{3,0},{4,7},{5,6},{6,5},{7,4},{8,11},{9,10},{10,... | collective-permute-start | bytes 196616 | tf_op jit(solution)/shard_map/shard_3/ppermute | solution.py:16
  58.5 0.9 %collective-permute-start.14 = (f32[8,8,256]{2,1,0:T(8,128)S(1)}, f32[8,8,256]{2,1,0:T(8,128)S(1)}, u32[]{:S(2)}, u32[]{:S(2)}) collective-permute-start(f32[8,8,256]{2,1,0:T(8,128)S(1)} %copy.58), channel_id=1, source_target_pairs={{0,2},{1,3},{2,0},{3,1},{4,6},{5,7},{6,4},{7,5},{8,10},{9,11},{10,... | collective-permute-start | bytes 196616 | tf_op jit(solution)/shard_map/shard_2/ppermute | solution.py:16
  59.4 1.9 %collective-permute-start.15 = (f32[8,8,256]{2,1,0:T(8,128)S(1)}, f32[8,8,256]{2,1,0:T(8,128)S(1)}, u32[]{:S(2)}, u32[]{:S(2)}) collective-permute-start(f32[8,8,256]{2,1,0:T(8,128)S(1)} %copy.59), channel_id=1, source_target_pairs={{0,1},{1,0},{2,3},{3,2},{4,5},{5,4},{6,7},{7,6},{8,9},{9,8},{10,11... | collective-permute-start | bytes 196616 | tf_op jit(solution)/shard_map/shard_1/ppermute | solution.py:16
  61.4 2.2 %collective-permute-done.13 = f32[8,8,256]{2,1,0:T(8,128)S(1)} collective-permute-done((f32[8,8,256]{2,1,0:T(8,128)S(1)}, f32[8,8,256]{2,1,0:T(8,128)S(1)}, u32[]{:S(2)}, u32[]{:S(2)}) %collective-permute-start.13) | collective-permute-done | bytes 65568 | tf_op jit(solution)/shard_map/shard_3/ppermute | solution.py:16
  63.6 2.2 %collective-permute-done.14 = f32[8,8,256]{2,1,0:T(8,128)S(1)} collective-permute-done((f32[8,8,256]{2,1,0:T(8,128)S(1)}, f32[8,8,256]{2,1,0:T(8,128)S(1)}, u32[]{:S(2)}, u32[]{:S(2)}) %collective-permute-start.14) | collective-permute-done | bytes 65568 | tf_op jit(solution)/shard_map/shard_2/ppermute | solution.py:16
  65.8 0.9 %collective-permute-start.18 = (f32[4,32,256]{2,1,0:T(8,128)S(1)}, f32[4,32,256]{2,1,0:T(8,128)S(1)}, u32[]{:S(2)}, u32[]{:S(2)}) collective-permute-start(f32[4,32,256]{2,1,0:T(8,128)S(1)} %get-tuple-element.52), channel_id=1, source_target_pairs={{0,8},{4,12},{8,0},{12,4},{16,24},{20,28},{24,16},{28,20},{1,9},{5... | collective-permute-start | bytes 393224 | tf_op jit(solution)/shard_map/rows_x_top/ppermute | solution.py:16
  67.3 1.5 %collective-permute-start.17 = (f32[4,32,256]{2,1,0:T(8,128)S(1)}, f32[4,32,256]{2,1,0:T(8,128)S(1)}, u32[]{:S(2)}, u32[]{:S(2)}) collective-permute-start(f32[4,32,256]{2,1,0:T(8,128)S(1)} %get-tuple-element.51), channel_id=1, source_target_pairs={{0,8},{4,12},{8,0},{12,4},{16,24},{20,28},{24,16},{28,20},{1,9},{5... | collective-permute-start | bytes 393224 | tf_op jit(solution)/shard_map/rows_x_low/ppermute | solution.py:16
  68.8 1.1 %collective-permute-start.19 = (f32[4,32,256]{2,1,0:T(8,128)S(1)}, f32[4,32,256]{2,1,0:T(8,128)S(1)}, u32[]{:S(2)}, u32[]{:S(2)}) collective-permute-start(f32[4,32,256]{2,1,0:T(8,128)S(1)} %get-tuple-element.52), channel_id=1, source_target_pairs={{0,16},{4,20},{8,24},{12,28},{16,0},{20,4},{24,8},{28,12},{1,17},{... | collective-permute-start | bytes 393224 | tf_op jit(solution)/shard_map/rows_y_top/ppermute | solution.py:16
  70.2 2.1 %collective-permute-done.18 = f32[4,32,256]{2,1,0:T(8,128)S(1)} collective-permute-done((f32[4,32,256]{2,1,0:T(8,128)S(1)}, f32[4,32,256]{2,1,0:T(8,128)S(1)}, u32[]{:S(2)}, u32[]{:S(2)}) %collective-permute-start.18) | collective-permute-done | bytes 131104 | tf_op jit(solution)/shard_map/rows_x_top/ppermute | solution.py:16
  72.3 0.9 %collective-permute-start.21 = (f32[4,32,256]{2,1,0:T(8,128)S(1)}, f32[4,32,256]{2,1,0:T(8,128)S(1)}, u32[]{:S(2)}, u32[]{:S(2)}) collective-permute-start(f32[4,32,256]{2,1,0:T(8,128)S(1)} %collective-permute-done.18), channel_id=1, source_target_pairs={{0,16},{4,20},{8,24},{12,28},{16,0},{20,4},{24,8},{28,12},{1,17},{... | collective-permute-start | bytes 393224 | tf_op jit(solution)/shard_map/rows_relay_top/ppermute | solution.py:16
  74.1 1.0 %collective-permute-done.19 = f32[4,32,256]{2,1,0:T(8,128)S(1)} collective-permute-done((f32[4,32,256]{2,1,0:T(8,128)S(1)}, f32[4,32,256]{2,1,0:T(8,128)S(1)}, u32[]{:S(2)}, u32[]{:S(2)}) %collective-permute-start.19) | collective-permute-done | bytes 131104 | tf_op jit(solution)/shard_map/rows_y_top/ppermute | solution.py:16
  75.2 2.4 %collective-permute-done.21 = f32[4,32,256]{2,1,0:T(8,128)S(1)} collective-permute-done((f32[4,32,256]{2,1,0:T(8,128)S(1)}, f32[4,32,256]{2,1,0:T(8,128)S(1)}, u32[]{:S(2)}, u32[]{:S(2)}) %collective-permute-start.21) | collective-permute-done | bytes 131104 | tf_op jit(solution)/shard_map/rows_relay_top/ppermute | solution.py:16
  78.3 0.8 collective-permute-done.22
  79.9 1.3 %copy-done.3 = f32[8,256,256]{2,1,0:T(8,128)} copy-done((f32[8,256,256]{2,1,0:T(8,128)}, f32[8,256,256]{2,1,0:T(8,128)S(1)}, u32[]{:S(2)}) %copy-start.3) | copy-done | bytes 2097176
  (101 shorter events, 8.7 us)
Async XLA Ops:
  0.6 40.8 %copy-start = (f32[1,1,1,256,256]{4,3,2,1,0:T(8,128)S(1)}, f32[1,1,1,256,256]{4,3,2,1,0:T(8,128)}, u32[]{:S(2)}) copy-start(f32[1,1,1,256,256]{4,3,2,1,0:T(8,128)} %param.10) | copy-start | bytes 786436
  2.1 1.7 %collective-permute-start = (f32[8,32,256]{2,1,0:T(8,128)S(1)}, f32[8,32,256]{2,1,0:T(8,128)S(1)}, u32[]{:S(2)}, u32[]{:S(2)}) collective-permute-start(f32[8,32,256]{2,1,0:T(8,128)S(1)} %get-tuple-element.50), channel_id=1, source_target_pairs={{0,4},{4,0},{8,12},{12,8},{16,20},{20,16},{24,28},{28,24},{1,5},{5... | collective-permute-start | bytes 786440 | tf_op jit(solution)/shard_map/sum_core_6/ppermute | solution.py:16
  2.7 5.7 %collective-permute-start.4 = (f32[8,32,256]{2,1,0:T(8,128)S(1)}, f32[8,32,256]{2,1,0:T(8,128)S(1)}, u32[]{:S(2)}, u32[]{:S(2)}) collective-permute-start(f32[8,32,256]{2,1,0:T(8,128)S(1)} %bitcast_convert_fusion), channel_id=1, source_target_pairs={{0,4},{4,0},{8,12},{12,8},{16,20},{20,16},{24,28},{28,24},{1,5},{5... | collective-permute-start | bytes 786440 | tf_op jit(solution)/shard_map/sum_core_4/ppermute | solution.py:16
  2.8 5.5 %collective-permute-start.2 = (f32[8,32,256]{2,1,0:T(8,128)S(1)}, f32[8,32,256]{2,1,0:T(8,128)S(1)}, u32[]{:S(2)}, u32[]{:S(2)}) collective-permute-start(f32[8,32,256]{2,1,0:T(8,128)S(1)} %get-tuple-element.48), channel_id=1, source_target_pairs={{0,4},{4,0},{8,12},{12,8},{16,20},{20,16},{24,28},{28,24},{1,5},{5... | collective-permute-start | bytes 786440 | tf_op jit(solution)/shard_map/sum_core_2/ppermute | solution.py:16
  3.3 5.1 %collective-permute-start.1 = (f32[8,32,256]{2,1,0:T(8,128)S(1)}, f32[8,32,256]{2,1,0:T(8,128)S(1)}, u32[]{:S(2)}, u32[]{:S(2)}) collective-permute-start(f32[8,32,256]{2,1,0:T(8,128)S(1)} %get-tuple-element.49), channel_id=1, source_target_pairs={{0,4},{4,0},{8,12},{12,8},{16,20},{20,16},{24,28},{28,24},{1,5},{5... | collective-permute-start | bytes 786440 | tf_op jit(solution)/shard_map/sum_core_0/ppermute | solution.py:16
  3.9 6.8 %collective-permute-start.8 = (f32[4,32,256]{2,1,0:T(8,128)S(1)}, f32[4,32,256]{2,1,0:T(8,128)S(1)}, u32[]{:S(2)}, u32[]{:S(2)}) collective-permute-start(f32[4,32,256]{2,1,0:T(8,128)S(1)} %get-tuple-element.37), channel_id=1, source_target_pairs={{0,16},{4,20},{8,24},{12,28},{16,0},{20,4},{24,8},{28,12},{1,17},{... | collective-permute-start | bytes 393224 | tf_op jit(solution)/shard_map/sum_far_top/ppermute | solution.py:16
  6.8 6.4 %collective-permute-start.6 = (f32[4,32,256]{2,1,0:T(8,128)S(1)}, f32[4,32,256]{2,1,0:T(8,128)S(1)}, u32[]{:S(2)}, u32[]{:S(2)}) collective-permute-start(f32[4,32,256]{2,1,0:T(8,128)S(1)} %get-tuple-element.34), channel_id=1, source_target_pairs={{0,8},{4,12},{8,0},{12,4},{16,24},{20,28},{24,16},{28,20},{1,9},{5... | collective-permute-start | bytes 393224 | tf_op jit(solution)/shard_map/sum_far_low/ppermute | solution.py:16
  8.5 7.5 %collective-permute-start.3 = (f32[4,32,256]{2,1,0:T(8,128)S(1)}, f32[4,32,256]{2,1,0:T(8,128)S(1)}, u32[]{:S(2)}, u32[]{:S(2)}) collective-permute-start(f32[4,32,256]{2,1,0:T(8,128)S(1)} %get-tuple-element.29), channel_id=1, source_target_pairs={{0,8},{4,12},{8,0},{12,4},{16,24},{20,28},{24,16},{28,20},{1,9},{5... | collective-permute-start | bytes 393224 | tf_op jit(solution)/shard_map/sum_x_low/ppermute | solution.py:16
  9.1 6.9 %collective-permute-start.5 = (f32[4,32,256]{2,1,0:T(8,128)S(1)}, f32[4,32,256]{2,1,0:T(8,128)S(1)}, u32[]{:S(2)}, u32[]{:S(2)}) collective-permute-start(f32[4,32,256]{2,1,0:T(8,128)S(1)} %get-tuple-element.31), channel_id=1, source_target_pairs={{0,16},{4,20},{8,24},{12,28},{16,0},{20,4},{24,8},{28,12},{1,17},{... | collective-permute-start | bytes 393224 | tf_op jit(solution)/shard_map/sum_y_top/ppermute | solution.py:16
  10.7 7.1 %collective-permute-start.9 = (f32[4,32,256]{2,1,0:T(8,128)S(1)}, f32[4,32,256]{2,1,0:T(8,128)S(1)}, u32[]{:S(2)}, u32[]{:S(2)}) collective-permute-start(f32[4,32,256]{2,1,0:T(8,128)S(1)} %add.153), channel_id=1, source_target_pairs={{0,8},{4,12},{8,0},{12,4},{16,24},{20,28},{24,16},{28,20},{1,9},{5... | collective-permute-start | bytes 393224 | tf_op jit(solution)/shard_map/sum_relay_top/ppermute | solution.py:16
  13.2 5.0 %collective-permute-start.7 = (f32[4,32,256]{2,1,0:T(8,128)S(1)}, f32[4,32,256]{2,1,0:T(8,128)S(1)}, u32[]{:S(2)}, u32[]{:S(2)}) collective-permute-start(f32[4,32,256]{2,1,0:T(8,128)S(1)} %add.151), channel_id=1, source_target_pairs={{0,16},{4,20},{8,24},{12,28},{16,0},{20,4},{24,8},{28,12},{1,17},{... | collective-permute-start | bytes 393224 | tf_op jit(solution)/shard_map/sum_relay_low/ppermute | solution.py:16
  17.7 23.3 %copy-start.4 = (f32[1,1,1,256,256]{4,3,2,1,0:T(8,128)S(1)}, f32[1,1,1,256,256]{4,3,2,1,0:T(8,128)}, u32[]{:S(2)}) copy-start(f32[1,1,1,256,256]{4,3,2,1,0:T(8,128)} %param.9) | copy-start | bytes 786436
  18.3 23.1 %copy-start.5 = (f32[1,1,1,256,256]{4,3,2,1,0:T(8,128)S(1)}, f32[1,1,1,256,256]{4,3,2,1,0:T(8,128)}, u32[]{:S(2)}) copy-start(f32[1,1,1,256,256]{4,3,2,1,0:T(8,128)} %param.11) | copy-start | bytes 786436
  18.3 23.1 %copy-start.6 = (f32[1,1,1,256,256]{4,3,2,1,0:T(8,128)S(1)}, f32[1,1,1,256,256]{4,3,2,1,0:T(8,128)}, u32[]{:S(2)}) copy-start(f32[1,1,1,256,256]{4,3,2,1,0:T(8,128)} %param.12) | copy-start | bytes 786436
  18.4 6.1 %collective-permute-start.12 = (f32[8,8,256]{2,1,0:T(8,128)S(1)}, f32[8,8,256]{2,1,0:T(8,128)S(1)}, u32[]{:S(2)}, u32[]{:S(2)}) collective-permute-start(f32[8,8,256]{2,1,0:T(8,128)S(1)} %get-tuple-element.62), channel_id=1, source_target_pairs={{0,3},{1,2},{2,1},{3,0},{4,7},{5,6},{6,5},{7,4},{8,11},{9,10},{10,... | collective-permute-start | bytes 196616 | tf_op jit(solution)/shard_map/shard_3/ppermute | solution.py:16
  22.0 5.2 %collective-permute-start.11 = (f32[8,8,256]{2,1,0:T(8,128)S(1)}, f32[8,8,256]{2,1,0:T(8,128)S(1)}, u32[]{:S(2)}, u32[]{:S(2)}) collective-permute-start(f32[8,8,256]{2,1,0:T(8,128)S(1)} %get-tuple-element.60), channel_id=1, source_target_pairs={{0,2},{1,3},{2,0},{3,1},{4,6},{5,7},{6,4},{7,5},{8,10},{9,11},{10,... | collective-permute-start | bytes 196616 | tf_op jit(solution)/shard_map/shard_2/ppermute | solution.py:16
  22.1 5.2 %collective-permute-start.10 = (f32[8,8,256]{2,1,0:T(8,128)S(1)}, f32[8,8,256]{2,1,0:T(8,128)S(1)}, u32[]{:S(2)}, u32[]{:S(2)}) collective-permute-start(f32[8,8,256]{2,1,0:T(8,128)S(1)} %get-tuple-element.61), channel_id=1, source_target_pairs={{0,1},{1,0},{2,3},{3,2},{4,5},{5,4},{6,7},{7,6},{8,9},{9,8},{10,11... | collective-permute-start | bytes 196616 | tf_op jit(solution)/shard_map/shard_1/ppermute | solution.py:16
  42.3 21.3 %copy-start.1 = (f32[8,32,256]{2,1,0:T(8,128)S(1)}, f32[8,32,256]{2,1,0:T(8,128)}, u32[]{:S(2)}) copy-start(f32[8,32,256]{2,1,0:T(8,128)} %param.8) | copy-start | bytes 786436
  43.3 12.9 %all-to-all-start.1 = ((f32[32,8,256]{2,1,0:T(8,128)}), f32[32,8,256]{2,1,0:T(8,128)S(1)}, u32[]{:S(2)}, u32[]{:S(2)}) async-start(f32[32,8,256]{2,1,0:T(8,128)} %convolution_bitcast_fusion), calls=%async_computation.1 | async-start | bytes 524288 | tf_op jit(solution)/shard_map/all_to_all | solution.py:140
  56.7 6.9 %collective-permute-start.13 = (f32[8,8,256]{2,1,0:T(8,128)S(1)}, f32[8,8,256]{2,1,0:T(8,128)S(1)}, u32[]{:S(2)}, u32[]{:S(2)}) collective-permute-start(f32[8,8,256]{2,1,0:T(8,128)S(1)} %copy.57), channel_id=1, source_target_pairs={{0,3},{1,2},{2,1},{3,0},{4,7},{5,6},{6,5},{7,4},{8,11},{9,10},{10,... | collective-permute-start | bytes 196616 | tf_op jit(solution)/shard_map/shard_3/ppermute | solution.py:16
  58.5 7.2 %collective-permute-start.14 = (f32[8,8,256]{2,1,0:T(8,128)S(1)}, f32[8,8,256]{2,1,0:T(8,128)S(1)}, u32[]{:S(2)}, u32[]{:S(2)}) collective-permute-start(f32[8,8,256]{2,1,0:T(8,128)S(1)} %copy.58), channel_id=1, source_target_pairs={{0,2},{1,3},{2,0},{3,1},{4,6},{5,7},{6,4},{7,5},{8,10},{9,11},{10,... | collective-permute-start | bytes 196616 | tf_op jit(solution)/shard_map/shard_2/ppermute | solution.py:16
  59.4 6.4 %collective-permute-start.15 = (f32[8,8,256]{2,1,0:T(8,128)S(1)}, f32[8,8,256]{2,1,0:T(8,128)S(1)}, u32[]{:S(2)}, u32[]{:S(2)}) collective-permute-start(f32[8,8,256]{2,1,0:T(8,128)S(1)} %copy.59), channel_id=1, source_target_pairs={{0,1},{1,0},{2,3},{3,2},{4,5},{5,4},{6,7},{7,6},{8,9},{9,8},{10,11... | collective-permute-start | bytes 196616 | tf_op jit(solution)/shard_map/shard_1/ppermute | solution.py:16
  65.8 6.4 %collective-permute-start.18 = (f32[4,32,256]{2,1,0:T(8,128)S(1)}, f32[4,32,256]{2,1,0:T(8,128)S(1)}, u32[]{:S(2)}, u32[]{:S(2)}) collective-permute-start(f32[4,32,256]{2,1,0:T(8,128)S(1)} %get-tuple-element.52), channel_id=1, source_target_pairs={{0,8},{4,12},{8,0},{12,4},{16,24},{20,28},{24,16},{28,20},{1,9},{5... | collective-permute-start | bytes 393224 | tf_op jit(solution)/shard_map/rows_x_top/ppermute | solution.py:16
  66.8 6.4 %collective-permute-start.20 = (f32[4,32,256]{2,1,0:T(8,128)S(1)}, f32[4,32,256]{2,1,0:T(8,128)S(1)}, u32[]{:S(2)}, u32[]{:S(2)}) collective-permute-start(f32[4,32,256]{2,1,0:T(8,128)S(1)} %get-tuple-element.51), channel_id=1, source_target_pairs={{0,16},{4,20},{8,24},{12,28},{16,0},{20,4},{24,8},{28,12},{1,17},{... | collective-permute-start | bytes 393224 | tf_op jit(solution)/shard_map/rows_y_low/ppermute | solution.py:16
  67.3 6.8 %collective-permute-start.17 = (f32[4,32,256]{2,1,0:T(8,128)S(1)}, f32[4,32,256]{2,1,0:T(8,128)S(1)}, u32[]{:S(2)}, u32[]{:S(2)}) collective-permute-start(f32[4,32,256]{2,1,0:T(8,128)S(1)} %get-tuple-element.51), channel_id=1, source_target_pairs={{0,8},{4,12},{8,0},{12,4},{16,24},{20,28},{24,16},{28,20},{1,9},{5... | collective-permute-start | bytes 393224 | tf_op jit(solution)/shard_map/rows_x_low/ppermute | solution.py:16
  68.8 6.3 %collective-permute-start.16 = (f32[8,32,256]{2,1,0:T(8,128)S(1)}, f32[8,32,256]{2,1,0:T(8,128)S(1)}, u32[]{:S(2)}, u32[]{:S(2)}) collective-permute-start(f32[8,32,256]{2,1,0:T(8,128)S(1)} %subtract_dynamic-update-slice_fusion), channel_id=1, source_target_pairs={{0,4},{4,0},{8,12},{12,8},{16,20},{20,16},{24,28},{28,24},{1,5},{5... | collective-permute-start | bytes 786440 | tf_op jit(solution)/shard_map/rows_core_own/ppermute | solution.py:16
  68.8 6.3 %collective-permute-start.19 = (f32[4,32,256]{2,1,0:T(8,128)S(1)}, f32[4,32,256]{2,1,0:T(8,128)S(1)}, u32[]{:S(2)}, u32[]{:S(2)}) collective-permute-start(f32[4,32,256]{2,1,0:T(8,128)S(1)} %get-tuple-element.52), channel_id=1, source_target_pairs={{0,16},{4,20},{8,24},{12,28},{16,0},{20,4},{24,8},{28,12},{1,17},{... | collective-permute-start | bytes 393224 | tf_op jit(solution)/shard_map/rows_y_top/ppermute | solution.py:16
  72.3 5.3 %collective-permute-start.21 = (f32[4,32,256]{2,1,0:T(8,128)S(1)}, f32[4,32,256]{2,1,0:T(8,128)S(1)}, u32[]{:S(2)}, u32[]{:S(2)}) collective-permute-start(f32[4,32,256]{2,1,0:T(8,128)S(1)} %collective-permute-done.18), channel_id=1, source_target_pairs={{0,16},{4,20},{8,24},{12,28},{16,0},{20,4},{24,8},{28,12},{1,17},{... | collective-permute-start | bytes 393224 | tf_op jit(solution)/shard_map/rows_relay_top/ppermute | solution.py:16
  73.1 5.0 %collective-permute-start.24 = (f32[4,32,256]{2,1,0:T(8,128)S(1)}, f32[4,32,256]{2,1,0:T(8,128)S(1)}, u32[]{:S(2)}, u32[]{:S(2)}) collective-permute-start(f32[4,32,256]{2,1,0:T(8,128)S(1)} %collective-permute-done.20), channel_id=1, source_target_pairs={{0,8},{4,12},{8,0},{12,4},{16,24},{20,28},{24,16},{28,20},{1,9},{5... | collective-permute-start | bytes 393224 | tf_op jit(solution)/shard_map/rows_relay_low/ppermute | solution.py:16
  77.5 1.5 %collective-permute-start.22 = (f32[8,32,256]{2,1,0:T(8,128)S(1)}, f32[8,32,256]{2,1,0:T(8,128)S(1)}, u32[]{:S(2)}, u32[]{:S(2)}) collective-permute-start(f32[8,32,256]{2,1,0:T(8,128)S(1)} %pad_maximum_fusion.1), channel_id=1, source_target_pairs={{0,4},{4,0},{8,12},{12,8},{16,20},{20,16},{24,28},{28,24},{1,5},{5... | collective-permute-start | bytes 786440 | tf_op jit(solution)/shard_map/rows_core_x/ppermute | solution.py:16
  77.5 1.9 %collective-permute-start.23 = (f32[8,32,256]{2,1,0:T(8,128)S(1)}, f32[8,32,256]{2,1,0:T(8,128)S(1)}, u32[]{:S(2)}, u32[]{:S(2)}) collective-permute-start(f32[8,32,256]{2,1,0:T(8,128)S(1)} %pad_maximum_fusion.2), channel_id=1, source_target_pairs={{0,4},{4,0},{8,12},{12,8},{16,20},{20,16},{24,28},{28,24},{1,5},{5... | collective-permute-start | bytes 786440 | tf_op jit(solution)/shard_map/rows_core_y/ppermute | solution.py:16
  78.1 1.7 %collective-permute-start.25 = (f32[8,32,256]{2,1,0:T(8,128)S(1)}, f32[8,32,256]{2,1,0:T(8,128)S(1)}, u32[]{:S(2)}, u32[]{:S(2)}) collective-permute-start(f32[8,32,256]{2,1,0:T(8,128)S(1)} %constant_dynamic-update-slice_fusion.6), channel_id=1, source_target_pairs={{0,4},{4,0},{8,12},{12,8},{16,20},{20,16},{24,28},{28,24},{1,5},{5... | collective-permute-start | bytes 786440 | tf_op jit(solution)/shard_map/rows_core_far/ppermute | solution.py:16
  (5 other events, 52.5 us)

commit v4 on v3

--- a/solution.py
+++ b/solution.py
@@ -1,5 +1,6 @@
 import jax
 import jax.numpy as jnp
+import numpy as np
 from jax import lax
 from jax.sharding import PartitionSpec as P
 
@@ -86,14 +87,21 @@
     half = home_count // 2
     piece = (row_count // shard_count, width)
 
-    owners = unmix(owner_list.reshape(shard_count, home_count), shard_here).reshape(1, -1)
-    device_ids = jnp.arange(device_total, dtype=jnp.int32)
-    picker = (owners == device_ids[:, None]).astype(jnp.float32)
-
     chips = data_count // 2
+    my_core = data_here & core
+
+    groups = np.arange(device_total).reshape(chips, 2, shard_count).swapaxes(0, 1).reshape(2, -1).tolist()
+    left_mat = left_basis[0, 0, 0].reshape((chips, 2, shard_count) + piece)
+    left_mat = unmix(left_mat.swapaxes(1, 2), my_core, axis=2).reshape(width, width)
+
+    def core_groups(values):
+        return lax.all_to_all(
+            values, ("dp", "shard"), split_axis=0, concat_axis=0, axis_index_groups=groups, tiled=True
+        )
+
     grid = partials[0].reshape((home_count, chips, 2, row_count, width))
-    away_rows = take(grid, 2, 1 - (data_here & core))
-    own_rows = take(grid, 2, data_here & core)
+    away_rows = take(grid, 2, 1 - my_core)
+    own_rows = take(grid, 2, my_core)
     away_rows, own_rows = lax.optimization_barrier((away_rows, own_rows))
 
     def rows_of(values, mask):
@@ -101,9 +109,8 @@
 
     part = {}
     for mask in (across, along_x, along_y, 0):
-        total = rows_of(own_rows, mask) + swap(
-            rows_of(away_rows, mask), "dp", core, f"sum_core_{mask}"
-        )
+        away = rows_of(away_rows, mask)
+        total = rows_of(own_rows, mask) + swap(away, "dp", core, f"sum_core_{mask}")
         part[mask] = lax.optimization_barrier((total[:half], total[half:]))
         if mask == across:
             own_rows, part[mask] = lax.optimization_barrier((own_rows, part[mask]))
@@ -117,33 +124,25 @@
 
     summed = jnp.concatenate([low, top], axis=0)
     summed = summed.reshape((home_count, shard_count) + piece)
+    summed, owner_list = lax.optimization_barrier((summed, owner_list))
     mixed = shard_exchange([take(summed, 1, shard_here ^ k) for k in range(shard_count)])
+    owners = unmix(owner_list.reshape(shard_count, home_count), shard_here).reshape(1, -1)
+    lane, column = owners // shard_count, owners % shard_count
+    spot = (((lane & core) ^ my_core) * chips + lane // 2) * shard_count + column
+    picker = (spot == jnp.arange(device_total, dtype=jnp.int32)[:, None]).astype(jnp.float32)
     pieces = jnp.concatenate(mixed, axis=0).reshape(device_total, -1)
     leaving = jnp.einsum("eb,bn->en", picker, pieces, precision=high)
-    whole = lax.all_to_all(
-        leaving.reshape((device_total,) + piece),
-        ("dp", "shard"),
-        split_axis=0,
-        concat_axis=0,
-        tiled=True,
-    ).reshape(width, width)
+    leaving = leaving.reshape((2, device_total // 2) + piece)
+    leaving = [leaving[0], swap(leaving[1], "dp", core, "pieces_core")]
+    whole = core_groups(jnp.stack(leaving, axis=1)).reshape(width, width)
 
     first_new, second_new, change = adam(
-        left_basis[0, 0, 0],
-        right_basis[0, 0, 0],
-        first_moment[0, 0, 0],
-        second_moment[0, 0, 0],
-        whole,
-        high,
-    )
-
-    coming = lax.all_to_all(
-        change.reshape((device_total,) + piece),
-        ("dp", "shard"),
-        split_axis=0,
-        concat_axis=0,
-        tiled=True,
-    ).reshape(device_total, -1)
+        left_mat, right_basis[0, 0, 0], first_moment[0, 0, 0], second_moment[0, 0, 0], whole, high
+    )
+
+    coming = core_groups(change.reshape((device_total // 2, 2) + piece))
+    coming = [coming[:, 0], swap(coming[:, 1], "dp", core, "change_core")]
+    coming = jnp.concatenate(coming, axis=0).reshape(device_total, -1)
     back = jnp.einsum("eb,en->bn", picker, coming, precision=high)
     back = back.reshape((shard_count, home_count) + piece)
     new_home = params
@@ -158,6 +157,9 @@
     x_top = swap(top, "dp", along_x, "rows_x_top")
     y_low = swap(low, "dp", along_y, "rows_y_low")
     other = swap(new_home, "dp", core, "rows_core_own")
+    updated = jnp.zeros((home_count, width, width), jnp.float32)
+    updated = lax.dynamic_update_slice_in_dim(updated, new_home, data_here * row_count, axis=1)
+    low, top, updated = lax.optimization_barrier((low, top, updated))
     x_low = swap(low, "dp", along_x, "rows_x_low")
     y_top = swap(top, "dp", along_y, "rows_y_top")
     far_top = swap(x_top, "dp", along_y, "rows_relay_top")
@@ -169,9 +171,7 @@
     )
     far_rows = jnp.concatenate([far_low, far_top], axis=0)
     y_other = swap(y_rows, "dp", core, "rows_core_y")
-    updated = jnp.zeros((home_count, width, width), jnp.float32)
     for mask, block, values in (
-        (0, 0, new_home),
         (core, 0, other),
         (along_x, 0, x_rows),
         (along_y, half, y_rows[:half]),
@@ -179,11 +179,15 @@
         (along_x ^ core, 0, swap(x_rows, "dp", core, "rows_core_x")),
         (along_y ^ core, half, y_other[:half]),
         (along_y ^ core, 0, y_other[half:]),
-        (across, 0, far_rows),
-        (across ^ core, 0, swap(far_rows, "dp", core, "rows_core_far")),
     ):
         start = (data_here ^ mask) * row_count
         updated = lax.dynamic_update_slice(updated, values, (block, start, 0))
+    far_other = swap(far_rows, "dp", core, "rows_core_far")
+    updated = updated.reshape(home_count, data_count, row_count, width)
+    place = lax.broadcasted_iota(jnp.int32, updated.shape, 1) ^ data_here
+    far_both = jnp.where(place == across, far_rows[:, None], far_other[:, None])
+    updated = jnp.where(place < across, updated, far_both)
+    updated = updated.reshape(home_count, width, width)
     return updated, first_new[None, None, None], second_new[None, None, None]
 
 

time: 81.4 us -> 85.7 us (1.053)
  other arithmetic: 0.52 us -> 4.01 us
  starting transfers between devices: 28 us -> 30.8 us
  local copies, waits for them, and re-layouts: 3.81 us -> 2.78 us
    select_n x0 -> x1, other arithmetic: none -> 1.84 us  [routed(): updated = jnp.where(place < across, updated, far_both)]
    all_to_all x1, starting transfers between devices: 2.72 us -> 4.34 us  [core_groups(): lax.all_to_all(values, ('dp', 'shard'), split_axis=0, concat_axis=0, axis...]
    unnamed x27 -> x28, local copies, waits for them, and re-layouts: 1.59 us -> 0.37 us
    ppermute x26 -> x28, starting transfers between devices: 25.2 us -> 26.4 us  [swap(): lax.ppermute(values, name, [(i, i ^ mask) for i in range(lax.axis_size(na...]
    concatenate x1, other arithmetic: 0.02 us -> 0.92 us  [routed(): y_rows = jnp.concatenate([y_top, y_low], axis=0)]
    ppermute x26 -> x28, waiting for transfers between devices: 21.5 us -> 20.9 us  [swap(): lax.ppermute(values, name, [(i, i ^ mask) for i in range(lax.axis_size(na...]
  transfers between devices with their start and end apart: 27 -> 29, of which waited for: 19 -> 20; matrix products, arithmetic and copies ran while one was open for 1% -> 3% of each run, Pallas kernels for 0% -> 0%
where the time goes in v4:
time: 85.7 us; the launch traced here: 85.4 us
  waiting for transfers between devices  31.7 us (37%)
  starting transfers between devices  30.8 us (36%)
  blocking collectives  13 us (15%)
  other arithmetic  4.01 us (5%)
  local copies, waits for them, and re-layouts  2.78 us (3%)
  matrix products  1.82 us (2%)
  between operations  1.3 us (2%)
    ppermute x28, starting transfers between devices, swap(): lax.ppermute(values, name, [(i, i ^ mask) for i in range(lax.axis_size(na...  26.4 us
    ppermute x28, waiting for transfers between devices, swap(): lax.ppermute(values, name, [(i, i ^ mask) for i in range(lax.axis_size(na...  20.9 us
    all_to_all x1, blocking collectives, core_groups(): lax.all_to_all(values, ('dp', 'shard'), split_axis=0, concat_axis=0, axis...  13 us
    all_to_all x1, waiting for transfers between devices, core_groups(): lax.all_to_all(values, ('dp', 'shard'), split_axis=0, concat_axis=0, axis...  10.8 us
    all_to_all x1, starting transfers between devices, core_groups(): lax.all_to_all(values, ('dp', 'shard'), split_axis=0, concat_axis=0, axis...  4.34 us
    select_n x1, other arithmetic, routed(): updated = jnp.where(place < across, updated, far_both)  1.84 us
  transfers between devices with their start and end apart: 29, of which 20 were waited for; matrix products, arithmetic and copies ran while one was open for 3% of the time, Pallas kernels for 0%

profile of v4, /device:TPU:0, one launch (start us, length us, event | category | flops | bytes accessed | tf_op | source)
XLA Modules:
  0.0 85.4 jit_solution(3694388277893574077)
XLA Ops:
  0.7 1.3 %dynamic-slice_bitcast_fusion = (bf16[8,4,32,256]{3,2,1,0:T(8,128)(2,1)S(1)}, bf16[8,4,32,256]{3,2,1,0:T(8,128)(2,1)S(1)}) fusion(bf16[8,4,2,32,256]{4,3,2,1,0:T(8,128)(2,1)} %bitcast.104, s32[]{:T(128)S(6)} %select_n.156, s32[]{:T(128)S(6)} %select_n.155), kind=kLoop, calls=%fused_computation.3 | loop fusion | bytes 2097160 | tf_op jit(solution)/shard_map/jit(dynamic_index_in_dim)/squeeze | solution.py:21
  3.9 3.0 %collective-permute-start.8 = (f32[4,32,256]{2,1,0:T(8,128)S(1)}, f32[4,32,256]{2,1,0:T(8,128)S(1)}, u32[]{:S(2)}, u32[]{:S(2)}) collective-permute-start(f32[4,32,256]{2,1,0:T(8,128)S(1)} %get-tuple-element.42), channel_id=1, source_target_pairs={{0,16},{4,20},{8,24},{12,28},{16,0},{20,4},{24,8},{28,12},{1,17},{... | collective-permute-start | bytes 393224 | tf_op jit(solution)/shard_map/sum_far_top/ppermute | solution.py:17
  6.8 1.5 %collective-permute-start.6 = (f32[4,32,256]{2,1,0:T(8,128)S(1)}, f32[4,32,256]{2,1,0:T(8,128)S(1)}, u32[]{:S(2)}, u32[]{:S(2)}) collective-permute-start(f32[4,32,256]{2,1,0:T(8,128)S(1)} %get-tuple-element.39), channel_id=1, source_target_pairs={{0,8},{4,12},{8,0},{12,4},{16,24},{20,28},{24,16},{28,20},{1,9},{5... | collective-permute-start | bytes 393224 | tf_op jit(solution)/shard_map/sum_far_low/ppermute | solution.py:17
  9.6 1.1 %collective-permute-done.8 = f32[4,32,256]{2,1,0:T(8,128)S(1)} collective-permute-done((f32[4,32,256]{2,1,0:T(8,128)S(1)}, f32[4,32,256]{2,1,0:T(8,128)S(1)}, u32[]{:S(2)}, u32[]{:S(2)}) %collective-permute-start.8) | collective-permute-done | bytes 131104 | tf_op jit(solution)/shard_map/sum_far_top/ppermute | solution.py:17
  10.6 1.8 %collective-permute-start.9 = (f32[4,32,256]{2,1,0:T(8,128)S(1)}, f32[4,32,256]{2,1,0:T(8,128)S(1)}, u32[]{:S(2)}, u32[]{:S(2)}) collective-permute-start(f32[4,32,256]{2,1,0:T(8,128)S(1)} %add.186), channel_id=1, source_target_pairs={{0,8},{4,12},{8,0},{12,4},{16,24},{20,28},{24,16},{28,20},{1,9},{5... | collective-permute-start | bytes 393224 | tf_op jit(solution)/shard_map/sum_relay_top/ppermute | solution.py:17
  13.2 1.6 %collective-permute-start.7 = (f32[4,32,256]{2,1,0:T(8,128)S(1)}, f32[4,32,256]{2,1,0:T(8,128)S(1)}, u32[]{:S(2)}, u32[]{:S(2)}) collective-permute-start(f32[4,32,256]{2,1,0:T(8,128)S(1)} %add.184), channel_id=1, source_target_pairs={{0,16},{4,20},{8,24},{12,28},{16,0},{20,4},{24,8},{28,12},{1,17},{... | collective-permute-start | bytes 393224 | tf_op jit(solution)/shard_map/sum_relay_low/ppermute | solution.py:17
  14.9 1.2 %collective-permute-done.3 = f32[4,32,256]{2,1,0:T(8,128)S(1)} collective-permute-done((f32[4,32,256]{2,1,0:T(8,128)S(1)}, f32[4,32,256]{2,1,0:T(8,128)S(1)}, u32[]{:S(2)}, u32[]{:S(2)}) %collective-permute-start.3) | collective-permute-done | bytes 131104 | tf_op jit(solution)/shard_map/sum_x_low/ppermute | solution.py:17
  16.1 1.6 %collective-permute-done.9 = f32[4,32,256]{2,1,0:T(8,128)S(1)} collective-permute-done((f32[4,32,256]{2,1,0:T(8,128)S(1)}, f32[4,32,256]{2,1,0:T(8,128)S(1)}, u32[]{:S(2)}, u32[]{:S(2)}) %collective-permute-start.9) | collective-permute-done | bytes 131104 | tf_op jit(solution)/shard_map/sum_relay_top/ppermute | solution.py:17
  18.4 3.7 %collective-permute-start.12 = (f32[8,8,256]{2,1,0:T(8,128)S(1)}, f32[8,8,256]{2,1,0:T(8,128)S(1)}, u32[]{:S(2)}, u32[]{:S(2)}) collective-permute-start(f32[8,8,256]{2,1,0:T(8,128)S(1)} %get-tuple-element.74), channel_id=1, source_target_pairs={{0,3},{1,2},{2,1},{3,0},{4,7},{5,6},{6,5},{7,4},{8,11},{9,10},{10,... | collective-permute-start | bytes 196616 | tf_op jit(solution)/shard_map/shard_3/ppermute | solution.py:17
  22.0 0.8 collective-permute-start.10
  23.1 1.4 %collective-permute-done.12 = f32[8,8,256]{2,1,0:T(8,128)S(1)} collective-permute-done((f32[8,8,256]{2,1,0:T(8,128)S(1)}, f32[8,8,256]{2,1,0:T(8,128)S(1)}, u32[]{:S(2)}, u32[]{:S(2)}) %collective-permute-start.12) | collective-permute-done | bytes 65568 | tf_op jit(solution)/shard_map/shard_3/ppermute | solution.py:17
  24.5 2.7 %collective-permute-done.11 = f32[8,8,256]{2,1,0:T(8,128)S(1)} collective-permute-done((f32[8,8,256]{2,1,0:T(8,128)S(1)}, f32[8,8,256]{2,1,0:T(8,128)S(1)}, u32[]{:S(2)}, u32[]{:S(2)}) %collective-permute-start.11) | collective-permute-done | bytes 65568 | tf_op jit(solution)/shard_map/shard_2/ppermute | solution.py:17
  27.7 1.3 %collective-permute-done.13 = f32[16,8,256]{2,1,0:T(8,128)S(1)} collective-permute-done((f32[16,8,256]{2,1,0:T(8,128)S(1)}, f32[16,8,256]{2,1,0:T(8,128)S(1)}, u32[]{:S(2)}, u32[]{:S(2)}) %collective-permute-start.13) | collective-permute-done | bytes 131104 | tf_op jit(solution)/shard_map/pieces_core/ppermute | solution.py:17
  29.7 4.3 %all-to-all-start = ((f32[16,2,8,256]{3,2,1,0:T(8,128)}), f32[16,2,8,256]{3,2,1,0:T(8,128)S(1)}, u32[]{:S(2)}, u32[]{:S(2)}) async-start(f32[16,2,8,256]{3,2,1,0:T(8,128)} %pad_maximum_fusion), calls=%async_computation | async-start | bytes 524288 | tf_op jit(solution)/shard_map/all_to_all | solution.py:98
  34.1 10.8 %all-to-all-done = f32[16,2,8,256]{3,2,1,0:T(8,128)S(1)} async-done(((f32[16,2,8,256]{3,2,1,0:T(8,128)}), f32[16,2,8,256]{3,2,1,0:T(8,128)S(1)}, u32[]{:S(2)}, u32[]{:S(2)}) %all-to-all-start) | async-done | bytes 262176 | tf_op jit(solution)/shard_map/all_to_all | solution.py:98
  46.4 13.0 %all_to_all.10 = f32[16,2,8,256]{3,2,1,0:T(8,128)S(1)} all-to-all(f32[16,2,8,256]{3,2,1,0:T(8,128)S(1)} %fusion.47), channel_id=1, replica_groups={{0,1,2,3,8,9,10,11,16,17,18,19,24,25,26,27},{4,5,6,7,12,13,14,15,20,21,..., dimensions={0} | all-to-all | bytes 524288 | tf_op jit(solution)/shard_map/all_to_all | solution.py:98
  59.5 1.3 %collective-permute-done.14 = f32[16,8,256]{2,1,0:T(8,128)S(1)} collective-permute-done((f32[16,8,256]{2,1,0:T(8,128)S(1)}, f32[16,8,256]{2,1,0:T(8,128)S(1)}, u32[]{:S(2)}, u32[]{:S(2)}) %collective-permute-start.14) | collective-permute-done | bytes 131104 | tf_op jit(solution)/shard_map/change_core/ppermute | solution.py:17
  61.3 1.6 %collective-permute-start.16 = (f32[8,8,256]{2,1,0:T(8,128)S(1)}, f32[8,8,256]{2,1,0:T(8,128)S(1)}, u32[]{:S(2)}, u32[]{:S(2)}) collective-permute-start(f32[8,8,256]{2,1,0:T(8,128)S(1)} %copy.53), channel_id=1, source_target_pairs={{0,2},{1,3},{2,0},{3,1},{4,6},{5,7},{6,4},{7,5},{8,10},{9,11},{10,... | collective-permute-start | bytes 196616 | tf_op jit(solution)/shard_map/shard_2/ppermute | solution.py:17
  62.9 2.9 %collective-permute-start.17 = (f32[8,8,256]{2,1,0:T(8,128)S(1)}, f32[8,8,256]{2,1,0:T(8,128)S(1)}, u32[]{:S(2)}, u32[]{:S(2)}) collective-permute-start(f32[8,8,256]{2,1,0:T(8,128)S(1)} %copy.54), channel_id=1, source_target_pairs={{0,1},{1,0},{2,3},{3,2},{4,5},{5,4},{6,7},{7,6},{8,9},{9,8},{10,11... | collective-permute-start | bytes 196616 | tf_op jit(solution)/shard_map/shard_1/ppermute | solution.py:17
  65.9 2.2 %collective-permute-done.15 = f32[8,8,256]{2,1,0:T(8,128)S(1)} collective-permute-done((f32[8,8,256]{2,1,0:T(8,128)S(1)}, f32[8,8,256]{2,1,0:T(8,128)S(1)}, u32[]{:S(2)}, u32[]{:S(2)}) %collective-permute-start.15) | collective-permute-done | bytes 65568 | tf_op jit(solution)/shard_map/shard_3/ppermute | solution.py:17
  68.1 1.1 %collective-permute-done.16 = f32[8,8,256]{2,1,0:T(8,128)S(1)} collective-permute-done((f32[8,8,256]{2,1,0:T(8,128)S(1)}, f32[8,8,256]{2,1,0:T(8,128)S(1)}, u32[]{:S(2)}, u32[]{:S(2)}) %collective-permute-start.16) | collective-permute-done | bytes 65568 | tf_op jit(solution)/shard_map/shard_2/ppermute | solution.py:17
  70.1 1.2 %collective-permute-start.22 = (f32[4,32,256]{2,1,0:T(8,128)S(1)}, f32[4,32,256]{2,1,0:T(8,128)S(1)}, u32[]{:S(2)}, u32[]{:S(2)}) collective-permute-start(f32[4,32,256]{2,1,0:T(8,128)S(1)} %get-tuple-element.46), channel_id=1, source_target_pairs={{0,16},{4,20},{8,24},{12,28},{16,0},{20,4},{24,8},{28,12},{1,17},{... | collective-permute-start | bytes 393224 | tf_op jit(solution)/shard_map/rows_y_low/ppermute | solution.py:17
  71.5 1.0 %collective-permute-start.19 = (f32[4,32,256]{2,1,0:T(8,128)S(1)}, f32[4,32,256]{2,1,0:T(8,128)S(1)}, u32[]{:S(2)}, u32[]{:S(2)}) collective-permute-start(f32[4,32,256]{2,1,0:T(8,128)S(1)} %get-tuple-element.46), channel_id=1, source_target_pairs={{0,8},{4,12},{8,0},{12,4},{16,24},{20,28},{24,16},{28,20},{1,9},{5... | collective-permute-start | bytes 393224 | tf_op jit(solution)/shard_map/rows_x_low/ppermute | solution.py:17
  72.5 1.2 %collective-permute-start.21 = (f32[4,32,256]{2,1,0:T(8,128)S(1)}, f32[4,32,256]{2,1,0:T(8,128)}, u32[]{:S(2)}, u32[]{:S(2)}) collective-permute-start(f32[4,32,256]{2,1,0:T(8,128)S(1)} %get-tuple-element.47), channel_id=1, source_target_pairs={{0,16},{4,20},{8,24},{12,28},{16,0},{20,4},{24,8},{28,12},{1,17},{... | collective-permute-start | bytes 393224 | tf_op jit(solution)/shard_map/rows_y_top/ppermute | solution.py:17
  74.1 1.1 %collective-permute-done.20 = f32[4,32,256]{2,1,0:T(8,128)S(1)} collective-permute-done((f32[4,32,256]{2,1,0:T(8,128)S(1)}, f32[4,32,256]{2,1,0:T(8,128)S(1)}, u32[]{:S(2)}, u32[]{:S(2)}) %collective-permute-start.20) | collective-permute-done | bytes 131104 | tf_op jit(solution)/shard_map/rows_x_top/ppermute | solution.py:17
  75.2 0.8 collective-permute-start.23
  76.1 1.6 %collective-permute-start.26 = (f32[4,32,256]{2,1,0:T(8,128)S(1)}, f32[4,32,256]{2,1,0:T(8,128)S(1)}, u32[]{:S(2)}, u32[]{:S(2)}) collective-permute-start(f32[4,32,256]{2,1,0:T(8,128)S(1)} %collective-permute-done.22), channel_id=1, source_target_pairs={{0,8},{4,12},{8,0},{12,4},{16,24},{20,28},{24,16},{28,20},{1,9},{5... | collective-permute-start | bytes 393224 | tf_op jit(solution)/shard_map/rows_relay_low/ppermute | solution.py:17
  77.7 1.2 %collective-permute-done.21 = f32[4,32,256]{2,1,0:T(8,128)} collective-permute-done((f32[4,32,256]{2,1,0:T(8,128)S(1)}, f32[4,32,256]{2,1,0:T(8,128)}, u32[]{:S(2)}, u32[]{:S(2)}) %collective-permute-start.21) | collective-permute-done | bytes 131104 | tf_op jit(solution)/shard_map/rows_y_top/ppermute | solution.py:17
  78.9 0.9 %pad_maximum_fusion.2 = f32[8,32,256]{2,1,0:T(8,128)S(1)} fusion(f32[4,32,256]{2,1,0:T(8,128)S(1)} %collective-permute-done.22, f32[4,32,256]{2,1,0:T(8,128)} %collective-permute-done.21), kind=kLoop, calls=%fused_computation.23 | loop fusion | flops 65536 | bytes 524288 | tf_op jit(solution)/shard_map/concatenate | solution.py:168
  79.9 1.4 %collective-permute-done.23 = f32[4,32,256]{2,1,0:T(8,128)S(1)} collective-permute-done((f32[4,32,256]{2,1,0:T(8,128)S(1)}, f32[4,32,256]{2,1,0:T(8,128)S(1)}, u32[]{:S(2)}, u32[]{:S(2)}) %collective-permute-start.23) | collective-permute-done | bytes 131104 | tf_op jit(solution)/shard_map/rows_relay_top/ppermute | solution.py:17
  81.9 0.8 collective-permute-done.24
  83.5 1.8 %fusion = f32[8,256,256]{2,1,0:T(8,128)} fusion(f32[8,256,256]{2,1,0:T(8,128)S(1)} %slice_dynamic-update-slice_fusion, f32[8,32,256]{2,1,0:T(8,128)S(1)} %collective-permute-done.27, f32[8,32,256]{2,1,0:T(8,128)S(1)} %constant_dynamic-update-slice_fusion.4, pred[256]{0:T(512)(128)(4,1)S(1)} %iota.25, pred[256]{0:T(512)(128)(4,1)S(1)} %iota.22), kind=kLoop, calls=%fused_computation.1 | loop fusion | flops 1048576 | bytes 4719104 | tf_op jit(solution)/shard_map/jit(_where)/select_n | solution.py:189
  (114 shorter events, 10.9 us)
Async XLA Ops:
  0.6 44.7 %copy-start = (f32[1,1,1,256,256]{4,3,2,1,0:T(8,128)S(1)}, f32[1,1,1,256,256]{4,3,2,1,0:T(8,128)}, u32[]{:S(2)}) copy-start(f32[1,1,1,256,256]{4,3,2,1,0:T(8,128)} %param.10) | copy-start | bytes 786436
  2.1 1.7 %collective-permute-start = (f32[8,32,256]{2,1,0:T(8,128)S(1)}, f32[8,32,256]{2,1,0:T(8,128)S(1)}, u32[]{:S(2)}, u32[]{:S(2)}) collective-permute-start(f32[8,32,256]{2,1,0:T(8,128)S(1)} %get-tuple-element.60), channel_id=1, source_target_pairs={{0,4},{4,0},{8,12},{12,8},{16,20},{20,16},{24,28},{28,24},{1,5},{5... | collective-permute-start | bytes 786440 | tf_op jit(solution)/shard_map/sum_core_6/ppermute | solution.py:17
  2.7 5.7 %collective-permute-start.4 = (f32[8,32,256]{2,1,0:T(8,128)S(1)}, f32[8,32,256]{2,1,0:T(8,128)S(1)}, u32[]{:S(2)}, u32[]{:S(2)}) collective-permute-start(f32[8,32,256]{2,1,0:T(8,128)S(1)} %bitcast_convert_fusion), channel_id=1, source_target_pairs={{0,4},{4,0},{8,12},{12,8},{16,20},{20,16},{24,28},{28,24},{1,5},{5... | collective-permute-start | bytes 786440 | tf_op jit(solution)/shard_map/sum_core_4/ppermute | solution.py:17
  2.8 5.5 %collective-permute-start.2 = (f32[8,32,256]{2,1,0:T(8,128)S(1)}, f32[8,32,256]{2,1,0:T(8,128)S(1)}, u32[]{:S(2)}, u32[]{:S(2)}) collective-permute-start(f32[8,32,256]{2,1,0:T(8,128)S(1)} %get-tuple-element.58), channel_id=1, source_target_pairs={{0,4},{4,0},{8,12},{12,8},{16,20},{20,16},{24,28},{28,24},{1,5},{5... | collective-permute-start | bytes 786440 | tf_op jit(solution)/shard_map/sum_core_2/ppermute | solution.py:17
  3.2 5.1 %collective-permute-start.1 = (f32[8,32,256]{2,1,0:T(8,128)S(1)}, f32[8,32,256]{2,1,0:T(8,128)S(1)}, u32[]{:S(2)}, u32[]{:S(2)}) collective-permute-start(f32[8,32,256]{2,1,0:T(8,128)S(1)} %get-tuple-element.59), channel_id=1, source_target_pairs={{0,4},{4,0},{8,12},{12,8},{16,20},{20,16},{24,28},{28,24},{1,5},{5... | collective-permute-start | bytes 786440 | tf_op jit(solution)/shard_map/sum_core_0/ppermute | solution.py:17
  3.9 6.8 %collective-permute-start.8 = (f32[4,32,256]{2,1,0:T(8,128)S(1)}, f32[4,32,256]{2,1,0:T(8,128)S(1)}, u32[]{:S(2)}, u32[]{:S(2)}) collective-permute-start(f32[4,32,256]{2,1,0:T(8,128)S(1)} %get-tuple-element.42), channel_id=1, source_target_pairs={{0,16},{4,20},{8,24},{12,28},{16,0},{20,4},{24,8},{28,12},{1,17},{... | collective-permute-start | bytes 393224 | tf_op jit(solution)/shard_map/sum_far_top/ppermute | solution.py:17
  6.8 6.4 %collective-permute-start.6 = (f32[4,32,256]{2,1,0:T(8,128)S(1)}, f32[4,32,256]{2,1,0:T(8,128)S(1)}, u32[]{:S(2)}, u32[]{:S(2)}) collective-permute-start(f32[4,32,256]{2,1,0:T(8,128)S(1)} %get-tuple-element.39), channel_id=1, source_target_pairs={{0,8},{4,12},{8,0},{12,4},{16,24},{20,28},{24,16},{28,20},{1,9},{5... | collective-permute-start | bytes 393224 | tf_op jit(solution)/shard_map/sum_far_low/ppermute | solution.py:17
  8.5 7.5 %collective-permute-start.3 = (f32[4,32,256]{2,1,0:T(8,128)S(1)}, f32[4,32,256]{2,1,0:T(8,128)S(1)}, u32[]{:S(2)}, u32[]{:S(2)}) collective-permute-start(f32[4,32,256]{2,1,0:T(8,128)S(1)} %get-tuple-element.34), channel_id=1, source_target_pairs={{0,8},{4,12},{8,0},{12,4},{16,24},{20,28},{24,16},{28,20},{1,9},{5... | collective-permute-start | bytes 393224 | tf_op jit(solution)/shard_map/sum_x_low/ppermute | solution.py:17
  9.1 6.9 %collective-permute-start.5 = (f32[4,32,256]{2,1,0:T(8,128)S(1)}, f32[4,32,256]{2,1,0:T(8,128)S(1)}, u32[]{:S(2)}, u32[]{:S(2)}) collective-permute-start(f32[4,32,256]{2,1,0:T(8,128)S(1)} %get-tuple-element.36), channel_id=1, source_target_pairs={{0,16},{4,20},{8,24},{12,28},{16,0},{20,4},{24,8},{28,12},{1,17},{... | collective-permute-start | bytes 393224 | tf_op jit(solution)/shard_map/sum_y_top/ppermute | solution.py:17
  10.6 7.1 %collective-permute-start.9 = (f32[4,32,256]{2,1,0:T(8,128)S(1)}, f32[4,32,256]{2,1,0:T(8,128)S(1)}, u32[]{:S(2)}, u32[]{:S(2)}) collective-permute-start(f32[4,32,256]{2,1,0:T(8,128)S(1)} %add.186), channel_id=1, source_target_pairs={{0,8},{4,12},{8,0},{12,4},{16,24},{20,28},{24,16},{28,20},{1,9},{5... | collective-permute-start | bytes 393224 | tf_op jit(solution)/shard_map/sum_relay_top/ppermute | solution.py:17
  13.2 5.0 %collective-permute-start.7 = (f32[4,32,256]{2,1,0:T(8,128)S(1)}, f32[4,32,256]{2,1,0:T(8,128)S(1)}, u32[]{:S(2)}, u32[]{:S(2)}) collective-permute-start(f32[4,32,256]{2,1,0:T(8,128)S(1)} %add.184), channel_id=1, source_target_pairs={{0,16},{4,20},{8,24},{12,28},{16,0},{20,4},{24,8},{28,12},{1,17},{... | collective-permute-start | bytes 393224 | tf_op jit(solution)/shard_map/sum_relay_low/ppermute | solution.py:17
  18.4 6.1 %collective-permute-start.12 = (f32[8,8,256]{2,1,0:T(8,128)S(1)}, f32[8,8,256]{2,1,0:T(8,128)S(1)}, u32[]{:S(2)}, u32[]{:S(2)}) collective-permute-start(f32[8,8,256]{2,1,0:T(8,128)S(1)} %get-tuple-element.74), channel_id=1, source_target_pairs={{0,3},{1,2},{2,1},{3,0},{4,7},{5,6},{6,5},{7,4},{8,11},{9,10},{10,... | collective-permute-start | bytes 196616 | tf_op jit(solution)/shard_map/shard_3/ppermute | solution.py:17
  22.0 5.2 %collective-permute-start.11 = (f32[8,8,256]{2,1,0:T(8,128)S(1)}, f32[8,8,256]{2,1,0:T(8,128)S(1)}, u32[]{:S(2)}, u32[]{:S(2)}) collective-permute-start(f32[8,8,256]{2,1,0:T(8,128)S(1)} %get-tuple-element.75), channel_id=1, source_target_pairs={{0,2},{1,3},{2,0},{3,1},{4,6},{5,7},{6,4},{7,5},{8,10},{9,11},{10,... | collective-permute-start | bytes 196616 | tf_op jit(solution)/shard_map/shard_2/ppermute | solution.py:17
  22.0 5.2 %collective-permute-start.10 = (f32[8,8,256]{2,1,0:T(8,128)S(1)}, f32[8,8,256]{2,1,0:T(8,128)S(1)}, u32[]{:S(2)}, u32[]{:S(2)}) collective-permute-start(f32[8,8,256]{2,1,0:T(8,128)S(1)} %get-tuple-element.76), channel_id=1, source_target_pairs={{0,1},{1,0},{2,3},{3,2},{4,5},{5,4},{6,7},{7,6},{8,9},{9,8},{10,11... | collective-permute-start | bytes 196616 | tf_op jit(solution)/shard_map/shard_1/ppermute | solution.py:17
  27.6 1.4 %collective-permute-start.13 = (f32[16,8,256]{2,1,0:T(8,128)S(1)}, f32[16,8,256]{2,1,0:T(8,128)S(1)}, u32[]{:S(2)}, u32[]{:S(2)}) collective-permute-start(f32[16,8,256]{2,1,0:T(8,128)S(1)} %bitcast.123), channel_id=1, source_target_pairs={{0,4},{4,0},{8,12},{12,8},{16,20},{20,16},{24,28},{28,24},{1,5},{5... | collective-permute-start | bytes 393224 | tf_op jit(solution)/shard_map/pieces_core/ppermute | solution.py:17
  29.7 15.2 %all-to-all-start = ((f32[16,2,8,256]{3,2,1,0:T(8,128)}), f32[16,2,8,256]{3,2,1,0:T(8,128)S(1)}, u32[]{:S(2)}, u32[]{:S(2)}) async-start(f32[16,2,8,256]{3,2,1,0:T(8,128)} %pad_maximum_fusion), calls=%async_computation | async-start | bytes 524288 | tf_op jit(solution)/shard_map/all_to_all | solution.py:98
  46.1 19.7 %copy-start.2 = (f32[8,32,256]{2,1,0:T(8,128)S(1)}, f32[8,32,256]{2,1,0:T(8,128)}, u32[]{:S(2)}) copy-start(f32[8,32,256]{2,1,0:T(8,128)} %param.8) | copy-start | bytes 786436
  46.4 21.7 %copy-start.1 = (f32[8,32,256]{2,1,0:T(8,128)S(1)}, f32[8,32,256]{2,1,0:T(8,128)}, u32[]{:S(2)}) copy-start(f32[8,32,256]{2,1,0:T(8,128)} %param.8) | copy-start | bytes 786436
  59.4 1.4 %collective-permute-start.14 = (f32[16,8,256]{2,1,0:T(8,128)S(1)}, f32[16,8,256]{2,1,0:T(8,128)S(1)}, u32[]{:S(2)}, u32[]{:S(2)}) collective-permute-start(f32[16,8,256]{2,1,0:T(8,128)S(1)} %get-tuple-element.68), channel_id=1, source_target_pairs={{0,4},{4,0},{8,12},{12,8},{16,20},{20,16},{24,28},{28,24},{1,5},{5... | collective-permute-start | bytes 393224 | tf_op jit(solution)/shard_map/change_core/ppermute | solution.py:17
  61.2 6.9 %collective-permute-start.15 = (f32[8,8,256]{2,1,0:T(8,128)S(1)}, f32[8,8,256]{2,1,0:T(8,128)S(1)}, u32[]{:S(2)}, u32[]{:S(2)}) collective-permute-start(f32[8,8,256]{2,1,0:T(8,128)S(1)} %copy.52), channel_id=1, source_target_pairs={{0,3},{1,2},{2,1},{3,0},{4,7},{5,6},{6,5},{7,4},{8,11},{9,10},{10,... | collective-permute-start | bytes 196616 | tf_op jit(solution)/shard_map/shard_3/ppermute | solution.py:17
  61.3 7.9 %collective-permute-start.16 = (f32[8,8,256]{2,1,0:T(8,128)S(1)}, f32[8,8,256]{2,1,0:T(8,128)S(1)}, u32[]{:S(2)}, u32[]{:S(2)}) collective-permute-start(f32[8,8,256]{2,1,0:T(8,128)S(1)} %copy.53), channel_id=1, source_target_pairs={{0,2},{1,3},{2,0},{3,1},{4,6},{5,7},{6,4},{7,5},{8,10},{9,11},{10,... | collective-permute-start | bytes 196616 | tf_op jit(solution)/shard_map/shard_2/ppermute | solution.py:17
  62.9 6.4 %collective-permute-start.17 = (f32[8,8,256]{2,1,0:T(8,128)S(1)}, f32[8,8,256]{2,1,0:T(8,128)S(1)}, u32[]{:S(2)}, u32[]{:S(2)}) collective-permute-start(f32[8,8,256]{2,1,0:T(8,128)S(1)} %copy.54), channel_id=1, source_target_pairs={{0,1},{1,0},{2,3},{3,2},{4,5},{5,4},{6,7},{7,6},{8,9},{9,8},{10,11... | collective-permute-start | bytes 196616 | tf_op jit(solution)/shard_map/shard_1/ppermute | solution.py:17
  69.4 5.9 %collective-permute-start.20 = (f32[4,32,256]{2,1,0:T(8,128)S(1)}, f32[4,32,256]{2,1,0:T(8,128)S(1)}, u32[]{:S(2)}, u32[]{:S(2)}) collective-permute-start(f32[4,32,256]{2,1,0:T(8,128)S(1)} %get-tuple-element.47), channel_id=1, source_target_pairs={{0,8},{4,12},{8,0},{12,4},{16,24},{20,28},{24,16},{28,20},{1,9},{5... | collective-permute-start | bytes 393224 | tf_op jit(solution)/shard_map/rows_x_top/ppermute | solution.py:17
  70.1 6.0 %collective-permute-start.22 = (f32[4,32,256]{2,1,0:T(8,128)S(1)}, f32[4,32,256]{2,1,0:T(8,128)S(1)}, u32[]{:S(2)}, u32[]{:S(2)}) collective-permute-start(f32[4,32,256]{2,1,0:T(8,128)S(1)} %get-tuple-element.46), channel_id=1, source_target_pairs={{0,16},{4,20},{8,24},{12,28},{16,0},{20,4},{24,8},{28,12},{1,17},{... | collective-permute-start | bytes 393224 | tf_op jit(solution)/shard_map/rows_y_low/ppermute | solution.py:17
  71.5 6.2 %collective-permute-start.19 = (f32[4,32,256]{2,1,0:T(8,128)S(1)}, f32[4,32,256]{2,1,0:T(8,128)S(1)}, u32[]{:S(2)}, u32[]{:S(2)}) collective-permute-start(f32[4,32,256]{2,1,0:T(8,128)S(1)} %get-tuple-element.46), channel_id=1, source_target_pairs={{0,8},{4,12},{8,0},{12,4},{16,24},{20,28},{24,16},{28,20},{1,9},{5... | collective-permute-start | bytes 393224 | tf_op jit(solution)/shard_map/rows_x_low/ppermute | solution.py:17
  72.5 7.3 %collective-permute-start.18 = (f32[8,32,256]{2,1,0:T(8,128)S(1)}, f32[8,32,256]{2,1,0:T(8,128)S(1)}, u32[]{:S(2)}, u32[]{:S(2)}) collective-permute-start(f32[8,32,256]{2,1,0:T(8,128)S(1)} %subtract_dynamic-update-slice_fusion), channel_id=1, source_target_pairs={{0,4},{4,0},{8,12},{12,8},{16,20},{20,16},{24,28},{28,24},{1,5},{5... | collective-permute-start | bytes 786440 | tf_op jit(solution)/shard_map/rows_core_own/ppermute | solution.py:17
  72.5 6.4 %collective-permute-start.21 = (f32[4,32,256]{2,1,0:T(8,128)S(1)}, f32[4,32,256]{2,1,0:T(8,128)}, u32[]{:S(2)}, u32[]{:S(2)}) collective-permute-start(f32[4,32,256]{2,1,0:T(8,128)S(1)} %get-tuple-element.47), channel_id=1, source_target_pairs={{0,16},{4,20},{8,24},{12,28},{16,0},{20,4},{24,8},{28,12},{1,17},{... | collective-permute-start | bytes 393224 | tf_op jit(solution)/shard_map/rows_y_top/ppermute | solution.py:17
  75.2 6.0 %collective-permute-start.23 = (f32[4,32,256]{2,1,0:T(8,128)S(1)}, f32[4,32,256]{2,1,0:T(8,128)S(1)}, u32[]{:S(2)}, u32[]{:S(2)}) collective-permute-start(f32[4,32,256]{2,1,0:T(8,128)S(1)} %collective-permute-done.20), channel_id=1, source_target_pairs={{0,16},{4,20},{8,24},{12,28},{16,0},{20,4},{24,8},{28,12},{1,17},{... | collective-permute-start | bytes 393224 | tf_op jit(solution)/shard_map/rows_relay_top/ppermute | solution.py:17
  76.1 5.7 %collective-permute-start.26 = (f32[4,32,256]{2,1,0:T(8,128)S(1)}, f32[4,32,256]{2,1,0:T(8,128)S(1)}, u32[]{:S(2)}, u32[]{:S(2)}) collective-permute-start(f32[4,32,256]{2,1,0:T(8,128)S(1)} %collective-permute-done.22), channel_id=1, source_target_pairs={{0,8},{4,12},{8,0},{12,4},{16,24},{20,28},{24,16},{28,20},{1,9},{5... | collective-permute-start | bytes 393224 | tf_op jit(solution)/shard_map/rows_relay_low/ppermute | solution.py:17
  81.2 1.5 %collective-permute-start.24 = (f32[8,32,256]{2,1,0:T(8,128)S(1)}, f32[8,32,256]{2,1,0:T(8,128)S(1)}, u32[]{:S(2)}, u32[]{:S(2)}) collective-permute-start(f32[8,32,256]{2,1,0:T(8,128)S(1)} %pad_maximum_fusion.1), channel_id=1, source_target_pairs={{0,4},{4,0},{8,12},{12,8},{16,20},{20,16},{24,28},{28,24},{1,5},{5... | collective-permute-start | bytes 786440 | tf_op jit(solution)/shard_map/rows_core_x/ppermute | solution.py:17
  81.2 1.9 %collective-permute-start.25 = (f32[8,32,256]{2,1,0:T(8,128)S(1)}, f32[8,32,256]{2,1,0:T(8,128)S(1)}, u32[]{:S(2)}, u32[]{:S(2)}) collective-permute-start(f32[8,32,256]{2,1,0:T(8,128)S(1)} %pad_maximum_fusion.2), channel_id=1, source_target_pairs={{0,4},{4,0},{8,12},{12,8},{16,20},{20,16},{24,28},{28,24},{1,5},{5... | collective-permute-start | bytes 786440 | tf_op jit(solution)/shard_map/rows_core_y/ppermute | solution.py:17
  81.8 1.7 %collective-permute-start.27 = (f32[8,32,256]{2,1,0:T(8,128)S(1)}, f32[8,32,256]{2,1,0:T(8,128)S(1)}, u32[]{:S(2)}, u32[]{:S(2)}) collective-permute-start(f32[8,32,256]{2,1,0:T(8,128)S(1)} %constant_dynamic-update-slice_fusion.4), channel_id=1, source_target_pairs={{0,4},{4,0},{8,12},{12,8},{16,20},{20,16},{24,28},{28,24},{1,5},{5... | collective-permute-start | bytes 786440 | tf_op jit(solution)/shard_map/rows_core_far/ppermute | solution.py:17
  (6 other events, 96.8 us)

commit v5 on v3

--- a/solution.py
+++ b/solution.py
@@ -85,39 +85,54 @@
     home_count, row_count, width = params.shape
     half = home_count // 2
     piece = (row_count // shard_count, width)
-
-    owners = unmix(owner_list.reshape(shard_count, home_count), shard_here).reshape(1, -1)
-    device_ids = jnp.arange(device_total, dtype=jnp.int32)
-    picker = (owners == device_ids[:, None]).astype(jnp.float32)
-
     chips = data_count // 2
+    my_core = data_here & core
+    shard_half, shard_low = shard_here >> 1, shard_here & 1
+
+    def set_of(values, index):
+        split = values.reshape((home_count, 2, values.shape[1] // 2, width))
+        return take(split, 1, index)
+
     grid = partials[0].reshape((home_count, chips, 2, row_count, width))
-    away_rows = take(grid, 2, 1 - (data_here & core))
-    own_rows = take(grid, 2, data_here & core)
+    away_rows = take(grid, 2, 1 - my_core)
+    own_rows = take(grid, 2, my_core)
     away_rows, own_rows = lax.optimization_barrier((away_rows, own_rows))
 
     def rows_of(values, mask):
         return take(values, 1, (data_here ^ mask) // 2).astype(jnp.float32)
 
-    part = {}
+    near, far = {}, {}
     for mask in (across, along_x, along_y, 0):
         total = rows_of(own_rows, mask) + swap(
             rows_of(away_rows, mask), "dp", core, f"sum_core_{mask}"
         )
-        part[mask] = lax.optimization_barrier((total[:half], total[half:]))
+        near[mask], far[mask] = lax.optimization_barrier(
+            (set_of(total, shard_half), set_of(total, 1 - shard_half))
+        )
         if mask == across:
-            own_rows, part[mask] = lax.optimization_barrier((own_rows, part[mask]))
-    near_y = part[along_y][0] + swap(part[across][0], "dp", along_x, "sum_far_low")
-    near_x = part[along_x][1] + swap(part[across][1], "dp", along_y, "sum_far_top")
-    low = part[0][0] + swap(part[along_x][0], "dp", along_x, "sum_x_low")
-    top = part[0][1] + swap(part[along_y][1], "dp", along_y, "sum_y_top")
-    low, top = lax.optimization_barrier((low, top))
-    low = low + swap(near_y, "dp", along_y, "sum_relay_low")
-    top = top + swap(near_x, "dp", along_x, "sum_relay_top")
-
-    summed = jnp.concatenate([low, top], axis=0)
-    summed = summed.reshape((home_count, shard_count) + piece)
-    mixed = shard_exchange([take(summed, 1, shard_here ^ k) for k in range(shard_count)])
+            own_rows, near[mask], far[mask] = lax.optimization_barrier(
+                (own_rows, near[mask], far[mask])
+            )
+    far_relay = far[along_y] + swap(far[across], "dp", along_x, "sum_across_far")
+    near_relay = near[along_x] + swap(near[across], "dp", along_y, "sum_across_near")
+    far_sum = far[0] + swap(far[along_x], "dp", along_x, "sum_x_far")
+    far_sum = lax.optimization_barrier(far_sum)
+    far_sum = far_sum + swap(far_relay, "dp", along_y, "sum_relay_far")
+    near_sum = near[0] + swap(near_relay, "dp", along_x, "sum_relay_near")
+    near_sum = lax.optimization_barrier(near_sum)
+    near_sum = near_sum + swap(near[along_y], "dp", along_y, "sum_y_near")
+
+    mixed = shard_exchange(
+        [
+            set_of(near_sum, shard_low),
+            set_of(near_sum, 1 - shard_low),
+            set_of(far_sum, shard_low),
+            set_of(far_sum, 1 - shard_low),
+        ]
+    )
+    owners = unmix(owner_list.reshape(shard_count, home_count), shard_here).reshape(1, -1)
+    device_ids = jnp.arange(device_total, dtype=jnp.int32)
+    picker = (owners == device_ids[:, None]).astype(jnp.float32)
     pieces = jnp.concatenate(mixed, axis=0).reshape(device_total, -1)
     leaving = jnp.einsum("eb,bn->en", picker, pieces, precision=high)
     whole = lax.all_to_all(
@@ -146,8 +161,9 @@
     ).reshape(device_total, -1)
     back = jnp.einsum("eb,en->bn", picker, coming, precision=high)
     back = back.reshape((shard_count, home_count) + piece)
+    returned = shard_exchange([back[k] for k in range(shard_count)])
+
     new_home = params
-    returned = shard_exchange([back[k] for k in range(shard_count)])
     for k in (0, 3, 2, 1):
         start = (shard_here ^ k) * piece[0]
         home = lax.dynamic_slice_in_dim(params, start, piece[0], axis=1)

time: 81.4 us -> 81.3 us (level)
  waiting for transfers between devices: 31.7 us -> 30.2 us
    ppermute x26, waiting for transfers between devices: 21.5 us -> 20 us  [swap(): lax.ppermute(values, name, [(i, i ^ mask) for i in range(lax.axis_size(na...]
  transfers between devices with their start and end apart: 27 -> 27, of which waited for: 19 -> 17; matrix products, arithmetic and copies ran while one was open for 1% -> 1% of each run, Pallas kernels for 0% -> 0%
where the time goes in v5:
time: 81.3 us; the launch traced here: 81.1 us
  waiting for transfers between devices  30.2 us (37%)
  starting transfers between devices  28.6 us (35%)
  blocking collectives  14 us (17%)
  local copies, waits for them, and re-layouts  3.84 us (5%)
  matrix products  2.64 us (3%)
  between operations  1.26 us (2%)
    ppermute x26, starting transfers between devices, swap(): lax.ppermute(values, name, [(i, i ^ mask) for i in range(lax.axis_size(na...  25.9 us
    ppermute x26, waiting for transfers between devices, swap(): lax.ppermute(values, name, [(i, i ^ mask) for i in range(lax.axis_size(na...  20 us
    all_to_all x1, blocking collectives, routed(): lax.all_to_all(leaving.reshape((device_total,) + piece), ('dp', 'shard'),...  14 us
    all_to_all x1, waiting for transfers between devices, routed(): lax.all_to_all(change.reshape((device_total,) + piece), ('dp', 'shard'),...  10.2 us
    all_to_all x1, starting transfers between devices, routed(): lax.all_to_all(change.reshape((device_total,) + piece), ('dp', 'shard'),...  2.72 us
  transfers between devices with their start and end apart: 27, of which 17 were waited for; matrix products, arithmetic and copies ran while one was open for 1% of the time, Pallas kernels for 0%

profile of v5, /device:TPU:0, one launch (start us, length us, event | category | flops | bytes accessed | tf_op | source)
XLA Modules:
  0.0 81.1 jit_solution(2145898452171995580)
XLA Ops:
  0.7 1.3 %dynamic-slice_bitcast_fusion = (bf16[8,4,32,256]{3,2,1,0:T(8,128)(2,1)S(1)}, bf16[8,4,32,256]{3,2,1,0:T(8,128)(2,1)S(1)}) fusion(bf16[8,4,2,32,256]{4,3,2,1,0:T(8,128)(2,1)} %bitcast.122, s32[]{:T(128)S(6)} %select_n.126, s32[]{:T(128)S(6)} %select_n.125), kind=kLoop, calls=%fused_computation.1 | loop fusion | bytes 2097160 | tf_op jit(solution)/shard_map/jit(dynamic_index_in_dim)/squeeze | solution.py:20
  4.0 2.9 %collective-permute-start.9 = (f32[8,16,256]{2,1,0:T(8,128)S(1)}, f32[8,16,256]{2,1,0:T(8,128)S(1)}, u32[]{:S(2)}, u32[]{:S(2)}) collective-permute-start(f32[8,16,256]{2,1,0:T(8,128)S(1)} %get-tuple-element.33), channel_id=1, source_target_pairs={{0,8},{4,12},{8,0},{12,4},{16,24},{20,28},{24,16},{28,20},{1,9},{5... | collective-permute-start | bytes 393224 | tf_op jit(solution)/shard_map/sum_across_far/ppermute | solution.py:16
  7.1 1.0 %collective-permute-start.8 = (f32[8,16,256]{2,1,0:T(8,128)S(1)}, f32[8,16,256]{2,1,0:T(8,128)S(1)}, u32[]{:S(2)}, u32[]{:S(2)}) collective-permute-start(f32[8,16,256]{2,1,0:T(8,128)S(1)} %get-tuple-element.31), channel_id=1, source_target_pairs={{0,8},{4,12},{8,0},{12,4},{16,24},{20,28},{24,16},{28,20},{1,9},{5... | collective-permute-start | bytes 393224 | tf_op jit(solution)/shard_map/sum_x_far/ppermute | solution.py:16
  8.1 1.5 %collective-permute-start.3 = (f32[8,16,256]{2,1,0:T(8,128)S(1)}, f32[8,16,256]{2,1,0:T(8,128)S(1)}, u32[]{:S(2)}, u32[]{:S(2)}) collective-permute-start(f32[8,16,256]{2,1,0:T(8,128)S(1)} %get-tuple-element.28), channel_id=1, source_target_pairs={{0,16},{4,20},{8,24},{12,28},{16,0},{20,4},{24,8},{28,12},{1,17},{... | collective-permute-start | bytes 393224 | tf_op jit(solution)/shard_map/sum_across_near/ppermute | solution.py:16
  9.6 1.5 %collective-permute-done.9 = f32[8,16,256]{2,1,0:T(8,128)S(1)} collective-permute-done((f32[8,16,256]{2,1,0:T(8,128)S(1)}, f32[8,16,256]{2,1,0:T(8,128)S(1)}, u32[]{:S(2)}, u32[]{:S(2)}) %collective-permute-start.9) | collective-permute-done | bytes 131104 | tf_op jit(solution)/shard_map/sum_across_far/ppermute | solution.py:16
  11.2 2.2 %collective-permute-start.10 = (f32[8,16,256]{2,1,0:T(8,128)S(1)}, f32[8,16,256]{2,1,0:T(8,128)S(1)}, u32[]{:S(2)}, u32[]{:S(2)}) collective-permute-start(f32[8,16,256]{2,1,0:T(8,128)S(1)} %add.168), channel_id=1, source_target_pairs={{0,16},{4,20},{8,24},{12,28},{16,0},{20,4},{24,8},{28,12},{1,17},{... | collective-permute-start | bytes 393224 | tf_op jit(solution)/shard_map/sum_relay_far/ppermute | solution.py:16
  13.8 1.8 %collective-permute-start.4 = (f32[8,16,256]{2,1,0:T(8,128)S(1)}, f32[8,16,256]{2,1,0:T(8,128)S(1)}, u32[]{:S(2)}, u32[]{:S(2)}) collective-permute-start(f32[8,16,256]{2,1,0:T(8,128)S(1)} %add.160), channel_id=1, source_target_pairs={{0,8},{4,12},{8,0},{12,4},{16,24},{20,28},{24,16},{28,20},{1,9},{5... | collective-permute-start | bytes 393224 | tf_op jit(solution)/shard_map/sum_relay_near/ppermute | solution.py:16
  15.6 2.0 %collective-permute-done.10 = f32[8,16,256]{2,1,0:T(8,128)S(1)} collective-permute-done((f32[8,16,256]{2,1,0:T(8,128)S(1)}, f32[8,16,256]{2,1,0:T(8,128)S(1)}, u32[]{:S(2)}, u32[]{:S(2)}) %collective-permute-start.10) | collective-permute-done | bytes 131104 | tf_op jit(solution)/shard_map/sum_relay_far/ppermute | solution.py:16
  17.6 3.7 %collective-permute-start.12 = (f32[8,8,256]{2,1,0:T(8,128)S(1)}, f32[8,8,256]{2,1,0:T(8,128)S(1)}, u32[]{:S(2)}, u32[]{:S(2)}) collective-permute-start(f32[8,8,256]{2,1,0:T(8,128)S(1)} %get-tuple-element.67), channel_id=1, source_target_pairs={{0,3},{1,2},{2,1},{3,0},{4,7},{5,6},{6,5},{7,4},{8,11},{9,10},{10,... | collective-permute-start | bytes 196616 | tf_op jit(solution)/shard_map/shard_3/ppermute | solution.py:16
  21.4 0.8 %collective-permute-start.7 = (f32[8,8,256]{2,1,0:T(8,128)S(1)}, f32[8,8,256]{2,1,0:T(8,128)S(1)}, u32[]{:S(2)}, u32[]{:S(2)}) collective-permute-start(f32[8,8,256]{2,1,0:T(8,128)S(1)} %get-tuple-element.65), channel_id=1, source_target_pairs={{0,1},{1,0},{2,3},{3,2},{4,5},{5,4},{6,7},{7,6},{8,9},{9,8},{10,11... | collective-permute-start | bytes 196616 | tf_op jit(solution)/shard_map/shard_1/ppermute | solution.py:16
  22.4 1.9 %collective-permute-done.12 = f32[8,8,256]{2,1,0:T(8,128)S(1)} collective-permute-done((f32[8,8,256]{2,1,0:T(8,128)S(1)}, f32[8,8,256]{2,1,0:T(8,128)S(1)}, u32[]{:S(2)}, u32[]{:S(2)}) %collective-permute-start.12) | collective-permute-done | bytes 65568 | tf_op jit(solution)/shard_map/shard_3/ppermute | solution.py:16
  24.3 2.1 %collective-permute-done.11 = f32[8,8,256]{2,1,0:T(8,128)S(1)} collective-permute-done((f32[8,8,256]{2,1,0:T(8,128)S(1)}, f32[8,8,256]{2,1,0:T(8,128)S(1)}, u32[]{:S(2)}, u32[]{:S(2)}) %collective-permute-start.11) | collective-permute-done | bytes 65568 | tf_op jit(solution)/shard_map/shard_2/ppermute | solution.py:16
  26.9 14.0 %all_to_all.10 = f32[32,8,256]{2,1,0:T(8,128)S(1)} all-to-all(f32[32,8,256]{2,1,0:T(8,128)S(1)} %copy.56), channel_id=1, replica_groups=mesh['dp'=8,'shard'=4] {'dp','shard'}, dimensions={0} | all-to-all | bytes 524288 | tf_op jit(solution)/shard_map/all_to_all | solution.py:138
  42.2 1.0 %convolution_bitcast_fusion = f32[32,8,256]{2,1,0:T(8,128)} fusion(f32[256,256]{1,0:T(8,128)S(1)} %fusion.4, f32[1,1,1,256,256]{4,3,2,1,0:T(8,128)S(1)} %copy-done.4), kind=kOutput, calls=%fused_computation | convolution fusion | flops 100663296 | bytes 786432 | tf_op jit(solution)/shard_map/ia,aj->ij/dot_general | solution.py:68
  43.2 2.7 %all-to-all-start.1 = ((f32[32,8,256]{2,1,0:T(8,128)}), f32[32,8,256]{2,1,0:T(8,128)S(1)}, u32[]{:S(2)}, u32[]{:S(2)}) async-start(f32[32,8,256]{2,1,0:T(8,128)} %convolution_bitcast_fusion), calls=%async_computation.1 | async-start | bytes 524288 | tf_op jit(solution)/shard_map/all_to_all | solution.py:155
  45.9 10.2 %all-to-all-done.1 = f32[32,8,256]{2,1,0:T(8,128)S(1)} async-done(((f32[32,8,256]{2,1,0:T(8,128)}), f32[32,8,256]{2,1,0:T(8,128)S(1)}, u32[]{:S(2)}, u32[]{:S(2)}) %all-to-all-start.1) | async-done | bytes 262176 | tf_op jit(solution)/shard_map/all_to_all | solution.py:155
  56.5 1.8 %collective-permute-start.13 = (f32[8,8,256]{2,1,0:T(8,128)S(1)}, f32[8,8,256]{2,1,0:T(8,128)S(1)}, u32[]{:S(2)}, u32[]{:S(2)}) collective-permute-start(f32[8,8,256]{2,1,0:T(8,128)S(1)} %copy.58), channel_id=1, source_target_pairs={{0,3},{1,2},{2,1},{3,0},{4,7},{5,6},{6,5},{7,4},{8,11},{9,10},{10,... | collective-permute-start | bytes 196616 | tf_op jit(solution)/shard_map/shard_3/ppermute | solution.py:16
  58.4 0.9 %collective-permute-start.14 = (f32[8,8,256]{2,1,0:T(8,128)S(1)}, f32[8,8,256]{2,1,0:T(8,128)S(1)}, u32[]{:S(2)}, u32[]{:S(2)}) collective-permute-start(f32[8,8,256]{2,1,0:T(8,128)S(1)} %copy.59), channel_id=1, source_target_pairs={{0,2},{1,3},{2,0},{3,1},{4,6},{5,7},{6,4},{7,5},{8,10},{9,11},{10,... | collective-permute-start | bytes 196616 | tf_op jit(solution)/shard_map/shard_2/ppermute | solution.py:16
  59.3 1.9 %collective-permute-start.15 = (f32[8,8,256]{2,1,0:T(8,128)S(1)}, f32[8,8,256]{2,1,0:T(8,128)S(1)}, u32[]{:S(2)}, u32[]{:S(2)}) collective-permute-start(f32[8,8,256]{2,1,0:T(8,128)S(1)} %copy.60), channel_id=1, source_target_pairs={{0,1},{1,0},{2,3},{3,2},{4,5},{5,4},{6,7},{7,6},{8,9},{9,8},{10,11... | collective-permute-start | bytes 196616 | tf_op jit(solution)/shard_map/shard_1/ppermute | solution.py:16
  61.3 2.2 %collective-permute-done.13 = f32[8,8,256]{2,1,0:T(8,128)S(1)} collective-permute-done((f32[8,8,256]{2,1,0:T(8,128)S(1)}, f32[8,8,256]{2,1,0:T(8,128)S(1)}, u32[]{:S(2)}, u32[]{:S(2)}) %collective-permute-start.13) | collective-permute-done | bytes 65568 | tf_op jit(solution)/shard_map/shard_3/ppermute | solution.py:16
  63.5 2.2 %collective-permute-done.14 = f32[8,8,256]{2,1,0:T(8,128)S(1)} collective-permute-done((f32[8,8,256]{2,1,0:T(8,128)S(1)}, f32[8,8,256]{2,1,0:T(8,128)S(1)}, u32[]{:S(2)}, u32[]{:S(2)}) %collective-permute-start.14) | collective-permute-done | bytes 65568 | tf_op jit(solution)/shard_map/shard_2/ppermute | solution.py:16
  65.7 0.9 %collective-permute-start.18 = (f32[4,32,256]{2,1,0:T(8,128)S(1)}, f32[4,32,256]{2,1,0:T(8,128)S(1)}, u32[]{:S(2)}, u32[]{:S(2)}) collective-permute-start(f32[4,32,256]{2,1,0:T(8,128)S(1)} %get-tuple-element.49), channel_id=1, source_target_pairs={{0,8},{4,12},{8,0},{12,4},{16,24},{20,28},{24,16},{28,20},{1,9},{5... | collective-permute-start | bytes 393224 | tf_op jit(solution)/shard_map/rows_x_top/ppermute | solution.py:16
  66.7 0.6 collective-permute-start.20
  67.2 1.5 %collective-permute-start.17 = (f32[4,32,256]{2,1,0:T(8,128)S(1)}, f32[4,32,256]{2,1,0:T(8,128)S(1)}, u32[]{:S(2)}, u32[]{:S(2)}) collective-permute-start(f32[4,32,256]{2,1,0:T(8,128)S(1)} %get-tuple-element.48), channel_id=1, source_target_pairs={{0,8},{4,12},{8,0},{12,4},{16,24},{20,28},{24,16},{28,20},{1,9},{5... | collective-permute-start | bytes 393224 | tf_op jit(solution)/shard_map/rows_x_low/ppermute | solution.py:16
  68.7 1.1 %collective-permute-start.19 = (f32[4,32,256]{2,1,0:T(8,128)S(1)}, f32[4,32,256]{2,1,0:T(8,128)S(1)}, u32[]{:S(2)}, u32[]{:S(2)}) collective-permute-start(f32[4,32,256]{2,1,0:T(8,128)S(1)} %get-tuple-element.49), channel_id=1, source_target_pairs={{0,16},{4,20},{8,24},{12,28},{16,0},{20,4},{24,8},{28,12},{1,17},{... | collective-permute-start | bytes 393224 | tf_op jit(solution)/shard_map/rows_y_top/ppermute | solution.py:16
  70.0 2.1 %collective-permute-done.18 = f32[4,32,256]{2,1,0:T(8,128)S(1)} collective-permute-done((f32[4,32,256]{2,1,0:T(8,128)S(1)}, f32[4,32,256]{2,1,0:T(8,128)S(1)}, u32[]{:S(2)}, u32[]{:S(2)}) %collective-permute-start.18) | collective-permute-done | bytes 131104 | tf_op jit(solution)/shard_map/rows_x_top/ppermute | solution.py:16
  72.2 0.9 %collective-permute-start.21 = (f32[4,32,256]{2,1,0:T(8,128)S(1)}, f32[4,32,256]{2,1,0:T(8,128)S(1)}, u32[]{:S(2)}, u32[]{:S(2)}) collective-permute-start(f32[4,32,256]{2,1,0:T(8,128)S(1)} %collective-permute-done.18), channel_id=1, source_target_pairs={{0,16},{4,20},{8,24},{12,28},{16,0},{20,4},{24,8},{28,12},{1,17},{... | collective-permute-start | bytes 393224 | tf_op jit(solution)/shard_map/rows_relay_top/ppermute | solution.py:16
  73.0 0.5 collective-permute-start.24
  74.0 1.0 %collective-permute-done.19 = f32[4,32,256]{2,1,0:T(8,128)S(1)} collective-permute-done((f32[4,32,256]{2,1,0:T(8,128)S(1)}, f32[4,32,256]{2,1,0:T(8,128)S(1)}, u32[]{:S(2)}, u32[]{:S(2)}) %collective-permute-start.19) | collective-permute-done | bytes 131104 | tf_op jit(solution)/shard_map/rows_y_top/ppermute | solution.py:16
  75.1 2.4 %collective-permute-done.21 = f32[4,32,256]{2,1,0:T(8,128)S(1)} collective-permute-done((f32[4,32,256]{2,1,0:T(8,128)S(1)}, f32[4,32,256]{2,1,0:T(8,128)S(1)}, u32[]{:S(2)}, u32[]{:S(2)}) %collective-permute-start.21) | collective-permute-done | bytes 131104 | tf_op jit(solution)/shard_map/rows_relay_top/ppermute | solution.py:16
  78.2 0.8 collective-permute-done.22
  79.7 1.3 %copy-done.3 = f32[8,256,256]{2,1,0:T(8,128)} copy-done((f32[8,256,256]{2,1,0:T(8,128)}, f32[8,256,256]{2,1,0:T(8,128)S(1)}, u32[]{:S(2)}) %copy-start.3) | copy-done | bytes 2097176
  (100 shorter events, 7.0 us)
Async XLA Ops:
  0.6 40.7 %copy-start = (f32[1,1,1,256,256]{4,3,2,1,0:T(8,128)S(1)}, f32[1,1,1,256,256]{4,3,2,1,0:T(8,128)}, u32[]{:S(2)}) copy-start(f32[1,1,1,256,256]{4,3,2,1,0:T(8,128)} %param.10) | copy-start | bytes 786436
  2.2 1.7 %collective-permute-start = (f32[8,32,256]{2,1,0:T(8,128)S(1)}, f32[8,32,256]{2,1,0:T(8,128)S(1)}, u32[]{:S(2)}, u32[]{:S(2)}) collective-permute-start(f32[8,32,256]{2,1,0:T(8,128)S(1)} %get-tuple-element.47), channel_id=1, source_target_pairs={{0,4},{4,0},{8,12},{12,8},{16,20},{20,16},{24,28},{28,24},{1,5},{5... | collective-permute-start | bytes 786440 | tf_op jit(solution)/shard_map/sum_core_6/ppermute | solution.py:16
  2.7 4.2 %collective-permute-start.5 = (f32[8,32,256]{2,1,0:T(8,128)S(1)}, f32[8,32,256]{2,1,0:T(8,128)S(1)}, u32[]{:S(2)}, u32[]{:S(2)}) collective-permute-start(f32[8,32,256]{2,1,0:T(8,128)S(1)} %get-tuple-element.44), channel_id=1, source_target_pairs={{0,4},{4,0},{8,12},{12,8},{16,20},{20,16},{24,28},{28,24},{1,5},{5... | collective-permute-start | bytes 786440 | tf_op jit(solution)/shard_map/sum_core_4/ppermute | solution.py:16
  2.8 4.1 %collective-permute-start.2 = (f32[8,32,256]{2,1,0:T(8,128)S(1)}, f32[8,32,256]{2,1,0:T(8,128)S(1)}, u32[]{:S(2)}, u32[]{:S(2)}) collective-permute-start(f32[8,32,256]{2,1,0:T(8,128)S(1)} %get-tuple-element.45), channel_id=1, source_target_pairs={{0,4},{4,0},{8,12},{12,8},{16,20},{20,16},{24,28},{28,24},{1,5},{5... | collective-permute-start | bytes 786440 | tf_op jit(solution)/shard_map/sum_core_2/ppermute | solution.py:16
  3.2 3.7 %collective-permute-start.1 = (f32[8,32,256]{2,1,0:T(8,128)S(1)}, f32[8,32,256]{2,1,0:T(8,128)S(1)}, u32[]{:S(2)}, u32[]{:S(2)}) collective-permute-start(f32[8,32,256]{2,1,0:T(8,128)S(1)} %get-tuple-element.46), channel_id=1, source_target_pairs={{0,4},{4,0},{8,12},{12,8},{16,20},{20,16},{24,28},{28,24},{1,5},{5... | collective-permute-start | bytes 786440 | tf_op jit(solution)/shard_map/sum_core_0/ppermute | solution.py:16
  4.0 7.2 %collective-permute-start.9 = (f32[8,16,256]{2,1,0:T(8,128)S(1)}, f32[8,16,256]{2,1,0:T(8,128)S(1)}, u32[]{:S(2)}, u32[]{:S(2)}) collective-permute-start(f32[8,16,256]{2,1,0:T(8,128)S(1)} %get-tuple-element.33), channel_id=1, source_target_pairs={{0,8},{4,12},{8,0},{12,4},{16,24},{20,28},{24,16},{28,20},{1,9},{5... | collective-permute-start | bytes 393224 | tf_op jit(solution)/shard_map/sum_across_far/ppermute | solution.py:16
  7.1 6.4 %collective-permute-start.8 = (f32[8,16,256]{2,1,0:T(8,128)S(1)}, f32[8,16,256]{2,1,0:T(8,128)S(1)}, u32[]{:S(2)}, u32[]{:S(2)}) collective-permute-start(f32[8,16,256]{2,1,0:T(8,128)S(1)} %get-tuple-element.31), channel_id=1, source_target_pairs={{0,8},{4,12},{8,0},{12,4},{16,24},{20,28},{24,16},{28,20},{1,9},{5... | collective-permute-start | bytes 393224 | tf_op jit(solution)/shard_map/sum_x_far/ppermute | solution.py:16
  8.1 5.6 %collective-permute-start.3 = (f32[8,16,256]{2,1,0:T(8,128)S(1)}, f32[8,16,256]{2,1,0:T(8,128)S(1)}, u32[]{:S(2)}, u32[]{:S(2)}) collective-permute-start(f32[8,16,256]{2,1,0:T(8,128)S(1)} %get-tuple-element.28), channel_id=1, source_target_pairs={{0,16},{4,20},{8,24},{12,28},{16,0},{20,4},{24,8},{28,12},{1,17},{... | collective-permute-start | bytes 393224 | tf_op jit(solution)/shard_map/sum_across_near/ppermute | solution.py:16
  11.2 6.4 %collective-permute-start.10 = (f32[8,16,256]{2,1,0:T(8,128)S(1)}, f32[8,16,256]{2,1,0:T(8,128)S(1)}, u32[]{:S(2)}, u32[]{:S(2)}) collective-permute-start(f32[8,16,256]{2,1,0:T(8,128)S(1)} %add.168), channel_id=1, source_target_pairs={{0,16},{4,20},{8,24},{12,28},{16,0},{20,4},{24,8},{28,12},{1,17},{... | collective-permute-start | bytes 393224 | tf_op jit(solution)/shard_map/sum_relay_far/ppermute | solution.py:16
  13.4 8.0 %collective-permute-start.6 = (f32[8,16,256]{2,1,0:T(8,128)S(1)}, f32[8,16,256]{2,1,0:T(8,128)S(1)}, u32[]{:S(2)}, u32[]{:S(2)}) collective-permute-start(f32[8,16,256]{2,1,0:T(8,128)S(1)} %get-tuple-element.29), channel_id=1, source_target_pairs={{0,16},{4,20},{8,24},{12,28},{16,0},{20,4},{24,8},{28,12},{1,17},{... | collective-permute-start | bytes 393224 | tf_op jit(solution)/shard_map/sum_y_near/ppermute | solution.py:16
  13.7 27.2 %copy-start.4 = (f32[1,1,1,256,256]{4,3,2,1,0:T(8,128)S(1)}, f32[1,1,1,256,256]{4,3,2,1,0:T(8,128)}, u32[]{:S(2)}) copy-start(f32[1,1,1,256,256]{4,3,2,1,0:T(8,128)} %param.9) | copy-start | bytes 786436
  13.8 7.6 %collective-permute-start.4 = (f32[8,16,256]{2,1,0:T(8,128)S(1)}, f32[8,16,256]{2,1,0:T(8,128)S(1)}, u32[]{:S(2)}, u32[]{:S(2)}) collective-permute-start(f32[8,16,256]{2,1,0:T(8,128)S(1)} %add.160), channel_id=1, source_target_pairs={{0,8},{4,12},{8,0},{12,4},{16,24},{20,28},{24,16},{28,20},{1,9},{5... | collective-permute-start | bytes 393224 | tf_op jit(solution)/shard_map/sum_relay_near/ppermute | solution.py:16
  17.6 6.7 %collective-permute-start.12 = (f32[8,8,256]{2,1,0:T(8,128)S(1)}, f32[8,8,256]{2,1,0:T(8,128)S(1)}, u32[]{:S(2)}, u32[]{:S(2)}) collective-permute-start(f32[8,8,256]{2,1,0:T(8,128)S(1)} %get-tuple-element.67), channel_id=1, source_target_pairs={{0,3},{1,2},{2,1},{3,0},{4,7},{5,6},{6,5},{7,4},{8,11},{9,10},{10,... | collective-permute-start | bytes 196616 | tf_op jit(solution)/shard_map/shard_3/ppermute | solution.py:16
  21.3 5.2 %collective-permute-start.11 = (f32[8,8,256]{2,1,0:T(8,128)S(1)}, f32[8,8,256]{2,1,0:T(8,128)S(1)}, u32[]{:S(2)}, u32[]{:S(2)}) collective-permute-start(f32[8,8,256]{2,1,0:T(8,128)S(1)} %get-tuple-element.66), channel_id=1, source_target_pairs={{0,2},{1,3},{2,0},{3,1},{4,6},{5,7},{6,4},{7,5},{8,10},{9,11},{10,... | collective-permute-start | bytes 196616 | tf_op jit(solution)/shard_map/shard_2/ppermute | solution.py:16
  21.3 20.0 %copy-start.5 = (f32[1,1,1,256,256]{4,3,2,1,0:T(8,128)S(1)}, f32[1,1,1,256,256]{4,3,2,1,0:T(8,128)}, u32[]{:S(2)}) copy-start(f32[1,1,1,256,256]{4,3,2,1,0:T(8,128)} %param.11) | copy-start | bytes 786436
  21.3 20.0 %copy-start.6 = (f32[1,1,1,256,256]{4,3,2,1,0:T(8,128)S(1)}, f32[1,1,1,256,256]{4,3,2,1,0:T(8,128)}, u32[]{:S(2)}) copy-start(f32[1,1,1,256,256]{4,3,2,1,0:T(8,128)} %param.12) | copy-start | bytes 786436
  21.4 5.1 %collective-permute-start.7 = (f32[8,8,256]{2,1,0:T(8,128)S(1)}, f32[8,8,256]{2,1,0:T(8,128)S(1)}, u32[]{:S(2)}, u32[]{:S(2)}) collective-permute-start(f32[8,8,256]{2,1,0:T(8,128)S(1)} %get-tuple-element.65), channel_id=1, source_target_pairs={{0,1},{1,0},{2,3},{3,2},{4,5},{5,4},{6,7},{7,6},{8,9},{9,8},{10,11... | collective-permute-start | bytes 196616 | tf_op jit(solution)/shard_map/shard_1/ppermute | solution.py:16
  42.2 21.3 %copy-start.1 = (f32[8,32,256]{2,1,0:T(8,128)S(1)}, f32[8,32,256]{2,1,0:T(8,128)}, u32[]{:S(2)}) copy-start(f32[8,32,256]{2,1,0:T(8,128)} %param.8) | copy-start | bytes 786436
  43.2 12.9 %all-to-all-start.1 = ((f32[32,8,256]{2,1,0:T(8,128)}), f32[32,8,256]{2,1,0:T(8,128)S(1)}, u32[]{:S(2)}, u32[]{:S(2)}) async-start(f32[32,8,256]{2,1,0:T(8,128)} %convolution_bitcast_fusion), calls=%async_computation.1 | async-start | bytes 524288 | tf_op jit(solution)/shard_map/all_to_all | solution.py:155
  56.5 6.9 %collective-permute-start.13 = (f32[8,8,256]{2,1,0:T(8,128)S(1)}, f32[8,8,256]{2,1,0:T(8,128)S(1)}, u32[]{:S(2)}, u32[]{:S(2)}) collective-permute-start(f32[8,8,256]{2,1,0:T(8,128)S(1)} %copy.58), channel_id=1, source_target_pairs={{0,3},{1,2},{2,1},{3,0},{4,7},{5,6},{6,5},{7,4},{8,11},{9,10},{10,... | collective-permute-start | bytes 196616 | tf_op jit(solution)/shard_map/shard_3/ppermute | solution.py:16
  58.4 7.2 %collective-permute-start.14 = (f32[8,8,256]{2,1,0:T(8,128)S(1)}, f32[8,8,256]{2,1,0:T(8,128)S(1)}, u32[]{:S(2)}, u32[]{:S(2)}) collective-permute-start(f32[8,8,256]{2,1,0:T(8,128)S(1)} %copy.59), channel_id=1, source_target_pairs={{0,2},{1,3},{2,0},{3,1},{4,6},{5,7},{6,4},{7,5},{8,10},{9,11},{10,... | collective-permute-start | bytes 196616 | tf_op jit(solution)/shard_map/shard_2/ppermute | solution.py:16
  59.3 6.4 %collective-permute-start.15 = (f32[8,8,256]{2,1,0:T(8,128)S(1)}, f32[8,8,256]{2,1,0:T(8,128)S(1)}, u32[]{:S(2)}, u32[]{:S(2)}) collective-permute-start(f32[8,8,256]{2,1,0:T(8,128)S(1)} %copy.60), channel_id=1, source_target_pairs={{0,1},{1,0},{2,3},{3,2},{4,5},{5,4},{6,7},{7,6},{8,9},{9,8},{10,11... | collective-permute-start | bytes 196616 | tf_op jit(solution)/shard_map/shard_1/ppermute | solution.py:16
  65.7 6.4 %collective-permute-start.18 = (f32[4,32,256]{2,1,0:T(8,128)S(1)}, f32[4,32,256]{2,1,0:T(8,128)S(1)}, u32[]{:S(2)}, u32[]{:S(2)}) collective-permute-start(f32[4,32,256]{2,1,0:T(8,128)S(1)} %get-tuple-element.49), channel_id=1, source_target_pairs={{0,8},{4,12},{8,0},{12,4},{16,24},{20,28},{24,16},{28,20},{1,9},{5... | collective-permute-start | bytes 393224 | tf_op jit(solution)/shard_map/rows_x_top/ppermute | solution.py:16
  66.7 6.4 %collective-permute-start.20 = (f32[4,32,256]{2,1,0:T(8,128)S(1)}, f32[4,32,256]{2,1,0:T(8,128)S(1)}, u32[]{:S(2)}, u32[]{:S(2)}) collective-permute-start(f32[4,32,256]{2,1,0:T(8,128)S(1)} %get-tuple-element.48), channel_id=1, source_target_pairs={{0,16},{4,20},{8,24},{12,28},{16,0},{20,4},{24,8},{28,12},{1,17},{... | collective-permute-start | bytes 393224 | tf_op jit(solution)/shard_map/rows_y_low/ppermute | solution.py:16
  67.2 6.8 %collective-permute-start.17 = (f32[4,32,256]{2,1,0:T(8,128)S(1)}, f32[4,32,256]{2,1,0:T(8,128)S(1)}, u32[]{:S(2)}, u32[]{:S(2)}) collective-permute-start(f32[4,32,256]{2,1,0:T(8,128)S(1)} %get-tuple-element.48), channel_id=1, source_target_pairs={{0,8},{4,12},{8,0},{12,4},{16,24},{20,28},{24,16},{28,20},{1,9},{5... | collective-permute-start | bytes 393224 | tf_op jit(solution)/shard_map/rows_x_low/ppermute | solution.py:16
  68.7 6.3 %collective-permute-start.16 = (f32[8,32,256]{2,1,0:T(8,128)S(1)}, f32[8,32,256]{2,1,0:T(8,128)S(1)}, u32[]{:S(2)}, u32[]{:S(2)}) collective-permute-start(f32[8,32,256]{2,1,0:T(8,128)S(1)} %subtract_dynamic-update-slice_fusion), channel_id=1, source_target_pairs={{0,4},{4,0},{8,12},{12,8},{16,20},{20,16},{24,28},{28,24},{1,5},{5... | collective-permute-start | bytes 786440 | tf_op jit(solution)/shard_map/rows_core_own/ppermute | solution.py:16
  68.7 6.3 %collective-permute-start.19 = (f32[4,32,256]{2,1,0:T(8,128)S(1)}, f32[4,32,256]{2,1,0:T(8,128)S(1)}, u32[]{:S(2)}, u32[]{:S(2)}) collective-permute-start(f32[4,32,256]{2,1,0:T(8,128)S(1)} %get-tuple-element.49), channel_id=1, source_target_pairs={{0,16},{4,20},{8,24},{12,28},{16,0},{20,4},{24,8},{28,12},{1,17},{... | collective-permute-start | bytes 393224 | tf_op jit(solution)/shard_map/rows_y_top/ppermute | solution.py:16
  72.2 5.3 %collective-permute-start.21 = (f32[4,32,256]{2,1,0:T(8,128)S(1)}, f32[4,32,256]{2,1,0:T(8,128)S(1)}, u32[]{:S(2)}, u32[]{:S(2)}) collective-permute-start(f32[4,32,256]{2,1,0:T(8,128)S(1)} %collective-permute-done.18), channel_id=1, source_target_pairs={{0,16},{4,20},{8,24},{12,28},{16,0},{20,4},{24,8},{28,12},{1,17},{... | collective-permute-start | bytes 393224 | tf_op jit(solution)/shard_map/rows_relay_top/ppermute | solution.py:16
  73.0 5.0 %collective-permute-start.24 = (f32[4,32,256]{2,1,0:T(8,128)S(1)}, f32[4,32,256]{2,1,0:T(8,128)S(1)}, u32[]{:S(2)}, u32[]{:S(2)}) collective-permute-start(f32[4,32,256]{2,1,0:T(8,128)S(1)} %collective-permute-done.20), channel_id=1, source_target_pairs={{0,8},{4,12},{8,0},{12,4},{16,24},{20,28},{24,16},{28,20},{1,9},{5... | collective-permute-start | bytes 393224 | tf_op jit(solution)/shard_map/rows_relay_low/ppermute | solution.py:16
  77.4 1.5 %collective-permute-start.22 = (f32[8,32,256]{2,1,0:T(8,128)S(1)}, f32[8,32,256]{2,1,0:T(8,128)S(1)}, u32[]{:S(2)}, u32[]{:S(2)}) collective-permute-start(f32[8,32,256]{2,1,0:T(8,128)S(1)} %pad_maximum_fusion.1), channel_id=1, source_target_pairs={{0,4},{4,0},{8,12},{12,8},{16,20},{20,16},{24,28},{28,24},{1,5},{5... | collective-permute-start | bytes 786440 | tf_op jit(solution)/shard_map/rows_core_x/ppermute | solution.py:16
  77.4 1.9 %collective-permute-start.23 = (f32[8,32,256]{2,1,0:T(8,128)S(1)}, f32[8,32,256]{2,1,0:T(8,128)S(1)}, u32[]{:S(2)}, u32[]{:S(2)}) collective-permute-start(f32[8,32,256]{2,1,0:T(8,128)S(1)} %pad_maximum_fusion.2), channel_id=1, source_target_pairs={{0,4},{4,0},{8,12},{12,8},{16,20},{20,16},{24,28},{28,24},{1,5},{5... | collective-permute-start | bytes 786440 | tf_op jit(solution)/shard_map/rows_core_y/ppermute | solution.py:16
  78.0 1.7 %collective-permute-start.25 = (f32[8,32,256]{2,1,0:T(8,128)S(1)}, f32[8,32,256]{2,1,0:T(8,128)S(1)}, u32[]{:S(2)}, u32[]{:S(2)}) collective-permute-start(f32[8,32,256]{2,1,0:T(8,128)S(1)} %constant_dynamic-update-slice_fusion.6), channel_id=1, source_target_pairs={{0,4},{4,0},{8,12},{12,8},{16,20},{20,16},{24,28},{28,24},{1,5},{5... | collective-permute-start | bytes 786440 | tf_op jit(solution)/shard_map/rows_core_far/ppermute | solution.py:16
  (5 other events, 52.5 us)

commit v6 on v5

--- a/solution.py
+++ b/solution.py
@@ -12,8 +12,10 @@
 
 
 def swap(values, name, mask, what="swap"):
+    masks = mask if isinstance(mask, tuple) else (mask, mask)
+    pairs = [(i, i ^ masks[i & 1]) for i in range(lax.axis_size(name))]
     with jax.named_scope(what):
-        return lax.ppermute(values, name, [(i, i ^ mask) for i in range(lax.axis_size(name))])
+        return lax.ppermute(values, name, pairs)
 
 
 def take(values, axis, index):
@@ -76,7 +78,8 @@
 
 def routed(partials, params, left_basis, right_basis, first_moment, second_moment, owner_list):
     high = lax.Precision.HIGH
-    core, along_x, along_y, across = 1, 2, 4, 6
+    core, across = 1, 6
+    first_link, second_link = (2, 4), (4, 2)
     shard_here = lax.axis_index("shard")
     data_here = lax.axis_index("dp")
     shard_count = lax.axis_size("shard")
@@ -87,6 +90,8 @@
     piece = (row_count // shard_count, width)
     chips = data_count // 2
     my_core = data_here & core
+    first_chip = jnp.where(my_core == 0, *first_link)
+    second_chip = across - first_chip
     shard_half, shard_low = shard_here >> 1, shard_here & 1
 
     def set_of(values, index):
@@ -102,25 +107,30 @@
         return take(values, 1, (data_here ^ mask) // 2).astype(jnp.float32)
 
     near, far = {}, {}
-    for mask in (across, along_x, along_y, 0):
+    for name, mask, other_mask in (
+        ("across", across, across),
+        ("first", first_chip, second_chip),
+        ("second", second_chip, first_chip),
+        ("own", 0, 0),
+    ):
         total = rows_of(own_rows, mask) + swap(
-            rows_of(away_rows, mask), "dp", core, f"sum_core_{mask}"
+            rows_of(away_rows, other_mask), "dp", core, f"sum_core_{name}"
         )
-        near[mask], far[mask] = lax.optimization_barrier(
+        near[name], far[name] = lax.optimization_barrier(
             (set_of(total, shard_half), set_of(total, 1 - shard_half))
         )
-        if mask == across:
-            own_rows, near[mask], far[mask] = lax.optimization_barrier(
-                (own_rows, near[mask], far[mask])
+        if name == "across":
+            own_rows, near[name], far[name] = lax.optimization_barrier(
+                (own_rows, near[name], far[name])
             )
-    far_relay = far[along_y] + swap(far[across], "dp", along_x, "sum_across_far")
-    near_relay = near[along_x] + swap(near[across], "dp", along_y, "sum_across_near")
-    far_sum = far[0] + swap(far[along_x], "dp", along_x, "sum_x_far")
-    far_sum = lax.optimization_barrier(far_sum)
-    far_sum = far_sum + swap(far_relay, "dp", along_y, "sum_relay_far")
-    near_sum = near[0] + swap(near_relay, "dp", along_x, "sum_relay_near")
-    near_sum = lax.optimization_barrier(near_sum)
-    near_sum = near_sum + swap(near[along_y], "dp", along_y, "sum_y_near")
+    far_relay = far["second"] + swap(far["across"], "dp", first_link, "sum_across_far")
+    near_relay = near["first"] + swap(near["across"], "dp", second_link, "sum_across_near")
+    far_relay, near_relay = lax.optimization_barrier((far_relay, near_relay))
+    far_sum = far["own"] + swap(far["first"], "dp", first_link, "sum_first_far")
+    near_sum = near["own"] + swap(near["second"], "dp", second_link, "sum_second_near")
+    far_sum, near_sum = lax.optimization_barrier((far_sum, near_sum))
+    far_sum = far_sum + swap(far_relay, "dp", second_link, "sum_relay_far")
+    near_sum = near_sum + swap(near_relay, "dp", first_link, "sum_relay_near")
 
     mixed = shard_exchange(
         [
@@ -171,30 +181,30 @@
         new_home = lax.dynamic_update_slice_in_dim(new_home, home, start, axis=1)
 
     low, top = new_home[:half], new_home[half:]
-    x_top = swap(top, "dp", along_x, "rows_x_top")
-    y_low = swap(low, "dp", along_y, "rows_y_low")
+    first_top = swap(top, "dp", first_link, "rows_first_top")
+    second_low = swap(low, "dp", second_link, "rows_second_low")
     other = swap(new_home, "dp", core, "rows_core_own")
-    x_low = swap(low, "dp", along_x, "rows_x_low")
-    y_top = swap(top, "dp", along_y, "rows_y_top")
-    far_top = swap(x_top, "dp", along_y, "rows_relay_top")
-    far_low = swap(y_low, "dp", along_x, "rows_relay_low")
-    x_rows = jnp.concatenate([x_low, x_top], axis=0)
-    y_rows = jnp.concatenate([y_top, y_low], axis=0)
-    x_rows, y_rows, far_top, first_new, second_new = lax.optimization_barrier(
-        (x_rows, y_rows, far_top, first_new, second_new)
+    first_low = swap(low, "dp", first_link, "rows_first_low")
+    second_top = swap(top, "dp", second_link, "rows_second_top")
+    far_top = swap(first_top, "dp", second_link, "rows_relay_top")
+    far_low = swap(second_low, "dp", first_link, "rows_relay_low")
+    first_rows = jnp.concatenate([first_low, first_top], axis=0)
+    second_rows = jnp.concatenate([second_top, second_low], axis=0)
+    first_rows, second_rows, far_top, first_new, second_new = lax.optimization_barrier(
+        (first_rows, second_rows, far_top, first_new, second_new)
     )
     far_rows = jnp.concatenate([far_low, far_top], axis=0)
-    y_other = swap(y_rows, "dp", core, "rows_core_y")
+    second_other = swap(second_rows, "dp", core, "rows_core_second")
     updated = jnp.zeros((home_count, width, width), jnp.float32)
     for mask, block, values in (
         (0, 0, new_home),
         (core, 0, other),
-        (along_x, 0, x_rows),
-        (along_y, half, y_rows[:half]),
-        (along_y, 0, y_rows[half:]),
-        (along_x ^ core, 0, swap(x_rows, "dp", core, "rows_core_x")),
-        (along_y ^ core, half, y_other[:half]),
-        (along_y ^ core, 0, y_other[half:]),
+        (first_chip, 0, first_rows),
+        (second_chip, half, second_rows[:half]),
+        (second_chip, 0, second_rows[half:]),
+        (second_chip ^ core, 0, swap(first_rows, "dp", core, "rows_core_first")),
+        (first_chip ^ core, half, second_other[:half]),
+        (first_chip ^ core, 0, second_other[half:]),
         (across, 0, far_rows),
         (across ^ core, 0, swap(far_rows, "dp", core, "rows_core_far")),
     ):

time: 81.3 us -> 82.4 us (1.014)
  waiting for transfers between devices: 30.2 us -> 32.8 us
  starting transfers between devices: 28.6 us -> 27.3 us
    ppermute x26, waiting for transfers between devices: 20 us -> 22.6 us  [swap(): return lax.ppermute(values, name, pairs)]
    ppermute x26, starting transfers between devices: 25.9 us -> 24.6 us  [swap(): return lax.ppermute(values, name, pairs)]
where the time goes in v6:
time: 82.4 us; the launch traced here: 82.1 us
  waiting for transfers between devices  32.8 us (40%)
  starting transfers between devices  27.3 us (33%)
  blocking collectives  13.8 us (17%)
  local copies, waits for them, and re-layouts  3.84 us (5%)
  matrix products  2.63 us (3%)
  between operations  1.28 us (2%)
    ppermute x26, starting transfers between devices, swap(): return lax.ppermute(values, name, pairs)  24.6 us
    ppermute x26, waiting for transfers between devices, swap(): return lax.ppermute(values, name, pairs)  22.6 us
    all_to_all x1, blocking collectives, routed(): lax.all_to_all(leaving.reshape((device_total,) + piece), ('dp', 'shard'),...  13.8 us
    all_to_all x1, waiting for transfers between devices, routed(): lax.all_to_all(change.reshape((device_total,) + piece), ('dp', 'shard'),...  10.2 us
    all_to_all x1, starting transfers between devices, routed(): lax.all_to_all(change.reshape((device_total,) + piece), ('dp', 'shard'),...  2.73 us
  transfers between devices with their start and end apart: 27, of which 17 were waited for; matrix products, arithmetic and copies ran while one was open for 1% of the time, Pallas kernels for 0%

profile of v6, /device:TPU:0, one launch (start us, length us, event | category | flops | bytes accessed | tf_op | source)
XLA Modules:
  0.0 82.1 jit_solution(3151058063426954470)
XLA Ops:
  0.8 1.3 %dynamic-slice_bitcast_fusion = (bf16[8,4,32,256]{3,2,1,0:T(8,128)(2,1)S(1)}, bf16[8,4,32,256]{3,2,1,0:T(8,128)(2,1)S(1)}) fusion(bf16[8,4,2,32,256]{4,3,2,1,0:T(8,128)(2,1)} %bitcast.124, s32[]{:T(128)S(6)} %select_n.130, s32[]{:T(128)S(6)} %select_n.129), kind=kLoop, calls=%fused_computation.1 | loop fusion | bytes 2097160 | tf_op jit(solution)/shard_map/jit(dynamic_index_in_dim)/squeeze | solution.py:22
  4.0 2.9 %collective-permute-start.6 = (f32[8,16,256]{2,1,0:T(8,128)S(1)}, f32[8,16,256]{2,1,0:T(8,128)S(1)}, u32[]{:S(2)}, u32[]{:S(2)}) collective-permute-start(f32[8,16,256]{2,1,0:T(8,128)S(1)} %get-tuple-element.36), channel_id=1, source_target_pairs={{0,8},{4,20},{8,0},{12,28},{16,24},{20,4},{24,16},{28,12},{1,9},{5... | collective-permute-start | bytes 393224 | tf_op jit(solution)/shard_map/sum_across_far/ppermute | solution.py:18
  6.9 1.5 %collective-permute-start.7 = (f32[8,16,256]{2,1,0:T(8,128)S(1)}, f32[8,16,256]{2,1,0:T(8,128)S(1)}, u32[]{:S(2)}, u32[]{:S(2)}) collective-permute-start(f32[8,16,256]{2,1,0:T(8,128)S(1)} %get-tuple-element.38), channel_id=1, source_target_pairs={{0,16},{4,12},{8,24},{12,4},{16,0},{20,28},{24,8},{28,20},{1,17},{... | collective-permute-start | bytes 393224 | tf_op jit(solution)/shard_map/sum_across_near/ppermute | solution.py:18
  8.6 0.6 collective-permute-start.3
  9.6 0.8 collective-permute-done.6
  10.5 2.5 %collective-permute-done.7 = f32[8,16,256]{2,1,0:T(8,128)S(1)} collective-permute-done((f32[8,16,256]{2,1,0:T(8,128)S(1)}, f32[8,16,256]{2,1,0:T(8,128)S(1)}, u32[]{:S(2)}, u32[]{:S(2)}) %collective-permute-start.7) | collective-permute-done | bytes 131104 | tf_op jit(solution)/shard_map/sum_across_near/ppermute | solution.py:18
  13.0 1.3 %collective-permute-start.10 = (f32[8,16,256]{2,1,0:T(8,128)S(1)}, f32[8,16,256]{2,1,0:T(8,128)S(1)}, u32[]{:S(2)}, u32[]{:S(2)}) collective-permute-start(f32[8,16,256]{2,1,0:T(8,128)S(1)} %add.164), channel_id=1, source_target_pairs={{0,16},{4,12},{8,24},{12,4},{16,0},{20,28},{24,8},{28,20},{1,17},{... | collective-permute-start | bytes 393224 | tf_op jit(solution)/shard_map/sum_relay_far/ppermute | solution.py:18
  14.7 1.2 %collective-permute-start.8 = (f32[8,16,256]{2,1,0:T(8,128)S(1)}, f32[8,16,256]{2,1,0:T(8,128)S(1)}, u32[]{:S(2)}, u32[]{:S(2)}) collective-permute-start(f32[8,16,256]{2,1,0:T(8,128)S(1)} %add.165), channel_id=1, source_target_pairs={{0,8},{4,20},{8,0},{12,28},{16,24},{20,4},{24,16},{28,12},{1,9},{5... | collective-permute-start | bytes 393224 | tf_op jit(solution)/shard_map/sum_relay_near/ppermute | solution.py:18
  15.9 3.3 %collective-permute-done.10 = f32[8,16,256]{2,1,0:T(8,128)S(1)} collective-permute-done((f32[8,16,256]{2,1,0:T(8,128)S(1)}, f32[8,16,256]{2,1,0:T(8,128)S(1)}, u32[]{:S(2)}, u32[]{:S(2)}) %collective-permute-start.10) | collective-permute-done | bytes 131104 | tf_op jit(solution)/shard_map/sum_relay_far/ppermute | solution.py:18
  19.3 3.6 %collective-permute-start.12 = (f32[8,8,256]{2,1,0:T(8,128)S(1)}, f32[8,8,256]{2,1,0:T(8,128)S(1)}, u32[]{:S(2)}, u32[]{:S(2)}) collective-permute-start(f32[8,8,256]{2,1,0:T(8,128)S(1)} %get-tuple-element.75), channel_id=1, source_target_pairs={{0,3},{1,2},{2,1},{3,0},{4,7},{5,6},{6,5},{7,4},{8,11},{9,10},{10,... | collective-permute-start | bytes 196616 | tf_op jit(solution)/shard_map/shard_3/ppermute | solution.py:18
  23.0 0.9 %collective-permute-start.9 = (f32[8,8,256]{2,1,0:T(8,128)S(1)}, f32[8,8,256]{2,1,0:T(8,128)S(1)}, u32[]{:S(2)}, u32[]{:S(2)}) collective-permute-start(f32[8,8,256]{2,1,0:T(8,128)S(1)} %get-tuple-element.73), channel_id=1, source_target_pairs={{0,1},{1,0},{2,3},{3,2},{4,5},{5,4},{6,7},{7,6},{8,9},{9,8},{10,11... | collective-permute-start | bytes 196616 | tf_op jit(solution)/shard_map/shard_1/ppermute | solution.py:18
  24.0 1.7 %collective-permute-done.12 = f32[8,8,256]{2,1,0:T(8,128)S(1)} collective-permute-done((f32[8,8,256]{2,1,0:T(8,128)S(1)}, f32[8,8,256]{2,1,0:T(8,128)S(1)}, u32[]{:S(2)}, u32[]{:S(2)}) %collective-permute-start.12) | collective-permute-done | bytes 65568 | tf_op jit(solution)/shard_map/shard_3/ppermute | solution.py:18
  25.7 2.4 %collective-permute-done.11 = f32[8,8,256]{2,1,0:T(8,128)S(1)} collective-permute-done((f32[8,8,256]{2,1,0:T(8,128)S(1)}, f32[8,8,256]{2,1,0:T(8,128)S(1)}, u32[]{:S(2)}, u32[]{:S(2)}) %collective-permute-start.11) | collective-permute-done | bytes 65568 | tf_op jit(solution)/shard_map/shard_2/ppermute | solution.py:18
  28.6 13.8 %all_to_all.10 = f32[32,8,256]{2,1,0:T(8,128)S(1)} all-to-all(f32[32,8,256]{2,1,0:T(8,128)S(1)} %copy.59), channel_id=1, replica_groups=mesh['dp'=8,'shard'=4] {'dp','shard'}, dimensions={0} | all-to-all | bytes 524288 | tf_op jit(solution)/shard_map/all_to_all | solution.py:148
  43.6 1.0 %convolution_bitcast_fusion = f32[32,8,256]{2,1,0:T(8,128)} fusion(f32[256,256]{1,0:T(8,128)S(1)} %fusion.4, f32[1,1,1,256,256]{4,3,2,1,0:T(8,128)S(1)} %copy-done.4), kind=kOutput, calls=%fused_computation | convolution fusion | flops 100663296 | bytes 786432 | tf_op jit(solution)/shard_map/ia,aj->ij/dot_general | solution.py:70
  44.6 2.7 %all-to-all-start.1 = ((f32[32,8,256]{2,1,0:T(8,128)}), f32[32,8,256]{2,1,0:T(8,128)S(1)}, u32[]{:S(2)}, u32[]{:S(2)}) async-start(f32[32,8,256]{2,1,0:T(8,128)} %convolution_bitcast_fusion), calls=%async_computation.1 | async-start | bytes 524288 | tf_op jit(solution)/shard_map/all_to_all | solution.py:165
  47.3 10.2 %all-to-all-done.1 = f32[32,8,256]{2,1,0:T(8,128)S(1)} async-done(((f32[32,8,256]{2,1,0:T(8,128)}), f32[32,8,256]{2,1,0:T(8,128)S(1)}, u32[]{:S(2)}, u32[]{:S(2)}) %all-to-all-start.1) | async-done | bytes 262176 | tf_op jit(solution)/shard_map/all_to_all | solution.py:165
  58.0 1.8 %collective-permute-start.13 = (f32[8,8,256]{2,1,0:T(8,128)S(1)}, f32[8,8,256]{2,1,0:T(8,128)S(1)}, u32[]{:S(2)}, u32[]{:S(2)}) collective-permute-start(f32[8,8,256]{2,1,0:T(8,128)S(1)} %copy.61), channel_id=1, source_target_pairs={{0,3},{1,2},{2,1},{3,0},{4,7},{5,6},{6,5},{7,4},{8,11},{9,10},{10,... | collective-permute-start | bytes 196616 | tf_op jit(solution)/shard_map/shard_3/ppermute | solution.py:18
  59.8 0.9 %collective-permute-start.14 = (f32[8,8,256]{2,1,0:T(8,128)S(1)}, f32[8,8,256]{2,1,0:T(8,128)S(1)}, u32[]{:S(2)}, u32[]{:S(2)}) collective-permute-start(f32[8,8,256]{2,1,0:T(8,128)S(1)} %copy.62), channel_id=1, source_target_pairs={{0,2},{1,3},{2,0},{3,1},{4,6},{5,7},{6,4},{7,5},{8,10},{9,11},{10,... | collective-permute-start | bytes 196616 | tf_op jit(solution)/shard_map/shard_2/ppermute | solution.py:18
  60.7 1.9 %collective-permute-start.15 = (f32[8,8,256]{2,1,0:T(8,128)S(1)}, f32[8,8,256]{2,1,0:T(8,128)S(1)}, u32[]{:S(2)}, u32[]{:S(2)}) collective-permute-start(f32[8,8,256]{2,1,0:T(8,128)S(1)} %copy.63), channel_id=1, source_target_pairs={{0,1},{1,0},{2,3},{3,2},{4,5},{5,4},{6,7},{7,6},{8,9},{9,8},{10,11... | collective-permute-start | bytes 196616 | tf_op jit(solution)/shard_map/shard_1/ppermute | solution.py:18
  62.6 2.2 %collective-permute-done.13 = f32[8,8,256]{2,1,0:T(8,128)S(1)} collective-permute-done((f32[8,8,256]{2,1,0:T(8,128)S(1)}, f32[8,8,256]{2,1,0:T(8,128)S(1)}, u32[]{:S(2)}, u32[]{:S(2)}) %collective-permute-start.13) | collective-permute-done | bytes 65568 | tf_op jit(solution)/shard_map/shard_3/ppermute | solution.py:18
  64.8 2.2 %collective-permute-done.14 = f32[8,8,256]{2,1,0:T(8,128)S(1)} collective-permute-done((f32[8,8,256]{2,1,0:T(8,128)S(1)}, f32[8,8,256]{2,1,0:T(8,128)S(1)}, u32[]{:S(2)}, u32[]{:S(2)}) %collective-permute-start.14) | collective-permute-done | bytes 65568 | tf_op jit(solution)/shard_map/shard_2/ppermute | solution.py:18
  67.1 0.9 %collective-permute-start.18 = (f32[4,32,256]{2,1,0:T(8,128)S(1)}, f32[4,32,256]{2,1,0:T(8,128)S(1)}, u32[]{:S(2)}, u32[]{:S(2)}) collective-permute-start(f32[4,32,256]{2,1,0:T(8,128)S(1)} %get-tuple-element.57), channel_id=1, source_target_pairs={{0,8},{4,20},{8,0},{12,28},{16,24},{20,4},{24,16},{28,12},{1,9},{5... | collective-permute-start | bytes 393224 | tf_op jit(solution)/shard_map/rows_first_top/ppermute | solution.py:18
  68.6 1.5 %collective-permute-start.17 = (f32[4,32,256]{2,1,0:T(8,128)S(1)}, f32[4,32,256]{2,1,0:T(8,128)S(1)}, u32[]{:S(2)}, u32[]{:S(2)}) collective-permute-start(f32[4,32,256]{2,1,0:T(8,128)S(1)} %get-tuple-element.56), channel_id=1, source_target_pairs={{0,8},{4,20},{8,0},{12,28},{16,24},{20,4},{24,16},{28,12},{1,9},{5... | collective-permute-start | bytes 393224 | tf_op jit(solution)/shard_map/rows_first_low/ppermute | solution.py:18
  70.1 1.1 %collective-permute-start.19 = (f32[4,32,256]{2,1,0:T(8,128)S(1)}, f32[4,32,256]{2,1,0:T(8,128)S(1)}, u32[]{:S(2)}, u32[]{:S(2)}) collective-permute-start(f32[4,32,256]{2,1,0:T(8,128)S(1)} %get-tuple-element.57), channel_id=1, source_target_pairs={{0,16},{4,12},{8,24},{12,4},{16,0},{20,28},{24,8},{28,20},{1,17},{... | collective-permute-start | bytes 393224 | tf_op jit(solution)/shard_map/rows_second_top/ppermute | solution.py:18
  71.5 1.8 %collective-permute-done.18 = f32[4,32,256]{2,1,0:T(8,128)S(1)} collective-permute-done((f32[4,32,256]{2,1,0:T(8,128)S(1)}, f32[4,32,256]{2,1,0:T(8,128)S(1)}, u32[]{:S(2)}, u32[]{:S(2)}) %collective-permute-start.18) | collective-permute-done | bytes 131104 | tf_op jit(solution)/shard_map/rows_first_top/ppermute | solution.py:18
  73.2 0.9 %collective-permute-start.21 = (f32[4,32,256]{2,1,0:T(8,128)S(1)}, f32[4,32,256]{2,1,0:T(8,128)S(1)}, u32[]{:S(2)}, u32[]{:S(2)}) collective-permute-start(f32[4,32,256]{2,1,0:T(8,128)S(1)} %collective-permute-done.18), channel_id=1, source_target_pairs={{0,16},{4,12},{8,24},{12,4},{16,0},{20,28},{24,8},{28,20},{1,17},{... | collective-permute-start | bytes 393224 | tf_op jit(solution)/shard_map/rows_relay_top/ppermute | solution.py:18
  74.2 0.8 collective-permute-start.24
  75.0 1.0 %collective-permute-done.17 = f32[4,32,256]{2,1,0:T(8,128)S(1)} collective-permute-done((f32[4,32,256]{2,1,0:T(8,128)S(1)}, f32[4,32,256]{2,1,0:T(8,128)S(1)}, u32[]{:S(2)}, u32[]{:S(2)}) %collective-permute-start.17) | collective-permute-done | bytes 131104 | tf_op jit(solution)/shard_map/rows_first_low/ppermute | solution.py:18
  76.1 2.4 %collective-permute-done.21 = f32[4,32,256]{2,1,0:T(8,128)S(1)} collective-permute-done((f32[4,32,256]{2,1,0:T(8,128)S(1)}, f32[4,32,256]{2,1,0:T(8,128)S(1)}, u32[]{:S(2)}, u32[]{:S(2)}) %collective-permute-start.21) | collective-permute-done | bytes 131104 | tf_op jit(solution)/shard_map/rows_relay_top/ppermute | solution.py:18
  79.3 0.6 collective-permute-done.22
  80.8 1.3 %copy-done.3 = f32[8,256,256]{2,1,0:T(8,128)} copy-done((f32[8,256,256]{2,1,0:T(8,128)}, f32[8,256,256]{2,1,0:T(8,128)S(1)}, u32[]{:S(2)}) %copy-start.3) | copy-done | bytes 2097176
  (100 shorter events, 7.9 us)
Async XLA Ops:
  0.6 42.1 %copy-start = (f32[1,1,1,256,256]{4,3,2,1,0:T(8,128)S(1)}, f32[1,1,1,256,256]{4,3,2,1,0:T(8,128)}, u32[]{:S(2)}) copy-start(f32[1,1,1,256,256]{4,3,2,1,0:T(8,128)} %param.10) | copy-start | bytes 786436
  2.2 1.7 %collective-permute-start = (f32[8,32,256]{2,1,0:T(8,128)S(1)}, f32[8,32,256]{2,1,0:T(8,128)S(1)}, u32[]{:S(2)}, u32[]{:S(2)}) collective-permute-start(f32[8,32,256]{2,1,0:T(8,128)S(1)} %get-tuple-element.55), channel_id=1, source_target_pairs={{0,4},{4,0},{8,12},{12,8},{16,20},{20,16},{24,28},{28,24},{1,5},{5... | collective-permute-start | bytes 786440 | tf_op jit(solution)/shard_map/sum_core_across/ppermute | solution.py:18
  2.7 5.7 %collective-permute-start.4 = (f32[8,32,256]{2,1,0:T(8,128)S(1)}, f32[8,32,256]{2,1,0:T(8,128)S(1)}, u32[]{:S(2)}, u32[]{:S(2)}) collective-permute-start(f32[8,32,256]{2,1,0:T(8,128)S(1)} %get-tuple-element.52), channel_id=1, source_target_pairs={{0,4},{4,0},{8,12},{12,8},{16,20},{20,16},{24,28},{28,24},{1,5},{5... | collective-permute-start | bytes 786440 | tf_op jit(solution)/shard_map/sum_core_second/ppermute | solution.py:18
  2.8 5.6 %collective-permute-start.2 = (f32[8,32,256]{2,1,0:T(8,128)S(1)}, f32[8,32,256]{2,1,0:T(8,128)S(1)}, u32[]{:S(2)}, u32[]{:S(2)}) collective-permute-start(f32[8,32,256]{2,1,0:T(8,128)S(1)} %get-tuple-element.53), channel_id=1, source_target_pairs={{0,4},{4,0},{8,12},{12,8},{16,20},{20,16},{24,28},{28,24},{1,5},{5... | collective-permute-start | bytes 786440 | tf_op jit(solution)/shard_map/sum_core_first/ppermute | solution.py:18
  3.2 5.2 %collective-permute-start.1 = (f32[8,32,256]{2,1,0:T(8,128)S(1)}, f32[8,32,256]{2,1,0:T(8,128)S(1)}, u32[]{:S(2)}, u32[]{:S(2)}) collective-permute-start(f32[8,32,256]{2,1,0:T(8,128)S(1)} %get-tuple-element.54), channel_id=1, source_target_pairs={{0,4},{4,0},{8,12},{12,8},{16,20},{20,16},{24,28},{28,24},{1,5},{5... | collective-permute-start | bytes 786440 | tf_op jit(solution)/shard_map/sum_core_own/ppermute | solution.py:18
  4.0 6.5 %collective-permute-start.6 = (f32[8,16,256]{2,1,0:T(8,128)S(1)}, f32[8,16,256]{2,1,0:T(8,128)S(1)}, u32[]{:S(2)}, u32[]{:S(2)}) collective-permute-start(f32[8,16,256]{2,1,0:T(8,128)S(1)} %get-tuple-element.36), channel_id=1, source_target_pairs={{0,8},{4,20},{8,0},{12,28},{16,24},{20,4},{24,16},{28,12},{1,9},{5... | collective-permute-start | bytes 393224 | tf_op jit(solution)/shard_map/sum_across_far/ppermute | solution.py:18
  6.9 6.1 %collective-permute-start.7 = (f32[8,16,256]{2,1,0:T(8,128)S(1)}, f32[8,16,256]{2,1,0:T(8,128)S(1)}, u32[]{:S(2)}, u32[]{:S(2)}) collective-permute-start(f32[8,16,256]{2,1,0:T(8,128)S(1)} %get-tuple-element.38), channel_id=1, source_target_pairs={{0,16},{4,12},{8,24},{12,4},{16,0},{20,28},{24,8},{28,20},{1,17},{... | collective-permute-start | bytes 393224 | tf_op jit(solution)/shard_map/sum_across_near/ppermute | solution.py:18
  8.6 5.7 %collective-permute-start.3 = (f32[8,16,256]{2,1,0:T(8,128)S(1)}, f32[8,16,256]{2,1,0:T(8,128)S(1)}, u32[]{:S(2)}, u32[]{:S(2)}) collective-permute-start(f32[8,16,256]{2,1,0:T(8,128)S(1)} %get-tuple-element.31), channel_id=1, source_target_pairs={{0,8},{4,20},{8,0},{12,28},{16,24},{20,4},{24,16},{28,12},{1,9},{5... | collective-permute-start | bytes 393224 | tf_op jit(solution)/shard_map/sum_first_far/ppermute | solution.py:18
  9.2 5.5 %collective-permute-start.5 = (f32[8,16,256]{2,1,0:T(8,128)S(1)}, f32[8,16,256]{2,1,0:T(8,128)S(1)}, u32[]{:S(2)}, u32[]{:S(2)}) collective-permute-start(f32[8,16,256]{2,1,0:T(8,128)S(1)} %get-tuple-element.33), channel_id=1, source_target_pairs={{0,16},{4,12},{8,24},{12,4},{16,0},{20,28},{24,8},{28,20},{1,17},{... | collective-permute-start | bytes 393224 | tf_op jit(solution)/shard_map/sum_second_near/ppermute | solution.py:18
  13.0 6.2 %collective-permute-start.10 = (f32[8,16,256]{2,1,0:T(8,128)S(1)}, f32[8,16,256]{2,1,0:T(8,128)S(1)}, u32[]{:S(2)}, u32[]{:S(2)}) collective-permute-start(f32[8,16,256]{2,1,0:T(8,128)S(1)} %add.164), channel_id=1, source_target_pairs={{0,16},{4,12},{8,24},{12,4},{16,0},{20,28},{24,8},{28,20},{1,17},{... | collective-permute-start | bytes 393224 | tf_op jit(solution)/shard_map/sum_relay_far/ppermute | solution.py:18
  14.3 28.0 %copy-start.4 = (f32[1,1,1,256,256]{4,3,2,1,0:T(8,128)S(1)}, f32[1,1,1,256,256]{4,3,2,1,0:T(8,128)}, u32[]{:S(2)}) copy-start(f32[1,1,1,256,256]{4,3,2,1,0:T(8,128)} %param.9) | copy-start | bytes 786436
  14.7 8.3 %collective-permute-start.8 = (f32[8,16,256]{2,1,0:T(8,128)S(1)}, f32[8,16,256]{2,1,0:T(8,128)S(1)}, u32[]{:S(2)}, u32[]{:S(2)}) collective-permute-start(f32[8,16,256]{2,1,0:T(8,128)S(1)} %add.165), channel_id=1, source_target_pairs={{0,8},{4,20},{8,0},{12,28},{16,24},{20,4},{24,16},{28,12},{1,9},{5... | collective-permute-start | bytes 393224 | tf_op jit(solution)/shard_map/sum_relay_near/ppermute | solution.py:18
  19.3 23.5 %copy-start.5 = (f32[1,1,1,256,256]{4,3,2,1,0:T(8,128)S(1)}, f32[1,1,1,256,256]{4,3,2,1,0:T(8,128)}, u32[]{:S(2)}) copy-start(f32[1,1,1,256,256]{4,3,2,1,0:T(8,128)} %param.11) | copy-start | bytes 786436
  19.3 23.5 %copy-start.6 = (f32[1,1,1,256,256]{4,3,2,1,0:T(8,128)S(1)}, f32[1,1,1,256,256]{4,3,2,1,0:T(8,128)}, u32[]{:S(2)}) copy-start(f32[1,1,1,256,256]{4,3,2,1,0:T(8,128)} %param.12) | copy-start | bytes 786436
  19.3 6.4 %collective-permute-start.12 = (f32[8,8,256]{2,1,0:T(8,128)S(1)}, f32[8,8,256]{2,1,0:T(8,128)S(1)}, u32[]{:S(2)}, u32[]{:S(2)}) collective-permute-start(f32[8,8,256]{2,1,0:T(8,128)S(1)} %get-tuple-element.75), channel_id=1, source_target_pairs={{0,3},{1,2},{2,1},{3,0},{4,7},{5,6},{6,5},{7,4},{8,11},{9,10},{10,... | collective-permute-start | bytes 196616 | tf_op jit(solution)/shard_map/shard_3/ppermute | solution.py:18
  22.9 5.2 %collective-permute-start.11 = (f32[8,8,256]{2,1,0:T(8,128)S(1)}, f32[8,8,256]{2,1,0:T(8,128)S(1)}, u32[]{:S(2)}, u32[]{:S(2)}) collective-permute-start(f32[8,8,256]{2,1,0:T(8,128)S(1)} %get-tuple-element.74), channel_id=1, source_target_pairs={{0,2},{1,3},{2,0},{3,1},{4,6},{5,7},{6,4},{7,5},{8,10},{9,11},{10,... | collective-permute-start | bytes 196616 | tf_op jit(solution)/shard_map/shard_2/ppermute | solution.py:18
  23.0 5.1 %collective-permute-start.9 = (f32[8,8,256]{2,1,0:T(8,128)S(1)}, f32[8,8,256]{2,1,0:T(8,128)S(1)}, u32[]{:S(2)}, u32[]{:S(2)}) collective-permute-start(f32[8,8,256]{2,1,0:T(8,128)S(1)} %get-tuple-element.73), channel_id=1, source_target_pairs={{0,1},{1,0},{2,3},{3,2},{4,5},{5,4},{6,7},{7,6},{8,9},{9,8},{10,11... | collective-permute-start | bytes 196616 | tf_op jit(solution)/shard_map/shard_1/ppermute | solution.py:18
  43.6 21.2 %copy-start.1 = (f32[8,32,256]{2,1,0:T(8,128)S(1)}, f32[8,32,256]{2,1,0:T(8,128)}, u32[]{:S(2)}) copy-start(f32[8,32,256]{2,1,0:T(8,128)} %param.8) | copy-start | bytes 786436
  44.6 12.9 %all-to-all-start.1 = ((f32[32,8,256]{2,1,0:T(8,128)}), f32[32,8,256]{2,1,0:T(8,128)S(1)}, u32[]{:S(2)}, u32[]{:S(2)}) async-start(f32[32,8,256]{2,1,0:T(8,128)} %convolution_bitcast_fusion), calls=%async_computation.1 | async-start | bytes 524288 | tf_op jit(solution)/shard_map/all_to_all | solution.py:165
  58.0 6.9 %collective-permute-start.13 = (f32[8,8,256]{2,1,0:T(8,128)S(1)}, f32[8,8,256]{2,1,0:T(8,128)S(1)}, u32[]{:S(2)}, u32[]{:S(2)}) collective-permute-start(f32[8,8,256]{2,1,0:T(8,128)S(1)} %copy.61), channel_id=1, source_target_pairs={{0,3},{1,2},{2,1},{3,0},{4,7},{5,6},{6,5},{7,4},{8,11},{9,10},{10,... | collective-permute-start | bytes 196616 | tf_op jit(solution)/shard_map/shard_3/ppermute | solution.py:18
  59.8 7.2 %collective-permute-start.14 = (f32[8,8,256]{2,1,0:T(8,128)S(1)}, f32[8,8,256]{2,1,0:T(8,128)S(1)}, u32[]{:S(2)}, u32[]{:S(2)}) collective-permute-start(f32[8,8,256]{2,1,0:T(8,128)S(1)} %copy.62), channel_id=1, source_target_pairs={{0,2},{1,3},{2,0},{3,1},{4,6},{5,7},{6,4},{7,5},{8,10},{9,11},{10,... | collective-permute-start | bytes 196616 | tf_op jit(solution)/shard_map/shard_2/ppermute | solution.py:18
  60.7 6.4 %collective-permute-start.15 = (f32[8,8,256]{2,1,0:T(8,128)S(1)}, f32[8,8,256]{2,1,0:T(8,128)S(1)}, u32[]{:S(2)}, u32[]{:S(2)}) collective-permute-start(f32[8,8,256]{2,1,0:T(8,128)S(1)} %copy.63), channel_id=1, source_target_pairs={{0,1},{1,0},{2,3},{3,2},{4,5},{5,4},{6,7},{7,6},{8,9},{9,8},{10,11... | collective-permute-start | bytes 196616 | tf_op jit(solution)/shard_map/shard_1/ppermute | solution.py:18
  67.1 6.1 %collective-permute-start.18 = (f32[4,32,256]{2,1,0:T(8,128)S(1)}, f32[4,32,256]{2,1,0:T(8,128)S(1)}, u32[]{:S(2)}, u32[]{:S(2)}) collective-permute-start(f32[4,32,256]{2,1,0:T(8,128)S(1)} %get-tuple-element.57), channel_id=1, source_target_pairs={{0,8},{4,20},{8,0},{12,28},{16,24},{20,4},{24,16},{28,12},{1,9},{5... | collective-permute-start | bytes 393224 | tf_op jit(solution)/shard_map/rows_first_top/ppermute | solution.py:18
  68.1 6.1 %collective-permute-start.20 = (f32[4,32,256]{2,1,0:T(8,128)S(1)}, f32[4,32,256]{2,1,0:T(8,128)S(1)}, u32[]{:S(2)}, u32[]{:S(2)}) collective-permute-start(f32[4,32,256]{2,1,0:T(8,128)S(1)} %get-tuple-element.56), channel_id=1, source_target_pairs={{0,16},{4,12},{8,24},{12,4},{16,0},{20,28},{24,8},{28,20},{1,17},{... | collective-permute-start | bytes 393224 | tf_op jit(solution)/shard_map/rows_second_low/ppermute | solution.py:18
  68.6 7.3 %collective-permute-start.17 = (f32[4,32,256]{2,1,0:T(8,128)S(1)}, f32[4,32,256]{2,1,0:T(8,128)S(1)}, u32[]{:S(2)}, u32[]{:S(2)}) collective-permute-start(f32[4,32,256]{2,1,0:T(8,128)S(1)} %get-tuple-element.56), channel_id=1, source_target_pairs={{0,8},{4,20},{8,0},{12,28},{16,24},{20,4},{24,16},{28,12},{1,9},{5... | collective-permute-start | bytes 393224 | tf_op jit(solution)/shard_map/rows_first_low/ppermute | solution.py:18
  70.1 5.9 %collective-permute-start.16 = (f32[8,32,256]{2,1,0:T(8,128)S(1)}, f32[8,32,256]{2,1,0:T(8,128)S(1)}, u32[]{:S(2)}, u32[]{:S(2)}) collective-permute-start(f32[8,32,256]{2,1,0:T(8,128)S(1)} %subtract_dynamic-update-slice_fusion), channel_id=1, source_target_pairs={{0,4},{4,0},{8,12},{12,8},{16,20},{20,16},{24,28},{28,24},{1,5},{5... | collective-permute-start | bytes 786440 | tf_op jit(solution)/shard_map/rows_core_own/ppermute | solution.py:18
  70.1 5.8 %collective-permute-start.19 = (f32[4,32,256]{2,1,0:T(8,128)S(1)}, f32[4,32,256]{2,1,0:T(8,128)S(1)}, u32[]{:S(2)}, u32[]{:S(2)}) collective-permute-start(f32[4,32,256]{2,1,0:T(8,128)S(1)} %get-tuple-element.57), channel_id=1, source_target_pairs={{0,16},{4,12},{8,24},{12,4},{16,0},{20,28},{24,8},{28,20},{1,17},{... | collective-permute-start | bytes 393224 | tf_op jit(solution)/shard_map/rows_second_top/ppermute | solution.py:18
  73.2 5.2 %collective-permute-start.21 = (f32[4,32,256]{2,1,0:T(8,128)S(1)}, f32[4,32,256]{2,1,0:T(8,128)S(1)}, u32[]{:S(2)}, u32[]{:S(2)}) collective-permute-start(f32[4,32,256]{2,1,0:T(8,128)S(1)} %collective-permute-done.18), channel_id=1, source_target_pairs={{0,16},{4,12},{8,24},{12,4},{16,0},{20,28},{24,8},{28,20},{1,17},{... | collective-permute-start | bytes 393224 | tf_op jit(solution)/shard_map/rows_relay_top/ppermute | solution.py:18
  74.2 5.0 %collective-permute-start.24 = (f32[4,32,256]{2,1,0:T(8,128)S(1)}, f32[4,32,256]{2,1,0:T(8,128)S(1)}, u32[]{:S(2)}, u32[]{:S(2)}) collective-permute-start(f32[4,32,256]{2,1,0:T(8,128)S(1)} %collective-permute-done.20), channel_id=1, source_target_pairs={{0,8},{4,20},{8,0},{12,28},{16,24},{20,4},{24,16},{28,12},{1,9},{5... | collective-permute-start | bytes 393224 | tf_op jit(solution)/shard_map/rows_relay_low/ppermute | solution.py:18
  78.4 1.5 %collective-permute-start.22 = (f32[8,32,256]{2,1,0:T(8,128)S(1)}, f32[8,32,256]{2,1,0:T(8,128)S(1)}, u32[]{:S(2)}, u32[]{:S(2)}) collective-permute-start(f32[8,32,256]{2,1,0:T(8,128)S(1)} %pad_maximum_fusion.1), channel_id=1, source_target_pairs={{0,4},{4,0},{8,12},{12,8},{16,20},{20,16},{24,28},{28,24},{1,5},{5... | collective-permute-start | bytes 786440 | tf_op jit(solution)/shard_map/rows_core_first/ppermute | solution.py:18
  78.4 1.9 %collective-permute-start.23 = (f32[8,32,256]{2,1,0:T(8,128)S(1)}, f32[8,32,256]{2,1,0:T(8,128)S(1)}, u32[]{:S(2)}, u32[]{:S(2)}) collective-permute-start(f32[8,32,256]{2,1,0:T(8,128)S(1)} %pad_maximum_fusion.2), channel_id=1, source_target_pairs={{0,4},{4,0},{8,12},{12,8},{16,20},{20,16},{24,28},{28,24},{1,5},{5... | collective-permute-start | bytes 786440 | tf_op jit(solution)/shard_map/rows_core_second/ppermute | solution.py:18
  79.2 1.6 %collective-permute-start.25 = (f32[8,32,256]{2,1,0:T(8,128)S(1)}, f32[8,32,256]{2,1,0:T(8,128)S(1)}, u32[]{:S(2)}, u32[]{:S(2)}) collective-permute-start(f32[8,32,256]{2,1,0:T(8,128)S(1)} %constant_dynamic-update-slice_fusion.6), channel_id=1, source_target_pairs={{0,4},{4,0},{8,12},{12,8},{16,20},{20,16},{24,28},{28,24},{1,5},{5... | collective-permute-start | bytes 786440 | tf_op jit(solution)/shard_map/rows_core_far/ppermute | solution.py:18
  (5 other events, 52.5 us)

commit v7 on v6

--- a/solution.py
+++ b/solution.py
@@ -80,6 +80,7 @@
     high = lax.Precision.HIGH
     core, across = 1, 6
     first_link, second_link = (2, 4), (4, 2)
+    near_order = (0, 1, 3, 2)
     shard_here = lax.axis_index("shard")
     data_here = lax.axis_index("dp")
     shard_count = lax.axis_size("shard")
@@ -106,31 +107,29 @@
     def rows_of(values, mask):
         return take(values, 1, (data_here ^ mask) // 2).astype(jnp.float32)
 
+    along_x, along_y = (2, 2), (4, 4)
     near, far = {}, {}
-    for name, mask, other_mask in (
-        ("across", across, across),
-        ("first", first_chip, second_chip),
-        ("second", second_chip, first_chip),
-        ("own", 0, 0),
-    ):
+    for mask in (across, 2, 4, 0):
         total = rows_of(own_rows, mask) + swap(
-            rows_of(away_rows, other_mask), "dp", core, f"sum_core_{name}"
+            rows_of(away_rows, mask), "dp", core, f"sum_core_{mask}"
         )
-        near[name], far[name] = lax.optimization_barrier(
+        near[mask], far[mask] = lax.optimization_barrier(
             (set_of(total, shard_half), set_of(total, 1 - shard_half))
         )
-        if name == "across":
-            own_rows, near[name], far[name] = lax.optimization_barrier(
-                (own_rows, near[name], far[name])
+        if mask == across:
+            own_rows, near[mask], far[mask] = lax.optimization_barrier(
+                (own_rows, near[mask], far[mask])
             )
-    far_relay = far["second"] + swap(far["across"], "dp", first_link, "sum_across_far")
-    near_relay = near["first"] + swap(near["across"], "dp", second_link, "sum_across_near")
-    far_relay, near_relay = lax.optimization_barrier((far_relay, near_relay))
-    far_sum = far["own"] + swap(far["first"], "dp", first_link, "sum_first_far")
-    near_sum = near["own"] + swap(near["second"], "dp", second_link, "sum_second_near")
-    far_sum, near_sum = lax.optimization_barrier((far_sum, near_sum))
-    far_sum = far_sum + swap(far_relay, "dp", second_link, "sum_relay_far")
-    near_sum = near_sum + swap(near_relay, "dp", first_link, "sum_relay_near")
+    far_relay = far[4] + swap(far[across], "dp", along_x, "sum_across_far")
+    near_relay = near[2] + swap(near[across], "dp", along_y, "sum_across_near")
+    far_sum = far[0] + swap(far[2], "dp", along_x, "sum_x_far")
+    far_sum = lax.optimization_barrier(far_sum)
+    far_sum = far_sum + swap(far_relay, "dp", along_y, "sum_relay_far")
+    near_sum = near[0] + swap(near_relay, "dp", along_x, "sum_relay_near")
+    near_sum = lax.optimization_barrier(near_sum)
+    near_sum = near_sum + swap(near[4], "dp", along_y, "sum_y_near")
+
+    near_sum, owner_list = lax.optimization_barrier((near_sum, owner_list))
 
     mixed = shard_exchange(
         [
@@ -140,10 +139,11 @@
             set_of(far_sum, 1 - shard_low),
         ]
     )
-    owners = unmix(owner_list.reshape(shard_count, home_count), shard_here).reshape(1, -1)
+    owners = unmix(owner_list.reshape(shard_count, home_count), shard_here)
+    owners = jnp.concatenate([owners[k] for k in near_order])[None, :]
     device_ids = jnp.arange(device_total, dtype=jnp.int32)
     picker = (owners == device_ids[:, None]).astype(jnp.float32)
-    pieces = jnp.concatenate(mixed, axis=0).reshape(device_total, -1)
+    pieces = jnp.concatenate([mixed[k] for k in near_order], axis=0).reshape(device_total, -1)
     leaving = jnp.einsum("eb,bn->en", picker, pieces, precision=high)
     whole = lax.all_to_all(
         leaving.reshape((device_total,) + piece),
@@ -171,7 +171,7 @@
     ).reshape(device_total, -1)
     back = jnp.einsum("eb,en->bn", picker, coming, precision=high)
     back = back.reshape((shard_count, home_count) + piece)
-    returned = shard_exchange([back[k] for k in range(shard_count)])
+    returned = shard_exchange([back[near_order.index(k)] for k in range(shard_count)])
 
     new_home = params
     for k in (0, 3, 2, 1):

time: 82.4 us -> 80.8 us (0.981)
  waiting for transfers between devices: 32.8 us -> 30.1 us
  starting transfers between devices: 27.3 us -> 28.7 us
    ppermute x26, waiting for transfers between devices: 22.6 us -> 19.9 us  [swap(): return lax.ppermute(values, name, pairs)]
    ppermute x26, starting transfers between devices: 24.6 us -> 25.9 us  [swap(): return lax.ppermute(values, name, pairs)]
where the time goes in v7:
time: 80.8 us; the launch traced here: 80.6 us
  waiting for transfers between devices  30.1 us (37%)
  starting transfers between devices  28.7 us (36%)
  blocking collectives  13.6 us (17%)
  local copies, waits for them, and re-layouts  3.76 us (5%)
  matrix products  2.64 us (3%)
  between operations  1.26 us (2%)
    ppermute x26, starting transfers between devices, swap(): return lax.ppermute(values, name, pairs)  25.9 us
    ppermute x26, waiting for transfers between devices, swap(): return lax.ppermute(values, name, pairs)  19.9 us
    all_to_all x1, blocking collectives, routed(): lax.all_to_all(leaving.reshape((device_total,) + piece), ('dp', 'shard'),...  13.6 us
    all_to_all x1, waiting for transfers between devices, routed(): lax.all_to_all(change.reshape((device_total,) + piece), ('dp', 'shard'),...  10.2 us
    all_to_all x1, starting transfers between devices, routed(): lax.all_to_all(change.reshape((device_total,) + piece), ('dp', 'shard'),...  2.72 us
  transfers between devices with their start and end apart: 27, of which 17 were waited for; matrix products, arithmetic and copies ran while one was open for 1% of the time, Pallas kernels for 0%

profile of v7, /device:TPU:0, one launch (start us, length us, event | category | flops | bytes accessed | tf_op | source)
XLA Modules:
  0.0 80.6 jit_solution(8698532142900243530)
XLA Ops:
  0.7 1.3 %dynamic-slice_bitcast_fusion = (bf16[8,4,32,256]{3,2,1,0:T(8,128)(2,1)S(1)}, bf16[8,4,32,256]{3,2,1,0:T(8,128)(2,1)S(1)}) fusion(bf16[8,4,2,32,256]{4,3,2,1,0:T(8,128)(2,1)} %bitcast.130, s32[]{:T(128)S(6)} %select_n.128, s32[]{:T(128)S(6)} %select_n.127), kind=kLoop, calls=%fused_computation.1 | loop fusion | bytes 2097160 | tf_op jit(solution)/shard_map/jit(dynamic_index_in_dim)/squeeze | solution.py:22
  3.3 0.6 collective-permute-done
  3.9 2.9 %collective-permute-start.9 = (f32[8,16,256]{2,1,0:T(8,128)S(1)}, f32[8,16,256]{2,1,0:T(8,128)S(1)}, u32[]{:S(2)}, u32[]{:S(2)}) collective-permute-start(f32[8,16,256]{2,1,0:T(8,128)S(1)} %get-tuple-element.37), channel_id=1, source_target_pairs={{0,8},{4,12},{8,0},{12,4},{16,24},{20,28},{24,16},{28,20},{1,9},{5... | collective-permute-start | bytes 393224 | tf_op jit(solution)/shard_map/sum_across_far/ppermute | solution.py:18
  7.1 1.0 %collective-permute-start.8 = (f32[8,16,256]{2,1,0:T(8,128)S(1)}, f32[8,16,256]{2,1,0:T(8,128)S(1)}, u32[]{:S(2)}, u32[]{:S(2)}) collective-permute-start(f32[8,16,256]{2,1,0:T(8,128)S(1)} %get-tuple-element.35), channel_id=1, source_target_pairs={{0,8},{4,12},{8,0},{12,4},{16,24},{20,28},{24,16},{28,20},{1,9},{5... | collective-permute-start | bytes 393224 | tf_op jit(solution)/shard_map/sum_x_far/ppermute | solution.py:18
  8.1 1.5 %collective-permute-start.3 = (f32[8,16,256]{2,1,0:T(8,128)S(1)}, f32[8,16,256]{2,1,0:T(8,128)S(1)}, u32[]{:S(2)}, u32[]{:S(2)}) collective-permute-start(f32[8,16,256]{2,1,0:T(8,128)S(1)} %get-tuple-element.30), channel_id=1, source_target_pairs={{0,16},{4,20},{8,24},{12,28},{16,0},{20,4},{24,8},{28,12},{1,17},{... | collective-permute-start | bytes 393224 | tf_op jit(solution)/shard_map/sum_across_near/ppermute | solution.py:18
  9.6 1.5 %collective-permute-done.9 = f32[8,16,256]{2,1,0:T(8,128)S(1)} collective-permute-done((f32[8,16,256]{2,1,0:T(8,128)S(1)}, f32[8,16,256]{2,1,0:T(8,128)S(1)}, u32[]{:S(2)}, u32[]{:S(2)}) %collective-permute-start.9) | collective-permute-done | bytes 131104 | tf_op jit(solution)/shard_map/sum_across_far/ppermute | solution.py:18
  11.2 2.2 %collective-permute-start.10 = (f32[8,16,256]{2,1,0:T(8,128)S(1)}, f32[8,16,256]{2,1,0:T(8,128)S(1)}, u32[]{:S(2)}, u32[]{:S(2)}) collective-permute-start(f32[8,16,256]{2,1,0:T(8,128)S(1)} %add.168), channel_id=1, source_target_pairs={{0,16},{4,20},{8,24},{12,28},{16,0},{20,4},{24,8},{28,12},{1,17},{... | collective-permute-start | bytes 393224 | tf_op jit(solution)/shard_map/sum_relay_far/ppermute | solution.py:18
  13.8 1.8 %collective-permute-start.4 = (f32[8,16,256]{2,1,0:T(8,128)S(1)}, f32[8,16,256]{2,1,0:T(8,128)S(1)}, u32[]{:S(2)}, u32[]{:S(2)}) collective-permute-start(f32[8,16,256]{2,1,0:T(8,128)S(1)} %add.160), channel_id=1, source_target_pairs={{0,8},{4,12},{8,0},{12,4},{16,24},{20,28},{24,16},{28,20},{1,9},{5... | collective-permute-start | bytes 393224 | tf_op jit(solution)/shard_map/sum_relay_near/ppermute | solution.py:18
  15.6 2.0 %collective-permute-done.10 = f32[8,16,256]{2,1,0:T(8,128)S(1)} collective-permute-done((f32[8,16,256]{2,1,0:T(8,128)S(1)}, f32[8,16,256]{2,1,0:T(8,128)S(1)}, u32[]{:S(2)}, u32[]{:S(2)}) %collective-permute-start.10) | collective-permute-done | bytes 131104 | tf_op jit(solution)/shard_map/sum_relay_far/ppermute | solution.py:18
  17.6 2.7 %collective-permute-start.12 = (f32[8,8,256]{2,1,0:T(8,128)S(1)}, f32[8,8,256]{2,1,0:T(8,128)S(1)}, u32[]{:S(2)}, u32[]{:S(2)}) collective-permute-start(f32[8,8,256]{2,1,0:T(8,128)S(1)} %get-tuple-element.71), channel_id=1, source_target_pairs={{0,2},{1,3},{2,0},{3,1},{4,6},{5,7},{6,4},{7,5},{8,10},{9,11},{10,... | collective-permute-start | bytes 196616 | tf_op jit(solution)/shard_map/shard_2/ppermute | solution.py:18
  20.3 1.3 %collective-permute-start.11 = (f32[8,8,256]{2,1,0:T(8,128)S(1)}, f32[8,8,256]{2,1,0:T(8,128)S(1)}, u32[]{:S(2)}, u32[]{:S(2)}) collective-permute-start(f32[8,8,256]{2,1,0:T(8,128)S(1)} %get-tuple-element.70), channel_id=1, source_target_pairs={{0,3},{1,2},{2,1},{3,0},{4,7},{5,6},{6,5},{7,4},{8,11},{9,10},{10,... | collective-permute-start | bytes 196616 | tf_op jit(solution)/shard_map/shard_3/ppermute | solution.py:18
  22.3 0.6 collective-permute-done.12
  22.9 3.5 %collective-permute-done.11 = f32[8,8,256]{2,1,0:T(8,128)S(1)} collective-permute-done((f32[8,8,256]{2,1,0:T(8,128)S(1)}, f32[8,8,256]{2,1,0:T(8,128)S(1)}, u32[]{:S(2)}, u32[]{:S(2)}) %collective-permute-start.11) | collective-permute-done | bytes 65568 | tf_op jit(solution)/shard_map/shard_3/ppermute | solution.py:18
  27.2 13.6 %all_to_all.10 = f32[32,8,256]{2,1,0:T(8,128)S(1)} all-to-all(f32[32,8,256]{2,1,0:T(8,128)S(1)} %copy.56), channel_id=1, replica_groups=mesh['dp'=8,'shard'=4] {'dp','shard'}, dimensions={0} | all-to-all | bytes 524288 | tf_op jit(solution)/shard_map/all_to_all | solution.py:148
  42.1 1.0 %convolution_bitcast_fusion = f32[32,8,256]{2,1,0:T(8,128)} fusion(f32[256,256]{1,0:T(8,128)S(1)} %fusion.4, f32[1,1,1,256,256]{4,3,2,1,0:T(8,128)S(1)} %copy-done.4), kind=kOutput, calls=%fused_computation | convolution fusion | flops 100663296 | bytes 786432 | tf_op jit(solution)/shard_map/ia,aj->ij/dot_general | solution.py:70
  43.0 2.7 %all-to-all-start.1 = ((f32[32,8,256]{2,1,0:T(8,128)}), f32[32,8,256]{2,1,0:T(8,128)S(1)}, u32[]{:S(2)}, u32[]{:S(2)}) async-start(f32[32,8,256]{2,1,0:T(8,128)} %convolution_bitcast_fusion), calls=%async_computation.1 | async-start | bytes 524288 | tf_op jit(solution)/shard_map/all_to_all | solution.py:165
  45.8 10.2 %all-to-all-done.1 = f32[32,8,256]{2,1,0:T(8,128)S(1)} async-done(((f32[32,8,256]{2,1,0:T(8,128)}), f32[32,8,256]{2,1,0:T(8,128)S(1)}, u32[]{:S(2)}, u32[]{:S(2)}) %all-to-all-start.1) | async-done | bytes 262176 | tf_op jit(solution)/shard_map/all_to_all | solution.py:165
  56.4 1.8 %collective-permute-start.13 = (f32[8,8,256]{2,1,0:T(8,128)S(1)}, f32[8,8,256]{2,1,0:T(8,128)S(1)}, u32[]{:S(2)}, u32[]{:S(2)}) collective-permute-start(f32[8,8,256]{2,1,0:T(8,128)S(1)} %copy.58), channel_id=1, source_target_pairs={{0,3},{1,2},{2,1},{3,0},{4,7},{5,6},{6,5},{7,4},{8,11},{9,10},{10,... | collective-permute-start | bytes 196616 | tf_op jit(solution)/shard_map/shard_3/ppermute | solution.py:18
  58.3 0.9 %collective-permute-start.14 = (f32[8,8,256]{2,1,0:T(8,128)S(1)}, f32[8,8,256]{2,1,0:T(8,128)S(1)}, u32[]{:S(2)}, u32[]{:S(2)}) collective-permute-start(f32[8,8,256]{2,1,0:T(8,128)S(1)} %copy.59), channel_id=1, source_target_pairs={{0,2},{1,3},{2,0},{3,1},{4,6},{5,7},{6,4},{7,5},{8,10},{9,11},{10,... | collective-permute-start | bytes 196616 | tf_op jit(solution)/shard_map/shard_2/ppermute | solution.py:18
  59.2 1.9 %collective-permute-start.15 = (f32[8,8,256]{2,1,0:T(8,128)S(1)}, f32[8,8,256]{2,1,0:T(8,128)S(1)}, u32[]{:S(2)}, u32[]{:S(2)}) collective-permute-start(f32[8,8,256]{2,1,0:T(8,128)S(1)} %copy.60), channel_id=1, source_target_pairs={{0,1},{1,0},{2,3},{3,2},{4,5},{5,4},{6,7},{7,6},{8,9},{9,8},{10,11... | collective-permute-start | bytes 196616 | tf_op jit(solution)/shard_map/shard_1/ppermute | solution.py:18
  61.1 2.2 %collective-permute-done.13 = f32[8,8,256]{2,1,0:T(8,128)S(1)} collective-permute-done((f32[8,8,256]{2,1,0:T(8,128)S(1)}, f32[8,8,256]{2,1,0:T(8,128)S(1)}, u32[]{:S(2)}, u32[]{:S(2)}) %collective-permute-start.13) | collective-permute-done | bytes 65568 | tf_op jit(solution)/shard_map/shard_3/ppermute | solution.py:18
  63.3 2.2 %collective-permute-done.14 = f32[8,8,256]{2,1,0:T(8,128)S(1)} collective-permute-done((f32[8,8,256]{2,1,0:T(8,128)S(1)}, f32[8,8,256]{2,1,0:T(8,128)S(1)}, u32[]{:S(2)}, u32[]{:S(2)}) %collective-permute-start.14) | collective-permute-done | bytes 65568 | tf_op jit(solution)/shard_map/shard_2/ppermute | solution.py:18
  65.6 0.9 %collective-permute-start.18 = (f32[4,32,256]{2,1,0:T(8,128)S(1)}, f32[4,32,256]{2,1,0:T(8,128)S(1)}, u32[]{:S(2)}, u32[]{:S(2)}) collective-permute-start(f32[4,32,256]{2,1,0:T(8,128)S(1)} %get-tuple-element.53), channel_id=1, source_target_pairs={{0,8},{4,20},{8,0},{12,28},{16,24},{20,4},{24,16},{28,12},{1,9},{5... | collective-permute-start | bytes 393224 | tf_op jit(solution)/shard_map/rows_first_top/ppermute | solution.py:18
  67.1 1.5 %collective-permute-start.17 = (f32[4,32,256]{2,1,0:T(8,128)S(1)}, f32[4,32,256]{2,1,0:T(8,128)S(1)}, u32[]{:S(2)}, u32[]{:S(2)}) collective-permute-start(f32[4,32,256]{2,1,0:T(8,128)S(1)} %get-tuple-element.52), channel_id=1, source_target_pairs={{0,8},{4,20},{8,0},{12,28},{16,24},{20,4},{24,16},{28,12},{1,9},{5... | collective-permute-start | bytes 393224 | tf_op jit(solution)/shard_map/rows_first_low/ppermute | solution.py:18
  68.6 1.1 %collective-permute-start.19 = (f32[4,32,256]{2,1,0:T(8,128)S(1)}, f32[4,32,256]{2,1,0:T(8,128)S(1)}, u32[]{:S(2)}, u32[]{:S(2)}) collective-permute-start(f32[4,32,256]{2,1,0:T(8,128)S(1)} %get-tuple-element.53), channel_id=1, source_target_pairs={{0,16},{4,12},{8,24},{12,4},{16,0},{20,28},{24,8},{28,20},{1,17},{... | collective-permute-start | bytes 393224 | tf_op jit(solution)/shard_map/rows_second_top/ppermute | solution.py:18
  69.9 1.8 %collective-permute-done.18 = f32[4,32,256]{2,1,0:T(8,128)S(1)} collective-permute-done((f32[4,32,256]{2,1,0:T(8,128)S(1)}, f32[4,32,256]{2,1,0:T(8,128)S(1)}, u32[]{:S(2)}, u32[]{:S(2)}) %collective-permute-start.18) | collective-permute-done | bytes 131104 | tf_op jit(solution)/shard_map/rows_first_top/ppermute | solution.py:18
  71.7 0.9 %collective-permute-start.21 = (f32[4,32,256]{2,1,0:T(8,128)S(1)}, f32[4,32,256]{2,1,0:T(8,128)S(1)}, u32[]{:S(2)}, u32[]{:S(2)}) collective-permute-start(f32[4,32,256]{2,1,0:T(8,128)S(1)} %collective-permute-done.18), channel_id=1, source_target_pairs={{0,16},{4,12},{8,24},{12,4},{16,0},{20,28},{24,8},{28,20},{1,17},{... | collective-permute-start | bytes 393224 | tf_op jit(solution)/shard_map/rows_relay_top/ppermute | solution.py:18
  72.6 0.8 collective-permute-start.24
  73.4 1.0 %collective-permute-done.17 = f32[4,32,256]{2,1,0:T(8,128)S(1)} collective-permute-done((f32[4,32,256]{2,1,0:T(8,128)S(1)}, f32[4,32,256]{2,1,0:T(8,128)S(1)}, u32[]{:S(2)}, u32[]{:S(2)}) %collective-permute-start.17) | collective-permute-done | bytes 131104 | tf_op jit(solution)/shard_map/rows_first_low/ppermute | solution.py:18
  74.5 2.3 %collective-permute-done.21 = f32[4,32,256]{2,1,0:T(8,128)S(1)} collective-permute-done((f32[4,32,256]{2,1,0:T(8,128)S(1)}, f32[4,32,256]{2,1,0:T(8,128)S(1)}, u32[]{:S(2)}, u32[]{:S(2)}) %collective-permute-start.21) | collective-permute-done | bytes 131104 | tf_op jit(solution)/shard_map/rows_relay_top/ppermute | solution.py:18
  77.8 0.6 collective-permute-done.22
  79.3 1.3 %copy-done.3 = f32[8,256,256]{2,1,0:T(8,128)} copy-done((f32[8,256,256]{2,1,0:T(8,128)}, f32[8,256,256]{2,1,0:T(8,128)S(1)}, u32[]{:S(2)}) %copy-start.3) | copy-done | bytes 2097176
  (101 shorter events, 7.6 us)
Async XLA Ops:
  0.6 40.6 %copy-start = (f32[1,1,1,256,256]{4,3,2,1,0:T(8,128)S(1)}, f32[1,1,1,256,256]{4,3,2,1,0:T(8,128)}, u32[]{:S(2)}) copy-start(f32[1,1,1,256,256]{4,3,2,1,0:T(8,128)} %param.10) | copy-start | bytes 786436
  2.2 1.7 %collective-permute-start = (f32[8,32,256]{2,1,0:T(8,128)S(1)}, f32[8,32,256]{2,1,0:T(8,128)S(1)}, u32[]{:S(2)}, u32[]{:S(2)}) collective-permute-start(f32[8,32,256]{2,1,0:T(8,128)S(1)} %get-tuple-element.51), channel_id=1, source_target_pairs={{0,4},{4,0},{8,12},{12,8},{16,20},{20,16},{24,28},{28,24},{1,5},{5... | collective-permute-start | bytes 786440 | tf_op jit(solution)/shard_map/sum_core_6/ppermute | solution.py:18
  2.7 4.2 %collective-permute-start.5 = (f32[8,32,256]{2,1,0:T(8,128)S(1)}, f32[8,32,256]{2,1,0:T(8,128)S(1)}, u32[]{:S(2)}, u32[]{:S(2)}) collective-permute-start(f32[8,32,256]{2,1,0:T(8,128)S(1)} %get-tuple-element.48), channel_id=1, source_target_pairs={{0,4},{4,0},{8,12},{12,8},{16,20},{20,16},{24,28},{28,24},{1,5},{5... | collective-permute-start | bytes 786440 | tf_op jit(solution)/shard_map/sum_core_4/ppermute | solution.py:18
  2.8 4.1 %collective-permute-start.2 = (f32[8,32,256]{2,1,0:T(8,128)S(1)}, f32[8,32,256]{2,1,0:T(8,128)S(1)}, u32[]{:S(2)}, u32[]{:S(2)}) collective-permute-start(f32[8,32,256]{2,1,0:T(8,128)S(1)} %get-tuple-element.49), channel_id=1, source_target_pairs={{0,4},{4,0},{8,12},{12,8},{16,20},{20,16},{24,28},{28,24},{1,5},{5... | collective-permute-start | bytes 786440 | tf_op jit(solution)/shard_map/sum_core_2/ppermute | solution.py:18
  3.2 3.7 %collective-permute-start.1 = (f32[8,32,256]{2,1,0:T(8,128)S(1)}, f32[8,32,256]{2,1,0:T(8,128)S(1)}, u32[]{:S(2)}, u32[]{:S(2)}) collective-permute-start(f32[8,32,256]{2,1,0:T(8,128)S(1)} %get-tuple-element.50), channel_id=1, source_target_pairs={{0,4},{4,0},{8,12},{12,8},{16,20},{20,16},{24,28},{28,24},{1,5},{5... | collective-permute-start | bytes 786440 | tf_op jit(solution)/shard_map/sum_core_0/ppermute | solution.py:18
  3.9 7.2 %collective-permute-start.9 = (f32[8,16,256]{2,1,0:T(8,128)S(1)}, f32[8,16,256]{2,1,0:T(8,128)S(1)}, u32[]{:S(2)}, u32[]{:S(2)}) collective-permute-start(f32[8,16,256]{2,1,0:T(8,128)S(1)} %get-tuple-element.37), channel_id=1, source_target_pairs={{0,8},{4,12},{8,0},{12,4},{16,24},{20,28},{24,16},{28,20},{1,9},{5... | collective-permute-start | bytes 393224 | tf_op jit(solution)/shard_map/sum_across_far/ppermute | solution.py:18
  7.1 6.4 %collective-permute-start.8 = (f32[8,16,256]{2,1,0:T(8,128)S(1)}, f32[8,16,256]{2,1,0:T(8,128)S(1)}, u32[]{:S(2)}, u32[]{:S(2)}) collective-permute-start(f32[8,16,256]{2,1,0:T(8,128)S(1)} %get-tuple-element.35), channel_id=1, source_target_pairs={{0,8},{4,12},{8,0},{12,4},{16,24},{20,28},{24,16},{28,20},{1,9},{5... | collective-permute-start | bytes 393224 | tf_op jit(solution)/shard_map/sum_x_far/ppermute | solution.py:18
  8.1 5.6 %collective-permute-start.3 = (f32[8,16,256]{2,1,0:T(8,128)S(1)}, f32[8,16,256]{2,1,0:T(8,128)S(1)}, u32[]{:S(2)}, u32[]{:S(2)}) collective-permute-start(f32[8,16,256]{2,1,0:T(8,128)S(1)} %get-tuple-element.30), channel_id=1, source_target_pairs={{0,16},{4,20},{8,24},{12,28},{16,0},{20,4},{24,8},{28,12},{1,17},{... | collective-permute-start | bytes 393224 | tf_op jit(solution)/shard_map/sum_across_near/ppermute | solution.py:18
  11.2 6.4 %collective-permute-start.10 = (f32[8,16,256]{2,1,0:T(8,128)S(1)}, f32[8,16,256]{2,1,0:T(8,128)S(1)}, u32[]{:S(2)}, u32[]{:S(2)}) collective-permute-start(f32[8,16,256]{2,1,0:T(8,128)S(1)} %add.168), channel_id=1, source_target_pairs={{0,16},{4,20},{8,24},{12,28},{16,0},{20,4},{24,8},{28,12},{1,17},{... | collective-permute-start | bytes 393224 | tf_op jit(solution)/shard_map/sum_relay_far/ppermute | solution.py:18
  13.3 8.3 %collective-permute-start.6 = (f32[8,16,256]{2,1,0:T(8,128)S(1)}, f32[8,16,256]{2,1,0:T(8,128)S(1)}, u32[]{:S(2)}, u32[]{:S(2)}) collective-permute-start(f32[8,16,256]{2,1,0:T(8,128)S(1)} %get-tuple-element.31), channel_id=1, source_target_pairs={{0,16},{4,20},{8,24},{12,28},{16,0},{20,4},{24,8},{28,12},{1,17},{... | collective-permute-start | bytes 393224 | tf_op jit(solution)/shard_map/sum_y_near/ppermute | solution.py:18
  13.8 27.0 %copy-start.4 = (f32[1,1,1,256,256]{4,3,2,1,0:T(8,128)S(1)}, f32[1,1,1,256,256]{4,3,2,1,0:T(8,128)}, u32[]{:S(2)}) copy-start(f32[1,1,1,256,256]{4,3,2,1,0:T(8,128)} %param.9) | copy-start | bytes 786436
  13.8 7.9 %collective-permute-start.4 = (f32[8,16,256]{2,1,0:T(8,128)S(1)}, f32[8,16,256]{2,1,0:T(8,128)S(1)}, u32[]{:S(2)}, u32[]{:S(2)}) collective-permute-start(f32[8,16,256]{2,1,0:T(8,128)S(1)} %add.160), channel_id=1, source_target_pairs={{0,8},{4,12},{8,0},{12,4},{16,24},{20,28},{24,16},{28,20},{1,9},{5... | collective-permute-start | bytes 393224 | tf_op jit(solution)/shard_map/sum_relay_near/ppermute | solution.py:18
  17.6 5.3 %collective-permute-start.12 = (f32[8,8,256]{2,1,0:T(8,128)S(1)}, f32[8,8,256]{2,1,0:T(8,128)S(1)}, u32[]{:S(2)}, u32[]{:S(2)}) collective-permute-start(f32[8,8,256]{2,1,0:T(8,128)S(1)} %get-tuple-element.71), channel_id=1, source_target_pairs={{0,2},{1,3},{2,0},{3,1},{4,6},{5,7},{6,4},{7,5},{8,10},{9,11},{10,... | collective-permute-start | bytes 196616 | tf_op jit(solution)/shard_map/shard_2/ppermute | solution.py:18
  20.3 6.2 %collective-permute-start.11 = (f32[8,8,256]{2,1,0:T(8,128)S(1)}, f32[8,8,256]{2,1,0:T(8,128)S(1)}, u32[]{:S(2)}, u32[]{:S(2)}) collective-permute-start(f32[8,8,256]{2,1,0:T(8,128)S(1)} %get-tuple-element.70), channel_id=1, source_target_pairs={{0,3},{1,2},{2,1},{3,0},{4,7},{5,6},{6,5},{7,4},{8,11},{9,10},{10,... | collective-permute-start | bytes 196616 | tf_op jit(solution)/shard_map/shard_3/ppermute | solution.py:18
  21.7 19.5 %copy-start.5 = (f32[1,1,1,256,256]{4,3,2,1,0:T(8,128)S(1)}, f32[1,1,1,256,256]{4,3,2,1,0:T(8,128)}, u32[]{:S(2)}) copy-start(f32[1,1,1,256,256]{4,3,2,1,0:T(8,128)} %param.11) | copy-start | bytes 786436
  21.7 19.5 %copy-start.6 = (f32[1,1,1,256,256]{4,3,2,1,0:T(8,128)S(1)}, f32[1,1,1,256,256]{4,3,2,1,0:T(8,128)}, u32[]{:S(2)}) copy-start(f32[1,1,1,256,256]{4,3,2,1,0:T(8,128)} %param.12) | copy-start | bytes 786436
  21.8 5.0 %collective-permute-start.7 = (f32[8,8,256]{2,1,0:T(8,128)S(1)}, f32[8,8,256]{2,1,0:T(8,128)S(1)}, u32[]{:S(2)}, u32[]{:S(2)}) collective-permute-start(f32[8,8,256]{2,1,0:T(8,128)S(1)} %get-tuple-element.69), channel_id=1, source_target_pairs={{0,1},{1,0},{2,3},{3,2},{4,5},{5,4},{6,7},{7,6},{8,9},{9,8},{10,11... | collective-permute-start | bytes 196616 | tf_op jit(solution)/shard_map/shard_1/ppermute | solution.py:18
  42.0 21.2 %copy-start.1 = (f32[8,32,256]{2,1,0:T(8,128)S(1)}, f32[8,32,256]{2,1,0:T(8,128)}, u32[]{:S(2)}) copy-start(f32[8,32,256]{2,1,0:T(8,128)} %param.8) | copy-start | bytes 786436
  43.0 12.9 %all-to-all-start.1 = ((f32[32,8,256]{2,1,0:T(8,128)}), f32[32,8,256]{2,1,0:T(8,128)S(1)}, u32[]{:S(2)}, u32[]{:S(2)}) async-start(f32[32,8,256]{2,1,0:T(8,128)} %convolution_bitcast_fusion), calls=%async_computation.1 | async-start | bytes 524288 | tf_op jit(solution)/shard_map/all_to_all | solution.py:165
  56.4 6.9 %collective-permute-start.13 = (f32[8,8,256]{2,1,0:T(8,128)S(1)}, f32[8,8,256]{2,1,0:T(8,128)S(1)}, u32[]{:S(2)}, u32[]{:S(2)}) collective-permute-start(f32[8,8,256]{2,1,0:T(8,128)S(1)} %copy.58), channel_id=1, source_target_pairs={{0,3},{1,2},{2,1},{3,0},{4,7},{5,6},{6,5},{7,4},{8,11},{9,10},{10,... | collective-permute-start | bytes 196616 | tf_op jit(solution)/shard_map/shard_3/ppermute | solution.py:18
  58.3 7.2 %collective-permute-start.14 = (f32[8,8,256]{2,1,0:T(8,128)S(1)}, f32[8,8,256]{2,1,0:T(8,128)S(1)}, u32[]{:S(2)}, u32[]{:S(2)}) collective-permute-start(f32[8,8,256]{2,1,0:T(8,128)S(1)} %copy.59), channel_id=1, source_target_pairs={{0,2},{1,3},{2,0},{3,1},{4,6},{5,7},{6,4},{7,5},{8,10},{9,11},{10,... | collective-permute-start | bytes 196616 | tf_op jit(solution)/shard_map/shard_2/ppermute | solution.py:18
  59.2 6.4 %collective-permute-start.15 = (f32[8,8,256]{2,1,0:T(8,128)S(1)}, f32[8,8,256]{2,1,0:T(8,128)S(1)}, u32[]{:S(2)}, u32[]{:S(2)}) collective-permute-start(f32[8,8,256]{2,1,0:T(8,128)S(1)} %copy.60), channel_id=1, source_target_pairs={{0,1},{1,0},{2,3},{3,2},{4,5},{5,4},{6,7},{7,6},{8,9},{9,8},{10,11... | collective-permute-start | bytes 196616 | tf_op jit(solution)/shard_map/shard_1/ppermute | solution.py:18
  65.6 6.1 %collective-permute-start.18 = (f32[4,32,256]{2,1,0:T(8,128)S(1)}, f32[4,32,256]{2,1,0:T(8,128)S(1)}, u32[]{:S(2)}, u32[]{:S(2)}) collective-permute-start(f32[4,32,256]{2,1,0:T(8,128)S(1)} %get-tuple-element.53), channel_id=1, source_target_pairs={{0,8},{4,20},{8,0},{12,28},{16,24},{20,4},{24,16},{28,12},{1,9},{5... | collective-permute-start | bytes 393224 | tf_op jit(solution)/shard_map/rows_first_top/ppermute | solution.py:18
  66.5 6.1 %collective-permute-start.20 = (f32[4,32,256]{2,1,0:T(8,128)S(1)}, f32[4,32,256]{2,1,0:T(8,128)S(1)}, u32[]{:S(2)}, u32[]{:S(2)}) collective-permute-start(f32[4,32,256]{2,1,0:T(8,128)S(1)} %get-tuple-element.52), channel_id=1, source_target_pairs={{0,16},{4,12},{8,24},{12,4},{16,0},{20,28},{24,8},{28,20},{1,17},{... | collective-permute-start | bytes 393224 | tf_op jit(solution)/shard_map/rows_second_low/ppermute | solution.py:18
  67.1 7.3 %collective-permute-start.17 = (f32[4,32,256]{2,1,0:T(8,128)S(1)}, f32[4,32,256]{2,1,0:T(8,128)S(1)}, u32[]{:S(2)}, u32[]{:S(2)}) collective-permute-start(f32[4,32,256]{2,1,0:T(8,128)S(1)} %get-tuple-element.52), channel_id=1, source_target_pairs={{0,8},{4,20},{8,0},{12,28},{16,24},{20,4},{24,16},{28,12},{1,9},{5... | collective-permute-start | bytes 393224 | tf_op jit(solution)/shard_map/rows_first_low/ppermute | solution.py:18
  68.6 5.9 %collective-permute-start.16 = (f32[8,32,256]{2,1,0:T(8,128)S(1)}, f32[8,32,256]{2,1,0:T(8,128)S(1)}, u32[]{:S(2)}, u32[]{:S(2)}) collective-permute-start(f32[8,32,256]{2,1,0:T(8,128)S(1)} %subtract_dynamic-update-slice_fusion), channel_id=1, source_target_pairs={{0,4},{4,0},{8,12},{12,8},{16,20},{20,16},{24,28},{28,24},{1,5},{5... | collective-permute-start | bytes 786440 | tf_op jit(solution)/shard_map/rows_core_own/ppermute | solution.py:18
  68.6 5.9 %collective-permute-start.19 = (f32[4,32,256]{2,1,0:T(8,128)S(1)}, f32[4,32,256]{2,1,0:T(8,128)S(1)}, u32[]{:S(2)}, u32[]{:S(2)}) collective-permute-start(f32[4,32,256]{2,1,0:T(8,128)S(1)} %get-tuple-element.53), channel_id=1, source_target_pairs={{0,16},{4,12},{8,24},{12,4},{16,0},{20,28},{24,8},{28,20},{1,17},{... | collective-permute-start | bytes 393224 | tf_op jit(solution)/shard_map/rows_second_top/ppermute | solution.py:18
  71.7 5.2 %collective-permute-start.21 = (f32[4,32,256]{2,1,0:T(8,128)S(1)}, f32[4,32,256]{2,1,0:T(8,128)S(1)}, u32[]{:S(2)}, u32[]{:S(2)}) collective-permute-start(f32[4,32,256]{2,1,0:T(8,128)S(1)} %collective-permute-done.18), channel_id=1, source_target_pairs={{0,16},{4,12},{8,24},{12,4},{16,0},{20,28},{24,8},{28,20},{1,17},{... | collective-permute-start | bytes 393224 | tf_op jit(solution)/shard_map/rows_relay_top/ppermute | solution.py:18
  72.6 5.0 %collective-permute-start.24 = (f32[4,32,256]{2,1,0:T(8,128)S(1)}, f32[4,32,256]{2,1,0:T(8,128)S(1)}, u32[]{:S(2)}, u32[]{:S(2)}) collective-permute-start(f32[4,32,256]{2,1,0:T(8,128)S(1)} %collective-permute-done.20), channel_id=1, source_target_pairs={{0,8},{4,20},{8,0},{12,28},{16,24},{20,4},{24,16},{28,12},{1,9},{5... | collective-permute-start | bytes 393224 | tf_op jit(solution)/shard_map/rows_relay_low/ppermute | solution.py:18
  76.9 1.5 %collective-permute-start.22 = (f32[8,32,256]{2,1,0:T(8,128)S(1)}, f32[8,32,256]{2,1,0:T(8,128)S(1)}, u32[]{:S(2)}, u32[]{:S(2)}) collective-permute-start(f32[8,32,256]{2,1,0:T(8,128)S(1)} %pad_maximum_fusion.1), channel_id=1, source_target_pairs={{0,4},{4,0},{8,12},{12,8},{16,20},{20,16},{24,28},{28,24},{1,5},{5... | collective-permute-start | bytes 786440 | tf_op jit(solution)/shard_map/rows_core_first/ppermute | solution.py:18
  76.9 1.9 %collective-permute-start.23 = (f32[8,32,256]{2,1,0:T(8,128)S(1)}, f32[8,32,256]{2,1,0:T(8,128)S(1)}, u32[]{:S(2)}, u32[]{:S(2)}) collective-permute-start(f32[8,32,256]{2,1,0:T(8,128)S(1)} %pad_maximum_fusion.2), channel_id=1, source_target_pairs={{0,4},{4,0},{8,12},{12,8},{16,20},{20,16},{24,28},{28,24},{1,5},{5... | collective-permute-start | bytes 786440 | tf_op jit(solution)/shard_map/rows_core_second/ppermute | solution.py:18
  77.6 1.6 %collective-permute-start.25 = (f32[8,32,256]{2,1,0:T(8,128)S(1)}, f32[8,32,256]{2,1,0:T(8,128)S(1)}, u32[]{:S(2)}, u32[]{:S(2)}) collective-permute-start(f32[8,32,256]{2,1,0:T(8,128)S(1)} %constant_dynamic-update-slice_fusion.6), channel_id=1, source_target_pairs={{0,4},{4,0},{8,12},{12,8},{16,20},{20,16},{24,28},{28,24},{1,5},{5... | collective-permute-start | bytes 786440 | tf_op jit(solution)/shard_map/rows_core_far/ppermute | solution.py:18
  (5 other events, 64.9 us)

commit v8 on v6

--- a/solution.py
+++ b/solution.py
@@ -80,6 +80,7 @@
     high = lax.Precision.HIGH
     core, across = 1, 6
     first_link, second_link = (2, 4), (4, 2)
+    near_order = (0, 1, 3, 2)
     shard_here = lax.axis_index("shard")
     data_here = lax.axis_index("dp")
     shard_count = lax.axis_size("shard")
@@ -99,12 +100,15 @@
         return take(split, 1, index)
 
     grid = partials[0].reshape((home_count, chips, 2, row_count, width))
+
+    def rows_of(values, mask):
+        return take(values, 1, (data_here ^ mask) // 2).astype(jnp.float32)
+
+    away = {"across": rows_of(take(grid, 2, 1 - my_core), across)}
+    grid, away["across"] = lax.optimization_barrier((grid, away["across"]))
     away_rows = take(grid, 2, 1 - my_core)
     own_rows = take(grid, 2, my_core)
     away_rows, own_rows = lax.optimization_barrier((away_rows, own_rows))
-
-    def rows_of(values, mask):
-        return take(values, 1, (data_here ^ mask) // 2).astype(jnp.float32)
 
     near, far = {}, {}
     for name, mask, other_mask in (
@@ -113,9 +117,9 @@
         ("second", second_chip, first_chip),
         ("own", 0, 0),
     ):
-        total = rows_of(own_rows, mask) + swap(
-            rows_of(away_rows, other_mask), "dp", core, f"sum_core_{name}"
-        )
+        if name != "across":
+            away[name] = rows_of(away_rows, other_mask)
+        total = rows_of(own_rows, mask) + swap(away[name], "dp", core, f"sum_core_{name}")
         near[name], far[name] = lax.optimization_barrier(
             (set_of(total, shard_half), set_of(total, 1 - shard_half))
         )
@@ -123,14 +127,17 @@
             own_rows, near[name], far[name] = lax.optimization_barrier(
                 (own_rows, near[name], far[name])
             )
-    far_relay = far["second"] + swap(far["across"], "dp", first_link, "sum_across_far")
-    near_relay = near["first"] + swap(near["across"], "dp", second_link, "sum_across_near")
-    far_relay, near_relay = lax.optimization_barrier((far_relay, near_relay))
-    far_sum = far["own"] + swap(far["first"], "dp", first_link, "sum_first_far")
-    near_sum = near["own"] + swap(near["second"], "dp", second_link, "sum_second_near")
-    far_sum, near_sum = lax.optimization_barrier((far_sum, near_sum))
-    far_sum = far_sum + swap(far_relay, "dp", second_link, "sum_relay_far")
-    near_sum = near_sum + swap(near_relay, "dp", first_link, "sum_relay_near")
+
+    def sends(rows, what):
+        relay = rows["second"] + swap(rows["across"], "dp", first_link, f"sum_across_{what}")
+        direct = swap(rows["first"], "dp", first_link, f"sum_first_{what}")
+        return direct, swap(relay, "dp", second_link, f"sum_relay_{what}")
+
+    direct, relayed = sends(far, "far")
+    far_sum = lax.optimization_barrier(far["own"] + direct) + relayed
+    direct, relayed = sends(near, "near")
+    near_sum = lax.optimization_barrier(near["own"] + relayed) + direct
+    near_sum, owner_list = lax.optimization_barrier((near_sum, owner_list))
 
     mixed = shard_exchange(
         [
@@ -140,10 +147,11 @@
             set_of(far_sum, 1 - shard_low),
         ]
     )
-    owners = unmix(owner_list.reshape(shard_count, home_count), shard_here).reshape(1, -1)
+    owners = unmix(owner_list.reshape(shard_count, home_count), shard_here)
+    owners = jnp.concatenate([owners[k] for k in near_order])[None, :]
     device_ids = jnp.arange(device_total, dtype=jnp.int32)
     picker = (owners == device_ids[:, None]).astype(jnp.float32)
-    pieces = jnp.concatenate(mixed, axis=0).reshape(device_total, -1)
+    pieces = jnp.concatenate([mixed[k] for k in near_order], axis=0).reshape(device_total, -1)
     leaving = jnp.einsum("eb,bn->en", picker, pieces, precision=high)
     whole = lax.all_to_all(
         leaving.reshape((device_total,) + piece),
@@ -169,9 +177,14 @@
         concat_axis=0,
         tiled=True,
     ).reshape(device_total, -1)
+    coming, data_here, shard_here, params = lax.optimization_barrier(
+        (coming, data_here, shard_here, params)
+    )
+    first_chip = jnp.where((data_here & core) == 0, *first_link)
+    second_chip = across - first_chip
     back = jnp.einsum("eb,en->bn", picker, coming, precision=high)
     back = back.reshape((shard_count, home_count) + piece)
-    returned = shard_exchange([back[k] for k in range(shard_count)])
+    returned = shard_exchange([back[near_order.index(k)] for k in range(shard_count)])
 
     new_home = params
     for k in (0, 3, 2, 1):

time: 82.4 us -> 79.5 us (0.965)
  waiting for transfers between devices: 32.8 us -> 16.8 us
  blocking collectives: 13.8 us -> 26.7 us
  other arithmetic: 0.54 us -> 1.53 us
    all_to_all x0 -> x1, blocking collectives: none -> 12.7 us  [routed(): lax.all_to_all(change.reshape((device_total,) + piece), ('dp', 'shard'),...]
    all_to_all x1 -> x0, waiting for transfers between devices: 10.2 us -> none  [routed(): lax.all_to_all(change.reshape((device_total,) + piece), ('dp', 'shard'),...]
    ppermute x26, waiting for transfers between devices: 22.6 us -> 16.8 us  [swap(): return lax.ppermute(values, name, pairs)]
    ppermute x26, starting transfers between devices: 24.6 us -> 27.4 us  [swap(): return lax.ppermute(values, name, pairs)]
    all_to_all x1 -> x0, starting transfers between devices: 2.73 us -> none  [routed(): lax.all_to_all(change.reshape((device_total,) + piece), ('dp', 'shard'),...]
    convert_element_type x1 -> x2, other arithmetic: 0.12 us -> 1.05 us  [rows_of(): return take(values, 1, (data_here ^ mask) // 2).astype(jnp.float32)]
  transfers between devices with their start and end apart: 27 -> 26, of which waited for: 17 -> 14; matrix products, arithmetic and copies ran while one was open for 1% -> 3% of each run, Pallas kernels for 0% -> 0%
where the time goes in v8:
time: 79.5 us; the launch traced here: 79.3 us
  starting transfers between devices  27.4 us (34%)
  blocking collectives  26.7 us (34%)
  waiting for transfers between devices  16.8 us (21%)
  local copies, waits for them, and re-layouts  3.75 us (5%)
  matrix products  1.94 us (2%)
  other arithmetic  1.53 us (2%)
  between operations  1.22 us (2%)
    ppermute x26, starting transfers between devices, swap(): return lax.ppermute(values, name, pairs)  27.4 us
    ppermute x26, waiting for transfers between devices, swap(): return lax.ppermute(values, name, pairs)  16.8 us
    all_to_all x1, blocking collectives, routed(): lax.all_to_all(leaving.reshape((device_total,) + piece), ('dp', 'shard'),...  14 us
    all_to_all x1, blocking collectives, routed(): lax.all_to_all(change.reshape((device_total,) + piece), ('dp', 'shard'),...  12.7 us
  transfers between devices with their start and end apart: 26, of which 14 were waited for; matrix products, arithmetic and copies ran while one was open for 3% of the time, Pallas kernels for 0%

profile of v8, /device:TPU:0, one launch (start us, length us, event | category | flops | bytes accessed | tf_op | source)
XLA Modules:
  0.0 79.3 jit_solution(1660737117876650071)
XLA Ops:
  0.7 1.0 %bitcast_convert_fusion.3 = f32[8,32,256]{2,1,0:T(8,128)S(1)} fusion(bf16[8,4,2,32,256]{4,3,2,1,0:T(8,128)(2,1)} %bitcast.123, s32[]{:T(128)S(6)} %select_n.136, s32[]{:T(128)S(6)} %select_n.138), kind=kLoop, calls=%fused_computation.34 | loop fusion | flops 65536 | bytes 393224 | tf_op jit(solution)/shard_map/convert_element_type | solution.py:105
  2.2 1.3 %dynamic-slice_bitcast_fusion = (bf16[8,4,32,256]{3,2,1,0:T(8,128)(2,1)S(1)}, bf16[8,4,32,256]{3,2,1,0:T(8,128)(2,1)S(1)}) fusion(bf16[8,4,2,32,256]{4,3,2,1,0:T(8,128)(2,1)} %bitcast.124, s32[]{:T(128)S(6)} %select_n.139, s32[]{:T(128)S(6)} %select_n.137), kind=kLoop, calls=%fused_computation.1 | loop fusion | bytes 2097160 | tf_op jit(solution)/shard_map/jit(dynamic_index_in_dim)/squeeze | solution.py:22
  4.3 3.0 %collective-permute-start.9 = (f32[8,16,256]{2,1,0:T(8,128)S(1)}, f32[8,16,256]{2,1,0:T(8,128)S(1)}, u32[]{:S(2)}, u32[]{:S(2)}) collective-permute-start(f32[8,16,256]{2,1,0:T(8,128)S(1)} %get-tuple-element.45), channel_id=1, source_target_pairs={{0,8},{4,20},{8,0},{12,28},{16,24},{20,4},{24,16},{28,12},{1,9},{5... | collective-permute-start | bytes 393224 | tf_op jit(solution)/shard_map/sum_across_far/ppermute | solution.py:18
  7.5 1.3 %collective-permute-start.8 = (f32[8,16,256]{2,1,0:T(8,128)S(1)}, f32[8,16,256]{2,1,0:T(8,128)S(1)}, u32[]{:S(2)}, u32[]{:S(2)}) collective-permute-start(f32[8,16,256]{2,1,0:T(8,128)S(1)} %get-tuple-element.43), channel_id=1, source_target_pairs={{0,8},{4,20},{8,0},{12,28},{16,24},{20,4},{24,16},{28,12},{1,9},{5... | collective-permute-start | bytes 393224 | tf_op jit(solution)/shard_map/sum_first_far/ppermute | solution.py:18
  8.8 0.8 collective-permute-start.3
  9.6 0.7 collective-permute-done.9
  10.3 2.1 %collective-permute-start.10 = (f32[8,16,256]{2,1,0:T(8,128)S(1)}, f32[8,16,256]{2,1,0:T(8,128)S(1)}, u32[]{:S(2)}, u32[]{:S(2)}) collective-permute-start(f32[8,16,256]{2,1,0:T(8,128)S(1)} %add.173), channel_id=1, source_target_pairs={{0,16},{4,12},{8,24},{12,4},{16,0},{20,28},{24,8},{28,20},{1,17},{... | collective-permute-start | bytes 393224 | tf_op jit(solution)/shard_map/sum_relay_far/ppermute | solution.py:18
  12.4 1.6 %collective-permute-start.6 = (f32[8,16,256]{2,1,0:T(8,128)S(1)}, f32[8,16,256]{2,1,0:T(8,128)S(1)}, u32[]{:S(2)}, u32[]{:S(2)}) collective-permute-start(f32[8,16,256]{2,1,0:T(8,128)S(1)} %get-tuple-element.39), channel_id=1, source_target_pairs={{0,8},{4,20},{8,0},{12,28},{16,24},{20,4},{24,16},{28,12},{1,9},{5... | collective-permute-start | bytes 393224 | tf_op jit(solution)/shard_map/sum_first_near/ppermute | solution.py:18
  14.0 1.3 %collective-permute-done.3 = f32[8,16,256]{2,1,0:T(8,128)S(1)} collective-permute-done((f32[8,16,256]{2,1,0:T(8,128)S(1)}, f32[8,16,256]{2,1,0:T(8,128)S(1)}, u32[]{:S(2)}, u32[]{:S(2)}) %collective-permute-start.3) | collective-permute-done | bytes 131104 | tf_op jit(solution)/shard_map/sum_across_near/ppermute | solution.py:18
  15.3 1.3 %collective-permute-start.4 = (f32[8,16,256]{2,1,0:T(8,128)S(1)}, f32[8,16,256]{2,1,0:T(8,128)S(1)}, u32[]{:S(2)}, u32[]{:S(2)}) collective-permute-start(f32[8,16,256]{2,1,0:T(8,128)S(1)} %add.166), channel_id=1, source_target_pairs={{0,16},{4,12},{8,24},{12,4},{16,0},{20,28},{24,8},{28,20},{1,17},{... | collective-permute-start | bytes 393224 | tf_op jit(solution)/shard_map/sum_relay_near/ppermute | solution.py:18
  16.7 2.8 %collective-permute-start.12 = (f32[8,8,256]{2,1,0:T(8,128)S(1)}, f32[8,8,256]{2,1,0:T(8,128)S(1)}, u32[]{:S(2)}, u32[]{:S(2)}) collective-permute-start(f32[8,8,256]{2,1,0:T(8,128)S(1)} %get-tuple-element.82), channel_id=1, source_target_pairs={{0,2},{1,3},{2,0},{3,1},{4,6},{5,7},{6,4},{7,5},{8,10},{9,11},{10,... | collective-permute-start | bytes 196616 | tf_op jit(solution)/shard_map/shard_2/ppermute | solution.py:18
  19.5 1.3 %collective-permute-start.11 = (f32[8,8,256]{2,1,0:T(8,128)S(1)}, f32[8,8,256]{2,1,0:T(8,128)S(1)}, u32[]{:S(2)}, u32[]{:S(2)}) collective-permute-start(f32[8,8,256]{2,1,0:T(8,128)S(1)} %get-tuple-element.81), channel_id=1, source_target_pairs={{0,3},{1,2},{2,1},{3,0},{4,7},{5,6},{6,5},{7,4},{8,11},{9,10},{10,... | collective-permute-start | bytes 196616 | tf_op jit(solution)/shard_map/shard_3/ppermute | solution.py:18
  21.0 0.9 %collective-permute-start.7 = (f32[8,8,256]{2,1,0:T(8,128)S(1)}, f32[8,8,256]{2,1,0:T(8,128)S(1)}, u32[]{:S(2)}, u32[]{:S(2)}) collective-permute-start(f32[8,8,256]{2,1,0:T(8,128)S(1)} %get-tuple-element.80), channel_id=1, source_target_pairs={{0,1},{1,0},{2,3},{3,2},{4,5},{5,4},{6,7},{7,6},{8,9},{9,8},{10,11... | collective-permute-start | bytes 196616 | tf_op jit(solution)/shard_map/shard_1/ppermute | solution.py:18
  22.1 1.7 %collective-permute-done.12 = f32[8,8,256]{2,1,0:T(8,128)S(1)} collective-permute-done((f32[8,8,256]{2,1,0:T(8,128)S(1)}, f32[8,8,256]{2,1,0:T(8,128)S(1)}, u32[]{:S(2)}, u32[]{:S(2)}) %collective-permute-start.12) | collective-permute-done | bytes 65568 | tf_op jit(solution)/shard_map/shard_2/ppermute | solution.py:18
  23.9 1.8 %collective-permute-done.11 = f32[8,8,256]{2,1,0:T(8,128)S(1)} collective-permute-done((f32[8,8,256]{2,1,0:T(8,128)S(1)}, f32[8,8,256]{2,1,0:T(8,128)S(1)}, u32[]{:S(2)}, u32[]{:S(2)}) %collective-permute-start.11) | collective-permute-done | bytes 65568 | tf_op jit(solution)/shard_map/shard_3/ppermute | solution.py:18
  26.4 14.0 %all_to_all.10 = f32[32,8,256]{2,1,0:T(8,128)S(1)} all-to-all(f32[32,8,256]{2,1,0:T(8,128)S(1)} %copy.55), channel_id=1, replica_groups=mesh['dp'=8,'shard'=4] {'dp','shard'}, dimensions={0} | all-to-all | bytes 524288 | tf_op jit(solution)/shard_map/all_to_all | solution.py:156
  42.0 12.7 %all_to_all.11 = f32[32,8,256]{2,1,0:T(8,128)S(1)} all-to-all(f32[32,8,256]{2,1,0:T(8,128)S(1)} %convolution_bitcast_fusion), channel_id=1, replica_groups=mesh['dp'=8,'shard'=4] {'dp','shard'}, dimensions={0} | all-to-all | bytes 524288 | tf_op jit(solution)/shard_map/all_to_all | solution.py:173
  55.1 1.8 %collective-permute-start.13 = (f32[8,8,256]{2,1,0:T(8,128)S(1)}, f32[8,8,256]{2,1,0:T(8,128)S(1)}, u32[]{:S(2)}, u32[]{:S(2)}) collective-permute-start(f32[8,8,256]{2,1,0:T(8,128)S(1)} %copy.57), channel_id=1, source_target_pairs={{0,3},{1,2},{2,1},{3,0},{4,7},{5,6},{6,5},{7,4},{8,11},{9,10},{10,... | collective-permute-start | bytes 196616 | tf_op jit(solution)/shard_map/shard_3/ppermute | solution.py:18
  57.0 0.9 %collective-permute-start.14 = (f32[8,8,256]{2,1,0:T(8,128)S(1)}, f32[8,8,256]{2,1,0:T(8,128)S(1)}, u32[]{:S(2)}, u32[]{:S(2)}) collective-permute-start(f32[8,8,256]{2,1,0:T(8,128)S(1)} %copy.58), channel_id=1, source_target_pairs={{0,2},{1,3},{2,0},{3,1},{4,6},{5,7},{6,4},{7,5},{8,10},{9,11},{10,... | collective-permute-start | bytes 196616 | tf_op jit(solution)/shard_map/shard_2/ppermute | solution.py:18
  57.9 1.9 %collective-permute-start.15 = (f32[8,8,256]{2,1,0:T(8,128)S(1)}, f32[8,8,256]{2,1,0:T(8,128)S(1)}, u32[]{:S(2)}, u32[]{:S(2)}) collective-permute-start(f32[8,8,256]{2,1,0:T(8,128)S(1)} %copy.59), channel_id=1, source_target_pairs={{0,1},{1,0},{2,3},{3,2},{4,5},{5,4},{6,7},{7,6},{8,9},{9,8},{10,11... | collective-permute-start | bytes 196616 | tf_op jit(solution)/shard_map/shard_1/ppermute | solution.py:18
  59.9 2.2 %collective-permute-done.13 = f32[8,8,256]{2,1,0:T(8,128)S(1)} collective-permute-done((f32[8,8,256]{2,1,0:T(8,128)S(1)}, f32[8,8,256]{2,1,0:T(8,128)S(1)}, u32[]{:S(2)}, u32[]{:S(2)}) %collective-permute-start.13) | collective-permute-done | bytes 65568 | tf_op jit(solution)/shard_map/shard_3/ppermute | solution.py:18
  62.0 2.2 %collective-permute-done.14 = f32[8,8,256]{2,1,0:T(8,128)S(1)} collective-permute-done((f32[8,8,256]{2,1,0:T(8,128)S(1)}, f32[8,8,256]{2,1,0:T(8,128)S(1)}, u32[]{:S(2)}, u32[]{:S(2)}) %collective-permute-start.14) | collective-permute-done | bytes 65568 | tf_op jit(solution)/shard_map/shard_2/ppermute | solution.py:18
  64.3 0.9 %collective-permute-start.18 = (f32[4,32,256]{2,1,0:T(8,128)S(1)}, f32[4,32,256]{2,1,0:T(8,128)S(1)}, u32[]{:S(2)}, u32[]{:S(2)}) collective-permute-start(f32[4,32,256]{2,1,0:T(8,128)S(1)} %get-tuple-element.64), channel_id=1, source_target_pairs={{0,8},{4,20},{8,0},{12,28},{16,24},{20,4},{24,16},{28,12},{1,9},{5... | collective-permute-start | bytes 393224 | tf_op jit(solution)/shard_map/rows_first_top/ppermute | solution.py:18
  65.8 1.5 %collective-permute-start.17 = (f32[4,32,256]{2,1,0:T(8,128)S(1)}, f32[4,32,256]{2,1,0:T(8,128)S(1)}, u32[]{:S(2)}, u32[]{:S(2)}) collective-permute-start(f32[4,32,256]{2,1,0:T(8,128)S(1)} %get-tuple-element.63), channel_id=1, source_target_pairs={{0,8},{4,20},{8,0},{12,28},{16,24},{20,4},{24,16},{28,12},{1,9},{5... | collective-permute-start | bytes 393224 | tf_op jit(solution)/shard_map/rows_first_low/ppermute | solution.py:18
  67.3 1.1 %collective-permute-start.19 = (f32[4,32,256]{2,1,0:T(8,128)S(1)}, f32[4,32,256]{2,1,0:T(8,128)S(1)}, u32[]{:S(2)}, u32[]{:S(2)}) collective-permute-start(f32[4,32,256]{2,1,0:T(8,128)S(1)} %get-tuple-element.64), channel_id=1, source_target_pairs={{0,16},{4,12},{8,24},{12,4},{16,0},{20,28},{24,8},{28,20},{1,17},{... | collective-permute-start | bytes 393224 | tf_op jit(solution)/shard_map/rows_second_top/ppermute | solution.py:18
  68.6 1.8 %collective-permute-done.18 = f32[4,32,256]{2,1,0:T(8,128)S(1)} collective-permute-done((f32[4,32,256]{2,1,0:T(8,128)S(1)}, f32[4,32,256]{2,1,0:T(8,128)S(1)}, u32[]{:S(2)}, u32[]{:S(2)}) %collective-permute-start.18) | collective-permute-done | bytes 131104 | tf_op jit(solution)/shard_map/rows_first_top/ppermute | solution.py:18
  70.4 0.9 %collective-permute-start.21 = (f32[4,32,256]{2,1,0:T(8,128)S(1)}, f32[4,32,256]{2,1,0:T(8,128)S(1)}, u32[]{:S(2)}, u32[]{:S(2)}) collective-permute-start(f32[4,32,256]{2,1,0:T(8,128)S(1)} %collective-permute-done.18), channel_id=1, source_target_pairs={{0,16},{4,12},{8,24},{12,4},{16,0},{20,28},{24,8},{28,20},{1,17},{... | collective-permute-start | bytes 393224 | tf_op jit(solution)/shard_map/rows_relay_top/ppermute | solution.py:18
  71.3 0.8 %collective-permute-start.24 = (f32[4,32,256]{2,1,0:T(8,128)S(1)}, f32[4,32,256]{2,1,0:T(8,128)S(1)}, u32[]{:S(2)}, u32[]{:S(2)}) collective-permute-start(f32[4,32,256]{2,1,0:T(8,128)S(1)} %collective-permute-done.20), channel_id=1, source_target_pairs={{0,8},{4,20},{8,0},{12,28},{16,24},{20,4},{24,16},{28,12},{1,9},{5... | collective-permute-start | bytes 393224 | tf_op jit(solution)/shard_map/rows_relay_low/ppermute | solution.py:18
  72.1 1.0 %collective-permute-done.17 = f32[4,32,256]{2,1,0:T(8,128)S(1)} collective-permute-done((f32[4,32,256]{2,1,0:T(8,128)S(1)}, f32[4,32,256]{2,1,0:T(8,128)S(1)}, u32[]{:S(2)}, u32[]{:S(2)}) %collective-permute-start.17) | collective-permute-done | bytes 131104 | tf_op jit(solution)/shard_map/rows_first_low/ppermute | solution.py:18
  73.2 2.4 %collective-permute-done.21 = f32[4,32,256]{2,1,0:T(8,128)S(1)} collective-permute-done((f32[4,32,256]{2,1,0:T(8,128)S(1)}, f32[4,32,256]{2,1,0:T(8,128)S(1)}, u32[]{:S(2)}, u32[]{:S(2)}) %collective-permute-start.21) | collective-permute-done | bytes 131104 | tf_op jit(solution)/shard_map/rows_relay_top/ppermute | solution.py:18
  76.5 0.6 collective-permute-done.22
  78.0 1.3 %copy-done.3 = f32[8,256,256]{2,1,0:T(8,128)} copy-done((f32[8,256,256]{2,1,0:T(8,128)}, f32[8,256,256]{2,1,0:T(8,128)S(1)}, u32[]{:S(2)}) %copy-start.3) | copy-done | bytes 2097176
  (101 shorter events, 7.3 us)
Async XLA Ops:
  0.6 40.2 %copy-start = (f32[1,1,1,256,256]{4,3,2,1,0:T(8,128)S(1)}, f32[1,1,1,256,256]{4,3,2,1,0:T(8,128)}, u32[]{:S(2)}) copy-start(f32[1,1,1,256,256]{4,3,2,1,0:T(8,128)} %param.10) | copy-start | bytes 786436
  1.7 2.6 %collective-permute-start = (f32[8,32,256]{2,1,0:T(8,128)S(1)}, f32[8,32,256]{2,1,0:T(8,128)S(1)}, u32[]{:S(2)}, u32[]{:S(2)}) collective-permute-start(f32[8,32,256]{2,1,0:T(8,128)S(1)} %bitcast_convert_fusion.3), channel_id=1, source_target_pairs={{0,4},{4,0},{8,12},{12,8},{16,20},{20,16},{24,28},{28,24},{1,5},{5... | collective-permute-start | bytes 786440 | tf_op jit(solution)/shard_map/sum_core_across/ppermute | solution.py:18
  3.6 3.7 %collective-permute-start.2 = (f32[8,32,256]{2,1,0:T(8,128)S(1)}, f32[8,32,256]{2,1,0:T(8,128)S(1)}, u32[]{:S(2)}, u32[]{:S(2)}) collective-permute-start(f32[8,32,256]{2,1,0:T(8,128)S(1)} %get-tuple-element.60), channel_id=1, source_target_pairs={{0,4},{4,0},{8,12},{12,8},{16,20},{20,16},{24,28},{28,24},{1,5},{5... | collective-permute-start | bytes 786440 | tf_op jit(solution)/shard_map/sum_core_second/ppermute | solution.py:18
  3.7 3.5 %collective-permute-start.5 = (f32[8,32,256]{2,1,0:T(8,128)S(1)}, f32[8,32,256]{2,1,0:T(8,128)S(1)}, u32[]{:S(2)}, u32[]{:S(2)}) collective-permute-start(f32[8,32,256]{2,1,0:T(8,128)S(1)} %get-tuple-element.61), channel_id=1, source_target_pairs={{0,4},{4,0},{8,12},{12,8},{16,20},{20,16},{24,28},{28,24},{1,5},{5... | collective-permute-start | bytes 786440 | tf_op jit(solution)/shard_map/sum_core_first/ppermute | solution.py:18
  4.2 3.1 %collective-permute-start.1 = (f32[8,32,256]{2,1,0:T(8,128)S(1)}, f32[8,32,256]{2,1,0:T(8,128)S(1)}, u32[]{:S(2)}, u32[]{:S(2)}) collective-permute-start(f32[8,32,256]{2,1,0:T(8,128)S(1)} %get-tuple-element.62), channel_id=1, source_target_pairs={{0,4},{4,0},{8,12},{12,8},{16,20},{20,16},{24,28},{28,24},{1,5},{5... | collective-permute-start | bytes 786440 | tf_op jit(solution)/shard_map/sum_core_own/ppermute | solution.py:18
  4.3 5.9 %collective-permute-start.9 = (f32[8,16,256]{2,1,0:T(8,128)S(1)}, f32[8,16,256]{2,1,0:T(8,128)S(1)}, u32[]{:S(2)}, u32[]{:S(2)}) collective-permute-start(f32[8,16,256]{2,1,0:T(8,128)S(1)} %get-tuple-element.45), channel_id=1, source_target_pairs={{0,8},{4,20},{8,0},{12,28},{16,24},{20,4},{24,16},{28,12},{1,9},{5... | collective-permute-start | bytes 393224 | tf_op jit(solution)/shard_map/sum_across_far/ppermute | solution.py:18
  7.5 6.5 %collective-permute-start.8 = (f32[8,16,256]{2,1,0:T(8,128)S(1)}, f32[8,16,256]{2,1,0:T(8,128)S(1)}, u32[]{:S(2)}, u32[]{:S(2)}) collective-permute-start(f32[8,16,256]{2,1,0:T(8,128)S(1)} %get-tuple-element.43), channel_id=1, source_target_pairs={{0,8},{4,20},{8,0},{12,28},{16,24},{20,4},{24,16},{28,12},{1,9},{5... | collective-permute-start | bytes 393224 | tf_op jit(solution)/shard_map/sum_first_far/ppermute | solution.py:18
  8.8 6.5 %collective-permute-start.3 = (f32[8,16,256]{2,1,0:T(8,128)S(1)}, f32[8,16,256]{2,1,0:T(8,128)S(1)}, u32[]{:S(2)}, u32[]{:S(2)}) collective-permute-start(f32[8,16,256]{2,1,0:T(8,128)S(1)} %get-tuple-element.38), channel_id=1, source_target_pairs={{0,8},{4,20},{8,0},{12,28},{16,24},{20,4},{24,16},{28,12},{1,9},{5... | collective-permute-start | bytes 393224 | tf_op jit(solution)/shard_map/sum_across_near/ppermute | solution.py:18
  10.3 6.4 %collective-permute-start.10 = (f32[8,16,256]{2,1,0:T(8,128)S(1)}, f32[8,16,256]{2,1,0:T(8,128)S(1)}, u32[]{:S(2)}, u32[]{:S(2)}) collective-permute-start(f32[8,16,256]{2,1,0:T(8,128)S(1)} %add.173), channel_id=1, source_target_pairs={{0,16},{4,12},{8,24},{12,4},{16,0},{20,28},{24,8},{28,20},{1,17},{... | collective-permute-start | bytes 393224 | tf_op jit(solution)/shard_map/sum_relay_far/ppermute | solution.py:18
  12.4 8.5 %collective-permute-start.6 = (f32[8,16,256]{2,1,0:T(8,128)S(1)}, f32[8,16,256]{2,1,0:T(8,128)S(1)}, u32[]{:S(2)}, u32[]{:S(2)}) collective-permute-start(f32[8,16,256]{2,1,0:T(8,128)S(1)} %get-tuple-element.39), channel_id=1, source_target_pairs={{0,8},{4,20},{8,0},{12,28},{16,24},{20,4},{24,16},{28,12},{1,9},{5... | collective-permute-start | bytes 393224 | tf_op jit(solution)/shard_map/sum_first_near/ppermute | solution.py:18
  15.3 25.1 %copy-start.4 = (f32[1,1,1,256,256]{4,3,2,1,0:T(8,128)S(1)}, f32[1,1,1,256,256]{4,3,2,1,0:T(8,128)}, u32[]{:S(2)}) copy-start(f32[1,1,1,256,256]{4,3,2,1,0:T(8,128)} %param.9) | copy-start | bytes 786436
  15.3 5.5 %collective-permute-start.4 = (f32[8,16,256]{2,1,0:T(8,128)S(1)}, f32[8,16,256]{2,1,0:T(8,128)S(1)}, u32[]{:S(2)}, u32[]{:S(2)}) collective-permute-start(f32[8,16,256]{2,1,0:T(8,128)S(1)} %add.166), channel_id=1, source_target_pairs={{0,16},{4,12},{8,24},{12,4},{16,0},{20,28},{24,8},{28,20},{1,17},{... | collective-permute-start | bytes 393224 | tf_op jit(solution)/shard_map/sum_relay_near/ppermute | solution.py:18
  16.7 7.1 %collective-permute-start.12 = (f32[8,8,256]{2,1,0:T(8,128)S(1)}, f32[8,8,256]{2,1,0:T(8,128)S(1)}, u32[]{:S(2)}, u32[]{:S(2)}) collective-permute-start(f32[8,8,256]{2,1,0:T(8,128)S(1)} %get-tuple-element.82), channel_id=1, source_target_pairs={{0,2},{1,3},{2,0},{3,1},{4,6},{5,7},{6,4},{7,5},{8,10},{9,11},{10,... | collective-permute-start | bytes 196616 | tf_op jit(solution)/shard_map/shard_2/ppermute | solution.py:18
  19.5 6.2 %collective-permute-start.11 = (f32[8,8,256]{2,1,0:T(8,128)S(1)}, f32[8,8,256]{2,1,0:T(8,128)S(1)}, u32[]{:S(2)}, u32[]{:S(2)}) collective-permute-start(f32[8,8,256]{2,1,0:T(8,128)S(1)} %get-tuple-element.81), channel_id=1, source_target_pairs={{0,3},{1,2},{2,1},{3,0},{4,7},{5,6},{6,5},{7,4},{8,11},{9,10},{10,... | collective-permute-start | bytes 196616 | tf_op jit(solution)/shard_map/shard_3/ppermute | solution.py:18
  20.9 19.9 %copy-start.5 = (f32[1,1,1,256,256]{4,3,2,1,0:T(8,128)S(1)}, f32[1,1,1,256,256]{4,3,2,1,0:T(8,128)}, u32[]{:S(2)}) copy-start(f32[1,1,1,256,256]{4,3,2,1,0:T(8,128)} %param.11) | copy-start | bytes 786436
  20.9 19.9 %copy-start.6 = (f32[1,1,1,256,256]{4,3,2,1,0:T(8,128)S(1)}, f32[1,1,1,256,256]{4,3,2,1,0:T(8,128)}, u32[]{:S(2)}) copy-start(f32[1,1,1,256,256]{4,3,2,1,0:T(8,128)} %param.12) | copy-start | bytes 786436
  21.0 5.0 %collective-permute-start.7 = (f32[8,8,256]{2,1,0:T(8,128)S(1)}, f32[8,8,256]{2,1,0:T(8,128)S(1)}, u32[]{:S(2)}, u32[]{:S(2)}) collective-permute-start(f32[8,8,256]{2,1,0:T(8,128)S(1)} %get-tuple-element.80), channel_id=1, source_target_pairs={{0,1},{1,0},{2,3},{3,2},{4,5},{5,4},{6,7},{7,6},{8,9},{9,8},{10,11... | collective-permute-start | bytes 196616 | tf_op jit(solution)/shard_map/shard_1/ppermute | solution.py:18
  41.6 18.2 %copy-start.2 = (f32[8,32,256]{2,1,0:T(8,128)S(1)}, f32[8,32,256]{2,1,0:T(8,128)}, u32[]{:S(2)}) copy-start(f32[8,32,256]{2,1,0:T(8,128)} %param.8) | copy-start | bytes 786436
  41.6 20.4 %copy-start.1 = (f32[8,32,256]{2,1,0:T(8,128)S(1)}, f32[8,32,256]{2,1,0:T(8,128)}, u32[]{:S(2)}) copy-start(f32[8,32,256]{2,1,0:T(8,128)} %param.8) | copy-start | bytes 786436
  55.1 6.9 %collective-permute-start.13 = (f32[8,8,256]{2,1,0:T(8,128)S(1)}, f32[8,8,256]{2,1,0:T(8,128)S(1)}, u32[]{:S(2)}, u32[]{:S(2)}) collective-permute-start(f32[8,8,256]{2,1,0:T(8,128)S(1)} %copy.57), channel_id=1, source_target_pairs={{0,3},{1,2},{2,1},{3,0},{4,7},{5,6},{6,5},{7,4},{8,11},{9,10},{10,... | collective-permute-start | bytes 196616 | tf_op jit(solution)/shard_map/shard_3/ppermute | solution.py:18
  57.0 7.2 %collective-permute-start.14 = (f32[8,8,256]{2,1,0:T(8,128)S(1)}, f32[8,8,256]{2,1,0:T(8,128)S(1)}, u32[]{:S(2)}, u32[]{:S(2)}) collective-permute-start(f32[8,8,256]{2,1,0:T(8,128)S(1)} %copy.58), channel_id=1, source_target_pairs={{0,2},{1,3},{2,0},{3,1},{4,6},{5,7},{6,4},{7,5},{8,10},{9,11},{10,... | collective-permute-start | bytes 196616 | tf_op jit(solution)/shard_map/shard_2/ppermute | solution.py:18
  57.9 6.4 %collective-permute-start.15 = (f32[8,8,256]{2,1,0:T(8,128)S(1)}, f32[8,8,256]{2,1,0:T(8,128)S(1)}, u32[]{:S(2)}, u32[]{:S(2)}) collective-permute-start(f32[8,8,256]{2,1,0:T(8,128)S(1)} %copy.59), channel_id=1, source_target_pairs={{0,1},{1,0},{2,3},{3,2},{4,5},{5,4},{6,7},{7,6},{8,9},{9,8},{10,11... | collective-permute-start | bytes 196616 | tf_op jit(solution)/shard_map/shard_1/ppermute | solution.py:18
  64.3 6.1 %collective-permute-start.18 = (f32[4,32,256]{2,1,0:T(8,128)S(1)}, f32[4,32,256]{2,1,0:T(8,128)S(1)}, u32[]{:S(2)}, u32[]{:S(2)}) collective-permute-start(f32[4,32,256]{2,1,0:T(8,128)S(1)} %get-tuple-element.64), channel_id=1, source_target_pairs={{0,8},{4,20},{8,0},{12,28},{16,24},{20,4},{24,16},{28,12},{1,9},{5... | collective-permute-start | bytes 393224 | tf_op jit(solution)/shard_map/rows_first_top/ppermute | solution.py:18
  65.2 6.1 %collective-permute-start.20 = (f32[4,32,256]{2,1,0:T(8,128)S(1)}, f32[4,32,256]{2,1,0:T(8,128)S(1)}, u32[]{:S(2)}, u32[]{:S(2)}) collective-permute-start(f32[4,32,256]{2,1,0:T(8,128)S(1)} %get-tuple-element.63), channel_id=1, source_target_pairs={{0,16},{4,12},{8,24},{12,4},{16,0},{20,28},{24,8},{28,20},{1,17},{... | collective-permute-start | bytes 393224 | tf_op jit(solution)/shard_map/rows_second_low/ppermute | solution.py:18
  65.8 7.3 %collective-permute-start.17 = (f32[4,32,256]{2,1,0:T(8,128)S(1)}, f32[4,32,256]{2,1,0:T(8,128)S(1)}, u32[]{:S(2)}, u32[]{:S(2)}) collective-permute-start(f32[4,32,256]{2,1,0:T(8,128)S(1)} %get-tuple-element.63), channel_id=1, source_target_pairs={{0,8},{4,20},{8,0},{12,28},{16,24},{20,4},{24,16},{28,12},{1,9},{5... | collective-permute-start | bytes 393224 | tf_op jit(solution)/shard_map/rows_first_low/ppermute | solution.py:18
  67.3 5.9 %collective-permute-start.16 = (f32[8,32,256]{2,1,0:T(8,128)S(1)}, f32[8,32,256]{2,1,0:T(8,128)S(1)}, u32[]{:S(2)}, u32[]{:S(2)}) collective-permute-start(f32[8,32,256]{2,1,0:T(8,128)S(1)} %subtract_dynamic-update-slice_fusion), channel_id=1, source_target_pairs={{0,4},{4,0},{8,12},{12,8},{16,20},{20,16},{24,28},{28,24},{1,5},{5... | collective-permute-start | bytes 786440 | tf_op jit(solution)/shard_map/rows_core_own/ppermute | solution.py:18
  67.3 5.8 %collective-permute-start.19 = (f32[4,32,256]{2,1,0:T(8,128)S(1)}, f32[4,32,256]{2,1,0:T(8,128)S(1)}, u32[]{:S(2)}, u32[]{:S(2)}) collective-permute-start(f32[4,32,256]{2,1,0:T(8,128)S(1)} %get-tuple-element.64), channel_id=1, source_target_pairs={{0,16},{4,12},{8,24},{12,4},{16,0},{20,28},{24,8},{28,20},{1,17},{... | collective-permute-start | bytes 393224 | tf_op jit(solution)/shard_map/rows_second_top/ppermute | solution.py:18
  70.4 5.2 %collective-permute-start.21 = (f32[4,32,256]{2,1,0:T(8,128)S(1)}, f32[4,32,256]{2,1,0:T(8,128)S(1)}, u32[]{:S(2)}, u32[]{:S(2)}) collective-permute-start(f32[4,32,256]{2,1,0:T(8,128)S(1)} %collective-permute-done.18), channel_id=1, source_target_pairs={{0,16},{4,12},{8,24},{12,4},{16,0},{20,28},{24,8},{28,20},{1,17},{... | collective-permute-start | bytes 393224 | tf_op jit(solution)/shard_map/rows_relay_top/ppermute | solution.py:18
  71.3 5.0 %collective-permute-start.24 = (f32[4,32,256]{2,1,0:T(8,128)S(1)}, f32[4,32,256]{2,1,0:T(8,128)S(1)}, u32[]{:S(2)}, u32[]{:S(2)}) collective-permute-start(f32[4,32,256]{2,1,0:T(8,128)S(1)} %collective-permute-done.20), channel_id=1, source_target_pairs={{0,8},{4,20},{8,0},{12,28},{16,24},{20,4},{24,16},{28,12},{1,9},{5... | collective-permute-start | bytes 393224 | tf_op jit(solution)/shard_map/rows_relay_low/ppermute | solution.py:18
  75.6 1.5 %collective-permute-start.22 = (f32[8,32,256]{2,1,0:T(8,128)S(1)}, f32[8,32,256]{2,1,0:T(8,128)S(1)}, u32[]{:S(2)}, u32[]{:S(2)}) collective-permute-start(f32[8,32,256]{2,1,0:T(8,128)S(1)} %pad_maximum_fusion.1), channel_id=1, source_target_pairs={{0,4},{4,0},{8,12},{12,8},{16,20},{20,16},{24,28},{28,24},{1,5},{5... | collective-permute-start | bytes 786440 | tf_op jit(solution)/shard_map/rows_core_first/ppermute | solution.py:18
  75.6 1.9 %collective-permute-start.23 = (f32[8,32,256]{2,1,0:T(8,128)S(1)}, f32[8,32,256]{2,1,0:T(8,128)S(1)}, u32[]{:S(2)}, u32[]{:S(2)}) collective-permute-start(f32[8,32,256]{2,1,0:T(8,128)S(1)} %pad_maximum_fusion.2), channel_id=1, source_target_pairs={{0,4},{4,0},{8,12},{12,8},{16,20},{20,16},{24,28},{28,24},{1,5},{5... | collective-permute-start | bytes 786440 | tf_op jit(solution)/shard_map/rows_core_second/ppermute | solution.py:18
  76.3 1.6 %collective-permute-start.25 = (f32[8,32,256]{2,1,0:T(8,128)S(1)}, f32[8,32,256]{2,1,0:T(8,128)S(1)}, u32[]{:S(2)}, u32[]{:S(2)}) collective-permute-start(f32[8,32,256]{2,1,0:T(8,128)S(1)} %constant_dynamic-update-slice_fusion.6), channel_id=1, source_target_pairs={{0,4},{4,0},{8,12},{12,8},{16,20},{20,16},{24,28},{28,24},{1,5},{5... | collective-permute-start | bytes 786440 | tf_op jit(solution)/shard_map/rows_core_far/ppermute | solution.py:18
  (4 other events, 43.5 us)

commit v9 on v8

--- a/solution.py
+++ b/solution.py
@@ -100,15 +100,12 @@
         return take(split, 1, index)
 
     grid = partials[0].reshape((home_count, chips, 2, row_count, width))
-
-    def rows_of(values, mask):
-        return take(values, 1, (data_here ^ mask) // 2).astype(jnp.float32)
-
-    away = {"across": rows_of(take(grid, 2, 1 - my_core), across)}
-    grid, away["across"] = lax.optimization_barrier((grid, away["across"]))
     away_rows = take(grid, 2, 1 - my_core)
     own_rows = take(grid, 2, my_core)
     away_rows, own_rows = lax.optimization_barrier((away_rows, own_rows))
+
+    def rows_of(values, mask):
+        return take(values, 1, (data_here ^ mask) // 2).astype(jnp.float32)
 
     near, far = {}, {}
     for name, mask, other_mask in (
@@ -117,9 +114,9 @@
         ("second", second_chip, first_chip),
         ("own", 0, 0),
     ):
-        if name != "across":
-            away[name] = rows_of(away_rows, other_mask)
-        total = rows_of(own_rows, mask) + swap(away[name], "dp", core, f"sum_core_{name}")
+        total = rows_of(own_rows, mask) + swap(
+            rows_of(away_rows, other_mask), "dp", core, f"sum_core_{name}"
+        )
         near[name], far[name] = lax.optimization_barrier(
             (set_of(total, shard_half), set_of(total, 1 - shard_half))
         )

time: 79.5 us -> 78.9 us (level)
  other arithmetic: 1.53 us -> 0.62 us
    convert_element_type x2 -> x1, other arithmetic: 1.05 us -> 0.12 us  [rows_of(): return take(values, 1, (data_here ^ mask) // 2).astype(jnp.float32)]
  transfers between devices with their start and end apart: 26 -> 26, of which waited for: 14 -> 15; matrix products, arithmetic and copies ran while one was open for 3% -> 2% of each run, Pallas kernels for 0% -> 0%
where the time goes in v9:
time: 78.9 us; the launch traced here: 78.7 us
  starting transfers between devices  27.2 us (34%)
  blocking collectives  26.5 us (34%)
  waiting for transfers between devices  17.4 us (22%)
  local copies, waits for them, and re-layouts  3.76 us (5%)
  matrix products  1.93 us (2%)
  between operations  1.28 us (2%)
    ppermute x26, starting transfers between devices, swap(): return lax.ppermute(values, name, pairs)  27.2 us
    ppermute x26, waiting for transfers between devices, swap(): return lax.ppermute(values, name, pairs)  17.4 us
    all_to_all x1, blocking collectives, routed(): lax.all_to_all(leaving.reshape((device_total,) + piece), ('dp', 'shard'),...  13.7 us
    all_to_all x1, blocking collectives, routed(): lax.all_to_all(change.reshape((device_total,) + piece), ('dp', 'shard'),...  12.7 us
  transfers between devices with their start and end apart: 26, of which 15 were waited for; matrix products, arithmetic and copies ran while one was open for 2% of the time, Pallas kernels for 0%

profile of v9, /device:TPU:0, one launch (start us, length us, event | category | flops | bytes accessed | tf_op | source)
XLA Modules:
  0.0 78.7 jit_solution(13322813654987720864)
XLA Ops:
  0.7 1.3 %dynamic-slice_bitcast_fusion = (bf16[8,4,32,256]{3,2,1,0:T(8,128)(2,1)S(1)}, bf16[8,4,32,256]{3,2,1,0:T(8,128)(2,1)S(1)}) fusion(bf16[8,4,2,32,256]{4,3,2,1,0:T(8,128)(2,1)} %bitcast.130, s32[]{:T(128)S(6)} %select_n.130, s32[]{:T(128)S(6)} %select_n.129), kind=kLoop, calls=%fused_computation.1 | loop fusion | bytes 2097160 | tf_op jit(solution)/shard_map/jit(dynamic_index_in_dim)/squeeze | solution.py:22
  3.3 0.6 collective-permute-done
  4.0 2.9 %collective-permute-start.9 = (f32[8,16,256]{2,1,0:T(8,128)S(1)}, f32[8,16,256]{2,1,0:T(8,128)S(1)}, u32[]{:S(2)}, u32[]{:S(2)}) collective-permute-start(f32[8,16,256]{2,1,0:T(8,128)S(1)} %get-tuple-element.41), channel_id=1, source_target_pairs={{0,8},{4,20},{8,0},{12,28},{16,24},{20,4},{24,16},{28,12},{1,9},{5... | collective-permute-start | bytes 393224 | tf_op jit(solution)/shard_map/sum_across_far/ppermute | solution.py:18
  7.1 1.0 %collective-permute-start.8 = (f32[8,16,256]{2,1,0:T(8,128)S(1)}, f32[8,16,256]{2,1,0:T(8,128)S(1)}, u32[]{:S(2)}, u32[]{:S(2)}) collective-permute-start(f32[8,16,256]{2,1,0:T(8,128)S(1)} %get-tuple-element.39), channel_id=1, source_target_pairs={{0,8},{4,20},{8,0},{12,28},{16,24},{20,4},{24,16},{28,12},{1,9},{5... | collective-permute-start | bytes 393224 | tf_op jit(solution)/shard_map/sum_first_far/ppermute | solution.py:18
  8.1 1.1 %collective-permute-start.3 = (f32[8,16,256]{2,1,0:T(8,128)S(1)}, f32[8,16,256]{2,1,0:T(8,128)S(1)}, u32[]{:S(2)}, u32[]{:S(2)}) collective-permute-start(f32[8,16,256]{2,1,0:T(8,128)S(1)} %get-tuple-element.34), channel_id=1, source_target_pairs={{0,8},{4,20},{8,0},{12,28},{16,24},{20,4},{24,16},{28,12},{1,9},{5... | collective-permute-start | bytes 393224 | tf_op jit(solution)/shard_map/sum_across_near/ppermute | solution.py:18
  9.2 0.6 collective-permute-done.9
  9.8 2.1 %collective-permute-start.10 = (f32[8,16,256]{2,1,0:T(8,128)S(1)}, f32[8,16,256]{2,1,0:T(8,128)S(1)}, u32[]{:S(2)}, u32[]{:S(2)}) collective-permute-start(f32[8,16,256]{2,1,0:T(8,128)S(1)} %add.167), channel_id=1, source_target_pairs={{0,16},{4,12},{8,24},{12,4},{16,0},{20,28},{24,8},{28,20},{1,17},{... | collective-permute-start | bytes 393224 | tf_op jit(solution)/shard_map/sum_relay_far/ppermute | solution.py:18
  12.0 1.6 %collective-permute-start.6 = (f32[8,16,256]{2,1,0:T(8,128)S(1)}, f32[8,16,256]{2,1,0:T(8,128)S(1)}, u32[]{:S(2)}, u32[]{:S(2)}) collective-permute-start(f32[8,16,256]{2,1,0:T(8,128)S(1)} %get-tuple-element.35), channel_id=1, source_target_pairs={{0,8},{4,20},{8,0},{12,28},{16,24},{20,4},{24,16},{28,12},{1,9},{5... | collective-permute-start | bytes 393224 | tf_op jit(solution)/shard_map/sum_first_near/ppermute | solution.py:18
  13.6 1.3 %collective-permute-done.3 = f32[8,16,256]{2,1,0:T(8,128)S(1)} collective-permute-done((f32[8,16,256]{2,1,0:T(8,128)S(1)}, f32[8,16,256]{2,1,0:T(8,128)S(1)}, u32[]{:S(2)}, u32[]{:S(2)}) %collective-permute-start.3) | collective-permute-done | bytes 131104 | tf_op jit(solution)/shard_map/sum_across_near/ppermute | solution.py:18
  14.9 1.3 %collective-permute-start.4 = (f32[8,16,256]{2,1,0:T(8,128)S(1)}, f32[8,16,256]{2,1,0:T(8,128)S(1)}, u32[]{:S(2)}, u32[]{:S(2)}) collective-permute-start(f32[8,16,256]{2,1,0:T(8,128)S(1)} %add.160), channel_id=1, source_target_pairs={{0,16},{4,12},{8,24},{12,4},{16,0},{20,28},{24,8},{28,20},{1,17},{... | collective-permute-start | bytes 393224 | tf_op jit(solution)/shard_map/sum_relay_near/ppermute | solution.py:18
  16.3 2.8 %collective-permute-start.12 = (f32[8,8,256]{2,1,0:T(8,128)S(1)}, f32[8,8,256]{2,1,0:T(8,128)S(1)}, u32[]{:S(2)}, u32[]{:S(2)}) collective-permute-start(f32[8,8,256]{2,1,0:T(8,128)S(1)} %get-tuple-element.79), channel_id=1, source_target_pairs={{0,2},{1,3},{2,0},{3,1},{4,6},{5,7},{6,4},{7,5},{8,10},{9,11},{10,... | collective-permute-start | bytes 196616 | tf_op jit(solution)/shard_map/shard_2/ppermute | solution.py:18
  19.1 1.3 %collective-permute-start.11 = (f32[8,8,256]{2,1,0:T(8,128)S(1)}, f32[8,8,256]{2,1,0:T(8,128)S(1)}, u32[]{:S(2)}, u32[]{:S(2)}) collective-permute-start(f32[8,8,256]{2,1,0:T(8,128)S(1)} %get-tuple-element.78), channel_id=1, source_target_pairs={{0,3},{1,2},{2,1},{3,0},{4,7},{5,6},{6,5},{7,4},{8,11},{9,10},{10,... | collective-permute-start | bytes 196616 | tf_op jit(solution)/shard_map/shard_3/ppermute | solution.py:18
  20.6 0.9 %collective-permute-start.7 = (f32[8,8,256]{2,1,0:T(8,128)S(1)}, f32[8,8,256]{2,1,0:T(8,128)S(1)}, u32[]{:S(2)}, u32[]{:S(2)}) collective-permute-start(f32[8,8,256]{2,1,0:T(8,128)S(1)} %get-tuple-element.77), channel_id=1, source_target_pairs={{0,1},{1,0},{2,3},{3,2},{4,5},{5,4},{6,7},{7,6},{8,9},{9,8},{10,11... | collective-permute-start | bytes 196616 | tf_op jit(solution)/shard_map/shard_1/ppermute | solution.py:18
  21.7 1.7 %collective-permute-done.12 = f32[8,8,256]{2,1,0:T(8,128)S(1)} collective-permute-done((f32[8,8,256]{2,1,0:T(8,128)S(1)}, f32[8,8,256]{2,1,0:T(8,128)S(1)}, u32[]{:S(2)}, u32[]{:S(2)}) %collective-permute-start.12) | collective-permute-done | bytes 65568 | tf_op jit(solution)/shard_map/shard_2/ppermute | solution.py:18
  23.5 1.8 %collective-permute-done.11 = f32[8,8,256]{2,1,0:T(8,128)S(1)} collective-permute-done((f32[8,8,256]{2,1,0:T(8,128)S(1)}, f32[8,8,256]{2,1,0:T(8,128)S(1)}, u32[]{:S(2)}, u32[]{:S(2)}) %collective-permute-start.11) | collective-permute-done | bytes 65568 | tf_op jit(solution)/shard_map/shard_3/ppermute | solution.py:18
  26.1 13.7 %all_to_all.10 = f32[32,8,256]{2,1,0:T(8,128)S(1)} all-to-all(f32[32,8,256]{2,1,0:T(8,128)S(1)} %copy.56), channel_id=1, replica_groups=mesh['dp'=8,'shard'=4] {'dp','shard'}, dimensions={0} | all-to-all | bytes 524288 | tf_op jit(solution)/shard_map/all_to_all | solution.py:153
  41.3 12.7 %all_to_all.11 = f32[32,8,256]{2,1,0:T(8,128)S(1)} all-to-all(f32[32,8,256]{2,1,0:T(8,128)S(1)} %convolution_bitcast_fusion), channel_id=1, replica_groups=mesh['dp'=8,'shard'=4] {'dp','shard'}, dimensions={0} | all-to-all | bytes 524288 | tf_op jit(solution)/shard_map/all_to_all | solution.py:170
  54.5 1.8 %collective-permute-start.13 = (f32[8,8,256]{2,1,0:T(8,128)S(1)}, f32[8,8,256]{2,1,0:T(8,128)S(1)}, u32[]{:S(2)}, u32[]{:S(2)}) collective-permute-start(f32[8,8,256]{2,1,0:T(8,128)S(1)} %copy.58), channel_id=1, source_target_pairs={{0,3},{1,2},{2,1},{3,0},{4,7},{5,6},{6,5},{7,4},{8,11},{9,10},{10,... | collective-permute-start | bytes 196616 | tf_op jit(solution)/shard_map/shard_3/ppermute | solution.py:18
  56.4 0.9 %collective-permute-start.14 = (f32[8,8,256]{2,1,0:T(8,128)S(1)}, f32[8,8,256]{2,1,0:T(8,128)S(1)}, u32[]{:S(2)}, u32[]{:S(2)}) collective-permute-start(f32[8,8,256]{2,1,0:T(8,128)S(1)} %copy.59), channel_id=1, source_target_pairs={{0,2},{1,3},{2,0},{3,1},{4,6},{5,7},{6,4},{7,5},{8,10},{9,11},{10,... | collective-permute-start | bytes 196616 | tf_op jit(solution)/shard_map/shard_2/ppermute | solution.py:18
  57.3 1.9 %collective-permute-start.15 = (f32[8,8,256]{2,1,0:T(8,128)S(1)}, f32[8,8,256]{2,1,0:T(8,128)S(1)}, u32[]{:S(2)}, u32[]{:S(2)}) collective-permute-start(f32[8,8,256]{2,1,0:T(8,128)S(1)} %copy.60), channel_id=1, source_target_pairs={{0,1},{1,0},{2,3},{3,2},{4,5},{5,4},{6,7},{7,6},{8,9},{9,8},{10,11... | collective-permute-start | bytes 196616 | tf_op jit(solution)/shard_map/shard_1/ppermute | solution.py:18
  59.2 2.2 %collective-permute-done.13 = f32[8,8,256]{2,1,0:T(8,128)S(1)} collective-permute-done((f32[8,8,256]{2,1,0:T(8,128)S(1)}, f32[8,8,256]{2,1,0:T(8,128)S(1)}, u32[]{:S(2)}, u32[]{:S(2)}) %collective-permute-start.13) | collective-permute-done | bytes 65568 | tf_op jit(solution)/shard_map/shard_3/ppermute | solution.py:18
  61.4 2.2 %collective-permute-done.14 = f32[8,8,256]{2,1,0:T(8,128)S(1)} collective-permute-done((f32[8,8,256]{2,1,0:T(8,128)S(1)}, f32[8,8,256]{2,1,0:T(8,128)S(1)}, u32[]{:S(2)}, u32[]{:S(2)}) %collective-permute-start.14) | collective-permute-done | bytes 65568 | tf_op jit(solution)/shard_map/shard_2/ppermute | solution.py:18
  63.7 0.9 %collective-permute-start.18 = (f32[4,32,256]{2,1,0:T(8,128)S(1)}, f32[4,32,256]{2,1,0:T(8,128)S(1)}, u32[]{:S(2)}, u32[]{:S(2)}) collective-permute-start(f32[4,32,256]{2,1,0:T(8,128)S(1)} %get-tuple-element.61), channel_id=1, source_target_pairs={{0,8},{4,20},{8,0},{12,28},{16,24},{20,4},{24,16},{28,12},{1,9},{5... | collective-permute-start | bytes 393224 | tf_op jit(solution)/shard_map/rows_first_top/ppermute | solution.py:18
  65.2 1.5 %collective-permute-start.17 = (f32[4,32,256]{2,1,0:T(8,128)S(1)}, f32[4,32,256]{2,1,0:T(8,128)S(1)}, u32[]{:S(2)}, u32[]{:S(2)}) collective-permute-start(f32[4,32,256]{2,1,0:T(8,128)S(1)} %get-tuple-element.60), channel_id=1, source_target_pairs={{0,8},{4,20},{8,0},{12,28},{16,24},{20,4},{24,16},{28,12},{1,9},{5... | collective-permute-start | bytes 393224 | tf_op jit(solution)/shard_map/rows_first_low/ppermute | solution.py:18
  66.7 1.1 %collective-permute-start.19 = (f32[4,32,256]{2,1,0:T(8,128)S(1)}, f32[4,32,256]{2,1,0:T(8,128)S(1)}, u32[]{:S(2)}, u32[]{:S(2)}) collective-permute-start(f32[4,32,256]{2,1,0:T(8,128)S(1)} %get-tuple-element.61), channel_id=1, source_target_pairs={{0,16},{4,12},{8,24},{12,4},{16,0},{20,28},{24,8},{28,20},{1,17},{... | collective-permute-start | bytes 393224 | tf_op jit(solution)/shard_map/rows_second_top/ppermute | solution.py:18
  68.0 1.8 %collective-permute-done.18 = f32[4,32,256]{2,1,0:T(8,128)S(1)} collective-permute-done((f32[4,32,256]{2,1,0:T(8,128)S(1)}, f32[4,32,256]{2,1,0:T(8,128)S(1)}, u32[]{:S(2)}, u32[]{:S(2)}) %collective-permute-start.18) | collective-permute-done | bytes 131104 | tf_op jit(solution)/shard_map/rows_first_top/ppermute | solution.py:18
  69.8 0.9 %collective-permute-start.21 = (f32[4,32,256]{2,1,0:T(8,128)S(1)}, f32[4,32,256]{2,1,0:T(8,128)S(1)}, u32[]{:S(2)}, u32[]{:S(2)}) collective-permute-start(f32[4,32,256]{2,1,0:T(8,128)S(1)} %collective-permute-done.18), channel_id=1, source_target_pairs={{0,16},{4,12},{8,24},{12,4},{16,0},{20,28},{24,8},{28,20},{1,17},{... | collective-permute-start | bytes 393224 | tf_op jit(solution)/shard_map/rows_relay_top/ppermute | solution.py:18
  70.7 0.8 %collective-permute-start.24 = (f32[4,32,256]{2,1,0:T(8,128)S(1)}, f32[4,32,256]{2,1,0:T(8,128)S(1)}, u32[]{:S(2)}, u32[]{:S(2)}) collective-permute-start(f32[4,32,256]{2,1,0:T(8,128)S(1)} %collective-permute-done.20), channel_id=1, source_target_pairs={{0,8},{4,20},{8,0},{12,28},{16,24},{20,4},{24,16},{28,12},{1,9},{5... | collective-permute-start | bytes 393224 | tf_op jit(solution)/shard_map/rows_relay_low/ppermute | solution.py:18
  71.5 1.0 %collective-permute-done.17 = f32[4,32,256]{2,1,0:T(8,128)S(1)} collective-permute-done((f32[4,32,256]{2,1,0:T(8,128)S(1)}, f32[4,32,256]{2,1,0:T(8,128)S(1)}, u32[]{:S(2)}, u32[]{:S(2)}) %collective-permute-start.17) | collective-permute-done | bytes 131104 | tf_op jit(solution)/shard_map/rows_first_low/ppermute | solution.py:18
  72.6 2.3 %collective-permute-done.21 = f32[4,32,256]{2,1,0:T(8,128)S(1)} collective-permute-done((f32[4,32,256]{2,1,0:T(8,128)S(1)}, f32[4,32,256]{2,1,0:T(8,128)S(1)}, u32[]{:S(2)}, u32[]{:S(2)}) %collective-permute-start.21) | collective-permute-done | bytes 131104 | tf_op jit(solution)/shard_map/rows_relay_top/ppermute | solution.py:18
  75.9 0.6 collective-permute-done.22
  77.4 1.3 %copy-done.3 = f32[8,256,256]{2,1,0:T(8,128)} copy-done((f32[8,256,256]{2,1,0:T(8,128)}, f32[8,256,256]{2,1,0:T(8,128)S(1)}, u32[]{:S(2)}) %copy-start.3) | copy-done | bytes 2097176
  (100 shorter events, 7.2 us)
Async XLA Ops:
  0.6 39.6 %copy-start = (f32[1,1,1,256,256]{4,3,2,1,0:T(8,128)S(1)}, f32[1,1,1,256,256]{4,3,2,1,0:T(8,128)}, u32[]{:S(2)}) copy-start(f32[1,1,1,256,256]{4,3,2,1,0:T(8,128)} %param.10) | copy-start | bytes 786436
  2.2 1.7 %collective-permute-start = (f32[8,32,256]{2,1,0:T(8,128)S(1)}, f32[8,32,256]{2,1,0:T(8,128)S(1)}, u32[]{:S(2)}, u32[]{:S(2)}) collective-permute-start(f32[8,32,256]{2,1,0:T(8,128)S(1)} %get-tuple-element.59), channel_id=1, source_target_pairs={{0,4},{4,0},{8,12},{12,8},{16,20},{20,16},{24,28},{28,24},{1,5},{5... | collective-permute-start | bytes 786440 | tf_op jit(solution)/shard_map/sum_core_across/ppermute | solution.py:18
  2.7 4.2 %collective-permute-start.2 = (f32[8,32,256]{2,1,0:T(8,128)S(1)}, f32[8,32,256]{2,1,0:T(8,128)S(1)}, u32[]{:S(2)}, u32[]{:S(2)}) collective-permute-start(f32[8,32,256]{2,1,0:T(8,128)S(1)} %get-tuple-element.56), channel_id=1, source_target_pairs={{0,4},{4,0},{8,12},{12,8},{16,20},{20,16},{24,28},{28,24},{1,5},{5... | collective-permute-start | bytes 786440 | tf_op jit(solution)/shard_map/sum_core_second/ppermute | solution.py:18
  2.8 4.1 %collective-permute-start.5 = (f32[8,32,256]{2,1,0:T(8,128)S(1)}, f32[8,32,256]{2,1,0:T(8,128)S(1)}, u32[]{:S(2)}, u32[]{:S(2)}) collective-permute-start(f32[8,32,256]{2,1,0:T(8,128)S(1)} %get-tuple-element.57), channel_id=1, source_target_pairs={{0,4},{4,0},{8,12},{12,8},{16,20},{20,16},{24,28},{28,24},{1,5},{5... | collective-permute-start | bytes 786440 | tf_op jit(solution)/shard_map/sum_core_first/ppermute | solution.py:18
  3.2 3.6 %collective-permute-start.1 = (f32[8,32,256]{2,1,0:T(8,128)S(1)}, f32[8,32,256]{2,1,0:T(8,128)S(1)}, u32[]{:S(2)}, u32[]{:S(2)}) collective-permute-start(f32[8,32,256]{2,1,0:T(8,128)S(1)} %get-tuple-element.58), channel_id=1, source_target_pairs={{0,4},{4,0},{8,12},{12,8},{16,20},{20,16},{24,28},{28,24},{1,5},{5... | collective-permute-start | bytes 786440 | tf_op jit(solution)/shard_map/sum_core_own/ppermute | solution.py:18
  4.0 5.9 %collective-permute-start.9 = (f32[8,16,256]{2,1,0:T(8,128)S(1)}, f32[8,16,256]{2,1,0:T(8,128)S(1)}, u32[]{:S(2)}, u32[]{:S(2)}) collective-permute-start(f32[8,16,256]{2,1,0:T(8,128)S(1)} %get-tuple-element.41), channel_id=1, source_target_pairs={{0,8},{4,20},{8,0},{12,28},{16,24},{20,4},{24,16},{28,12},{1,9},{5... | collective-permute-start | bytes 393224 | tf_op jit(solution)/shard_map/sum_across_far/ppermute | solution.py:18
  7.1 6.5 %collective-permute-start.8 = (f32[8,16,256]{2,1,0:T(8,128)S(1)}, f32[8,16,256]{2,1,0:T(8,128)S(1)}, u32[]{:S(2)}, u32[]{:S(2)}) collective-permute-start(f32[8,16,256]{2,1,0:T(8,128)S(1)} %get-tuple-element.39), channel_id=1, source_target_pairs={{0,8},{4,20},{8,0},{12,28},{16,24},{20,4},{24,16},{28,12},{1,9},{5... | collective-permute-start | bytes 393224 | tf_op jit(solution)/shard_map/sum_first_far/ppermute | solution.py:18
  8.1 6.8 %collective-permute-start.3 = (f32[8,16,256]{2,1,0:T(8,128)S(1)}, f32[8,16,256]{2,1,0:T(8,128)S(1)}, u32[]{:S(2)}, u32[]{:S(2)}) collective-permute-start(f32[8,16,256]{2,1,0:T(8,128)S(1)} %get-tuple-element.34), channel_id=1, source_target_pairs={{0,8},{4,20},{8,0},{12,28},{16,24},{20,4},{24,16},{28,12},{1,9},{5... | collective-permute-start | bytes 393224 | tf_op jit(solution)/shard_map/sum_across_near/ppermute | solution.py:18
  9.8 6.4 %collective-permute-start.10 = (f32[8,16,256]{2,1,0:T(8,128)S(1)}, f32[8,16,256]{2,1,0:T(8,128)S(1)}, u32[]{:S(2)}, u32[]{:S(2)}) collective-permute-start(f32[8,16,256]{2,1,0:T(8,128)S(1)} %add.167), channel_id=1, source_target_pairs={{0,16},{4,12},{8,24},{12,4},{16,0},{20,28},{24,8},{28,20},{1,17},{... | collective-permute-start | bytes 393224 | tf_op jit(solution)/shard_map/sum_relay_far/ppermute | solution.py:18
  12.0 8.5 %collective-permute-start.6 = (f32[8,16,256]{2,1,0:T(8,128)S(1)}, f32[8,16,256]{2,1,0:T(8,128)S(1)}, u32[]{:S(2)}, u32[]{:S(2)}) collective-permute-start(f32[8,16,256]{2,1,0:T(8,128)S(1)} %get-tuple-element.35), channel_id=1, source_target_pairs={{0,8},{4,20},{8,0},{12,28},{16,24},{20,4},{24,16},{28,12},{1,9},{5... | collective-permute-start | bytes 393224 | tf_op jit(solution)/shard_map/sum_first_near/ppermute | solution.py:18
  14.9 24.9 %copy-start.4 = (f32[1,1,1,256,256]{4,3,2,1,0:T(8,128)S(1)}, f32[1,1,1,256,256]{4,3,2,1,0:T(8,128)}, u32[]{:S(2)}) copy-start(f32[1,1,1,256,256]{4,3,2,1,0:T(8,128)} %param.9) | copy-start | bytes 786436
  14.9 5.6 %collective-permute-start.4 = (f32[8,16,256]{2,1,0:T(8,128)S(1)}, f32[8,16,256]{2,1,0:T(8,128)S(1)}, u32[]{:S(2)}, u32[]{:S(2)}) collective-permute-start(f32[8,16,256]{2,1,0:T(8,128)S(1)} %add.160), channel_id=1, source_target_pairs={{0,16},{4,12},{8,24},{12,4},{16,0},{20,28},{24,8},{28,20},{1,17},{... | collective-permute-start | bytes 393224 | tf_op jit(solution)/shard_map/sum_relay_near/ppermute | solution.py:18
  16.3 7.1 %collective-permute-start.12 = (f32[8,8,256]{2,1,0:T(8,128)S(1)}, f32[8,8,256]{2,1,0:T(8,128)S(1)}, u32[]{:S(2)}, u32[]{:S(2)}) collective-permute-start(f32[8,8,256]{2,1,0:T(8,128)S(1)} %get-tuple-element.79), channel_id=1, source_target_pairs={{0,2},{1,3},{2,0},{3,1},{4,6},{5,7},{6,4},{7,5},{8,10},{9,11},{10,... | collective-permute-start | bytes 196616 | tf_op jit(solution)/shard_map/shard_2/ppermute | solution.py:18
  19.1 6.2 %collective-permute-start.11 = (f32[8,8,256]{2,1,0:T(8,128)S(1)}, f32[8,8,256]{2,1,0:T(8,128)S(1)}, u32[]{:S(2)}, u32[]{:S(2)}) collective-permute-start(f32[8,8,256]{2,1,0:T(8,128)S(1)} %get-tuple-element.78), channel_id=1, source_target_pairs={{0,3},{1,2},{2,1},{3,0},{4,7},{5,6},{6,5},{7,4},{8,11},{9,10},{10,... | collective-permute-start | bytes 196616 | tf_op jit(solution)/shard_map/shard_3/ppermute | solution.py:18
  20.5 19.7 %copy-start.5 = (f32[1,1,1,256,256]{4,3,2,1,0:T(8,128)S(1)}, f32[1,1,1,256,256]{4,3,2,1,0:T(8,128)}, u32[]{:S(2)}) copy-start(f32[1,1,1,256,256]{4,3,2,1,0:T(8,128)} %param.11) | copy-start | bytes 786436
  20.5 19.7 %copy-start.6 = (f32[1,1,1,256,256]{4,3,2,1,0:T(8,128)S(1)}, f32[1,1,1,256,256]{4,3,2,1,0:T(8,128)}, u32[]{:S(2)}) copy-start(f32[1,1,1,256,256]{4,3,2,1,0:T(8,128)} %param.12) | copy-start | bytes 786436
  20.6 5.0 %collective-permute-start.7 = (f32[8,8,256]{2,1,0:T(8,128)S(1)}, f32[8,8,256]{2,1,0:T(8,128)S(1)}, u32[]{:S(2)}, u32[]{:S(2)}) collective-permute-start(f32[8,8,256]{2,1,0:T(8,128)S(1)} %get-tuple-element.77), channel_id=1, source_target_pairs={{0,1},{1,0},{2,3},{3,2},{4,5},{5,4},{6,7},{7,6},{8,9},{9,8},{10,11... | collective-permute-start | bytes 196616 | tf_op jit(solution)/shard_map/shard_1/ppermute | solution.py:18
  41.0 18.1 %copy-start.2 = (f32[8,32,256]{2,1,0:T(8,128)S(1)}, f32[8,32,256]{2,1,0:T(8,128)}, u32[]{:S(2)}) copy-start(f32[8,32,256]{2,1,0:T(8,128)} %param.8) | copy-start | bytes 786436
  41.0 20.3 %copy-start.1 = (f32[8,32,256]{2,1,0:T(8,128)S(1)}, f32[8,32,256]{2,1,0:T(8,128)}, u32[]{:S(2)}) copy-start(f32[8,32,256]{2,1,0:T(8,128)} %param.8) | copy-start | bytes 786436
  54.5 6.9 %collective-permute-start.13 = (f32[8,8,256]{2,1,0:T(8,128)S(1)}, f32[8,8,256]{2,1,0:T(8,128)S(1)}, u32[]{:S(2)}, u32[]{:S(2)}) collective-permute-start(f32[8,8,256]{2,1,0:T(8,128)S(1)} %copy.58), channel_id=1, source_target_pairs={{0,3},{1,2},{2,1},{3,0},{4,7},{5,6},{6,5},{7,4},{8,11},{9,10},{10,... | collective-permute-start | bytes 196616 | tf_op jit(solution)/shard_map/shard_3/ppermute | solution.py:18
  56.4 7.2 %collective-permute-start.14 = (f32[8,8,256]{2,1,0:T(8,128)S(1)}, f32[8,8,256]{2,1,0:T(8,128)S(1)}, u32[]{:S(2)}, u32[]{:S(2)}) collective-permute-start(f32[8,8,256]{2,1,0:T(8,128)S(1)} %copy.59), channel_id=1, source_target_pairs={{0,2},{1,3},{2,0},{3,1},{4,6},{5,7},{6,4},{7,5},{8,10},{9,11},{10,... | collective-permute-start | bytes 196616 | tf_op jit(solution)/shard_map/shard_2/ppermute | solution.py:18
  57.3 6.4 %collective-permute-start.15 = (f32[8,8,256]{2,1,0:T(8,128)S(1)}, f32[8,8,256]{2,1,0:T(8,128)S(1)}, u32[]{:S(2)}, u32[]{:S(2)}) collective-permute-start(f32[8,8,256]{2,1,0:T(8,128)S(1)} %copy.60), channel_id=1, source_target_pairs={{0,1},{1,0},{2,3},{3,2},{4,5},{5,4},{6,7},{7,6},{8,9},{9,8},{10,11... | collective-permute-start | bytes 196616 | tf_op jit(solution)/shard_map/shard_1/ppermute | solution.py:18
  63.7 6.1 %collective-permute-start.18 = (f32[4,32,256]{2,1,0:T(8,128)S(1)}, f32[4,32,256]{2,1,0:T(8,128)S(1)}, u32[]{:S(2)}, u32[]{:S(2)}) collective-permute-start(f32[4,32,256]{2,1,0:T(8,128)S(1)} %get-tuple-element.61), channel_id=1, source_target_pairs={{0,8},{4,20},{8,0},{12,28},{16,24},{20,4},{24,16},{28,12},{1,9},{5... | collective-permute-start | bytes 393224 | tf_op jit(solution)/shard_map/rows_first_top/ppermute | solution.py:18
  64.6 6.1 %collective-permute-start.20 = (f32[4,32,256]{2,1,0:T(8,128)S(1)}, f32[4,32,256]{2,1,0:T(8,128)S(1)}, u32[]{:S(2)}, u32[]{:S(2)}) collective-permute-start(f32[4,32,256]{2,1,0:T(8,128)S(1)} %get-tuple-element.60), channel_id=1, source_target_pairs={{0,16},{4,12},{8,24},{12,4},{16,0},{20,28},{24,8},{28,20},{1,17},{... | collective-permute-start | bytes 393224 | tf_op jit(solution)/shard_map/rows_second_low/ppermute | solution.py:18
  65.2 7.3 %collective-permute-start.17 = (f32[4,32,256]{2,1,0:T(8,128)S(1)}, f32[4,32,256]{2,1,0:T(8,128)S(1)}, u32[]{:S(2)}, u32[]{:S(2)}) collective-permute-start(f32[4,32,256]{2,1,0:T(8,128)S(1)} %get-tuple-element.60), channel_id=1, source_target_pairs={{0,8},{4,20},{8,0},{12,28},{16,24},{20,4},{24,16},{28,12},{1,9},{5... | collective-permute-start | bytes 393224 | tf_op jit(solution)/shard_map/rows_first_low/ppermute | solution.py:18
  66.7 5.9 %collective-permute-start.16 = (f32[8,32,256]{2,1,0:T(8,128)S(1)}, f32[8,32,256]{2,1,0:T(8,128)S(1)}, u32[]{:S(2)}, u32[]{:S(2)}) collective-permute-start(f32[8,32,256]{2,1,0:T(8,128)S(1)} %subtract_dynamic-update-slice_fusion), channel_id=1, source_target_pairs={{0,4},{4,0},{8,12},{12,8},{16,20},{20,16},{24,28},{28,24},{1,5},{5... | collective-permute-start | bytes 786440 | tf_op jit(solution)/shard_map/rows_core_own/ppermute | solution.py:18
  66.7 5.9 %collective-permute-start.19 = (f32[4,32,256]{2,1,0:T(8,128)S(1)}, f32[4,32,256]{2,1,0:T(8,128)S(1)}, u32[]{:S(2)}, u32[]{:S(2)}) collective-permute-start(f32[4,32,256]{2,1,0:T(8,128)S(1)} %get-tuple-element.61), channel_id=1, source_target_pairs={{0,16},{4,12},{8,24},{12,4},{16,0},{20,28},{24,8},{28,20},{1,17},{... | collective-permute-start | bytes 393224 | tf_op jit(solution)/shard_map/rows_second_top/ppermute | solution.py:18
  69.8 5.2 %collective-permute-start.21 = (f32[4,32,256]{2,1,0:T(8,128)S(1)}, f32[4,32,256]{2,1,0:T(8,128)S(1)}, u32[]{:S(2)}, u32[]{:S(2)}) collective-permute-start(f32[4,32,256]{2,1,0:T(8,128)S(1)} %collective-permute-done.18), channel_id=1, source_target_pairs={{0,16},{4,12},{8,24},{12,4},{16,0},{20,28},{24,8},{28,20},{1,17},{... | collective-permute-start | bytes 393224 | tf_op jit(solution)/shard_map/rows_relay_top/ppermute | solution.py:18
  70.7 5.0 %collective-permute-start.24 = (f32[4,32,256]{2,1,0:T(8,128)S(1)}, f32[4,32,256]{2,1,0:T(8,128)S(1)}, u32[]{:S(2)}, u32[]{:S(2)}) collective-permute-start(f32[4,32,256]{2,1,0:T(8,128)S(1)} %collective-permute-done.20), channel_id=1, source_target_pairs={{0,8},{4,20},{8,0},{12,28},{16,24},{20,4},{24,16},{28,12},{1,9},{5... | collective-permute-start | bytes 393224 | tf_op jit(solution)/shard_map/rows_relay_low/ppermute | solution.py:18
  75.0 1.5 %collective-permute-start.22 = (f32[8,32,256]{2,1,0:T(8,128)S(1)}, f32[8,32,256]{2,1,0:T(8,128)S(1)}, u32[]{:S(2)}, u32[]{:S(2)}) collective-permute-start(f32[8,32,256]{2,1,0:T(8,128)S(1)} %pad_maximum_fusion.1), channel_id=1, source_target_pairs={{0,4},{4,0},{8,12},{12,8},{16,20},{20,16},{24,28},{28,24},{1,5},{5... | collective-permute-start | bytes 786440 | tf_op jit(solution)/shard_map/rows_core_first/ppermute | solution.py:18
  75.0 1.9 %collective-permute-start.23 = (f32[8,32,256]{2,1,0:T(8,128)S(1)}, f32[8,32,256]{2,1,0:T(8,128)S(1)}, u32[]{:S(2)}, u32[]{:S(2)}) collective-permute-start(f32[8,32,256]{2,1,0:T(8,128)S(1)} %pad_maximum_fusion.2), channel_id=1, source_target_pairs={{0,4},{4,0},{8,12},{12,8},{16,20},{20,16},{24,28},{28,24},{1,5},{5... | collective-permute-start | bytes 786440 | tf_op jit(solution)/shard_map/rows_core_second/ppermute | solution.py:18
  75.7 1.6 %collective-permute-start.25 = (f32[8,32,256]{2,1,0:T(8,128)S(1)}, f32[8,32,256]{2,1,0:T(8,128)S(1)}, u32[]{:S(2)}, u32[]{:S(2)}) collective-permute-start(f32[8,32,256]{2,1,0:T(8,128)S(1)} %constant_dynamic-update-slice_fusion.6), channel_id=1, source_target_pairs={{0,4},{4,0},{8,12},{12,8},{16,20},{20,16},{24,28},{28,24},{1,5},{5... | collective-permute-start | bytes 786440 | tf_op jit(solution)/shard_map/rows_core_far/ppermute | solution.py:18
  (4 other events, 43.5 us)

commit v10 on v9

--- a/solution.py
+++ b/solution.py
@@ -87,7 +87,6 @@
     data_count = lax.axis_size("dp")
     device_total = shard_count * data_count
     home_count, row_count, width = params.shape
-    half = home_count // 2
     piece = (row_count // shard_count, width)
     chips = data_count // 2
     my_core = data_here & core
@@ -183,43 +182,51 @@
     back = back.reshape((shard_count, home_count) + piece)
     returned = shard_exchange([back[near_order.index(k)] for k in range(shard_count)])
 
-    new_home = params
-    for k in (0, 3, 2, 1):
-        start = (shard_here ^ k) * piece[0]
-        home = lax.dynamic_slice_in_dim(params, start, piece[0], axis=1)
-        home = home - learn_rate * (returned[k] + decay_rate * home)
-        new_home = lax.dynamic_update_slice_in_dim(new_home, home, start, axis=1)
-
-    low, top = new_home[:half], new_home[half:]
-    first_top = swap(top, "dp", first_link, "rows_first_top")
-    second_low = swap(low, "dp", second_link, "rows_second_low")
-    other = swap(new_home, "dp", core, "rows_core_own")
-    first_low = swap(low, "dp", first_link, "rows_first_low")
-    second_top = swap(top, "dp", second_link, "rows_second_top")
-    far_top = swap(first_top, "dp", second_link, "rows_relay_top")
-    far_low = swap(second_low, "dp", first_link, "rows_relay_low")
-    first_rows = jnp.concatenate([first_low, first_top], axis=0)
-    second_rows = jnp.concatenate([second_top, second_low], axis=0)
-    first_rows, second_rows, far_top, first_new, second_new = lax.optimization_barrier(
-        (first_rows, second_rows, far_top, first_new, second_new)
-    )
-    far_rows = jnp.concatenate([far_low, far_top], axis=0)
-    second_other = swap(second_rows, "dp", core, "rows_core_second")
+
+    def both(first, second, flip):
+        return jnp.where(
+            flip == 0,
+            jnp.concatenate([first, second], axis=1),
+            jnp.concatenate([second, first], axis=1),
+        )
+
+    def stepped(change_rows, home):
+        return home - learn_rate * (change_rows + decay_rate * home)
+
+    near_own = stepped(both(returned[0], returned[1], shard_low), set_of(params, shard_half))
+    params, near_own = lax.optimization_barrier((params, near_own))
+    near_second = swap(near_own, "dp", second_link, "rows_second_near")
+    near_first = swap(near_own, "dp", first_link, "rows_first_near")
+    far_own = stepped(both(returned[2], returned[3], shard_low), set_of(params, 1 - shard_half))
+    far_second = swap(far_own, "dp", second_link, "rows_second_far")
+    far_first = swap(far_own, "dp", first_link, "rows_first_far")
+    near_second, near_first, _ = lax.optimization_barrier((near_second, near_first, far_own))
+    near_across = swap(near_second, "dp", first_link, "rows_relay_near")
+    far_across = swap(far_second, "dp", first_link, "rows_relay_far")
+    near_rows = jnp.stack([near_own, near_first, near_second, near_across])
+    near_rows, _, first_new, second_new = lax.optimization_barrier(
+        (near_rows, far_second, first_new, second_new)
+    )
+    far_rows = jnp.stack([far_own, far_first, far_second, far_across])
+
     updated = jnp.zeros((home_count, width, width), jnp.float32)
-    for mask, block, values in (
-        (0, 0, new_home),
-        (core, 0, other),
-        (first_chip, 0, first_rows),
-        (second_chip, half, second_rows[:half]),
-        (second_chip, 0, second_rows[half:]),
-        (second_chip ^ core, 0, swap(first_rows, "dp", core, "rows_core_first")),
-        (first_chip ^ core, half, second_other[:half]),
-        (first_chip ^ core, 0, second_other[half:]),
-        (across, 0, far_rows),
-        (across ^ core, 0, swap(far_rows, "dp", core, "rows_core_far")),
+    for what, place, rows in (
+        ("near", shard_half, near_rows),
+        ("far", 1 - shard_half, far_rows),
     ):
-        start = (data_here ^ mask) * row_count
-        updated = lax.dynamic_update_slice(updated, values, (block, start, 0))
+        other = swap(rows, "dp", core, f"rows_core_{what}")
+        for mask, values in (
+            (0, rows[0]),
+            (first_chip, rows[1]),
+            (second_chip, rows[2]),
+            (across, rows[3]),
+            (core, other[0]),
+            (second_chip ^ core, other[1]),
+            (first_chip ^ core, other[2]),
+            (across ^ core, other[3]),
+        ):
+            start = ((data_here ^ mask) * 2 + place) * (row_count // 2)
+            updated = lax.dynamic_update_slice_in_dim(updated, values, start, axis=1)
     return updated, first_new[None, None, None], second_new[None, None, None]
 
 

time: 78.9 us -> 79.5 us (level)
  waiting for transfers between devices: 17.4 us -> 19.8 us
  starting transfers between devices: 27.2 us -> 25.4 us
    ppermute x26 -> x24, waiting for transfers between devices: 17.4 us -> 19.8 us  [swap(): return lax.ppermute(values, name, pairs)]
    ppermute x26 -> x24, starting transfers between devices: 27.2 us -> 25.4 us  [swap(): return lax.ppermute(values, name, pairs)]
  transfers between devices with their start and end apart: 26 -> 24, of which waited for: 15 -> 12; matrix products, arithmetic and copies ran while one was open for 2% -> 2% of each run, Pallas kernels for 0% -> 0%
where the time goes in v10:
time: 79.5 us; the launch traced here: 79.3 us
  blocking collectives  26.5 us (33%)
  starting transfers between devices  25.4 us (32%)
  waiting for transfers between devices  19.8 us (25%)
  local copies, waits for them, and re-layouts  3.8 us (5%)
  matrix products  1.95 us (2%)
  between operations  1.27 us (2%)
    ppermute x24, starting transfers between devices, swap(): return lax.ppermute(values, name, pairs)  25.4 us
    ppermute x24, waiting for transfers between devices, swap(): return lax.ppermute(values, name, pairs)  19.8 us
    all_to_all x1, blocking collectives, routed(): lax.all_to_all(leaving.reshape((device_total,) + piece), ('dp', 'shard'),...  13.7 us
    all_to_all x1, blocking collectives, routed(): lax.all_to_all(change.reshape((device_total,) + piece), ('dp', 'shard'),...  12.7 us
  transfers between devices with their start and end apart: 24, of which 12 were waited for; matrix products, arithmetic and copies ran while one was open for 2% of the time, Pallas kernels for 0%

profile of v10, /device:TPU:0, one launch (start us, length us, event | category | flops | bytes accessed | tf_op | source)
XLA Modules:
  0.0 79.3 jit_solution(1802955582727214322)
XLA Ops:
  0.7 1.3 %dynamic-slice_bitcast_fusion = (bf16[8,4,32,256]{3,2,1,0:T(8,128)(2,1)S(1)}, bf16[8,4,32,256]{3,2,1,0:T(8,128)(2,1)S(1)}) fusion(bf16[8,4,2,32,256]{4,3,2,1,0:T(8,128)(2,1)} %bitcast.201, s32[]{:T(128)S(6)} %select_n.161, s32[]{:T(128)S(6)} %select_n.160), kind=kLoop, calls=%fused_computation.3 | loop fusion | bytes 2097160 | tf_op jit(solution)/shard_map/jit(dynamic_index_in_dim)/squeeze | solution.py:22
  3.3 0.6 collective-permute-done
  4.0 2.9 %collective-permute-start.9 = (f32[8,16,256]{2,1,0:T(8,128)S(1)}, f32[8,16,256]{2,1,0:T(8,128)S(1)}, u32[]{:S(2)}, u32[]{:S(2)}) collective-permute-start(f32[8,16,256]{2,1,0:T(8,128)S(1)} %get-tuple-element.42), channel_id=1, source_target_pairs={{0,8},{4,20},{8,0},{12,28},{16,24},{20,4},{24,16},{28,12},{1,9},{5... | collective-permute-start | bytes 393224 | tf_op jit(solution)/shard_map/sum_across_far/ppermute | solution.py:18
  7.1 1.0 %collective-permute-start.8 = (f32[8,16,256]{2,1,0:T(8,128)S(1)}, f32[8,16,256]{2,1,0:T(8,128)S(1)}, u32[]{:S(2)}, u32[]{:S(2)}) collective-permute-start(f32[8,16,256]{2,1,0:T(8,128)S(1)} %get-tuple-element.40), channel_id=1, source_target_pairs={{0,8},{4,20},{8,0},{12,28},{16,24},{20,4},{24,16},{28,12},{1,9},{5... | collective-permute-start | bytes 393224 | tf_op jit(solution)/shard_map/sum_first_far/ppermute | solution.py:18
  8.1 1.1 %collective-permute-start.3 = (f32[8,16,256]{2,1,0:T(8,128)S(1)}, f32[8,16,256]{2,1,0:T(8,128)S(1)}, u32[]{:S(2)}, u32[]{:S(2)}) collective-permute-start(f32[8,16,256]{2,1,0:T(8,128)S(1)} %get-tuple-element.35), channel_id=1, source_target_pairs={{0,8},{4,20},{8,0},{12,28},{16,24},{20,4},{24,16},{28,12},{1,9},{5... | collective-permute-start | bytes 393224 | tf_op jit(solution)/shard_map/sum_across_near/ppermute | solution.py:18
  9.2 0.6 collective-permute-done.9
  9.8 2.1 %collective-permute-start.10 = (f32[8,16,256]{2,1,0:T(8,128)S(1)}, f32[8,16,256]{2,1,0:T(8,128)S(1)}, u32[]{:S(2)}, u32[]{:S(2)}) collective-permute-start(f32[8,16,256]{2,1,0:T(8,128)S(1)} %add.226), channel_id=1, source_target_pairs={{0,16},{4,12},{8,24},{12,4},{16,0},{20,28},{24,8},{28,20},{1,17},{... | collective-permute-start | bytes 393224 | tf_op jit(solution)/shard_map/sum_relay_far/ppermute | solution.py:18
  12.0 1.6 %collective-permute-start.6 = (f32[8,16,256]{2,1,0:T(8,128)S(1)}, f32[8,16,256]{2,1,0:T(8,128)S(1)}, u32[]{:S(2)}, u32[]{:S(2)}) collective-permute-start(f32[8,16,256]{2,1,0:T(8,128)S(1)} %get-tuple-element.36), channel_id=1, source_target_pairs={{0,8},{4,20},{8,0},{12,28},{16,24},{20,4},{24,16},{28,12},{1,9},{5... | collective-permute-start | bytes 393224 | tf_op jit(solution)/shard_map/sum_first_near/ppermute | solution.py:18
  13.6 1.3 %collective-permute-done.3 = f32[8,16,256]{2,1,0:T(8,128)S(1)} collective-permute-done((f32[8,16,256]{2,1,0:T(8,128)S(1)}, f32[8,16,256]{2,1,0:T(8,128)S(1)}, u32[]{:S(2)}, u32[]{:S(2)}) %collective-permute-start.3) | collective-permute-done | bytes 131104 | tf_op jit(solution)/shard_map/sum_across_near/ppermute | solution.py:18
  14.9 1.3 %collective-permute-start.4 = (f32[8,16,256]{2,1,0:T(8,128)S(1)}, f32[8,16,256]{2,1,0:T(8,128)S(1)}, u32[]{:S(2)}, u32[]{:S(2)}) collective-permute-start(f32[8,16,256]{2,1,0:T(8,128)S(1)} %add.219), channel_id=1, source_target_pairs={{0,16},{4,12},{8,24},{12,4},{16,0},{20,28},{24,8},{28,20},{1,17},{... | collective-permute-start | bytes 393224 | tf_op jit(solution)/shard_map/sum_relay_near/ppermute | solution.py:18
  16.3 2.8 %collective-permute-start.12 = (f32[8,8,256]{2,1,0:T(8,128)S(1)}, f32[8,8,256]{2,1,0:T(8,128)S(1)}, u32[]{:S(2)}, u32[]{:S(2)}) collective-permute-start(f32[8,8,256]{2,1,0:T(8,128)S(1)} %get-tuple-element.79), channel_id=1, source_target_pairs={{0,2},{1,3},{2,0},{3,1},{4,6},{5,7},{6,4},{7,5},{8,10},{9,11},{10,... | collective-permute-start | bytes 196616 | tf_op jit(solution)/shard_map/shard_2/ppermute | solution.py:18
  19.1 1.3 %collective-permute-start.11 = (f32[8,8,256]{2,1,0:T(8,128)S(1)}, f32[8,8,256]{2,1,0:T(8,128)S(1)}, u32[]{:S(2)}, u32[]{:S(2)}) collective-permute-start(f32[8,8,256]{2,1,0:T(8,128)S(1)} %get-tuple-element.78), channel_id=1, source_target_pairs={{0,3},{1,2},{2,1},{3,0},{4,7},{5,6},{6,5},{7,4},{8,11},{9,10},{10,... | collective-permute-start | bytes 196616 | tf_op jit(solution)/shard_map/shard_3/ppermute | solution.py:18
  20.6 0.9 %collective-permute-start.7 = (f32[8,8,256]{2,1,0:T(8,128)S(1)}, f32[8,8,256]{2,1,0:T(8,128)S(1)}, u32[]{:S(2)}, u32[]{:S(2)}) collective-permute-start(f32[8,8,256]{2,1,0:T(8,128)S(1)} %get-tuple-element.77), channel_id=1, source_target_pairs={{0,1},{1,0},{2,3},{3,2},{4,5},{5,4},{6,7},{7,6},{8,9},{9,8},{10,11... | collective-permute-start | bytes 196616 | tf_op jit(solution)/shard_map/shard_1/ppermute | solution.py:18
  21.7 1.7 %collective-permute-done.12 = f32[8,8,256]{2,1,0:T(8,128)S(1)} collective-permute-done((f32[8,8,256]{2,1,0:T(8,128)S(1)}, f32[8,8,256]{2,1,0:T(8,128)S(1)}, u32[]{:S(2)}, u32[]{:S(2)}) %collective-permute-start.12) | collective-permute-done | bytes 65568 | tf_op jit(solution)/shard_map/shard_2/ppermute | solution.py:18
  23.5 1.8 %collective-permute-done.11 = f32[8,8,256]{2,1,0:T(8,128)S(1)} collective-permute-done((f32[8,8,256]{2,1,0:T(8,128)S(1)}, f32[8,8,256]{2,1,0:T(8,128)S(1)}, u32[]{:S(2)}, u32[]{:S(2)}) %collective-permute-start.11) | collective-permute-done | bytes 65568 | tf_op jit(solution)/shard_map/shard_3/ppermute | solution.py:18
  26.1 13.7 %all_to_all.10 = f32[32,8,256]{2,1,0:T(8,128)S(1)} all-to-all(f32[32,8,256]{2,1,0:T(8,128)S(1)} %copy.68), channel_id=1, replica_groups=mesh['dp'=8,'shard'=4] {'dp','shard'}, dimensions={0} | all-to-all | bytes 524288 | tf_op jit(solution)/shard_map/all_to_all | solution.py:152
  41.4 12.7 %all_to_all.11 = f32[32,8,256]{2,1,0:T(8,128)S(1)} all-to-all(f32[32,8,256]{2,1,0:T(8,128)S(1)} %convolution_bitcast_fusion), channel_id=1, replica_groups=mesh['dp'=8,'shard'=4] {'dp','shard'}, dimensions={0} | all-to-all | bytes 524288 | tf_op jit(solution)/shard_map/all_to_all | solution.py:169
  54.5 1.2 %collective-permute-start.13 = (f32[8,8,256]{2,1,0:T(8,128)S(1)}, f32[8,8,256]{2,1,0:T(8,128)S(1)}, u32[]{:S(2)}, u32[]{:S(2)}) collective-permute-start(f32[8,8,256]{2,1,0:T(8,128)S(1)} %copy.70), channel_id=1, source_target_pairs={{0,1},{1,0},{2,3},{3,2},{4,5},{5,4},{6,7},{7,6},{8,9},{9,8},{10,11... | collective-permute-start | bytes 196616 | tf_op jit(solution)/shard_map/shard_1/ppermute | solution.py:18
  55.7 1.2 %collective-permute-start.17 = (f32[8,8,256]{2,1,0:T(8,128)S(1)}, f32[8,8,256]{2,1,0:T(8,128)S(1)}, u32[]{:S(2)}, u32[]{:S(2)}) collective-permute-start(f32[8,8,256]{2,1,0:T(8,128)S(1)} %copy.75), channel_id=1, source_target_pairs={{0,3},{1,2},{2,1},{3,0},{4,7},{5,6},{6,5},{7,4},{8,11},{9,10},{10,... | collective-permute-start | bytes 196616 | tf_op jit(solution)/shard_map/shard_3/ppermute | solution.py:18
  57.0 1.4 %collective-permute-start.16 = (f32[8,8,256]{2,1,0:T(8,128)S(1)}, f32[8,8,256]{2,1,0:T(8,128)S(1)}, u32[]{:S(2)}, u32[]{:S(2)}) collective-permute-start(f32[8,8,256]{2,1,0:T(8,128)S(1)} %copy.74), channel_id=1, source_target_pairs={{0,2},{1,3},{2,0},{3,1},{4,6},{5,7},{6,4},{7,5},{8,10},{9,11},{10,... | collective-permute-start | bytes 196616 | tf_op jit(solution)/shard_map/shard_2/ppermute | solution.py:18
  58.3 0.7 collective-permute-done.13
  59.0 1.0 %collective-permute-start.14 = (f32[8,16,256]{2,1,0:T(8,128)S(1)}, f32[8,16,256]{2,1,0:T(8,128)S(1)}, u32[]{:S(2)}, u32[]{:S(2)}) collective-permute-start(f32[8,16,256]{2,1,0:T(8,128)S(1)} %fusion.27), channel_id=1, source_target_pairs={{0,16},{4,12},{8,24},{12,4},{16,0},{20,28},{24,8},{28,20},{1,17},{... | collective-permute-start | bytes 393224 | tf_op jit(solution)/shard_map/rows_second_near/ppermute | solution.py:18
  60.5 1.3 %collective-permute-done.17 = f32[8,8,256]{2,1,0:T(8,128)S(1)} collective-permute-done((f32[8,8,256]{2,1,0:T(8,128)S(1)}, f32[8,8,256]{2,1,0:T(8,128)S(1)}, u32[]{:S(2)}, u32[]{:S(2)}) %collective-permute-start.17) | collective-permute-done | bytes 65568 | tf_op jit(solution)/shard_map/shard_3/ppermute | solution.py:18
  61.9 2.6 %collective-permute-done.16 = f32[8,8,256]{2,1,0:T(8,128)S(1)} collective-permute-done((f32[8,8,256]{2,1,0:T(8,128)S(1)}, f32[8,8,256]{2,1,0:T(8,128)S(1)}, u32[]{:S(2)}, u32[]{:S(2)}) %collective-permute-start.16) | collective-permute-done | bytes 65568 | tf_op jit(solution)/shard_map/shard_2/ppermute | solution.py:18
  64.5 1.0 %collective-permute-start.19 = (f32[8,16,256]{2,1,0:T(8,128)S(1)}, f32[8,16,256]{2,1,0:T(8,128)S(1)}, u32[]{:S(2)}, u32[]{:S(2)}) collective-permute-start(f32[8,16,256]{2,1,0:T(8,128)S(1)} %fusion.30), channel_id=1, source_target_pairs={{0,16},{4,12},{8,24},{12,4},{16,0},{20,28},{24,8},{28,20},{1,17},{... | collective-permute-start | bytes 393224 | tf_op jit(solution)/shard_map/rows_second_far/ppermute | solution.py:18
  65.5 0.8 %collective-permute-start.18 = (f32[8,16,256]{2,1,0:T(8,128)S(1)}, f32[8,16,256]{2,1,0:T(8,128)S(1)}, u32[]{:S(2)}, u32[]{:S(2)}) collective-permute-start(f32[8,16,256]{2,1,0:T(8,128)S(1)} %collective-permute-done.14), channel_id=1, source_target_pairs={{0,8},{4,20},{8,0},{12,28},{16,24},{20,4},{24,16},{28,12},{1,9},{5... | collective-permute-start | bytes 393224 | tf_op jit(solution)/shard_map/rows_relay_near/ppermute | solution.py:18
  66.3 1.2 %collective-permute-start.21 = (f32[8,16,256]{2,1,0:T(8,128)S(1)}, f32[8,16,256]{2,1,0:T(8,128)S(1)}, u32[]{:S(2)}, u32[]{:S(2)}) collective-permute-start(f32[8,16,256]{2,1,0:T(8,128)S(1)} %fusion.30), channel_id=1, source_target_pairs={{0,8},{4,20},{8,0},{12,28},{16,24},{20,4},{24,16},{28,12},{1,9},{5... | collective-permute-start | bytes 393224 | tf_op jit(solution)/shard_map/rows_first_far/ppermute | solution.py:18
  67.5 3.4 %collective-permute-done.19 = f32[8,16,256]{2,1,0:T(8,128)S(1)} collective-permute-done((f32[8,16,256]{2,1,0:T(8,128)S(1)}, f32[8,16,256]{2,1,0:T(8,128)S(1)}, u32[]{:S(2)}, u32[]{:S(2)}) %collective-permute-start.19) | collective-permute-done | bytes 131104 | tf_op jit(solution)/shard_map/rows_second_far/ppermute | solution.py:18
  70.9 0.9 %collective-permute-start.22 = (f32[8,16,256]{2,1,0:T(8,128)S(1)}, f32[8,16,256]{2,1,0:T(8,128)S(1)}, u32[]{:S(2)}, u32[]{:S(2)}) collective-permute-start(f32[8,16,256]{2,1,0:T(8,128)S(1)} %collective-permute-done.19), channel_id=1, source_target_pairs={{0,8},{4,20},{8,0},{12,28},{16,24},{20,4},{24,16},{28,12},{1,9},{5... | collective-permute-start | bytes 393224 | tf_op jit(solution)/shard_map/rows_relay_far/ppermute | solution.py:18
  72.0 3.9 %collective-permute-done.22 = f32[8,16,256]{2,1,0:T(8,128)S(1)} collective-permute-done((f32[8,16,256]{2,1,0:T(8,128)S(1)}, f32[8,16,256]{2,1,0:T(8,128)S(1)}, u32[]{:S(2)}, u32[]{:S(2)}) %collective-permute-start.22) | collective-permute-done | bytes 131104 | tf_op jit(solution)/shard_map/rows_relay_far/ppermute | solution.py:18
  76.5 1.4 %collective-permute-done.23 = f32[4,8,16,256]{3,2,1,0:T(8,128)S(1)} collective-permute-done((f32[4,8,16,256]{3,2,1,0:T(8,128)S(1)}, f32[4,8,16,256]{3,2,1,0:T(8,128)S(1)}, u32[]{:S(2)}, u32[]{:S(2)}) %collective-permute-start.23) | collective-permute-done | bytes 524320 | tf_op jit(solution)/shard_map/rows_core_far/ppermute | solution.py:18
  78.0 1.3 %copy-done.1 = f32[8,256,256]{2,1,0:T(8,128)} copy-done((f32[8,256,256]{2,1,0:T(8,128)}, f32[8,256,256]{2,1,0:T(8,128)S(1)}, u32[]{:S(2)}) %copy-start.1) | copy-done | bytes 2097176
  (97 shorter events, 5.9 us)
Async XLA Ops:
  0.6 39.6 %copy-start = (f32[1,1,1,256,256]{4,3,2,1,0:T(8,128)S(1)}, f32[1,1,1,256,256]{4,3,2,1,0:T(8,128)}, u32[]{:S(2)}) copy-start(f32[1,1,1,256,256]{4,3,2,1,0:T(8,128)} %param.10) | copy-start | bytes 786436
  2.2 1.7 %collective-permute-start = (f32[8,32,256]{2,1,0:T(8,128)S(1)}, f32[8,32,256]{2,1,0:T(8,128)S(1)}, u32[]{:S(2)}, u32[]{:S(2)}) collective-permute-start(f32[8,32,256]{2,1,0:T(8,128)S(1)} %get-tuple-element.61), channel_id=1, source_target_pairs={{0,4},{4,0},{8,12},{12,8},{16,20},{20,16},{24,28},{28,24},{1,5},{5... | collective-permute-start | bytes 786440 | tf_op jit(solution)/shard_map/sum_core_across/ppermute | solution.py:18
  2.7 4.2 %collective-permute-start.2 = (f32[8,32,256]{2,1,0:T(8,128)S(1)}, f32[8,32,256]{2,1,0:T(8,128)S(1)}, u32[]{:S(2)}, u32[]{:S(2)}) collective-permute-start(f32[8,32,256]{2,1,0:T(8,128)S(1)} %get-tuple-element.58), channel_id=1, source_target_pairs={{0,4},{4,0},{8,12},{12,8},{16,20},{20,16},{24,28},{28,24},{1,5},{5... | collective-permute-start | bytes 786440 | tf_op jit(solution)/shard_map/sum_core_second/ppermute | solution.py:18
  2.8 4.1 %collective-permute-start.5 = (f32[8,32,256]{2,1,0:T(8,128)S(1)}, f32[8,32,256]{2,1,0:T(8,128)S(1)}, u32[]{:S(2)}, u32[]{:S(2)}) collective-permute-start(f32[8,32,256]{2,1,0:T(8,128)S(1)} %get-tuple-element.59), channel_id=1, source_target_pairs={{0,4},{4,0},{8,12},{12,8},{16,20},{20,16},{24,28},{28,24},{1,5},{5... | collective-permute-start | bytes 786440 | tf_op jit(solution)/shard_map/sum_core_first/ppermute | solution.py:18
  3.2 3.6 %collective-permute-start.1 = (f32[8,32,256]{2,1,0:T(8,128)S(1)}, f32[8,32,256]{2,1,0:T(8,128)S(1)}, u32[]{:S(2)}, u32[]{:S(2)}) collective-permute-start(f32[8,32,256]{2,1,0:T(8,128)S(1)} %get-tuple-element.60), channel_id=1, source_target_pairs={{0,4},{4,0},{8,12},{12,8},{16,20},{20,16},{24,28},{28,24},{1,5},{5... | collective-permute-start | bytes 786440 | tf_op jit(solution)/shard_map/sum_core_own/ppermute | solution.py:18
  4.0 5.9 %collective-permute-start.9 = (f32[8,16,256]{2,1,0:T(8,128)S(1)}, f32[8,16,256]{2,1,0:T(8,128)S(1)}, u32[]{:S(2)}, u32[]{:S(2)}) collective-permute-start(f32[8,16,256]{2,1,0:T(8,128)S(1)} %get-tuple-element.42), channel_id=1, source_target_pairs={{0,8},{4,20},{8,0},{12,28},{16,24},{20,4},{24,16},{28,12},{1,9},{5... | collective-permute-start | bytes 393224 | tf_op jit(solution)/shard_map/sum_across_far/ppermute | solution.py:18
  7.0 14.5 %copy-start.8 = (s32[32]{0:T(128)S(1)}, s32[32]{0:T(128)}, u32[]{:S(2)}) copy-start(s32[32]{0:T(128)} %param.13) | copy-start | bytes 388
  7.1 6.5 %collective-permute-start.8 = (f32[8,16,256]{2,1,0:T(8,128)S(1)}, f32[8,16,256]{2,1,0:T(8,128)S(1)}, u32[]{:S(2)}, u32[]{:S(2)}) collective-permute-start(f32[8,16,256]{2,1,0:T(8,128)S(1)} %get-tuple-element.40), channel_id=1, source_target_pairs={{0,8},{4,20},{8,0},{12,28},{16,24},{20,4},{24,16},{28,12},{1,9},{5... | collective-permute-start | bytes 393224 | tf_op jit(solution)/shard_map/sum_first_far/ppermute | solution.py:18
  8.1 6.8 %collective-permute-start.3 = (f32[8,16,256]{2,1,0:T(8,128)S(1)}, f32[8,16,256]{2,1,0:T(8,128)S(1)}, u32[]{:S(2)}, u32[]{:S(2)}) collective-permute-start(f32[8,16,256]{2,1,0:T(8,128)S(1)} %get-tuple-element.35), channel_id=1, source_target_pairs={{0,8},{4,20},{8,0},{12,28},{16,24},{20,4},{24,16},{28,12},{1,9},{5... | collective-permute-start | bytes 393224 | tf_op jit(solution)/shard_map/sum_across_near/ppermute | solution.py:18
  9.8 6.4 %collective-permute-start.10 = (f32[8,16,256]{2,1,0:T(8,128)S(1)}, f32[8,16,256]{2,1,0:T(8,128)S(1)}, u32[]{:S(2)}, u32[]{:S(2)}) collective-permute-start(f32[8,16,256]{2,1,0:T(8,128)S(1)} %add.226), channel_id=1, source_target_pairs={{0,16},{4,12},{8,24},{12,4},{16,0},{20,28},{24,8},{28,20},{1,17},{... | collective-permute-start | bytes 393224 | tf_op jit(solution)/shard_map/sum_relay_far/ppermute | solution.py:18
  12.0 8.5 %collective-permute-start.6 = (f32[8,16,256]{2,1,0:T(8,128)S(1)}, f32[8,16,256]{2,1,0:T(8,128)S(1)}, u32[]{:S(2)}, u32[]{:S(2)}) collective-permute-start(f32[8,16,256]{2,1,0:T(8,128)S(1)} %get-tuple-element.36), channel_id=1, source_target_pairs={{0,8},{4,20},{8,0},{12,28},{16,24},{20,4},{24,16},{28,12},{1,9},{5... | collective-permute-start | bytes 393224 | tf_op jit(solution)/shard_map/sum_first_near/ppermute | solution.py:18
  14.9 24.9 %copy-start.2 = (f32[1,1,1,256,256]{4,3,2,1,0:T(8,128)S(1)}, f32[1,1,1,256,256]{4,3,2,1,0:T(8,128)}, u32[]{:S(2)}) copy-start(f32[1,1,1,256,256]{4,3,2,1,0:T(8,128)} %param.9) | copy-start | bytes 786436
  14.9 5.6 %collective-permute-start.4 = (f32[8,16,256]{2,1,0:T(8,128)S(1)}, f32[8,16,256]{2,1,0:T(8,128)S(1)}, u32[]{:S(2)}, u32[]{:S(2)}) collective-permute-start(f32[8,16,256]{2,1,0:T(8,128)S(1)} %add.219), channel_id=1, source_target_pairs={{0,16},{4,12},{8,24},{12,4},{16,0},{20,28},{24,8},{28,20},{1,17},{... | collective-permute-start | bytes 393224 | tf_op jit(solution)/shard_map/sum_relay_near/ppermute | solution.py:18
  16.3 7.1 %collective-permute-start.12 = (f32[8,8,256]{2,1,0:T(8,128)S(1)}, f32[8,8,256]{2,1,0:T(8,128)S(1)}, u32[]{:S(2)}, u32[]{:S(2)}) collective-permute-start(f32[8,8,256]{2,1,0:T(8,128)S(1)} %get-tuple-element.79), channel_id=1, source_target_pairs={{0,2},{1,3},{2,0},{3,1},{4,6},{5,7},{6,4},{7,5},{8,10},{9,11},{10,... | collective-permute-start | bytes 196616 | tf_op jit(solution)/shard_map/shard_2/ppermute | solution.py:18
  19.1 6.2 %collective-permute-start.11 = (f32[8,8,256]{2,1,0:T(8,128)S(1)}, f32[8,8,256]{2,1,0:T(8,128)S(1)}, u32[]{:S(2)}, u32[]{:S(2)}) collective-permute-start(f32[8,8,256]{2,1,0:T(8,128)S(1)} %get-tuple-element.78), channel_id=1, source_target_pairs={{0,3},{1,2},{2,1},{3,0},{4,7},{5,6},{6,5},{7,4},{8,11},{9,10},{10,... | collective-permute-start | bytes 196616 | tf_op jit(solution)/shard_map/shard_3/ppermute | solution.py:18
  20.5 19.7 %copy-start.4 = (f32[1,1,1,256,256]{4,3,2,1,0:T(8,128)S(1)}, f32[1,1,1,256,256]{4,3,2,1,0:T(8,128)}, u32[]{:S(2)}) copy-start(f32[1,1,1,256,256]{4,3,2,1,0:T(8,128)} %param.11) | copy-start | bytes 786436
  20.5 19.7 %copy-start.5 = (f32[1,1,1,256,256]{4,3,2,1,0:T(8,128)S(1)}, f32[1,1,1,256,256]{4,3,2,1,0:T(8,128)}, u32[]{:S(2)}) copy-start(f32[1,1,1,256,256]{4,3,2,1,0:T(8,128)} %param.12) | copy-start | bytes 786436
  20.6 5.0 %collective-permute-start.7 = (f32[8,8,256]{2,1,0:T(8,128)S(1)}, f32[8,8,256]{2,1,0:T(8,128)S(1)}, u32[]{:S(2)}, u32[]{:S(2)}) collective-permute-start(f32[8,8,256]{2,1,0:T(8,128)S(1)} %get-tuple-element.77), channel_id=1, source_target_pairs={{0,1},{1,0},{2,3},{3,2},{4,5},{5,4},{6,7},{7,6},{8,9},{9,8},{10,11... | collective-permute-start | bytes 196616 | tf_op jit(solution)/shard_map/shard_1/ppermute | solution.py:18
  40.6 13.9 %copy-start.6 = (f32[256,256]{1,0:T(8,128)}, f32[256,256]{1,0:T(8,128)S(1)}, u32[]{:S(2)}) copy-start(f32[256,256]{1,0:T(8,128)S(1)} %get-tuple-element.51) | copy-start | bytes 786436
  40.6 13.9 %copy-start.7 = (f32[256,256]{1,0:T(8,128)}, f32[256,256]{1,0:T(8,128)S(1)}, u32[]{:S(2)}) copy-start(f32[256,256]{1,0:T(8,128)S(1)} %get-tuple-element.52) | copy-start | bytes 786436
  40.7 18.3 %copy-start.3 = (f32[8,32,256]{2,1,0:T(8,128)S(1)}, f32[8,32,256]{2,1,0:T(8,128)}, u32[]{:S(2)}) copy-start(f32[8,32,256]{2,1,0:T(8,128)} %param.8) | copy-start | bytes 786436
  54.5 4.5 %collective-permute-start.13 = (f32[8,8,256]{2,1,0:T(8,128)S(1)}, f32[8,8,256]{2,1,0:T(8,128)S(1)}, u32[]{:S(2)}, u32[]{:S(2)}) collective-permute-start(f32[8,8,256]{2,1,0:T(8,128)S(1)} %copy.70), channel_id=1, source_target_pairs={{0,1},{1,0},{2,3},{3,2},{4,5},{5,4},{6,7},{7,6},{8,9},{9,8},{10,11... | collective-permute-start | bytes 196616 | tf_op jit(solution)/shard_map/shard_1/ppermute | solution.py:18
  55.7 6.1 %collective-permute-start.17 = (f32[8,8,256]{2,1,0:T(8,128)S(1)}, f32[8,8,256]{2,1,0:T(8,128)S(1)}, u32[]{:S(2)}, u32[]{:S(2)}) collective-permute-start(f32[8,8,256]{2,1,0:T(8,128)S(1)} %copy.75), channel_id=1, source_target_pairs={{0,3},{1,2},{2,1},{3,0},{4,7},{5,6},{6,5},{7,4},{8,11},{9,10},{10,... | collective-permute-start | bytes 196616 | tf_op jit(solution)/shard_map/shard_3/ppermute | solution.py:18
  57.0 7.5 %collective-permute-start.16 = (f32[8,8,256]{2,1,0:T(8,128)S(1)}, f32[8,8,256]{2,1,0:T(8,128)S(1)}, u32[]{:S(2)}, u32[]{:S(2)}) collective-permute-start(f32[8,8,256]{2,1,0:T(8,128)S(1)} %copy.74), channel_id=1, source_target_pairs={{0,2},{1,3},{2,0},{3,1},{4,6},{5,7},{6,4},{7,5},{8,10},{9,11},{10,... | collective-permute-start | bytes 196616 | tf_op jit(solution)/shard_map/shard_2/ppermute | solution.py:18
  59.0 6.5 %collective-permute-start.14 = (f32[8,16,256]{2,1,0:T(8,128)S(1)}, f32[8,16,256]{2,1,0:T(8,128)S(1)}, u32[]{:S(2)}, u32[]{:S(2)}) collective-permute-start(f32[8,16,256]{2,1,0:T(8,128)S(1)} %fusion.27), channel_id=1, source_target_pairs={{0,16},{4,12},{8,24},{12,4},{16,0},{20,28},{24,8},{28,20},{1,17},{... | collective-permute-start | bytes 393224 | tf_op jit(solution)/shard_map/rows_second_near/ppermute | solution.py:18
  60.0 5.5 %collective-permute-start.15 = (f32[8,16,256]{2,1,0:T(8,128)S(1)}, f32[8,16,256]{2,1,0:T(8,128)S(1)}, u32[]{:S(2)}, u32[]{:S(2)}) collective-permute-start(f32[8,16,256]{2,1,0:T(8,128)S(1)} %fusion.27), channel_id=1, source_target_pairs={{0,8},{4,20},{8,0},{12,28},{16,24},{20,4},{24,16},{28,12},{1,9},{5... | collective-permute-start | bytes 393224 | tf_op jit(solution)/shard_map/rows_first_near/ppermute | solution.py:18
  64.5 6.4 %collective-permute-start.19 = (f32[8,16,256]{2,1,0:T(8,128)S(1)}, f32[8,16,256]{2,1,0:T(8,128)S(1)}, u32[]{:S(2)}, u32[]{:S(2)}) collective-permute-start(f32[8,16,256]{2,1,0:T(8,128)S(1)} %fusion.30), channel_id=1, source_target_pairs={{0,16},{4,12},{8,24},{12,4},{16,0},{20,28},{24,8},{28,20},{1,17},{... | collective-permute-start | bytes 393224 | tf_op jit(solution)/shard_map/rows_second_far/ppermute | solution.py:18
  65.5 6.3 %collective-permute-start.18 = (f32[8,16,256]{2,1,0:T(8,128)S(1)}, f32[8,16,256]{2,1,0:T(8,128)S(1)}, u32[]{:S(2)}, u32[]{:S(2)}) collective-permute-start(f32[8,16,256]{2,1,0:T(8,128)S(1)} %collective-permute-done.14), channel_id=1, source_target_pairs={{0,8},{4,20},{8,0},{12,28},{16,24},{20,4},{24,16},{28,12},{1,9},{5... | collective-permute-start | bytes 393224 | tf_op jit(solution)/shard_map/rows_relay_near/ppermute | solution.py:18
  66.3 5.6 %collective-permute-start.21 = (f32[8,16,256]{2,1,0:T(8,128)S(1)}, f32[8,16,256]{2,1,0:T(8,128)S(1)}, u32[]{:S(2)}, u32[]{:S(2)}) collective-permute-start(f32[8,16,256]{2,1,0:T(8,128)S(1)} %fusion.30), channel_id=1, source_target_pairs={{0,8},{4,20},{8,0},{12,28},{16,24},{20,4},{24,16},{28,12},{1,9},{5... | collective-permute-start | bytes 393224 | tf_op jit(solution)/shard_map/rows_first_far/ppermute | solution.py:18
  70.9 5.0 %collective-permute-start.22 = (f32[8,16,256]{2,1,0:T(8,128)S(1)}, f32[8,16,256]{2,1,0:T(8,128)S(1)}, u32[]{:S(2)}, u32[]{:S(2)}) collective-permute-start(f32[8,16,256]{2,1,0:T(8,128)S(1)} %collective-permute-done.19), channel_id=1, source_target_pairs={{0,8},{4,20},{8,0},{12,28},{16,24},{20,4},{24,16},{28,12},{1,9},{5... | collective-permute-start | bytes 393224 | tf_op jit(solution)/shard_map/rows_relay_far/ppermute | solution.py:18
  71.9 4.4 %collective-permute-start.20 = (f32[4,8,16,256]{3,2,1,0:T(8,128)S(1)}, f32[4,8,16,256]{3,2,1,0:T(8,128)S(1)}, u32[]{:S(2)}, u32[]{:S(2)}) collective-permute-start(f32[4,8,16,256]{3,2,1,0:T(8,128)S(1)} %pad_maximum_fusion), channel_id=1, source_target_pairs={{0,4},{4,0},{8,12},{12,8},{16,20},{20,16},{24,28},{28,24},{1,5},{5... | collective-permute-start | bytes 1572872 | tf_op jit(solution)/shard_map/rows_core_near/ppermute | solution.py:18
  76.0 2.0 %collective-permute-start.23 = (f32[4,8,16,256]{3,2,1,0:T(8,128)S(1)}, f32[4,8,16,256]{3,2,1,0:T(8,128)S(1)}, u32[]{:S(2)}, u32[]{:S(2)}) collective-permute-start(f32[4,8,16,256]{3,2,1,0:T(8,128)S(1)} %pad_maximum_fusion.1), channel_id=1, source_target_pairs={{0,4},{4,0},{8,12},{12,8},{16,20},{20,16},{24,28},{28,24},{1,5},{5... | collective-permute-start | bytes 1572872 | tf_op jit(solution)/shard_map/rows_core_far/ppermute | solution.py:18
  (1 other events, 1.3 us)

commit v11 on v10

--- a/solution.py
+++ b/solution.py
@@ -203,28 +203,25 @@
     near_second, near_first, _ = lax.optimization_barrier((near_second, near_first, far_own))
     near_across = swap(near_second, "dp", first_link, "rows_relay_near")
     far_across = swap(far_second, "dp", first_link, "rows_relay_far")
-    near_rows = jnp.stack([near_own, near_first, near_second, near_across])
-    near_rows, _, first_new, second_new = lax.optimization_barrier(
-        (near_rows, far_second, first_new, second_new)
-    )
-    far_rows = jnp.stack([far_own, far_first, far_second, far_across])
-
+    other = {}
+    rows_first = jnp.stack([near_own, near_first, near_second])
+    copied = swap(rows_first, "dp", core, "rows_core_first")
+    other.update(zip((0, 1, 2), copied))
+    rows_second = jnp.stack([near_across, far_own, far_second])
+    copied = swap(rows_second, "dp", core, "rows_core_second")
+    copied, first_new, second_new = lax.optimization_barrier((copied, first_new, second_new))
+    other.update(zip((3, 4, 6), copied))
+    rows_last = jnp.stack([far_first, far_across])
+    copied = swap(rows_last, "dp", core, "rows_core_last")
+    other.update(zip((5, 7), copied))
+
+    rows = [near_own, near_first, near_second, near_across, far_own, far_first, far_second, far_across]
+    masks = (0, first_chip, second_chip, across)
+    other_masks = (core, second_chip ^ core, first_chip ^ core, across ^ core)
     updated = jnp.zeros((home_count, width, width), jnp.float32)
-    for what, place, rows in (
-        ("near", shard_half, near_rows),
-        ("far", 1 - shard_half, far_rows),
-    ):
-        other = swap(rows, "dp", core, f"rows_core_{what}")
-        for mask, values in (
-            (0, rows[0]),
-            (first_chip, rows[1]),
-            (second_chip, rows[2]),
-            (across, rows[3]),
-            (core, other[0]),
-            (second_chip ^ core, other[1]),
-            (first_chip ^ core, other[2]),
-            (across ^ core, other[3]),
-        ):
+    for part in (0, 1, 2, 3, 4, 6, 5, 7):
+        place = shard_half if part < 4 else 1 - shard_half
+        for mask, values in ((masks[part % 4], rows[part]), (other_masks[part % 4], other[part])):
             start = ((data_here ^ mask) * 2 + place) * (row_count // 2)
             updated = lax.dynamic_update_slice_in_dim(updated, values, start, axis=1)
     return updated, first_new[None, None, None], second_new[None, None, None]

time: 79.5 us -> 79.1 us (level)
    ppermute x24 -> x25, waiting for transfers between devices: 19.8 us -> 19.3 us  [swap(): return lax.ppermute(values, name, pairs)]
    ppermute x24 -> x25, starting transfers between devices: 25.4 us -> 25.5 us  [swap(): return lax.ppermute(values, name, pairs)]
  transfers between devices with their start and end apart: 24 -> 25, of which waited for: 12 -> 12; matrix products, arithmetic and copies ran while one was open for 2% -> 2% of each run, Pallas kernels for 0% -> 0%
where the time goes in v11:
time: 79.1 us; the launch traced here: 78.9 us
  blocking collectives  26.5 us (34%)
  starting transfers between devices  25.5 us (32%)
  waiting for transfers between devices  19.3 us (24%)
  local copies, waits for them, and re-layouts  3.8 us (5%)
  matrix products  1.95 us (2%)
  between operations  1.28 us (2%)
    ppermute x25, starting transfers between devices, swap(): return lax.ppermute(values, name, pairs)  25.5 us
    ppermute x25, waiting for transfers between devices, swap(): return lax.ppermute(values, name, pairs)  19.3 us
    all_to_all x1, blocking collectives, routed(): lax.all_to_all(leaving.reshape((device_total,) + piece), ('dp', 'shard'),...  13.7 us
    all_to_all x1, blocking collectives, routed(): lax.all_to_all(change.reshape((device_total,) + piece), ('dp', 'shard'),...  12.7 us
  transfers between devices with their start and end apart: 25, of which 12 were waited for; matrix products, arithmetic and copies ran while one was open for 2% of the time, Pallas kernels for 0%

profile of v11, /device:TPU:0, one launch (start us, length us, event | category | flops | bytes accessed | tf_op | source)
XLA Modules:
  0.0 78.9 jit_solution(16510854276520985596)
XLA Ops:
  0.7 1.3 %dynamic-slice_bitcast_fusion = (bf16[8,4,32,256]{3,2,1,0:T(8,128)(2,1)S(1)}, bf16[8,4,32,256]{3,2,1,0:T(8,128)(2,1)S(1)}) fusion(bf16[8,4,2,32,256]{4,3,2,1,0:T(8,128)(2,1)} %bitcast.188, s32[]{:T(128)S(6)} %select_n.161, s32[]{:T(128)S(6)} %select_n.160), kind=kLoop, calls=%fused_computation.1 | loop fusion | bytes 2097160 | tf_op jit(solution)/shard_map/jit(dynamic_index_in_dim)/squeeze | solution.py:22
  3.3 0.6 collective-permute-done
  4.0 2.9 %collective-permute-start.9 = (f32[8,16,256]{2,1,0:T(8,128)S(1)}, f32[8,16,256]{2,1,0:T(8,128)S(1)}, u32[]{:S(2)}, u32[]{:S(2)}) collective-permute-start(f32[8,16,256]{2,1,0:T(8,128)S(1)} %get-tuple-element.42), channel_id=1, source_target_pairs={{0,8},{4,20},{8,0},{12,28},{16,24},{20,4},{24,16},{28,12},{1,9},{5... | collective-permute-start | bytes 393224 | tf_op jit(solution)/shard_map/sum_across_far/ppermute | solution.py:18
  7.1 1.0 %collective-permute-start.8 = (f32[8,16,256]{2,1,0:T(8,128)S(1)}, f32[8,16,256]{2,1,0:T(8,128)S(1)}, u32[]{:S(2)}, u32[]{:S(2)}) collective-permute-start(f32[8,16,256]{2,1,0:T(8,128)S(1)} %get-tuple-element.40), channel_id=1, source_target_pairs={{0,8},{4,20},{8,0},{12,28},{16,24},{20,4},{24,16},{28,12},{1,9},{5... | collective-permute-start | bytes 393224 | tf_op jit(solution)/shard_map/sum_first_far/ppermute | solution.py:18
  8.1 1.1 %collective-permute-start.3 = (f32[8,16,256]{2,1,0:T(8,128)S(1)}, f32[8,16,256]{2,1,0:T(8,128)S(1)}, u32[]{:S(2)}, u32[]{:S(2)}) collective-permute-start(f32[8,16,256]{2,1,0:T(8,128)S(1)} %get-tuple-element.35), channel_id=1, source_target_pairs={{0,8},{4,20},{8,0},{12,28},{16,24},{20,4},{24,16},{28,12},{1,9},{5... | collective-permute-start | bytes 393224 | tf_op jit(solution)/shard_map/sum_across_near/ppermute | solution.py:18
  9.2 0.6 collective-permute-done.9
  9.8 2.1 %collective-permute-start.10 = (f32[8,16,256]{2,1,0:T(8,128)S(1)}, f32[8,16,256]{2,1,0:T(8,128)S(1)}, u32[]{:S(2)}, u32[]{:S(2)}) collective-permute-start(f32[8,16,256]{2,1,0:T(8,128)S(1)} %add.226), channel_id=1, source_target_pairs={{0,16},{4,12},{8,24},{12,4},{16,0},{20,28},{24,8},{28,20},{1,17},{... | collective-permute-start | bytes 393224 | tf_op jit(solution)/shard_map/sum_relay_far/ppermute | solution.py:18
  12.0 1.6 %collective-permute-start.6 = (f32[8,16,256]{2,1,0:T(8,128)S(1)}, f32[8,16,256]{2,1,0:T(8,128)S(1)}, u32[]{:S(2)}, u32[]{:S(2)}) collective-permute-start(f32[8,16,256]{2,1,0:T(8,128)S(1)} %get-tuple-element.36), channel_id=1, source_target_pairs={{0,8},{4,20},{8,0},{12,28},{16,24},{20,4},{24,16},{28,12},{1,9},{5... | collective-permute-start | bytes 393224 | tf_op jit(solution)/shard_map/sum_first_near/ppermute | solution.py:18
  13.6 1.3 %collective-permute-done.3 = f32[8,16,256]{2,1,0:T(8,128)S(1)} collective-permute-done((f32[8,16,256]{2,1,0:T(8,128)S(1)}, f32[8,16,256]{2,1,0:T(8,128)S(1)}, u32[]{:S(2)}, u32[]{:S(2)}) %collective-permute-start.3) | collective-permute-done | bytes 131104 | tf_op jit(solution)/shard_map/sum_across_near/ppermute | solution.py:18
  14.9 1.3 %collective-permute-start.4 = (f32[8,16,256]{2,1,0:T(8,128)S(1)}, f32[8,16,256]{2,1,0:T(8,128)S(1)}, u32[]{:S(2)}, u32[]{:S(2)}) collective-permute-start(f32[8,16,256]{2,1,0:T(8,128)S(1)} %add.219), channel_id=1, source_target_pairs={{0,16},{4,12},{8,24},{12,4},{16,0},{20,28},{24,8},{28,20},{1,17},{... | collective-permute-start | bytes 393224 | tf_op jit(solution)/shard_map/sum_relay_near/ppermute | solution.py:18
  16.3 2.8 %collective-permute-start.12 = (f32[8,8,256]{2,1,0:T(8,128)S(1)}, f32[8,8,256]{2,1,0:T(8,128)S(1)}, u32[]{:S(2)}, u32[]{:S(2)}) collective-permute-start(f32[8,8,256]{2,1,0:T(8,128)S(1)} %get-tuple-element.79), channel_id=1, source_target_pairs={{0,2},{1,3},{2,0},{3,1},{4,6},{5,7},{6,4},{7,5},{8,10},{9,11},{10,... | collective-permute-start | bytes 196616 | tf_op jit(solution)/shard_map/shard_2/ppermute | solution.py:18
  19.1 1.3 %collective-permute-start.11 = (f32[8,8,256]{2,1,0:T(8,128)S(1)}, f32[8,8,256]{2,1,0:T(8,128)S(1)}, u32[]{:S(2)}, u32[]{:S(2)}) collective-permute-start(f32[8,8,256]{2,1,0:T(8,128)S(1)} %get-tuple-element.78), channel_id=1, source_target_pairs={{0,3},{1,2},{2,1},{3,0},{4,7},{5,6},{6,5},{7,4},{8,11},{9,10},{10,... | collective-permute-start | bytes 196616 | tf_op jit(solution)/shard_map/shard_3/ppermute | solution.py:18
  20.6 0.9 %collective-permute-start.7 = (f32[8,8,256]{2,1,0:T(8,128)S(1)}, f32[8,8,256]{2,1,0:T(8,128)S(1)}, u32[]{:S(2)}, u32[]{:S(2)}) collective-permute-start(f32[8,8,256]{2,1,0:T(8,128)S(1)} %get-tuple-element.77), channel_id=1, source_target_pairs={{0,1},{1,0},{2,3},{3,2},{4,5},{5,4},{6,7},{7,6},{8,9},{9,8},{10,11... | collective-permute-start | bytes 196616 | tf_op jit(solution)/shard_map/shard_1/ppermute | solution.py:18
  21.7 1.7 %collective-permute-done.12 = f32[8,8,256]{2,1,0:T(8,128)S(1)} collective-permute-done((f32[8,8,256]{2,1,0:T(8,128)S(1)}, f32[8,8,256]{2,1,0:T(8,128)S(1)}, u32[]{:S(2)}, u32[]{:S(2)}) %collective-permute-start.12) | collective-permute-done | bytes 65568 | tf_op jit(solution)/shard_map/shard_2/ppermute | solution.py:18
  23.5 1.8 %collective-permute-done.11 = f32[8,8,256]{2,1,0:T(8,128)S(1)} collective-permute-done((f32[8,8,256]{2,1,0:T(8,128)S(1)}, f32[8,8,256]{2,1,0:T(8,128)S(1)}, u32[]{:S(2)}, u32[]{:S(2)}) %collective-permute-start.11) | collective-permute-done | bytes 65568 | tf_op jit(solution)/shard_map/shard_3/ppermute | solution.py:18
  26.1 13.7 %all_to_all.10 = f32[32,8,256]{2,1,0:T(8,128)S(1)} all-to-all(f32[32,8,256]{2,1,0:T(8,128)S(1)} %copy.68), channel_id=1, replica_groups=mesh['dp'=8,'shard'=4] {'dp','shard'}, dimensions={0} | all-to-all | bytes 524288 | tf_op jit(solution)/shard_map/all_to_all | solution.py:152
  41.4 12.7 %all_to_all.11 = f32[32,8,256]{2,1,0:T(8,128)S(1)} all-to-all(f32[32,8,256]{2,1,0:T(8,128)S(1)} %convolution_bitcast_fusion), channel_id=1, replica_groups=mesh['dp'=8,'shard'=4] {'dp','shard'}, dimensions={0} | all-to-all | bytes 524288 | tf_op jit(solution)/shard_map/all_to_all | solution.py:169
  54.5 1.2 %collective-permute-start.13 = (f32[8,8,256]{2,1,0:T(8,128)S(1)}, f32[8,8,256]{2,1,0:T(8,128)S(1)}, u32[]{:S(2)}, u32[]{:S(2)}) collective-permute-start(f32[8,8,256]{2,1,0:T(8,128)S(1)} %copy.70), channel_id=1, source_target_pairs={{0,1},{1,0},{2,3},{3,2},{4,5},{5,4},{6,7},{7,6},{8,9},{9,8},{10,11... | collective-permute-start | bytes 196616 | tf_op jit(solution)/shard_map/shard_1/ppermute | solution.py:18
  55.7 1.2 %collective-permute-start.17 = (f32[8,8,256]{2,1,0:T(8,128)S(1)}, f32[8,8,256]{2,1,0:T(8,128)S(1)}, u32[]{:S(2)}, u32[]{:S(2)}) collective-permute-start(f32[8,8,256]{2,1,0:T(8,128)S(1)} %copy.75), channel_id=1, source_target_pairs={{0,3},{1,2},{2,1},{3,0},{4,7},{5,6},{6,5},{7,4},{8,11},{9,10},{10,... | collective-permute-start | bytes 196616 | tf_op jit(solution)/shard_map/shard_3/ppermute | solution.py:18
  57.0 1.4 %collective-permute-start.16 = (f32[8,8,256]{2,1,0:T(8,128)S(1)}, f32[8,8,256]{2,1,0:T(8,128)S(1)}, u32[]{:S(2)}, u32[]{:S(2)}) collective-permute-start(f32[8,8,256]{2,1,0:T(8,128)S(1)} %copy.74), channel_id=1, source_target_pairs={{0,2},{1,3},{2,0},{3,1},{4,6},{5,7},{6,4},{7,5},{8,10},{9,11},{10,... | collective-permute-start | bytes 196616 | tf_op jit(solution)/shard_map/shard_2/ppermute | solution.py:18
  58.3 0.7 collective-permute-done.13
  59.0 1.0 %collective-permute-start.14 = (f32[8,16,256]{2,1,0:T(8,128)S(1)}, f32[8,16,256]{2,1,0:T(8,128)S(1)}, u32[]{:S(2)}, u32[]{:S(2)}) collective-permute-start(f32[8,16,256]{2,1,0:T(8,128)S(1)} %fusion.24), channel_id=1, source_target_pairs={{0,16},{4,12},{8,24},{12,4},{16,0},{20,28},{24,8},{28,20},{1,17},{... | collective-permute-start | bytes 393224 | tf_op jit(solution)/shard_map/rows_second_near/ppermute | solution.py:18
  60.5 1.3 %collective-permute-done.17 = f32[8,8,256]{2,1,0:T(8,128)S(1)} collective-permute-done((f32[8,8,256]{2,1,0:T(8,128)S(1)}, f32[8,8,256]{2,1,0:T(8,128)S(1)}, u32[]{:S(2)}, u32[]{:S(2)}) %collective-permute-start.17) | collective-permute-done | bytes 65568 | tf_op jit(solution)/shard_map/shard_3/ppermute | solution.py:18
  61.9 2.6 %collective-permute-done.16 = f32[8,8,256]{2,1,0:T(8,128)S(1)} collective-permute-done((f32[8,8,256]{2,1,0:T(8,128)S(1)}, f32[8,8,256]{2,1,0:T(8,128)S(1)}, u32[]{:S(2)}, u32[]{:S(2)}) %collective-permute-start.16) | collective-permute-done | bytes 65568 | tf_op jit(solution)/shard_map/shard_2/ppermute | solution.py:18
  64.5 1.0 %collective-permute-start.20 = (f32[8,16,256]{2,1,0:T(8,128)S(1)}, f32[8,16,256]{2,1,0:T(8,128)S(1)}, u32[]{:S(2)}, u32[]{:S(2)}) collective-permute-start(f32[8,16,256]{2,1,0:T(8,128)S(1)} %fusion.27), channel_id=1, source_target_pairs={{0,16},{4,12},{8,24},{12,4},{16,0},{20,28},{24,8},{28,20},{1,17},{... | collective-permute-start | bytes 393224 | tf_op jit(solution)/shard_map/rows_second_far/ppermute | solution.py:18
  65.5 0.8 %collective-permute-start.22 = (f32[8,16,256]{2,1,0:T(8,128)S(1)}, f32[8,16,256]{2,1,0:T(8,128)S(1)}, u32[]{:S(2)}, u32[]{:S(2)}) collective-permute-start(f32[8,16,256]{2,1,0:T(8,128)S(1)} %fusion.27), channel_id=1, source_target_pairs={{0,8},{4,20},{8,0},{12,28},{16,24},{20,4},{24,16},{28,12},{1,9},{5... | collective-permute-start | bytes 393224 | tf_op jit(solution)/shard_map/rows_first_far/ppermute | solution.py:18
  66.3 1.2 %collective-permute-start.19 = (f32[8,16,256]{2,1,0:T(8,128)S(1)}, f32[8,16,256]{2,1,0:T(8,128)S(1)}, u32[]{:S(2)}, u32[]{:S(2)}) collective-permute-start(f32[8,16,256]{2,1,0:T(8,128)S(1)} %collective-permute-done.14), channel_id=1, source_target_pairs={{0,8},{4,20},{8,0},{12,28},{16,24},{20,4},{24,16},{28,12},{1,9},{5... | collective-permute-start | bytes 393224 | tf_op jit(solution)/shard_map/rows_relay_near/ppermute | solution.py:18
  67.9 3.1 %collective-permute-done.20 = f32[8,16,256]{2,1,0:T(8,128)S(1)} collective-permute-done((f32[8,16,256]{2,1,0:T(8,128)S(1)}, f32[8,16,256]{2,1,0:T(8,128)S(1)}, u32[]{:S(2)}, u32[]{:S(2)}) %collective-permute-start.20) | collective-permute-done | bytes 131104 | tf_op jit(solution)/shard_map/rows_second_far/ppermute | solution.py:18
  70.9 0.9 %collective-permute-start.23 = (f32[8,16,256]{2,1,0:T(8,128)S(1)}, f32[8,16,256]{2,1,0:T(8,128)S(1)}, u32[]{:S(2)}, u32[]{:S(2)}) collective-permute-start(f32[8,16,256]{2,1,0:T(8,128)S(1)} %collective-permute-done.20), channel_id=1, source_target_pairs={{0,8},{4,20},{8,0},{12,28},{16,24},{20,4},{24,16},{28,12},{1,9},{5... | collective-permute-start | bytes 393224 | tf_op jit(solution)/shard_map/rows_relay_far/ppermute | solution.py:18
  72.0 3.9 %collective-permute-done.23 = f32[8,16,256]{2,1,0:T(8,128)S(1)} collective-permute-done((f32[8,16,256]{2,1,0:T(8,128)S(1)}, f32[8,16,256]{2,1,0:T(8,128)S(1)}, u32[]{:S(2)}, u32[]{:S(2)}) %collective-permute-start.23) | collective-permute-done | bytes 131104 | tf_op jit(solution)/shard_map/rows_relay_far/ppermute | solution.py:18
  76.3 1.2 %collective-permute-done.24 = f32[2,8,16,256]{3,2,1,0:T(8,128)S(1)} collective-permute-done((f32[2,8,16,256]{3,2,1,0:T(8,128)S(1)}, f32[2,8,16,256]{3,2,1,0:T(8,128)S(1)}, u32[]{:S(2)}, u32[]{:S(2)}) %collective-permute-start.24) | collective-permute-done | bytes 262176 | tf_op jit(solution)/shard_map/rows_core_last/ppermute | solution.py:18
  77.6 1.3 %copy-done.1 = f32[8,256,256]{2,1,0:T(8,128)} copy-done((f32[8,256,256]{2,1,0:T(8,128)}, f32[8,256,256]{2,1,0:T(8,128)S(1)}, u32[]{:S(2)}) %copy-start.1) | copy-done | bytes 2097176
  (100 shorter events, 6.0 us)
Async XLA Ops:
  0.6 39.6 %copy-start = (f32[1,1,1,256,256]{4,3,2,1,0:T(8,128)S(1)}, f32[1,1,1,256,256]{4,3,2,1,0:T(8,128)}, u32[]{:S(2)}) copy-start(f32[1,1,1,256,256]{4,3,2,1,0:T(8,128)} %param.10) | copy-start | bytes 786436
  2.2 1.7 %collective-permute-start = (f32[8,32,256]{2,1,0:T(8,128)S(1)}, f32[8,32,256]{2,1,0:T(8,128)S(1)}, u32[]{:S(2)}, u32[]{:S(2)}) collective-permute-start(f32[8,32,256]{2,1,0:T(8,128)S(1)} %get-tuple-element.61), channel_id=1, source_target_pairs={{0,4},{4,0},{8,12},{12,8},{16,20},{20,16},{24,28},{28,24},{1,5},{5... | collective-permute-start | bytes 786440 | tf_op jit(solution)/shard_map/sum_core_across/ppermute | solution.py:18
  2.7 4.2 %collective-permute-start.2 = (f32[8,32,256]{2,1,0:T(8,128)S(1)}, f32[8,32,256]{2,1,0:T(8,128)S(1)}, u32[]{:S(2)}, u32[]{:S(2)}) collective-permute-start(f32[8,32,256]{2,1,0:T(8,128)S(1)} %get-tuple-element.58), channel_id=1, source_target_pairs={{0,4},{4,0},{8,12},{12,8},{16,20},{20,16},{24,28},{28,24},{1,5},{5... | collective-permute-start | bytes 786440 | tf_op jit(solution)/shard_map/sum_core_second/ppermute | solution.py:18
  2.8 4.1 %collective-permute-start.5 = (f32[8,32,256]{2,1,0:T(8,128)S(1)}, f32[8,32,256]{2,1,0:T(8,128)S(1)}, u32[]{:S(2)}, u32[]{:S(2)}) collective-permute-start(f32[8,32,256]{2,1,0:T(8,128)S(1)} %get-tuple-element.59), channel_id=1, source_target_pairs={{0,4},{4,0},{8,12},{12,8},{16,20},{20,16},{24,28},{28,24},{1,5},{5... | collective-permute-start | bytes 786440 | tf_op jit(solution)/shard_map/sum_core_first/ppermute | solution.py:18
  3.2 3.6 %collective-permute-start.1 = (f32[8,32,256]{2,1,0:T(8,128)S(1)}, f32[8,32,256]{2,1,0:T(8,128)S(1)}, u32[]{:S(2)}, u32[]{:S(2)}) collective-permute-start(f32[8,32,256]{2,1,0:T(8,128)S(1)} %get-tuple-element.60), channel_id=1, source_target_pairs={{0,4},{4,0},{8,12},{12,8},{16,20},{20,16},{24,28},{28,24},{1,5},{5... | collective-permute-start | bytes 786440 | tf_op jit(solution)/shard_map/sum_core_own/ppermute | solution.py:18
  4.0 5.9 %collective-permute-start.9 = (f32[8,16,256]{2,1,0:T(8,128)S(1)}, f32[8,16,256]{2,1,0:T(8,128)S(1)}, u32[]{:S(2)}, u32[]{:S(2)}) collective-permute-start(f32[8,16,256]{2,1,0:T(8,128)S(1)} %get-tuple-element.42), channel_id=1, source_target_pairs={{0,8},{4,20},{8,0},{12,28},{16,24},{20,4},{24,16},{28,12},{1,9},{5... | collective-permute-start | bytes 393224 | tf_op jit(solution)/shard_map/sum_across_far/ppermute | solution.py:18
  7.0 14.5 %copy-start.8 = (s32[32]{0:T(128)S(1)}, s32[32]{0:T(128)}, u32[]{:S(2)}) copy-start(s32[32]{0:T(128)} %param.13) | copy-start | bytes 388
  7.1 6.5 %collective-permute-start.8 = (f32[8,16,256]{2,1,0:T(8,128)S(1)}, f32[8,16,256]{2,1,0:T(8,128)S(1)}, u32[]{:S(2)}, u32[]{:S(2)}) collective-permute-start(f32[8,16,256]{2,1,0:T(8,128)S(1)} %get-tuple-element.40), channel_id=1, source_target_pairs={{0,8},{4,20},{8,0},{12,28},{16,24},{20,4},{24,16},{28,12},{1,9},{5... | collective-permute-start | bytes 393224 | tf_op jit(solution)/shard_map/sum_first_far/ppermute | solution.py:18
  8.1 6.8 %collective-permute-start.3 = (f32[8,16,256]{2,1,0:T(8,128)S(1)}, f32[8,16,256]{2,1,0:T(8,128)S(1)}, u32[]{:S(2)}, u32[]{:S(2)}) collective-permute-start(f32[8,16,256]{2,1,0:T(8,128)S(1)} %get-tuple-element.35), channel_id=1, source_target_pairs={{0,8},{4,20},{8,0},{12,28},{16,24},{20,4},{24,16},{28,12},{1,9},{5... | collective-permute-start | bytes 393224 | tf_op jit(solution)/shard_map/sum_across_near/ppermute | solution.py:18
  9.8 6.4 %collective-permute-start.10 = (f32[8,16,256]{2,1,0:T(8,128)S(1)}, f32[8,16,256]{2,1,0:T(8,128)S(1)}, u32[]{:S(2)}, u32[]{:S(2)}) collective-permute-start(f32[8,16,256]{2,1,0:T(8,128)S(1)} %add.226), channel_id=1, source_target_pairs={{0,16},{4,12},{8,24},{12,4},{16,0},{20,28},{24,8},{28,20},{1,17},{... | collective-permute-start | bytes 393224 | tf_op jit(solution)/shard_map/sum_relay_far/ppermute | solution.py:18
  12.0 8.5 %collective-permute-start.6 = (f32[8,16,256]{2,1,0:T(8,128)S(1)}, f32[8,16,256]{2,1,0:T(8,128)S(1)}, u32[]{:S(2)}, u32[]{:S(2)}) collective-permute-start(f32[8,16,256]{2,1,0:T(8,128)S(1)} %get-tuple-element.36), channel_id=1, source_target_pairs={{0,8},{4,20},{8,0},{12,28},{16,24},{20,4},{24,16},{28,12},{1,9},{5... | collective-permute-start | bytes 393224 | tf_op jit(solution)/shard_map/sum_first_near/ppermute | solution.py:18
  14.9 24.9 %copy-start.2 = (f32[1,1,1,256,256]{4,3,2,1,0:T(8,128)S(1)}, f32[1,1,1,256,256]{4,3,2,1,0:T(8,128)}, u32[]{:S(2)}) copy-start(f32[1,1,1,256,256]{4,3,2,1,0:T(8,128)} %param.9) | copy-start | bytes 786436
  14.9 5.6 %collective-permute-start.4 = (f32[8,16,256]{2,1,0:T(8,128)S(1)}, f32[8,16,256]{2,1,0:T(8,128)S(1)}, u32[]{:S(2)}, u32[]{:S(2)}) collective-permute-start(f32[8,16,256]{2,1,0:T(8,128)S(1)} %add.219), channel_id=1, source_target_pairs={{0,16},{4,12},{8,24},{12,4},{16,0},{20,28},{24,8},{28,20},{1,17},{... | collective-permute-start | bytes 393224 | tf_op jit(solution)/shard_map/sum_relay_near/ppermute | solution.py:18
  16.3 7.1 %collective-permute-start.12 = (f32[8,8,256]{2,1,0:T(8,128)S(1)}, f32[8,8,256]{2,1,0:T(8,128)S(1)}, u32[]{:S(2)}, u32[]{:S(2)}) collective-permute-start(f32[8,8,256]{2,1,0:T(8,128)S(1)} %get-tuple-element.79), channel_id=1, source_target_pairs={{0,2},{1,3},{2,0},{3,1},{4,6},{5,7},{6,4},{7,5},{8,10},{9,11},{10,... | collective-permute-start | bytes 196616 | tf_op jit(solution)/shard_map/shard_2/ppermute | solution.py:18
  19.1 6.2 %collective-permute-start.11 = (f32[8,8,256]{2,1,0:T(8,128)S(1)}, f32[8,8,256]{2,1,0:T(8,128)S(1)}, u32[]{:S(2)}, u32[]{:S(2)}) collective-permute-start(f32[8,8,256]{2,1,0:T(8,128)S(1)} %get-tuple-element.78), channel_id=1, source_target_pairs={{0,3},{1,2},{2,1},{3,0},{4,7},{5,6},{6,5},{7,4},{8,11},{9,10},{10,... | collective-permute-start | bytes 196616 | tf_op jit(solution)/shard_map/shard_3/ppermute | solution.py:18
  20.5 19.7 %copy-start.4 = (f32[1,1,1,256,256]{4,3,2,1,0:T(8,128)S(1)}, f32[1,1,1,256,256]{4,3,2,1,0:T(8,128)}, u32[]{:S(2)}) copy-start(f32[1,1,1,256,256]{4,3,2,1,0:T(8,128)} %param.11) | copy-start | bytes 786436
  20.5 19.7 %copy-start.5 = (f32[1,1,1,256,256]{4,3,2,1,0:T(8,128)S(1)}, f32[1,1,1,256,256]{4,3,2,1,0:T(8,128)}, u32[]{:S(2)}) copy-start(f32[1,1,1,256,256]{4,3,2,1,0:T(8,128)} %param.12) | copy-start | bytes 786436
  20.6 5.0 %collective-permute-start.7 = (f32[8,8,256]{2,1,0:T(8,128)S(1)}, f32[8,8,256]{2,1,0:T(8,128)S(1)}, u32[]{:S(2)}, u32[]{:S(2)}) collective-permute-start(f32[8,8,256]{2,1,0:T(8,128)S(1)} %get-tuple-element.77), channel_id=1, source_target_pairs={{0,1},{1,0},{2,3},{3,2},{4,5},{5,4},{6,7},{7,6},{8,9},{9,8},{10,11... | collective-permute-start | bytes 196616 | tf_op jit(solution)/shard_map/shard_1/ppermute | solution.py:18
  40.6 13.9 %copy-start.6 = (f32[256,256]{1,0:T(8,128)}, f32[256,256]{1,0:T(8,128)S(1)}, u32[]{:S(2)}) copy-start(f32[256,256]{1,0:T(8,128)S(1)} %get-tuple-element.51) | copy-start | bytes 786436
  40.7 18.3 %copy-start.3 = (f32[8,32,256]{2,1,0:T(8,128)S(1)}, f32[8,32,256]{2,1,0:T(8,128)}, u32[]{:S(2)}) copy-start(f32[8,32,256]{2,1,0:T(8,128)} %param.8) | copy-start | bytes 786436
  54.5 4.5 %collective-permute-start.13 = (f32[8,8,256]{2,1,0:T(8,128)S(1)}, f32[8,8,256]{2,1,0:T(8,128)S(1)}, u32[]{:S(2)}, u32[]{:S(2)}) collective-permute-start(f32[8,8,256]{2,1,0:T(8,128)S(1)} %copy.70), channel_id=1, source_target_pairs={{0,1},{1,0},{2,3},{3,2},{4,5},{5,4},{6,7},{7,6},{8,9},{9,8},{10,11... | collective-permute-start | bytes 196616 | tf_op jit(solution)/shard_map/shard_1/ppermute | solution.py:18
  55.7 6.1 %collective-permute-start.17 = (f32[8,8,256]{2,1,0:T(8,128)S(1)}, f32[8,8,256]{2,1,0:T(8,128)S(1)}, u32[]{:S(2)}, u32[]{:S(2)}) collective-permute-start(f32[8,8,256]{2,1,0:T(8,128)S(1)} %copy.75), channel_id=1, source_target_pairs={{0,3},{1,2},{2,1},{3,0},{4,7},{5,6},{6,5},{7,4},{8,11},{9,10},{10,... | collective-permute-start | bytes 196616 | tf_op jit(solution)/shard_map/shard_3/ppermute | solution.py:18
  57.0 7.5 %collective-permute-start.16 = (f32[8,8,256]{2,1,0:T(8,128)S(1)}, f32[8,8,256]{2,1,0:T(8,128)S(1)}, u32[]{:S(2)}, u32[]{:S(2)}) collective-permute-start(f32[8,8,256]{2,1,0:T(8,128)S(1)} %copy.74), channel_id=1, source_target_pairs={{0,2},{1,3},{2,0},{3,1},{4,6},{5,7},{6,4},{7,5},{8,10},{9,11},{10,... | collective-permute-start | bytes 196616 | tf_op jit(solution)/shard_map/shard_2/ppermute | solution.py:18
  59.0 7.3 %collective-permute-start.14 = (f32[8,16,256]{2,1,0:T(8,128)S(1)}, f32[8,16,256]{2,1,0:T(8,128)S(1)}, u32[]{:S(2)}, u32[]{:S(2)}) collective-permute-start(f32[8,16,256]{2,1,0:T(8,128)S(1)} %fusion.24), channel_id=1, source_target_pairs={{0,16},{4,12},{8,24},{12,4},{16,0},{20,28},{24,8},{28,20},{1,17},{... | collective-permute-start | bytes 393224 | tf_op jit(solution)/shard_map/rows_second_near/ppermute | solution.py:18
  60.0 6.3 %collective-permute-start.15 = (f32[8,16,256]{2,1,0:T(8,128)S(1)}, f32[8,16,256]{2,1,0:T(8,128)S(1)}, u32[]{:S(2)}, u32[]{:S(2)}) collective-permute-start(f32[8,16,256]{2,1,0:T(8,128)S(1)} %fusion.24), channel_id=1, source_target_pairs={{0,8},{4,20},{8,0},{12,28},{16,24},{20,4},{24,16},{28,12},{1,9},{5... | collective-permute-start | bytes 393224 | tf_op jit(solution)/shard_map/rows_first_near/ppermute | solution.py:18
  64.5 6.4 %collective-permute-start.20 = (f32[8,16,256]{2,1,0:T(8,128)S(1)}, f32[8,16,256]{2,1,0:T(8,128)S(1)}, u32[]{:S(2)}, u32[]{:S(2)}) collective-permute-start(f32[8,16,256]{2,1,0:T(8,128)S(1)} %fusion.27), channel_id=1, source_target_pairs={{0,16},{4,12},{8,24},{12,4},{16,0},{20,28},{24,8},{28,20},{1,17},{... | collective-permute-start | bytes 393224 | tf_op jit(solution)/shard_map/rows_second_far/ppermute | solution.py:18
  65.5 6.5 %collective-permute-start.22 = (f32[8,16,256]{2,1,0:T(8,128)S(1)}, f32[8,16,256]{2,1,0:T(8,128)S(1)}, u32[]{:S(2)}, u32[]{:S(2)}) collective-permute-start(f32[8,16,256]{2,1,0:T(8,128)S(1)} %fusion.27), channel_id=1, source_target_pairs={{0,8},{4,20},{8,0},{12,28},{16,24},{20,4},{24,16},{28,12},{1,9},{5... | collective-permute-start | bytes 393224 | tf_op jit(solution)/shard_map/rows_first_far/ppermute | solution.py:18
  66.3 5.5 %collective-permute-start.19 = (f32[8,16,256]{2,1,0:T(8,128)S(1)}, f32[8,16,256]{2,1,0:T(8,128)S(1)}, u32[]{:S(2)}, u32[]{:S(2)}) collective-permute-start(f32[8,16,256]{2,1,0:T(8,128)S(1)} %collective-permute-done.14), channel_id=1, source_target_pairs={{0,8},{4,20},{8,0},{12,28},{16,24},{20,4},{24,16},{28,12},{1,9},{5... | collective-permute-start | bytes 393224 | tf_op jit(solution)/shard_map/rows_relay_near/ppermute | solution.py:18
  67.6 8.4 %collective-permute-start.18 = (f32[3,8,16,256]{3,2,1,0:T(8,128)S(1)}, f32[3,8,16,256]{3,2,1,0:T(8,128)S(1)}, u32[]{:S(2)}, u32[]{:S(2)}) collective-permute-start(f32[3,8,16,256]{3,2,1,0:T(8,128)S(1)} %pad_maximum_fusion), channel_id=1, source_target_pairs={{0,4},{4,0},{8,12},{12,8},{16,20},{20,16},{24,28},{28,24},{1,5},{5... | collective-permute-start | bytes 1179656 | tf_op jit(solution)/shard_map/rows_core_first/ppermute | solution.py:18
  70.9 5.0 %collective-permute-start.23 = (f32[8,16,256]{2,1,0:T(8,128)S(1)}, f32[8,16,256]{2,1,0:T(8,128)S(1)}, u32[]{:S(2)}, u32[]{:S(2)}) collective-permute-start(f32[8,16,256]{2,1,0:T(8,128)S(1)} %collective-permute-done.20), channel_id=1, source_target_pairs={{0,8},{4,20},{8,0},{12,28},{16,24},{20,4},{24,16},{28,12},{1,9},{5... | collective-permute-start | bytes 393224 | tf_op jit(solution)/shard_map/rows_relay_far/ppermute | solution.py:18
  71.9 4.3 %collective-permute-start.21 = (f32[3,8,16,256]{3,2,1,0:T(8,128)S(1)}, f32[3,8,16,256]{3,2,1,0:T(8,128)S(1)}, u32[]{:S(2)}, u32[]{:S(2)}) collective-permute-start(f32[3,8,16,256]{3,2,1,0:T(8,128)S(1)} %pad_maximum_fusion.1), channel_id=1, source_target_pairs={{0,4},{4,0},{8,12},{12,8},{16,20},{20,16},{24,28},{28,24},{1,5},{5... | collective-permute-start | bytes 1179656 | tf_op jit(solution)/shard_map/rows_core_second/ppermute | solution.py:18
  75.9 1.6 %collective-permute-start.24 = (f32[2,8,16,256]{3,2,1,0:T(8,128)S(1)}, f32[2,8,16,256]{3,2,1,0:T(8,128)S(1)}, u32[]{:S(2)}, u32[]{:S(2)}) collective-permute-start(f32[2,8,16,256]{3,2,1,0:T(8,128)S(1)} %pad_maximum_fusion.3), channel_id=1, source_target_pairs={{0,4},{4,0},{8,12},{12,8},{16,20},{20,16},{24,28},{28,24},{1,5},{5... | collective-permute-start | bytes 786440 | tf_op jit(solution)/shard_map/rows_core_last/ppermute | solution.py:18
  (2 other events, 15.2 us)

commit v12 on v11

--- a/solution.py
+++ b/solution.py
@@ -199,10 +199,11 @@
     near_first = swap(near_own, "dp", first_link, "rows_first_near")
     far_own = stepped(both(returned[2], returned[3], shard_low), set_of(params, 1 - shard_half))
     far_second = swap(far_own, "dp", second_link, "rows_second_far")
-    far_first = swap(far_own, "dp", first_link, "rows_first_far")
     near_second, near_first, _ = lax.optimization_barrier((near_second, near_first, far_own))
     near_across = swap(near_second, "dp", first_link, "rows_relay_near")
     far_across = swap(far_second, "dp", first_link, "rows_relay_far")
+    far_last, _ = lax.optimization_barrier((far_own, near_across))
+    far_first = swap(far_last, "dp", first_link, "rows_first_far")
     other = {}
     rows_first = jnp.stack([near_own, near_first, near_second])
     copied = swap(rows_first, "dp", core, "rows_core_first")

time: 79.1 us -> 79.6 us (level)
  transfers between devices with their start and end apart: 25 -> 25, of which waited for: 12 -> 13; matrix products, arithmetic and copies ran while one was open for 2% -> 2% of each run, Pallas kernels for 0% -> 0%
where the time goes in v12:
time: 79.6 us; the launch traced here: 79.5 us
  blocking collectives  26.5 us (33%)
  starting transfers between devices  25.4 us (32%)
  waiting for transfers between devices  19.9 us (25%)
  local copies, waits for them, and re-layouts  3.8 us (5%)
  matrix products  1.95 us (2%)
  between operations  1.28 us (2%)
    ppermute x25, starting transfers between devices, swap(): return lax.ppermute(values, name, pairs)  25.4 us
    ppermute x25, waiting for transfers between devices, swap(): return lax.ppermute(values, name, pairs)  19.9 us
    all_to_all x1, blocking collectives, routed(): lax.all_to_all(leaving.reshape((device_total,) + piece), ('dp', 'shard'),...  13.7 us
    all_to_all x1, blocking collectives, routed(): lax.all_to_all(change.reshape((device_total,) + piece), ('dp', 'shard'),...  12.7 us
  transfers between devices with their start and end apart: 25, of which 13 were waited for; matrix products, arithmetic and copies ran while one was open for 2% of the time, Pallas kernels for 0%

profile of v12, /device:TPU:0, one launch (start us, length us, event | category | flops | bytes accessed | tf_op | source)
XLA Modules:
  0.0 79.5 jit_solution(16068694619697077064)
XLA Ops:
  0.7 1.3 %dynamic-slice_bitcast_fusion = (bf16[8,4,32,256]{3,2,1,0:T(8,128)(2,1)S(1)}, bf16[8,4,32,256]{3,2,1,0:T(8,128)(2,1)S(1)}) fusion(bf16[8,4,2,32,256]{4,3,2,1,0:T(8,128)(2,1)} %bitcast.188, s32[]{:T(128)S(6)} %select_n.161, s32[]{:T(128)S(6)} %select_n.160), kind=kLoop, calls=%fused_computation.1 | loop fusion | bytes 2097160 | tf_op jit(solution)/shard_map/jit(dynamic_index_in_dim)/squeeze | solution.py:22
  4.0 2.9 %collective-permute-start.9 = (f32[8,16,256]{2,1,0:T(8,128)S(1)}, f32[8,16,256]{2,1,0:T(8,128)S(1)}, u32[]{:S(2)}, u32[]{:S(2)}) collective-permute-start(f32[8,16,256]{2,1,0:T(8,128)S(1)} %get-tuple-element.43), channel_id=1, source_target_pairs={{0,8},{4,20},{8,0},{12,28},{16,24},{20,4},{24,16},{28,12},{1,9},{5... | collective-permute-start | bytes 393224 | tf_op jit(solution)/shard_map/sum_across_far/ppermute | solution.py:18
  7.1 1.0 %collective-permute-start.8 = (f32[8,16,256]{2,1,0:T(8,128)S(1)}, f32[8,16,256]{2,1,0:T(8,128)S(1)}, u32[]{:S(2)}, u32[]{:S(2)}) collective-permute-start(f32[8,16,256]{2,1,0:T(8,128)S(1)} %get-tuple-element.41), channel_id=1, source_target_pairs={{0,8},{4,20},{8,0},{12,28},{16,24},{20,4},{24,16},{28,12},{1,9},{5... | collective-permute-start | bytes 393224 | tf_op jit(solution)/shard_map/sum_first_far/ppermute | solution.py:18
  8.1 1.1 %collective-permute-start.3 = (f32[8,16,256]{2,1,0:T(8,128)S(1)}, f32[8,16,256]{2,1,0:T(8,128)S(1)}, u32[]{:S(2)}, u32[]{:S(2)}) collective-permute-start(f32[8,16,256]{2,1,0:T(8,128)S(1)} %get-tuple-element.36), channel_id=1, source_target_pairs={{0,8},{4,20},{8,0},{12,28},{16,24},{20,4},{24,16},{28,12},{1,9},{5... | collective-permute-start | bytes 393224 | tf_op jit(solution)/shard_map/sum_across_near/ppermute | solution.py:18
  9.2 0.6 collective-permute-done.9
  9.8 2.1 %collective-permute-start.10 = (f32[8,16,256]{2,1,0:T(8,128)S(1)}, f32[8,16,256]{2,1,0:T(8,128)S(1)}, u32[]{:S(2)}, u32[]{:S(2)}) collective-permute-start(f32[8,16,256]{2,1,0:T(8,128)S(1)} %add.226), channel_id=1, source_target_pairs={{0,16},{4,12},{8,24},{12,4},{16,0},{20,28},{24,8},{28,20},{1,17},{... | collective-permute-start | bytes 393224 | tf_op jit(solution)/shard_map/sum_relay_far/ppermute | solution.py:18
  12.0 1.6 %collective-permute-start.6 = (f32[8,16,256]{2,1,0:T(8,128)S(1)}, f32[8,16,256]{2,1,0:T(8,128)S(1)}, u32[]{:S(2)}, u32[]{:S(2)}) collective-permute-start(f32[8,16,256]{2,1,0:T(8,128)S(1)} %get-tuple-element.37), channel_id=1, source_target_pairs={{0,8},{4,20},{8,0},{12,28},{16,24},{20,4},{24,16},{28,12},{1,9},{5... | collective-permute-start | bytes 393224 | tf_op jit(solution)/shard_map/sum_first_near/ppermute | solution.py:18
  13.6 1.3 %collective-permute-done.3 = f32[8,16,256]{2,1,0:T(8,128)S(1)} collective-permute-done((f32[8,16,256]{2,1,0:T(8,128)S(1)}, f32[8,16,256]{2,1,0:T(8,128)S(1)}, u32[]{:S(2)}, u32[]{:S(2)}) %collective-permute-start.3) | collective-permute-done | bytes 131104 | tf_op jit(solution)/shard_map/sum_across_near/ppermute | solution.py:18
  14.9 1.3 %collective-permute-start.4 = (f32[8,16,256]{2,1,0:T(8,128)S(1)}, f32[8,16,256]{2,1,0:T(8,128)S(1)}, u32[]{:S(2)}, u32[]{:S(2)}) collective-permute-start(f32[8,16,256]{2,1,0:T(8,128)S(1)} %add.219), channel_id=1, source_target_pairs={{0,16},{4,12},{8,24},{12,4},{16,0},{20,28},{24,8},{28,20},{1,17},{... | collective-permute-start | bytes 393224 | tf_op jit(solution)/shard_map/sum_relay_near/ppermute | solution.py:18
  16.3 2.8 %collective-permute-start.12 = (f32[8,8,256]{2,1,0:T(8,128)S(1)}, f32[8,8,256]{2,1,0:T(8,128)S(1)}, u32[]{:S(2)}, u32[]{:S(2)}) collective-permute-start(f32[8,8,256]{2,1,0:T(8,128)S(1)} %get-tuple-element.81), channel_id=1, source_target_pairs={{0,2},{1,3},{2,0},{3,1},{4,6},{5,7},{6,4},{7,5},{8,10},{9,11},{10,... | collective-permute-start | bytes 196616 | tf_op jit(solution)/shard_map/shard_2/ppermute | solution.py:18
  19.1 1.3 %collective-permute-start.11 = (f32[8,8,256]{2,1,0:T(8,128)S(1)}, f32[8,8,256]{2,1,0:T(8,128)S(1)}, u32[]{:S(2)}, u32[]{:S(2)}) collective-permute-start(f32[8,8,256]{2,1,0:T(8,128)S(1)} %get-tuple-element.80), channel_id=1, source_target_pairs={{0,3},{1,2},{2,1},{3,0},{4,7},{5,6},{6,5},{7,4},{8,11},{9,10},{10,... | collective-permute-start | bytes 196616 | tf_op jit(solution)/shard_map/shard_3/ppermute | solution.py:18
  20.6 0.9 %collective-permute-start.7 = (f32[8,8,256]{2,1,0:T(8,128)S(1)}, f32[8,8,256]{2,1,0:T(8,128)S(1)}, u32[]{:S(2)}, u32[]{:S(2)}) collective-permute-start(f32[8,8,256]{2,1,0:T(8,128)S(1)} %get-tuple-element.79), channel_id=1, source_target_pairs={{0,1},{1,0},{2,3},{3,2},{4,5},{5,4},{6,7},{7,6},{8,9},{9,8},{10,11... | collective-permute-start | bytes 196616 | tf_op jit(solution)/shard_map/shard_1/ppermute | solution.py:18
  21.7 1.7 %collective-permute-done.12 = f32[8,8,256]{2,1,0:T(8,128)S(1)} collective-permute-done((f32[8,8,256]{2,1,0:T(8,128)S(1)}, f32[8,8,256]{2,1,0:T(8,128)S(1)}, u32[]{:S(2)}, u32[]{:S(2)}) %collective-permute-start.12) | collective-permute-done | bytes 65568 | tf_op jit(solution)/shard_map/shard_2/ppermute | solution.py:18
  23.5 1.8 %collective-permute-done.11 = f32[8,8,256]{2,1,0:T(8,128)S(1)} collective-permute-done((f32[8,8,256]{2,1,0:T(8,128)S(1)}, f32[8,8,256]{2,1,0:T(8,128)S(1)}, u32[]{:S(2)}, u32[]{:S(2)}) %collective-permute-start.11) | collective-permute-done | bytes 65568 | tf_op jit(solution)/shard_map/shard_3/ppermute | solution.py:18
  26.1 13.7 %all_to_all.10 = f32[32,8,256]{2,1,0:T(8,128)S(1)} all-to-all(f32[32,8,256]{2,1,0:T(8,128)S(1)} %copy.68), channel_id=1, replica_groups=mesh['dp'=8,'shard'=4] {'dp','shard'}, dimensions={0} | all-to-all | bytes 524288 | tf_op jit(solution)/shard_map/all_to_all | solution.py:152
  41.4 12.7 %all_to_all.11 = f32[32,8,256]{2,1,0:T(8,128)S(1)} all-to-all(f32[32,8,256]{2,1,0:T(8,128)S(1)} %convolution_bitcast_fusion), channel_id=1, replica_groups=mesh['dp'=8,'shard'=4] {'dp','shard'}, dimensions={0} | all-to-all | bytes 524288 | tf_op jit(solution)/shard_map/all_to_all | solution.py:169
  54.5 1.2 %collective-permute-start.13 = (f32[8,8,256]{2,1,0:T(8,128)S(1)}, f32[8,8,256]{2,1,0:T(8,128)S(1)}, u32[]{:S(2)}, u32[]{:S(2)}) collective-permute-start(f32[8,8,256]{2,1,0:T(8,128)S(1)} %copy.70), channel_id=1, source_target_pairs={{0,1},{1,0},{2,3},{3,2},{4,5},{5,4},{6,7},{7,6},{8,9},{9,8},{10,11... | collective-permute-start | bytes 196616 | tf_op jit(solution)/shard_map/shard_1/ppermute | solution.py:18
  55.7 1.2 %collective-permute-start.17 = (f32[8,8,256]{2,1,0:T(8,128)S(1)}, f32[8,8,256]{2,1,0:T(8,128)S(1)}, u32[]{:S(2)}, u32[]{:S(2)}) collective-permute-start(f32[8,8,256]{2,1,0:T(8,128)S(1)} %copy.75), channel_id=1, source_target_pairs={{0,3},{1,2},{2,1},{3,0},{4,7},{5,6},{6,5},{7,4},{8,11},{9,10},{10,... | collective-permute-start | bytes 196616 | tf_op jit(solution)/shard_map/shard_3/ppermute | solution.py:18
  57.0 1.4 %collective-permute-start.16 = (f32[8,8,256]{2,1,0:T(8,128)S(1)}, f32[8,8,256]{2,1,0:T(8,128)S(1)}, u32[]{:S(2)}, u32[]{:S(2)}) collective-permute-start(f32[8,8,256]{2,1,0:T(8,128)S(1)} %copy.74), channel_id=1, source_target_pairs={{0,2},{1,3},{2,0},{3,1},{4,6},{5,7},{6,4},{7,5},{8,10},{9,11},{10,... | collective-permute-start | bytes 196616 | tf_op jit(solution)/shard_map/shard_2/ppermute | solution.py:18
  58.3 0.7 collective-permute-done.13
  59.0 1.0 %collective-permute-start.14 = (f32[8,16,256]{2,1,0:T(8,128)S(1)}, f32[8,16,256]{2,1,0:T(8,128)S(1)}, u32[]{:S(2)}, u32[]{:S(2)}) collective-permute-start(f32[8,16,256]{2,1,0:T(8,128)S(1)} %fusion.24), channel_id=1, source_target_pairs={{0,16},{4,12},{8,24},{12,4},{16,0},{20,28},{24,8},{28,20},{1,17},{... | collective-permute-start | bytes 393224 | tf_op jit(solution)/shard_map/rows_second_near/ppermute | solution.py:18
  60.5 1.3 %collective-permute-done.17 = f32[8,8,256]{2,1,0:T(8,128)S(1)} collective-permute-done((f32[8,8,256]{2,1,0:T(8,128)S(1)}, f32[8,8,256]{2,1,0:T(8,128)S(1)}, u32[]{:S(2)}, u32[]{:S(2)}) %collective-permute-start.17) | collective-permute-done | bytes 65568 | tf_op jit(solution)/shard_map/shard_3/ppermute | solution.py:18
  61.9 2.6 %collective-permute-done.16 = f32[8,8,256]{2,1,0:T(8,128)S(1)} collective-permute-done((f32[8,8,256]{2,1,0:T(8,128)S(1)}, f32[8,8,256]{2,1,0:T(8,128)S(1)}, u32[]{:S(2)}, u32[]{:S(2)}) %collective-permute-start.16) | collective-permute-done | bytes 65568 | tf_op jit(solution)/shard_map/shard_2/ppermute | solution.py:18
  64.5 1.0 %collective-permute-start.20 = (f32[8,16,256]{2,1,0:T(8,128)S(1)}, f32[8,16,256]{2,1,0:T(8,128)S(1)}, u32[]{:S(2)}, u32[]{:S(2)}) collective-permute-start(f32[8,16,256]{2,1,0:T(8,128)S(1)} %fusion.27), channel_id=1, source_target_pairs={{0,16},{4,12},{8,24},{12,4},{16,0},{20,28},{24,8},{28,20},{1,17},{... | collective-permute-start | bytes 393224 | tf_op jit(solution)/shard_map/rows_second_far/ppermute | solution.py:18
  65.5 0.8 %collective-permute-start.19 = (f32[8,16,256]{2,1,0:T(8,128)S(1)}, f32[8,16,256]{2,1,0:T(8,128)S(1)}, u32[]{:S(2)}, u32[]{:S(2)}) collective-permute-start(f32[8,16,256]{2,1,0:T(8,128)S(1)} %collective-permute-done.14), channel_id=1, source_target_pairs={{0,8},{4,20},{8,0},{12,28},{16,24},{20,4},{24,16},{28,12},{1,9},{5... | collective-permute-start | bytes 393224 | tf_op jit(solution)/shard_map/rows_relay_near/ppermute | solution.py:18
  66.7 3.4 %collective-permute-done.20 = f32[8,16,256]{2,1,0:T(8,128)S(1)} collective-permute-done((f32[8,16,256]{2,1,0:T(8,128)S(1)}, f32[8,16,256]{2,1,0:T(8,128)S(1)}, u32[]{:S(2)}, u32[]{:S(2)}) %collective-permute-start.20) | collective-permute-done | bytes 131104 | tf_op jit(solution)/shard_map/rows_second_far/ppermute | solution.py:18
  70.1 1.1 %collective-permute-start.23 = (f32[8,16,256]{2,1,0:T(8,128)S(1)}, f32[8,16,256]{2,1,0:T(8,128)S(1)}, u32[]{:S(2)}, u32[]{:S(2)}) collective-permute-start(f32[8,16,256]{2,1,0:T(8,128)S(1)} %collective-permute-done.20), channel_id=1, source_target_pairs={{0,8},{4,20},{8,0},{12,28},{16,24},{20,4},{24,16},{28,12},{1,9},{5... | collective-permute-start | bytes 393224 | tf_op jit(solution)/shard_map/rows_relay_far/ppermute | solution.py:18
  71.2 0.9 %collective-permute-start.22 = (f32[8,16,256]{2,1,0:T(8,128)S(1)}, f32[8,16,256]{2,1,0:T(8,128)S(1)}, u32[]{:S(2)}, u32[]{:S(2)}) collective-permute-start(f32[8,16,256]{2,1,0:T(8,128)S(1)} %fusion.27), channel_id=1, source_target_pairs={{0,8},{4,20},{8,0},{12,28},{16,24},{20,4},{24,16},{28,12},{1,9},{5... | collective-permute-start | bytes 393224 | tf_op jit(solution)/shard_map/rows_first_far/ppermute | solution.py:18
  72.2 2.8 %collective-permute-done.23 = f32[8,16,256]{2,1,0:T(8,128)S(1)} collective-permute-done((f32[8,16,256]{2,1,0:T(8,128)S(1)}, f32[8,16,256]{2,1,0:T(8,128)S(1)}, u32[]{:S(2)}, u32[]{:S(2)}) %collective-permute-start.23) | collective-permute-done | bytes 131104 | tf_op jit(solution)/shard_map/rows_relay_far/ppermute | solution.py:18
  75.0 1.4 %collective-permute-done.22 = f32[8,16,256]{2,1,0:T(8,128)S(1)} collective-permute-done((f32[8,16,256]{2,1,0:T(8,128)S(1)}, f32[8,16,256]{2,1,0:T(8,128)S(1)}, u32[]{:S(2)}, u32[]{:S(2)}) %collective-permute-start.22) | collective-permute-done | bytes 131104 | tf_op jit(solution)/shard_map/rows_first_far/ppermute | solution.py:18
  76.9 1.2 %collective-permute-done.24 = f32[2,8,16,256]{3,2,1,0:T(8,128)S(1)} collective-permute-done((f32[2,8,16,256]{3,2,1,0:T(8,128)S(1)}, f32[2,8,16,256]{3,2,1,0:T(8,128)S(1)}, u32[]{:S(2)}, u32[]{:S(2)}) %collective-permute-start.24) | collective-permute-done | bytes 262176 | tf_op jit(solution)/shard_map/rows_core_last/ppermute | solution.py:18
  78.1 1.3 %copy-done.1 = f32[8,256,256]{2,1,0:T(8,128)} copy-done((f32[8,256,256]{2,1,0:T(8,128)}, f32[8,256,256]{2,1,0:T(8,128)S(1)}, u32[]{:S(2)}) %copy-start.1) | copy-done | bytes 2097176
  (100 shorter events, 6.5 us)
Async XLA Ops:
  0.6 39.6 %copy-start = (f32[1,1,1,256,256]{4,3,2,1,0:T(8,128)S(1)}, f32[1,1,1,256,256]{4,3,2,1,0:T(8,128)}, u32[]{:S(2)}) copy-start(f32[1,1,1,256,256]{4,3,2,1,0:T(8,128)} %param.10) | copy-start | bytes 786436
  2.2 1.7 %collective-permute-start = (f32[8,32,256]{2,1,0:T(8,128)S(1)}, f32[8,32,256]{2,1,0:T(8,128)S(1)}, u32[]{:S(2)}, u32[]{:S(2)}) collective-permute-start(f32[8,32,256]{2,1,0:T(8,128)S(1)} %get-tuple-element.63), channel_id=1, source_target_pairs={{0,4},{4,0},{8,12},{12,8},{16,20},{20,16},{24,28},{28,24},{1,5},{5... | collective-permute-start | bytes 786440 | tf_op jit(solution)/shard_map/sum_core_across/ppermute | solution.py:18
  2.7 4.2 %collective-permute-start.2 = (f32[8,32,256]{2,1,0:T(8,128)S(1)}, f32[8,32,256]{2,1,0:T(8,128)S(1)}, u32[]{:S(2)}, u32[]{:S(2)}) collective-permute-start(f32[8,32,256]{2,1,0:T(8,128)S(1)} %get-tuple-element.60), channel_id=1, source_target_pairs={{0,4},{4,0},{8,12},{12,8},{16,20},{20,16},{24,28},{28,24},{1,5},{5... | collective-permute-start | bytes 786440 | tf_op jit(solution)/shard_map/sum_core_second/ppermute | solution.py:18
  2.8 4.1 %collective-permute-start.5 = (f32[8,32,256]{2,1,0:T(8,128)S(1)}, f32[8,32,256]{2,1,0:T(8,128)S(1)}, u32[]{:S(2)}, u32[]{:S(2)}) collective-permute-start(f32[8,32,256]{2,1,0:T(8,128)S(1)} %get-tuple-element.61), channel_id=1, source_target_pairs={{0,4},{4,0},{8,12},{12,8},{16,20},{20,16},{24,28},{28,24},{1,5},{5... | collective-permute-start | bytes 786440 | tf_op jit(solution)/shard_map/sum_core_first/ppermute | solution.py:18
  3.2 3.6 %collective-permute-start.1 = (f32[8,32,256]{2,1,0:T(8,128)S(1)}, f32[8,32,256]{2,1,0:T(8,128)S(1)}, u32[]{:S(2)}, u32[]{:S(2)}) collective-permute-start(f32[8,32,256]{2,1,0:T(8,128)S(1)} %get-tuple-element.62), channel_id=1, source_target_pairs={{0,4},{4,0},{8,12},{12,8},{16,20},{20,16},{24,28},{28,24},{1,5},{5... | collective-permute-start | bytes 786440 | tf_op jit(solution)/shard_map/sum_core_own/ppermute | solution.py:18
  4.0 5.9 %collective-permute-start.9 = (f32[8,16,256]{2,1,0:T(8,128)S(1)}, f32[8,16,256]{2,1,0:T(8,128)S(1)}, u32[]{:S(2)}, u32[]{:S(2)}) collective-permute-start(f32[8,16,256]{2,1,0:T(8,128)S(1)} %get-tuple-element.43), channel_id=1, source_target_pairs={{0,8},{4,20},{8,0},{12,28},{16,24},{20,4},{24,16},{28,12},{1,9},{5... | collective-permute-start | bytes 393224 | tf_op jit(solution)/shard_map/sum_across_far/ppermute | solution.py:18
  7.0 14.5 %copy-start.8 = (s32[32]{0:T(128)S(1)}, s32[32]{0:T(128)}, u32[]{:S(2)}) copy-start(s32[32]{0:T(128)} %param.13) | copy-start | bytes 388
  7.1 6.5 %collective-permute-start.8 = (f32[8,16,256]{2,1,0:T(8,128)S(1)}, f32[8,16,256]{2,1,0:T(8,128)S(1)}, u32[]{:S(2)}, u32[]{:S(2)}) collective-permute-start(f32[8,16,256]{2,1,0:T(8,128)S(1)} %get-tuple-element.41), channel_id=1, source_target_pairs={{0,8},{4,20},{8,0},{12,28},{16,24},{20,4},{24,16},{28,12},{1,9},{5... | collective-permute-start | bytes 393224 | tf_op jit(solution)/shard_map/sum_first_far/ppermute | solution.py:18
  8.1 6.8 %collective-permute-start.3 = (f32[8,16,256]{2,1,0:T(8,128)S(1)}, f32[8,16,256]{2,1,0:T(8,128)S(1)}, u32[]{:S(2)}, u32[]{:S(2)}) collective-permute-start(f32[8,16,256]{2,1,0:T(8,128)S(1)} %get-tuple-element.36), channel_id=1, source_target_pairs={{0,8},{4,20},{8,0},{12,28},{16,24},{20,4},{24,16},{28,12},{1,9},{5... | collective-permute-start | bytes 393224 | tf_op jit(solution)/shard_map/sum_across_near/ppermute | solution.py:18
  9.8 6.4 %collective-permute-start.10 = (f32[8,16,256]{2,1,0:T(8,128)S(1)}, f32[8,16,256]{2,1,0:T(8,128)S(1)}, u32[]{:S(2)}, u32[]{:S(2)}) collective-permute-start(f32[8,16,256]{2,1,0:T(8,128)S(1)} %add.226), channel_id=1, source_target_pairs={{0,16},{4,12},{8,24},{12,4},{16,0},{20,28},{24,8},{28,20},{1,17},{... | collective-permute-start | bytes 393224 | tf_op jit(solution)/shard_map/sum_relay_far/ppermute | solution.py:18
  12.0 8.5 %collective-permute-start.6 = (f32[8,16,256]{2,1,0:T(8,128)S(1)}, f32[8,16,256]{2,1,0:T(8,128)S(1)}, u32[]{:S(2)}, u32[]{:S(2)}) collective-permute-start(f32[8,16,256]{2,1,0:T(8,128)S(1)} %get-tuple-element.37), channel_id=1, source_target_pairs={{0,8},{4,20},{8,0},{12,28},{16,24},{20,4},{24,16},{28,12},{1,9},{5... | collective-permute-start | bytes 393224 | tf_op jit(solution)/shard_map/sum_first_near/ppermute | solution.py:18
  14.9 24.9 %copy-start.2 = (f32[1,1,1,256,256]{4,3,2,1,0:T(8,128)S(1)}, f32[1,1,1,256,256]{4,3,2,1,0:T(8,128)}, u32[]{:S(2)}) copy-start(f32[1,1,1,256,256]{4,3,2,1,0:T(8,128)} %param.9) | copy-start | bytes 786436
  14.9 5.6 %collective-permute-start.4 = (f32[8,16,256]{2,1,0:T(8,128)S(1)}, f32[8,16,256]{2,1,0:T(8,128)S(1)}, u32[]{:S(2)}, u32[]{:S(2)}) collective-permute-start(f32[8,16,256]{2,1,0:T(8,128)S(1)} %add.219), channel_id=1, source_target_pairs={{0,16},{4,12},{8,24},{12,4},{16,0},{20,28},{24,8},{28,20},{1,17},{... | collective-permute-start | bytes 393224 | tf_op jit(solution)/shard_map/sum_relay_near/ppermute | solution.py:18
  16.3 7.1 %collective-permute-start.12 = (f32[8,8,256]{2,1,0:T(8,128)S(1)}, f32[8,8,256]{2,1,0:T(8,128)S(1)}, u32[]{:S(2)}, u32[]{:S(2)}) collective-permute-start(f32[8,8,256]{2,1,0:T(8,128)S(1)} %get-tuple-element.81), channel_id=1, source_target_pairs={{0,2},{1,3},{2,0},{3,1},{4,6},{5,7},{6,4},{7,5},{8,10},{9,11},{10,... | collective-permute-start | bytes 196616 | tf_op jit(solution)/shard_map/shard_2/ppermute | solution.py:18
  19.1 6.2 %collective-permute-start.11 = (f32[8,8,256]{2,1,0:T(8,128)S(1)}, f32[8,8,256]{2,1,0:T(8,128)S(1)}, u32[]{:S(2)}, u32[]{:S(2)}) collective-permute-start(f32[8,8,256]{2,1,0:T(8,128)S(1)} %get-tuple-element.80), channel_id=1, source_target_pairs={{0,3},{1,2},{2,1},{3,0},{4,7},{5,6},{6,5},{7,4},{8,11},{9,10},{10,... | collective-permute-start | bytes 196616 | tf_op jit(solution)/shard_map/shard_3/ppermute | solution.py:18
  20.5 19.7 %copy-start.4 = (f32[1,1,1,256,256]{4,3,2,1,0:T(8,128)S(1)}, f32[1,1,1,256,256]{4,3,2,1,0:T(8,128)}, u32[]{:S(2)}) copy-start(f32[1,1,1,256,256]{4,3,2,1,0:T(8,128)} %param.11) | copy-start | bytes 786436
  20.5 19.7 %copy-start.5 = (f32[1,1,1,256,256]{4,3,2,1,0:T(8,128)S(1)}, f32[1,1,1,256,256]{4,3,2,1,0:T(8,128)}, u32[]{:S(2)}) copy-start(f32[1,1,1,256,256]{4,3,2,1,0:T(8,128)} %param.12) | copy-start | bytes 786436
  20.6 5.0 %collective-permute-start.7 = (f32[8,8,256]{2,1,0:T(8,128)S(1)}, f32[8,8,256]{2,1,0:T(8,128)S(1)}, u32[]{:S(2)}, u32[]{:S(2)}) collective-permute-start(f32[8,8,256]{2,1,0:T(8,128)S(1)} %get-tuple-element.79), channel_id=1, source_target_pairs={{0,1},{1,0},{2,3},{3,2},{4,5},{5,4},{6,7},{7,6},{8,9},{9,8},{10,11... | collective-permute-start | bytes 196616 | tf_op jit(solution)/shard_map/shard_1/ppermute | solution.py:18
  40.6 13.9 %copy-start.6 = (f32[256,256]{1,0:T(8,128)}, f32[256,256]{1,0:T(8,128)S(1)}, u32[]{:S(2)}) copy-start(f32[256,256]{1,0:T(8,128)S(1)} %get-tuple-element.53) | copy-start | bytes 786436
  40.7 18.3 %copy-start.3 = (f32[8,32,256]{2,1,0:T(8,128)S(1)}, f32[8,32,256]{2,1,0:T(8,128)}, u32[]{:S(2)}) copy-start(f32[8,32,256]{2,1,0:T(8,128)} %param.8) | copy-start | bytes 786436
  54.5 4.5 %collective-permute-start.13 = (f32[8,8,256]{2,1,0:T(8,128)S(1)}, f32[8,8,256]{2,1,0:T(8,128)S(1)}, u32[]{:S(2)}, u32[]{:S(2)}) collective-permute-start(f32[8,8,256]{2,1,0:T(8,128)S(1)} %copy.70), channel_id=1, source_target_pairs={{0,1},{1,0},{2,3},{3,2},{4,5},{5,4},{6,7},{7,6},{8,9},{9,8},{10,11... | collective-permute-start | bytes 196616 | tf_op jit(solution)/shard_map/shard_1/ppermute | solution.py:18
  55.7 6.1 %collective-permute-start.17 = (f32[8,8,256]{2,1,0:T(8,128)S(1)}, f32[8,8,256]{2,1,0:T(8,128)S(1)}, u32[]{:S(2)}, u32[]{:S(2)}) collective-permute-start(f32[8,8,256]{2,1,0:T(8,128)S(1)} %copy.75), channel_id=1, source_target_pairs={{0,3},{1,2},{2,1},{3,0},{4,7},{5,6},{6,5},{7,4},{8,11},{9,10},{10,... | collective-permute-start | bytes 196616 | tf_op jit(solution)/shard_map/shard_3/ppermute | solution.py:18
  57.0 7.5 %collective-permute-start.16 = (f32[8,8,256]{2,1,0:T(8,128)S(1)}, f32[8,8,256]{2,1,0:T(8,128)S(1)}, u32[]{:S(2)}, u32[]{:S(2)}) collective-permute-start(f32[8,8,256]{2,1,0:T(8,128)S(1)} %copy.74), channel_id=1, source_target_pairs={{0,2},{1,3},{2,0},{3,1},{4,6},{5,7},{6,4},{7,5},{8,10},{9,11},{10,... | collective-permute-start | bytes 196616 | tf_op jit(solution)/shard_map/shard_2/ppermute | solution.py:18
  59.0 6.5 %collective-permute-start.14 = (f32[8,16,256]{2,1,0:T(8,128)S(1)}, f32[8,16,256]{2,1,0:T(8,128)S(1)}, u32[]{:S(2)}, u32[]{:S(2)}) collective-permute-start(f32[8,16,256]{2,1,0:T(8,128)S(1)} %fusion.24), channel_id=1, source_target_pairs={{0,16},{4,12},{8,24},{12,4},{16,0},{20,28},{24,8},{28,20},{1,17},{... | collective-permute-start | bytes 393224 | tf_op jit(solution)/shard_map/rows_second_near/ppermute | solution.py:18
  60.0 5.5 %collective-permute-start.15 = (f32[8,16,256]{2,1,0:T(8,128)S(1)}, f32[8,16,256]{2,1,0:T(8,128)S(1)}, u32[]{:S(2)}, u32[]{:S(2)}) collective-permute-start(f32[8,16,256]{2,1,0:T(8,128)S(1)} %fusion.24), channel_id=1, source_target_pairs={{0,8},{4,20},{8,0},{12,28},{16,24},{20,4},{24,16},{28,12},{1,9},{5... | collective-permute-start | bytes 393224 | tf_op jit(solution)/shard_map/rows_first_near/ppermute | solution.py:18
  64.5 5.5 %collective-permute-start.20 = (f32[8,16,256]{2,1,0:T(8,128)S(1)}, f32[8,16,256]{2,1,0:T(8,128)S(1)}, u32[]{:S(2)}, u32[]{:S(2)}) collective-permute-start(f32[8,16,256]{2,1,0:T(8,128)S(1)} %fusion.27), channel_id=1, source_target_pairs={{0,16},{4,12},{8,24},{12,4},{16,0},{20,28},{24,8},{28,20},{1,17},{... | collective-permute-start | bytes 393224 | tf_op jit(solution)/shard_map/rows_second_far/ppermute | solution.py:18
  65.5 5.7 %collective-permute-start.19 = (f32[8,16,256]{2,1,0:T(8,128)S(1)}, f32[8,16,256]{2,1,0:T(8,128)S(1)}, u32[]{:S(2)}, u32[]{:S(2)}) collective-permute-start(f32[8,16,256]{2,1,0:T(8,128)S(1)} %collective-permute-done.14), channel_id=1, source_target_pairs={{0,8},{4,20},{8,0},{12,28},{16,24},{20,4},{24,16},{28,12},{1,9},{5... | collective-permute-start | bytes 393224 | tf_op jit(solution)/shard_map/rows_relay_near/ppermute | solution.py:18
  66.4 10.2 %collective-permute-start.18 = (f32[3,8,16,256]{3,2,1,0:T(8,128)S(1)}, f32[3,8,16,256]{3,2,1,0:T(8,128)S(1)}, u32[]{:S(2)}, u32[]{:S(2)}) collective-permute-start(f32[3,8,16,256]{3,2,1,0:T(8,128)S(1)} %pad_maximum_fusion), channel_id=1, source_target_pairs={{0,4},{4,0},{8,12},{12,8},{16,20},{20,16},{24,28},{28,24},{1,5},{5... | collective-permute-start | bytes 1179656 | tf_op jit(solution)/shard_map/rows_core_first/ppermute | solution.py:18
  70.1 5.0 %collective-permute-start.23 = (f32[8,16,256]{2,1,0:T(8,128)S(1)}, f32[8,16,256]{2,1,0:T(8,128)S(1)}, u32[]{:S(2)}, u32[]{:S(2)}) collective-permute-start(f32[8,16,256]{2,1,0:T(8,128)S(1)} %collective-permute-done.20), channel_id=1, source_target_pairs={{0,8},{4,20},{8,0},{12,28},{16,24},{20,4},{24,16},{28,12},{1,9},{5... | collective-permute-start | bytes 393224 | tf_op jit(solution)/shard_map/rows_relay_far/ppermute | solution.py:18
  71.2 5.2 %collective-permute-start.22 = (f32[8,16,256]{2,1,0:T(8,128)S(1)}, f32[8,16,256]{2,1,0:T(8,128)S(1)}, u32[]{:S(2)}, u32[]{:S(2)}) collective-permute-start(f32[8,16,256]{2,1,0:T(8,128)S(1)} %fusion.27), channel_id=1, source_target_pairs={{0,8},{4,20},{8,0},{12,28},{16,24},{20,4},{24,16},{28,12},{1,9},{5... | collective-permute-start | bytes 393224 | tf_op jit(solution)/shard_map/rows_first_far/ppermute | solution.py:18
  72.2 4.5 %collective-permute-start.21 = (f32[3,8,16,256]{3,2,1,0:T(8,128)S(1)}, f32[3,8,16,256]{3,2,1,0:T(8,128)S(1)}, u32[]{:S(2)}, u32[]{:S(2)}) collective-permute-start(f32[3,8,16,256]{3,2,1,0:T(8,128)S(1)} %pad_maximum_fusion.1), channel_id=1, source_target_pairs={{0,4},{4,0},{8,12},{12,8},{16,20},{20,16},{24,28},{28,24},{1,5},{5... | collective-permute-start | bytes 1179656 | tf_op jit(solution)/shard_map/rows_core_second/ppermute | solution.py:18
  76.5 1.6 %collective-permute-start.24 = (f32[2,8,16,256]{3,2,1,0:T(8,128)S(1)}, f32[2,8,16,256]{3,2,1,0:T(8,128)S(1)}, u32[]{:S(2)}, u32[]{:S(2)}) collective-permute-start(f32[2,8,16,256]{3,2,1,0:T(8,128)S(1)} %pad_maximum_fusion.3), channel_id=1, source_target_pairs={{0,4},{4,0},{8,12},{12,8},{16,20},{20,16},{24,28},{28,24},{1,5},{5... | collective-permute-start | bytes 786440 | tf_op jit(solution)/shard_map/rows_core_last/ppermute | solution.py:18
  (2 other events, 15.2 us)

commit v13 on v9

--- a/solution.py
+++ b/solution.py
@@ -193,11 +193,12 @@
     low, top = new_home[:half], new_home[half:]
     first_top = swap(top, "dp", first_link, "rows_first_top")
     second_low = swap(low, "dp", second_link, "rows_second_low")
-    other = swap(new_home, "dp", core, "rows_core_own")
     first_low = swap(low, "dp", first_link, "rows_first_low")
     second_top = swap(top, "dp", second_link, "rows_second_top")
     far_top = swap(first_top, "dp", second_link, "rows_relay_top")
     far_low = swap(second_low, "dp", first_link, "rows_relay_low")
+    own_home, _ = lax.optimization_barrier((new_home, first_top))
+    other = swap(own_home, "dp", core, "rows_core_own")
     first_rows = jnp.concatenate([first_low, first_top], axis=0)
     second_rows = jnp.concatenate([second_top, second_low], axis=0)
     first_rows, second_rows, far_top, first_new, second_new = lax.optimization_barrier(

time: 78.9 us -> 80.2 us (1.016)
  waiting for transfers between devices: 17.4 us -> 19.1 us
    ppermute x26, waiting for transfers between devices: 17.4 us -> 19.1 us  [swap(): return lax.ppermute(values, name, pairs)]
  transfers between devices with their start and end apart: 26 -> 26, of which waited for: 15 -> 14; matrix products, arithmetic and copies ran while one was open for 2% -> 1% of each run, Pallas kernels for 0% -> 0%
where the time goes in v13:
time: 80.2 us; the launch traced here: 80 us
  starting transfers between devices  26.9 us (34%)
  blocking collectives  26.5 us (33%)
  waiting for transfers between devices  19.1 us (24%)
  local copies, waits for them, and re-layouts  3.76 us (5%)
  matrix products  1.93 us (2%)
  between operations  1.28 us (2%)
    ppermute x26, starting transfers between devices, swap(): return lax.ppermute(values, name, pairs)  26.9 us
    ppermute x26, waiting for transfers between devices, swap(): return lax.ppermute(values, name, pairs)  19.1 us
    all_to_all x1, blocking collectives, routed(): lax.all_to_all(leaving.reshape((device_total,) + piece), ('dp', 'shard'),...  13.7 us
    all_to_all x1, blocking collectives, routed(): lax.all_to_all(change.reshape((device_total,) + piece), ('dp', 'shard'),...  12.7 us
  transfers between devices with their start and end apart: 26, of which 14 were waited for; matrix products, arithmetic and copies ran while one was open for 1% of the time, Pallas kernels for 0%

profile of v13, /device:TPU:0, one launch (start us, length us, event | category | flops | bytes accessed | tf_op | source)
XLA Modules:
  0.0 80.0 jit_solution(11298925886523570945)
XLA Ops:
  0.7 1.3 %dynamic-slice_bitcast_fusion = (bf16[8,4,32,256]{3,2,1,0:T(8,128)(2,1)S(1)}, bf16[8,4,32,256]{3,2,1,0:T(8,128)(2,1)S(1)}) fusion(bf16[8,4,2,32,256]{4,3,2,1,0:T(8,128)(2,1)} %bitcast.130, s32[]{:T(128)S(6)} %select_n.130, s32[]{:T(128)S(6)} %select_n.129), kind=kLoop, calls=%fused_computation.1 | loop fusion | bytes 2097160 | tf_op jit(solution)/shard_map/jit(dynamic_index_in_dim)/squeeze | solution.py:22
  3.3 0.6 collective-permute-done
  4.0 2.9 %collective-permute-start.9 = (f32[8,16,256]{2,1,0:T(8,128)S(1)}, f32[8,16,256]{2,1,0:T(8,128)S(1)}, u32[]{:S(2)}, u32[]{:S(2)}) collective-permute-start(f32[8,16,256]{2,1,0:T(8,128)S(1)} %get-tuple-element.42), channel_id=1, source_target_pairs={{0,8},{4,20},{8,0},{12,28},{16,24},{20,4},{24,16},{28,12},{1,9},{5... | collective-permute-start | bytes 393224 | tf_op jit(solution)/shard_map/sum_across_far/ppermute | solution.py:18
  7.1 1.0 %collective-permute-start.8 = (f32[8,16,256]{2,1,0:T(8,128)S(1)}, f32[8,16,256]{2,1,0:T(8,128)S(1)}, u32[]{:S(2)}, u32[]{:S(2)}) collective-permute-start(f32[8,16,256]{2,1,0:T(8,128)S(1)} %get-tuple-element.40), channel_id=1, source_target_pairs={{0,8},{4,20},{8,0},{12,28},{16,24},{20,4},{24,16},{28,12},{1,9},{5... | collective-permute-start | bytes 393224 | tf_op jit(solution)/shard_map/sum_first_far/ppermute | solution.py:18
  8.1 1.1 %collective-permute-start.3 = (f32[8,16,256]{2,1,0:T(8,128)S(1)}, f32[8,16,256]{2,1,0:T(8,128)S(1)}, u32[]{:S(2)}, u32[]{:S(2)}) collective-permute-start(f32[8,16,256]{2,1,0:T(8,128)S(1)} %get-tuple-element.35), channel_id=1, source_target_pairs={{0,8},{4,20},{8,0},{12,28},{16,24},{20,4},{24,16},{28,12},{1,9},{5... | collective-permute-start | bytes 393224 | tf_op jit(solution)/shard_map/sum_across_near/ppermute | solution.py:18
  9.2 0.6 collective-permute-done.9
  9.8 2.1 %collective-permute-start.10 = (f32[8,16,256]{2,1,0:T(8,128)S(1)}, f32[8,16,256]{2,1,0:T(8,128)S(1)}, u32[]{:S(2)}, u32[]{:S(2)}) collective-permute-start(f32[8,16,256]{2,1,0:T(8,128)S(1)} %add.167), channel_id=1, source_target_pairs={{0,16},{4,12},{8,24},{12,4},{16,0},{20,28},{24,8},{28,20},{1,17},{... | collective-permute-start | bytes 393224 | tf_op jit(solution)/shard_map/sum_relay_far/ppermute | solution.py:18
  12.0 1.6 %collective-permute-start.6 = (f32[8,16,256]{2,1,0:T(8,128)S(1)}, f32[8,16,256]{2,1,0:T(8,128)S(1)}, u32[]{:S(2)}, u32[]{:S(2)}) collective-permute-start(f32[8,16,256]{2,1,0:T(8,128)S(1)} %get-tuple-element.36), channel_id=1, source_target_pairs={{0,8},{4,20},{8,0},{12,28},{16,24},{20,4},{24,16},{28,12},{1,9},{5... | collective-permute-start | bytes 393224 | tf_op jit(solution)/shard_map/sum_first_near/ppermute | solution.py:18
  13.6 1.3 %collective-permute-done.3 = f32[8,16,256]{2,1,0:T(8,128)S(1)} collective-permute-done((f32[8,16,256]{2,1,0:T(8,128)S(1)}, f32[8,16,256]{2,1,0:T(8,128)S(1)}, u32[]{:S(2)}, u32[]{:S(2)}) %collective-permute-start.3) | collective-permute-done | bytes 131104 | tf_op jit(solution)/shard_map/sum_across_near/ppermute | solution.py:18
  14.9 1.3 %collective-permute-start.4 = (f32[8,16,256]{2,1,0:T(8,128)S(1)}, f32[8,16,256]{2,1,0:T(8,128)S(1)}, u32[]{:S(2)}, u32[]{:S(2)}) collective-permute-start(f32[8,16,256]{2,1,0:T(8,128)S(1)} %add.160), channel_id=1, source_target_pairs={{0,16},{4,12},{8,24},{12,4},{16,0},{20,28},{24,8},{28,20},{1,17},{... | collective-permute-start | bytes 393224 | tf_op jit(solution)/shard_map/sum_relay_near/ppermute | solution.py:18
  16.3 2.8 %collective-permute-start.12 = (f32[8,8,256]{2,1,0:T(8,128)S(1)}, f32[8,8,256]{2,1,0:T(8,128)S(1)}, u32[]{:S(2)}, u32[]{:S(2)}) collective-permute-start(f32[8,8,256]{2,1,0:T(8,128)S(1)} %get-tuple-element.81), channel_id=1, source_target_pairs={{0,2},{1,3},{2,0},{3,1},{4,6},{5,7},{6,4},{7,5},{8,10},{9,11},{10,... | collective-permute-start | bytes 196616 | tf_op jit(solution)/shard_map/shard_2/ppermute | solution.py:18
  19.1 1.3 %collective-permute-start.11 = (f32[8,8,256]{2,1,0:T(8,128)S(1)}, f32[8,8,256]{2,1,0:T(8,128)S(1)}, u32[]{:S(2)}, u32[]{:S(2)}) collective-permute-start(f32[8,8,256]{2,1,0:T(8,128)S(1)} %get-tuple-element.80), channel_id=1, source_target_pairs={{0,3},{1,2},{2,1},{3,0},{4,7},{5,6},{6,5},{7,4},{8,11},{9,10},{10,... | collective-permute-start | bytes 196616 | tf_op jit(solution)/shard_map/shard_3/ppermute | solution.py:18
  20.6 0.9 %collective-permute-start.7 = (f32[8,8,256]{2,1,0:T(8,128)S(1)}, f32[8,8,256]{2,1,0:T(8,128)S(1)}, u32[]{:S(2)}, u32[]{:S(2)}) collective-permute-start(f32[8,8,256]{2,1,0:T(8,128)S(1)} %get-tuple-element.79), channel_id=1, source_target_pairs={{0,1},{1,0},{2,3},{3,2},{4,5},{5,4},{6,7},{7,6},{8,9},{9,8},{10,11... | collective-permute-start | bytes 196616 | tf_op jit(solution)/shard_map/shard_1/ppermute | solution.py:18
  21.7 1.7 %collective-permute-done.12 = f32[8,8,256]{2,1,0:T(8,128)S(1)} collective-permute-done((f32[8,8,256]{2,1,0:T(8,128)S(1)}, f32[8,8,256]{2,1,0:T(8,128)S(1)}, u32[]{:S(2)}, u32[]{:S(2)}) %collective-permute-start.12) | collective-permute-done | bytes 65568 | tf_op jit(solution)/shard_map/shard_2/ppermute | solution.py:18
  23.5 1.8 %collective-permute-done.11 = f32[8,8,256]{2,1,0:T(8,128)S(1)} collective-permute-done((f32[8,8,256]{2,1,0:T(8,128)S(1)}, f32[8,8,256]{2,1,0:T(8,128)S(1)}, u32[]{:S(2)}, u32[]{:S(2)}) %collective-permute-start.11) | collective-permute-done | bytes 65568 | tf_op jit(solution)/shard_map/shard_3/ppermute | solution.py:18
  26.1 13.7 %all_to_all.10 = f32[32,8,256]{2,1,0:T(8,128)S(1)} all-to-all(f32[32,8,256]{2,1,0:T(8,128)S(1)} %copy.56), channel_id=1, replica_groups=mesh['dp'=8,'shard'=4] {'dp','shard'}, dimensions={0} | all-to-all | bytes 524288 | tf_op jit(solution)/shard_map/all_to_all | solution.py:153
  41.3 12.7 %all_to_all.11 = f32[32,8,256]{2,1,0:T(8,128)S(1)} all-to-all(f32[32,8,256]{2,1,0:T(8,128)S(1)} %convolution_bitcast_fusion), channel_id=1, replica_groups=mesh['dp'=8,'shard'=4] {'dp','shard'}, dimensions={0} | all-to-all | bytes 524288 | tf_op jit(solution)/shard_map/all_to_all | solution.py:170
  54.5 1.8 %collective-permute-start.13 = (f32[8,8,256]{2,1,0:T(8,128)S(1)}, f32[8,8,256]{2,1,0:T(8,128)S(1)}, u32[]{:S(2)}, u32[]{:S(2)}) collective-permute-start(f32[8,8,256]{2,1,0:T(8,128)S(1)} %copy.58), channel_id=1, source_target_pairs={{0,3},{1,2},{2,1},{3,0},{4,7},{5,6},{6,5},{7,4},{8,11},{9,10},{10,... | collective-permute-start | bytes 196616 | tf_op jit(solution)/shard_map/shard_3/ppermute | solution.py:18
  56.4 0.9 %collective-permute-start.14 = (f32[8,8,256]{2,1,0:T(8,128)S(1)}, f32[8,8,256]{2,1,0:T(8,128)S(1)}, u32[]{:S(2)}, u32[]{:S(2)}) collective-permute-start(f32[8,8,256]{2,1,0:T(8,128)S(1)} %copy.59), channel_id=1, source_target_pairs={{0,2},{1,3},{2,0},{3,1},{4,6},{5,7},{6,4},{7,5},{8,10},{9,11},{10,... | collective-permute-start | bytes 196616 | tf_op jit(solution)/shard_map/shard_2/ppermute | solution.py:18
  57.3 1.9 %collective-permute-start.15 = (f32[8,8,256]{2,1,0:T(8,128)S(1)}, f32[8,8,256]{2,1,0:T(8,128)S(1)}, u32[]{:S(2)}, u32[]{:S(2)}) collective-permute-start(f32[8,8,256]{2,1,0:T(8,128)S(1)} %copy.60), channel_id=1, source_target_pairs={{0,1},{1,0},{2,3},{3,2},{4,5},{5,4},{6,7},{7,6},{8,9},{9,8},{10,11... | collective-permute-start | bytes 196616 | tf_op jit(solution)/shard_map/shard_1/ppermute | solution.py:18
  59.2 2.2 %collective-permute-done.13 = f32[8,8,256]{2,1,0:T(8,128)S(1)} collective-permute-done((f32[8,8,256]{2,1,0:T(8,128)S(1)}, f32[8,8,256]{2,1,0:T(8,128)S(1)}, u32[]{:S(2)}, u32[]{:S(2)}) %collective-permute-start.13) | collective-permute-done | bytes 65568 | tf_op jit(solution)/shard_map/shard_3/ppermute | solution.py:18
  61.4 2.2 %collective-permute-done.14 = f32[8,8,256]{2,1,0:T(8,128)S(1)} collective-permute-done((f32[8,8,256]{2,1,0:T(8,128)S(1)}, f32[8,8,256]{2,1,0:T(8,128)S(1)}, u32[]{:S(2)}, u32[]{:S(2)}) %collective-permute-start.14) | collective-permute-done | bytes 65568 | tf_op jit(solution)/shard_map/shard_2/ppermute | solution.py:18
  63.7 0.9 %collective-permute-start.16 = (f32[4,32,256]{2,1,0:T(8,128)S(1)}, f32[4,32,256]{2,1,0:T(8,128)S(1)}, u32[]{:S(2)}, u32[]{:S(2)}) collective-permute-start(f32[4,32,256]{2,1,0:T(8,128)S(1)} %get-tuple-element.63), channel_id=1, source_target_pairs={{0,8},{4,20},{8,0},{12,28},{16,24},{20,4},{24,16},{28,12},{1,9},{5... | collective-permute-start | bytes 393224 | tf_op jit(solution)/shard_map/rows_first_top/ppermute | solution.py:18
  64.6 0.6 collective-permute-start.20
  65.2 1.5 %collective-permute-start.18 = (f32[4,32,256]{2,1,0:T(8,128)S(1)}, f32[4,32,256]{2,1,0:T(8,128)S(1)}, u32[]{:S(2)}, u32[]{:S(2)}) collective-permute-start(f32[4,32,256]{2,1,0:T(8,128)S(1)} %get-tuple-element.62), channel_id=1, source_target_pairs={{0,8},{4,20},{8,0},{12,28},{16,24},{20,4},{24,16},{28,12},{1,9},{5... | collective-permute-start | bytes 393224 | tf_op jit(solution)/shard_map/rows_first_low/ppermute | solution.py:18
  66.7 1.1 %collective-permute-start.19 = (f32[4,32,256]{2,1,0:T(8,128)S(1)}, f32[4,32,256]{2,1,0:T(8,128)S(1)}, u32[]{:S(2)}, u32[]{:S(2)}) collective-permute-start(f32[4,32,256]{2,1,0:T(8,128)S(1)} %get-tuple-element.63), channel_id=1, source_target_pairs={{0,16},{4,12},{8,24},{12,4},{16,0},{20,28},{24,8},{28,20},{1,17},{... | collective-permute-start | bytes 393224 | tf_op jit(solution)/shard_map/rows_second_top/ppermute | solution.py:18
  68.0 2.1 %collective-permute-done.16 = f32[4,32,256]{2,1,0:T(8,128)S(1)} collective-permute-done((f32[4,32,256]{2,1,0:T(8,128)S(1)}, f32[4,32,256]{2,1,0:T(8,128)S(1)}, u32[]{:S(2)}, u32[]{:S(2)}) %collective-permute-start.16) | collective-permute-done | bytes 131104 | tf_op jit(solution)/shard_map/rows_first_top/ppermute | solution.py:18
  70.1 0.9 %collective-permute-start.21 = (f32[4,32,256]{2,1,0:T(8,128)S(1)}, f32[4,32,256]{2,1,0:T(8,128)S(1)}, u32[]{:S(2)}, u32[]{:S(2)}) collective-permute-start(f32[4,32,256]{2,1,0:T(8,128)S(1)} %collective-permute-done.16), channel_id=1, source_target_pairs={{0,16},{4,12},{8,24},{12,4},{16,0},{20,28},{24,8},{28,20},{1,17},{... | collective-permute-start | bytes 393224 | tf_op jit(solution)/shard_map/rows_relay_top/ppermute | solution.py:18
  71.5 1.1 %collective-permute-done.18 = f32[4,32,256]{2,1,0:T(8,128)S(1)} collective-permute-done((f32[4,32,256]{2,1,0:T(8,128)S(1)}, f32[4,32,256]{2,1,0:T(8,128)S(1)}, u32[]{:S(2)}, u32[]{:S(2)}) %collective-permute-start.18) | collective-permute-done | bytes 131104 | tf_op jit(solution)/shard_map/rows_first_low/ppermute | solution.py:18
  72.7 3.7 %collective-permute-done.21 = f32[4,32,256]{2,1,0:T(8,128)S(1)} collective-permute-done((f32[4,32,256]{2,1,0:T(8,128)S(1)}, f32[4,32,256]{2,1,0:T(8,128)S(1)}, u32[]{:S(2)}, u32[]{:S(2)}) %collective-permute-start.21) | collective-permute-done | bytes 131104 | tf_op jit(solution)/shard_map/rows_relay_top/ppermute | solution.py:18
  77.2 0.8 collective-permute-done.22
  78.7 1.3 %copy-done.3 = f32[8,256,256]{2,1,0:T(8,128)} copy-done((f32[8,256,256]{2,1,0:T(8,128)}, f32[8,256,256]{2,1,0:T(8,128)S(1)}, u32[]{:S(2)}) %copy-start.3) | copy-done | bytes 2097176
  (100 shorter events, 6.9 us)
Async XLA Ops:
  0.6 39.6 %copy-start = (f32[1,1,1,256,256]{4,3,2,1,0:T(8,128)S(1)}, f32[1,1,1,256,256]{4,3,2,1,0:T(8,128)}, u32[]{:S(2)}) copy-start(f32[1,1,1,256,256]{4,3,2,1,0:T(8,128)} %param.10) | copy-start | bytes 786436
  2.2 1.7 %collective-permute-start = (f32[8,32,256]{2,1,0:T(8,128)S(1)}, f32[8,32,256]{2,1,0:T(8,128)S(1)}, u32[]{:S(2)}, u32[]{:S(2)}) collective-permute-start(f32[8,32,256]{2,1,0:T(8,128)S(1)} %get-tuple-element.61), channel_id=1, source_target_pairs={{0,4},{4,0},{8,12},{12,8},{16,20},{20,16},{24,28},{28,24},{1,5},{5... | collective-permute-start | bytes 786440 | tf_op jit(solution)/shard_map/sum_core_across/ppermute | solution.py:18
  2.7 4.2 %collective-permute-start.2 = (f32[8,32,256]{2,1,0:T(8,128)S(1)}, f32[8,32,256]{2,1,0:T(8,128)S(1)}, u32[]{:S(2)}, u32[]{:S(2)}) collective-permute-start(f32[8,32,256]{2,1,0:T(8,128)S(1)} %get-tuple-element.58), channel_id=1, source_target_pairs={{0,4},{4,0},{8,12},{12,8},{16,20},{20,16},{24,28},{28,24},{1,5},{5... | collective-permute-start | bytes 786440 | tf_op jit(solution)/shard_map/sum_core_second/ppermute | solution.py:18
  2.8 4.1 %collective-permute-start.5 = (f32[8,32,256]{2,1,0:T(8,128)S(1)}, f32[8,32,256]{2,1,0:T(8,128)S(1)}, u32[]{:S(2)}, u32[]{:S(2)}) collective-permute-start(f32[8,32,256]{2,1,0:T(8,128)S(1)} %get-tuple-element.59), channel_id=1, source_target_pairs={{0,4},{4,0},{8,12},{12,8},{16,20},{20,16},{24,28},{28,24},{1,5},{5... | collective-permute-start | bytes 786440 | tf_op jit(solution)/shard_map/sum_core_first/ppermute | solution.py:18
  3.2 3.6 %collective-permute-start.1 = (f32[8,32,256]{2,1,0:T(8,128)S(1)}, f32[8,32,256]{2,1,0:T(8,128)S(1)}, u32[]{:S(2)}, u32[]{:S(2)}) collective-permute-start(f32[8,32,256]{2,1,0:T(8,128)S(1)} %get-tuple-element.60), channel_id=1, source_target_pairs={{0,4},{4,0},{8,12},{12,8},{16,20},{20,16},{24,28},{28,24},{1,5},{5... | collective-permute-start | bytes 786440 | tf_op jit(solution)/shard_map/sum_core_own/ppermute | solution.py:18
  4.0 5.9 %collective-permute-start.9 = (f32[8,16,256]{2,1,0:T(8,128)S(1)}, f32[8,16,256]{2,1,0:T(8,128)S(1)}, u32[]{:S(2)}, u32[]{:S(2)}) collective-permute-start(f32[8,16,256]{2,1,0:T(8,128)S(1)} %get-tuple-element.42), channel_id=1, source_target_pairs={{0,8},{4,20},{8,0},{12,28},{16,24},{20,4},{24,16},{28,12},{1,9},{5... | collective-permute-start | bytes 393224 | tf_op jit(solution)/shard_map/sum_across_far/ppermute | solution.py:18
  7.1 6.5 %collective-permute-start.8 = (f32[8,16,256]{2,1,0:T(8,128)S(1)}, f32[8,16,256]{2,1,0:T(8,128)S(1)}, u32[]{:S(2)}, u32[]{:S(2)}) collective-permute-start(f32[8,16,256]{2,1,0:T(8,128)S(1)} %get-tuple-element.40), channel_id=1, source_target_pairs={{0,8},{4,20},{8,0},{12,28},{16,24},{20,4},{24,16},{28,12},{1,9},{5... | collective-permute-start | bytes 393224 | tf_op jit(solution)/shard_map/sum_first_far/ppermute | solution.py:18
  8.1 6.8 %collective-permute-start.3 = (f32[8,16,256]{2,1,0:T(8,128)S(1)}, f32[8,16,256]{2,1,0:T(8,128)S(1)}, u32[]{:S(2)}, u32[]{:S(2)}) collective-permute-start(f32[8,16,256]{2,1,0:T(8,128)S(1)} %get-tuple-element.35), channel_id=1, source_target_pairs={{0,8},{4,20},{8,0},{12,28},{16,24},{20,4},{24,16},{28,12},{1,9},{5... | collective-permute-start | bytes 393224 | tf_op jit(solution)/shard_map/sum_across_near/ppermute | solution.py:18
  9.8 6.4 %collective-permute-start.10 = (f32[8,16,256]{2,1,0:T(8,128)S(1)}, f32[8,16,256]{2,1,0:T(8,128)S(1)}, u32[]{:S(2)}, u32[]{:S(2)}) collective-permute-start(f32[8,16,256]{2,1,0:T(8,128)S(1)} %add.167), channel_id=1, source_target_pairs={{0,16},{4,12},{8,24},{12,4},{16,0},{20,28},{24,8},{28,20},{1,17},{... | collective-permute-start | bytes 393224 | tf_op jit(solution)/shard_map/sum_relay_far/ppermute | solution.py:18
  12.0 8.5 %collective-permute-start.6 = (f32[8,16,256]{2,1,0:T(8,128)S(1)}, f32[8,16,256]{2,1,0:T(8,128)S(1)}, u32[]{:S(2)}, u32[]{:S(2)}) collective-permute-start(f32[8,16,256]{2,1,0:T(8,128)S(1)} %get-tuple-element.36), channel_id=1, source_target_pairs={{0,8},{4,20},{8,0},{12,28},{16,24},{20,4},{24,16},{28,12},{1,9},{5... | collective-permute-start | bytes 393224 | tf_op jit(solution)/shard_map/sum_first_near/ppermute | solution.py:18
  14.9 24.9 %copy-start.4 = (f32[1,1,1,256,256]{4,3,2,1,0:T(8,128)S(1)}, f32[1,1,1,256,256]{4,3,2,1,0:T(8,128)}, u32[]{:S(2)}) copy-start(f32[1,1,1,256,256]{4,3,2,1,0:T(8,128)} %param.9) | copy-start | bytes 786436
  14.9 5.6 %collective-permute-start.4 = (f32[8,16,256]{2,1,0:T(8,128)S(1)}, f32[8,16,256]{2,1,0:T(8,128)S(1)}, u32[]{:S(2)}, u32[]{:S(2)}) collective-permute-start(f32[8,16,256]{2,1,0:T(8,128)S(1)} %add.160), channel_id=1, source_target_pairs={{0,16},{4,12},{8,24},{12,4},{16,0},{20,28},{24,8},{28,20},{1,17},{... | collective-permute-start | bytes 393224 | tf_op jit(solution)/shard_map/sum_relay_near/ppermute | solution.py:18
  16.3 7.1 %collective-permute-start.12 = (f32[8,8,256]{2,1,0:T(8,128)S(1)}, f32[8,8,256]{2,1,0:T(8,128)S(1)}, u32[]{:S(2)}, u32[]{:S(2)}) collective-permute-start(f32[8,8,256]{2,1,0:T(8,128)S(1)} %get-tuple-element.81), channel_id=1, source_target_pairs={{0,2},{1,3},{2,0},{3,1},{4,6},{5,7},{6,4},{7,5},{8,10},{9,11},{10,... | collective-permute-start | bytes 196616 | tf_op jit(solution)/shard_map/shard_2/ppermute | solution.py:18
  19.1 6.2 %collective-permute-start.11 = (f32[8,8,256]{2,1,0:T(8,128)S(1)}, f32[8,8,256]{2,1,0:T(8,128)S(1)}, u32[]{:S(2)}, u32[]{:S(2)}) collective-permute-start(f32[8,8,256]{2,1,0:T(8,128)S(1)} %get-tuple-element.80), channel_id=1, source_target_pairs={{0,3},{1,2},{2,1},{3,0},{4,7},{5,6},{6,5},{7,4},{8,11},{9,10},{10,... | collective-permute-start | bytes 196616 | tf_op jit(solution)/shard_map/shard_3/ppermute | solution.py:18
  20.5 19.7 %copy-start.5 = (f32[1,1,1,256,256]{4,3,2,1,0:T(8,128)S(1)}, f32[1,1,1,256,256]{4,3,2,1,0:T(8,128)}, u32[]{:S(2)}) copy-start(f32[1,1,1,256,256]{4,3,2,1,0:T(8,128)} %param.11) | copy-start | bytes 786436
  20.5 19.7 %copy-start.6 = (f32[1,1,1,256,256]{4,3,2,1,0:T(8,128)S(1)}, f32[1,1,1,256,256]{4,3,2,1,0:T(8,128)}, u32[]{:S(2)}) copy-start(f32[1,1,1,256,256]{4,3,2,1,0:T(8,128)} %param.12) | copy-start | bytes 786436
  20.6 5.0 %collective-permute-start.7 = (f32[8,8,256]{2,1,0:T(8,128)S(1)}, f32[8,8,256]{2,1,0:T(8,128)S(1)}, u32[]{:S(2)}, u32[]{:S(2)}) collective-permute-start(f32[8,8,256]{2,1,0:T(8,128)S(1)} %get-tuple-element.79), channel_id=1, source_target_pairs={{0,1},{1,0},{2,3},{3,2},{4,5},{5,4},{6,7},{7,6},{8,9},{9,8},{10,11... | collective-permute-start | bytes 196616 | tf_op jit(solution)/shard_map/shard_1/ppermute | solution.py:18
  41.0 18.1 %copy-start.2 = (f32[8,32,256]{2,1,0:T(8,128)S(1)}, f32[8,32,256]{2,1,0:T(8,128)}, u32[]{:S(2)}) copy-start(f32[8,32,256]{2,1,0:T(8,128)} %param.8) | copy-start | bytes 786436
  41.0 20.3 %copy-start.1 = (f32[8,32,256]{2,1,0:T(8,128)S(1)}, f32[8,32,256]{2,1,0:T(8,128)}, u32[]{:S(2)}) copy-start(f32[8,32,256]{2,1,0:T(8,128)} %param.8) | copy-start | bytes 786436
  54.5 6.9 %collective-permute-start.13 = (f32[8,8,256]{2,1,0:T(8,128)S(1)}, f32[8,8,256]{2,1,0:T(8,128)S(1)}, u32[]{:S(2)}, u32[]{:S(2)}) collective-permute-start(f32[8,8,256]{2,1,0:T(8,128)S(1)} %copy.58), channel_id=1, source_target_pairs={{0,3},{1,2},{2,1},{3,0},{4,7},{5,6},{6,5},{7,4},{8,11},{9,10},{10,... | collective-permute-start | bytes 196616 | tf_op jit(solution)/shard_map/shard_3/ppermute | solution.py:18
  56.4 7.2 %collective-permute-start.14 = (f32[8,8,256]{2,1,0:T(8,128)S(1)}, f32[8,8,256]{2,1,0:T(8,128)S(1)}, u32[]{:S(2)}, u32[]{:S(2)}) collective-permute-start(f32[8,8,256]{2,1,0:T(8,128)S(1)} %copy.59), channel_id=1, source_target_pairs={{0,2},{1,3},{2,0},{3,1},{4,6},{5,7},{6,4},{7,5},{8,10},{9,11},{10,... | collective-permute-start | bytes 196616 | tf_op jit(solution)/shard_map/shard_2/ppermute | solution.py:18
  57.3 6.4 %collective-permute-start.15 = (f32[8,8,256]{2,1,0:T(8,128)S(1)}, f32[8,8,256]{2,1,0:T(8,128)S(1)}, u32[]{:S(2)}, u32[]{:S(2)}) collective-permute-start(f32[8,8,256]{2,1,0:T(8,128)S(1)} %copy.60), channel_id=1, source_target_pairs={{0,1},{1,0},{2,3},{3,2},{4,5},{5,4},{6,7},{7,6},{8,9},{9,8},{10,11... | collective-permute-start | bytes 196616 | tf_op jit(solution)/shard_map/shard_1/ppermute | solution.py:18
  63.7 6.4 %collective-permute-start.16 = (f32[4,32,256]{2,1,0:T(8,128)S(1)}, f32[4,32,256]{2,1,0:T(8,128)S(1)}, u32[]{:S(2)}, u32[]{:S(2)}) collective-permute-start(f32[4,32,256]{2,1,0:T(8,128)S(1)} %get-tuple-element.63), channel_id=1, source_target_pairs={{0,8},{4,20},{8,0},{12,28},{16,24},{20,4},{24,16},{28,12},{1,9},{5... | collective-permute-start | bytes 393224 | tf_op jit(solution)/shard_map/rows_first_top/ppermute | solution.py:18
  64.6 6.4 %collective-permute-start.20 = (f32[4,32,256]{2,1,0:T(8,128)S(1)}, f32[4,32,256]{2,1,0:T(8,128)S(1)}, u32[]{:S(2)}, u32[]{:S(2)}) collective-permute-start(f32[4,32,256]{2,1,0:T(8,128)S(1)} %get-tuple-element.62), channel_id=1, source_target_pairs={{0,16},{4,12},{8,24},{12,4},{16,0},{20,28},{24,8},{28,20},{1,17},{... | collective-permute-start | bytes 393224 | tf_op jit(solution)/shard_map/rows_second_low/ppermute | solution.py:18
  65.2 7.4 %collective-permute-start.18 = (f32[4,32,256]{2,1,0:T(8,128)S(1)}, f32[4,32,256]{2,1,0:T(8,128)S(1)}, u32[]{:S(2)}, u32[]{:S(2)}) collective-permute-start(f32[4,32,256]{2,1,0:T(8,128)S(1)} %get-tuple-element.62), channel_id=1, source_target_pairs={{0,8},{4,20},{8,0},{12,28},{16,24},{20,4},{24,16},{28,12},{1,9},{5... | collective-permute-start | bytes 393224 | tf_op jit(solution)/shard_map/rows_first_low/ppermute | solution.py:18
  66.7 5.9 %collective-permute-start.19 = (f32[4,32,256]{2,1,0:T(8,128)S(1)}, f32[4,32,256]{2,1,0:T(8,128)S(1)}, u32[]{:S(2)}, u32[]{:S(2)}) collective-permute-start(f32[4,32,256]{2,1,0:T(8,128)S(1)} %get-tuple-element.63), channel_id=1, source_target_pairs={{0,16},{4,12},{8,24},{12,4},{16,0},{20,28},{24,8},{28,20},{1,17},{... | collective-permute-start | bytes 393224 | tf_op jit(solution)/shard_map/rows_second_top/ppermute | solution.py:18
  70.1 6.9 %collective-permute-start.17 = (f32[8,32,256]{2,1,0:T(8,128)S(1)}, f32[8,32,256]{2,1,0:T(8,128)S(1)}, u32[]{:S(2)}, u32[]{:S(2)}) collective-permute-start(f32[8,32,256]{2,1,0:T(8,128)S(1)} %subtract_dynamic-update-slice_fusion), channel_id=1, source_target_pairs={{0,4},{4,0},{8,12},{12,8},{16,20},{20,16},{24,28},{28,24},{1,5},{5... | collective-permute-start | bytes 786440 | tf_op jit(solution)/shard_map/rows_core_own/ppermute | solution.py:18
  70.1 6.3 %collective-permute-start.21 = (f32[4,32,256]{2,1,0:T(8,128)S(1)}, f32[4,32,256]{2,1,0:T(8,128)S(1)}, u32[]{:S(2)}, u32[]{:S(2)}) collective-permute-start(f32[4,32,256]{2,1,0:T(8,128)S(1)} %collective-permute-done.16), channel_id=1, source_target_pairs={{0,16},{4,12},{8,24},{12,4},{16,0},{20,28},{24,8},{28,20},{1,17},{... | collective-permute-start | bytes 393224 | tf_op jit(solution)/shard_map/rows_relay_top/ppermute | solution.py:18
  71.0 5.9 %collective-permute-start.24 = (f32[4,32,256]{2,1,0:T(8,128)S(1)}, f32[4,32,256]{2,1,0:T(8,128)S(1)}, u32[]{:S(2)}, u32[]{:S(2)}) collective-permute-start(f32[4,32,256]{2,1,0:T(8,128)S(1)} %collective-permute-done.20), channel_id=1, source_target_pairs={{0,8},{4,20},{8,0},{12,28},{16,24},{20,4},{24,16},{28,12},{1,9},{5... | collective-permute-start | bytes 393224 | tf_op jit(solution)/shard_map/rows_relay_low/ppermute | solution.py:18
  76.4 1.5 %collective-permute-start.22 = (f32[8,32,256]{2,1,0:T(8,128)S(1)}, f32[8,32,256]{2,1,0:T(8,128)S(1)}, u32[]{:S(2)}, u32[]{:S(2)}) collective-permute-start(f32[8,32,256]{2,1,0:T(8,128)S(1)} %pad_maximum_fusion.1), channel_id=1, source_target_pairs={{0,4},{4,0},{8,12},{12,8},{16,20},{20,16},{24,28},{28,24},{1,5},{5... | collective-permute-start | bytes 786440 | tf_op jit(solution)/shard_map/rows_core_first/ppermute | solution.py:18
  76.4 1.9 %collective-permute-start.23 = (f32[8,32,256]{2,1,0:T(8,128)S(1)}, f32[8,32,256]{2,1,0:T(8,128)S(1)}, u32[]{:S(2)}, u32[]{:S(2)}) collective-permute-start(f32[8,32,256]{2,1,0:T(8,128)S(1)} %pad_maximum_fusion.2), channel_id=1, source_target_pairs={{0,4},{4,0},{8,12},{12,8},{16,20},{20,16},{24,28},{28,24},{1,5},{5... | collective-permute-start | bytes 786440 | tf_op jit(solution)/shard_map/rows_core_second/ppermute | solution.py:18
  76.9 1.7 %collective-permute-start.25 = (f32[8,32,256]{2,1,0:T(8,128)S(1)}, f32[8,32,256]{2,1,0:T(8,128)S(1)}, u32[]{:S(2)}, u32[]{:S(2)}) collective-permute-start(f32[8,32,256]{2,1,0:T(8,128)S(1)} %constant_dynamic-update-slice_fusion.6), channel_id=1, source_target_pairs={{0,4},{4,0},{8,12},{12,8},{16,20},{20,16},{24,28},{28,24},{1,5},{5... | collective-permute-start | bytes 786440 | tf_op jit(solution)/shard_map/rows_core_far/ppermute | solution.py:18
  (4 other events, 43.5 us)

commit v14 on v9

--- a/solution.py
+++ b/solution.py
@@ -79,7 +79,7 @@
 def routed(partials, params, left_basis, right_basis, first_moment, second_moment, owner_list):
     high = lax.Precision.HIGH
     core, across = 1, 6
-    first_link, second_link = (2, 4), (4, 2)
+    first_link, second_link = (4, 2), (2, 4)
     near_order = (0, 1, 3, 2)
     shard_here = lax.axis_index("shard")
     data_here = lax.axis_index("dp")

time: 78.9 us -> 78.9 us (level)
  no operation moved by 1% of the time
where the time goes in v14:
time: 78.9 us; the launch traced here: 78.7 us
  starting transfers between devices  27.2 us (34%)
  blocking collectives  26.4 us (33%)
  waiting for transfers between devices  17.4 us (22%)
  local copies, waits for them, and re-layouts  3.76 us (5%)
  matrix products  1.93 us (2%)
  between operations  1.27 us (2%)
    ppermute x26, starting transfers between devices, swap(): return lax.ppermute(values, name, pairs)  27.2 us
    ppermute x26, waiting for transfers between devices, swap(): return lax.ppermute(values, name, pairs)  17.4 us
    all_to_all x1, blocking collectives, routed(): lax.all_to_all(leaving.reshape((device_total,) + piece), ('dp', 'shard'),...  13.7 us
    all_to_all x1, blocking collectives, routed(): lax.all_to_all(change.reshape((device_total,) + piece), ('dp', 'shard'),...  12.7 us
  transfers between devices with their start and end apart: 26, of which 15 were waited for; matrix products, arithmetic and copies ran while one was open for 2% of the time, Pallas kernels for 0%

profile of v14, /device:TPU:0, one launch (start us, length us, event | category | flops | bytes accessed | tf_op | source)
XLA Modules:
  0.0 78.7 jit_solution(4976786118431770528)
XLA Ops:
  0.7 1.3 %dynamic-slice_bitcast_fusion = (bf16[8,4,32,256]{3,2,1,0:T(8,128)(2,1)S(1)}, bf16[8,4,32,256]{3,2,1,0:T(8,128)(2,1)S(1)}) fusion(bf16[8,4,2,32,256]{4,3,2,1,0:T(8,128)(2,1)} %bitcast.130, s32[]{:T(128)S(6)} %select_n.130, s32[]{:T(128)S(6)} %select_n.129), kind=kLoop, calls=%fused_computation.1 | loop fusion | bytes 2097160 | tf_op jit(solution)/shard_map/jit(dynamic_index_in_dim)/squeeze | solution.py:22
  3.3 0.6 collective-permute-done
  4.0 3.0 %collective-permute-start.9 = (f32[8,16,256]{2,1,0:T(8,128)S(1)}, f32[8,16,256]{2,1,0:T(8,128)S(1)}, u32[]{:S(2)}, u32[]{:S(2)}) collective-permute-start(f32[8,16,256]{2,1,0:T(8,128)S(1)} %get-tuple-element.41), channel_id=1, source_target_pairs={{0,16},{4,12},{8,24},{12,4},{16,0},{20,28},{24,8},{28,20},{1,17},{... | collective-permute-start | bytes 393224 | tf_op jit(solution)/shard_map/sum_across_far/ppermute | solution.py:18
  7.1 1.0 %collective-permute-start.8 = (f32[8,16,256]{2,1,0:T(8,128)S(1)}, f32[8,16,256]{2,1,0:T(8,128)S(1)}, u32[]{:S(2)}, u32[]{:S(2)}) collective-permute-start(f32[8,16,256]{2,1,0:T(8,128)S(1)} %get-tuple-element.39), channel_id=1, source_target_pairs={{0,16},{4,12},{8,24},{12,4},{16,0},{20,28},{24,8},{28,20},{1,17},{... | collective-permute-start | bytes 393224 | tf_op jit(solution)/shard_map/sum_first_far/ppermute | solution.py:18
  8.2 1.1 %collective-permute-start.3 = (f32[8,16,256]{2,1,0:T(8,128)S(1)}, f32[8,16,256]{2,1,0:T(8,128)S(1)}, u32[]{:S(2)}, u32[]{:S(2)}) collective-permute-start(f32[8,16,256]{2,1,0:T(8,128)S(1)} %get-tuple-element.34), channel_id=1, source_target_pairs={{0,16},{4,12},{8,24},{12,4},{16,0},{20,28},{24,8},{28,20},{1,17},{... | collective-permute-start | bytes 393224 | tf_op jit(solution)/shard_map/sum_across_near/ppermute | solution.py:18
  9.2 0.6 collective-permute-done.9
  9.9 2.1 %collective-permute-start.10 = (f32[8,16,256]{2,1,0:T(8,128)S(1)}, f32[8,16,256]{2,1,0:T(8,128)S(1)}, u32[]{:S(2)}, u32[]{:S(2)}) collective-permute-start(f32[8,16,256]{2,1,0:T(8,128)S(1)} %add.167), channel_id=1, source_target_pairs={{0,8},{4,20},{8,0},{12,28},{16,24},{20,4},{24,16},{28,12},{1,9},{5... | collective-permute-start | bytes 393224 | tf_op jit(solution)/shard_map/sum_relay_far/ppermute | solution.py:18
  12.0 1.6 %collective-permute-start.6 = (f32[8,16,256]{2,1,0:T(8,128)S(1)}, f32[8,16,256]{2,1,0:T(8,128)S(1)}, u32[]{:S(2)}, u32[]{:S(2)}) collective-permute-start(f32[8,16,256]{2,1,0:T(8,128)S(1)} %get-tuple-element.35), channel_id=1, source_target_pairs={{0,16},{4,12},{8,24},{12,4},{16,0},{20,28},{24,8},{28,20},{1,17},{... | collective-permute-start | bytes 393224 | tf_op jit(solution)/shard_map/sum_first_near/ppermute | solution.py:18
  13.6 1.4 %collective-permute-done.3 = f32[8,16,256]{2,1,0:T(8,128)S(1)} collective-permute-done((f32[8,16,256]{2,1,0:T(8,128)S(1)}, f32[8,16,256]{2,1,0:T(8,128)S(1)}, u32[]{:S(2)}, u32[]{:S(2)}) %collective-permute-start.3) | collective-permute-done | bytes 131104 | tf_op jit(solution)/shard_map/sum_across_near/ppermute | solution.py:18
  15.0 1.3 %collective-permute-start.4 = (f32[8,16,256]{2,1,0:T(8,128)S(1)}, f32[8,16,256]{2,1,0:T(8,128)S(1)}, u32[]{:S(2)}, u32[]{:S(2)}) collective-permute-start(f32[8,16,256]{2,1,0:T(8,128)S(1)} %add.160), channel_id=1, source_target_pairs={{0,8},{4,20},{8,0},{12,28},{16,24},{20,4},{24,16},{28,12},{1,9},{5... | collective-permute-start | bytes 393224 | tf_op jit(solution)/shard_map/sum_relay_near/ppermute | solution.py:18
  16.4 2.8 %collective-permute-start.12 = (f32[8,8,256]{2,1,0:T(8,128)S(1)}, f32[8,8,256]{2,1,0:T(8,128)S(1)}, u32[]{:S(2)}, u32[]{:S(2)}) collective-permute-start(f32[8,8,256]{2,1,0:T(8,128)S(1)} %get-tuple-element.79), channel_id=1, source_target_pairs={{0,2},{1,3},{2,0},{3,1},{4,6},{5,7},{6,4},{7,5},{8,10},{9,11},{10,... | collective-permute-start | bytes 196616 | tf_op jit(solution)/shard_map/shard_2/ppermute | solution.py:18
  19.2 1.3 %collective-permute-start.11 = (f32[8,8,256]{2,1,0:T(8,128)S(1)}, f32[8,8,256]{2,1,0:T(8,128)S(1)}, u32[]{:S(2)}, u32[]{:S(2)}) collective-permute-start(f32[8,8,256]{2,1,0:T(8,128)S(1)} %get-tuple-element.78), channel_id=1, source_target_pairs={{0,3},{1,2},{2,1},{3,0},{4,7},{5,6},{6,5},{7,4},{8,11},{9,10},{10,... | collective-permute-start | bytes 196616 | tf_op jit(solution)/shard_map/shard_3/ppermute | solution.py:18
  20.6 0.9 %collective-permute-start.7 = (f32[8,8,256]{2,1,0:T(8,128)S(1)}, f32[8,8,256]{2,1,0:T(8,128)S(1)}, u32[]{:S(2)}, u32[]{:S(2)}) collective-permute-start(f32[8,8,256]{2,1,0:T(8,128)S(1)} %get-tuple-element.77), channel_id=1, source_target_pairs={{0,1},{1,0},{2,3},{3,2},{4,5},{5,4},{6,7},{7,6},{8,9},{9,8},{10,11... | collective-permute-start | bytes 196616 | tf_op jit(solution)/shard_map/shard_1/ppermute | solution.py:18
  21.8 1.6 %collective-permute-done.12 = f32[8,8,256]{2,1,0:T(8,128)S(1)} collective-permute-done((f32[8,8,256]{2,1,0:T(8,128)S(1)}, f32[8,8,256]{2,1,0:T(8,128)S(1)}, u32[]{:S(2)}, u32[]{:S(2)}) %collective-permute-start.12) | collective-permute-done | bytes 65568 | tf_op jit(solution)/shard_map/shard_2/ppermute | solution.py:18
  23.5 1.9 %collective-permute-done.11 = f32[8,8,256]{2,1,0:T(8,128)S(1)} collective-permute-done((f32[8,8,256]{2,1,0:T(8,128)S(1)}, f32[8,8,256]{2,1,0:T(8,128)S(1)}, u32[]{:S(2)}, u32[]{:S(2)}) %collective-permute-start.11) | collective-permute-done | bytes 65568 | tf_op jit(solution)/shard_map/shard_3/ppermute | solution.py:18
  26.1 13.7 %all_to_all.10 = f32[32,8,256]{2,1,0:T(8,128)S(1)} all-to-all(f32[32,8,256]{2,1,0:T(8,128)S(1)} %copy.56), channel_id=1, replica_groups=mesh['dp'=8,'shard'=4] {'dp','shard'}, dimensions={0} | all-to-all | bytes 524288 | tf_op jit(solution)/shard_map/all_to_all | solution.py:153
  41.3 12.7 %all_to_all.11 = f32[32,8,256]{2,1,0:T(8,128)S(1)} all-to-all(f32[32,8,256]{2,1,0:T(8,128)S(1)} %convolution_bitcast_fusion), channel_id=1, replica_groups=mesh['dp'=8,'shard'=4] {'dp','shard'}, dimensions={0} | all-to-all | bytes 524288 | tf_op jit(solution)/shard_map/all_to_all | solution.py:170
  54.5 1.8 %collective-permute-start.13 = (f32[8,8,256]{2,1,0:T(8,128)S(1)}, f32[8,8,256]{2,1,0:T(8,128)S(1)}, u32[]{:S(2)}, u32[]{:S(2)}) collective-permute-start(f32[8,8,256]{2,1,0:T(8,128)S(1)} %copy.58), channel_id=1, source_target_pairs={{0,3},{1,2},{2,1},{3,0},{4,7},{5,6},{6,5},{7,4},{8,11},{9,10},{10,... | collective-permute-start | bytes 196616 | tf_op jit(solution)/shard_map/shard_3/ppermute | solution.py:18
  56.4 0.9 %collective-permute-start.14 = (f32[8,8,256]{2,1,0:T(8,128)S(1)}, f32[8,8,256]{2,1,0:T(8,128)S(1)}, u32[]{:S(2)}, u32[]{:S(2)}) collective-permute-start(f32[8,8,256]{2,1,0:T(8,128)S(1)} %copy.59), channel_id=1, source_target_pairs={{0,2},{1,3},{2,0},{3,1},{4,6},{5,7},{6,4},{7,5},{8,10},{9,11},{10,... | collective-permute-start | bytes 196616 | tf_op jit(solution)/shard_map/shard_2/ppermute | solution.py:18
  57.3 1.9 %collective-permute-start.15 = (f32[8,8,256]{2,1,0:T(8,128)S(1)}, f32[8,8,256]{2,1,0:T(8,128)S(1)}, u32[]{:S(2)}, u32[]{:S(2)}) collective-permute-start(f32[8,8,256]{2,1,0:T(8,128)S(1)} %copy.60), channel_id=1, source_target_pairs={{0,1},{1,0},{2,3},{3,2},{4,5},{5,4},{6,7},{7,6},{8,9},{9,8},{10,11... | collective-permute-start | bytes 196616 | tf_op jit(solution)/shard_map/shard_1/ppermute | solution.py:18
  59.3 2.2 %collective-permute-done.13 = f32[8,8,256]{2,1,0:T(8,128)S(1)} collective-permute-done((f32[8,8,256]{2,1,0:T(8,128)S(1)}, f32[8,8,256]{2,1,0:T(8,128)S(1)}, u32[]{:S(2)}, u32[]{:S(2)}) %collective-permute-start.13) | collective-permute-done | bytes 65568 | tf_op jit(solution)/shard_map/shard_3/ppermute | solution.py:18
  61.5 2.2 %collective-permute-done.14 = f32[8,8,256]{2,1,0:T(8,128)S(1)} collective-permute-done((f32[8,8,256]{2,1,0:T(8,128)S(1)}, f32[8,8,256]{2,1,0:T(8,128)S(1)}, u32[]{:S(2)}, u32[]{:S(2)}) %collective-permute-start.14) | collective-permute-done | bytes 65568 | tf_op jit(solution)/shard_map/shard_2/ppermute | solution.py:18
  63.7 1.0 %collective-permute-start.18 = (f32[4,32,256]{2,1,0:T(8,128)S(1)}, f32[4,32,256]{2,1,0:T(8,128)S(1)}, u32[]{:S(2)}, u32[]{:S(2)}) collective-permute-start(f32[4,32,256]{2,1,0:T(8,128)S(1)} %get-tuple-element.61), channel_id=1, source_target_pairs={{0,16},{4,12},{8,24},{12,4},{16,0},{20,28},{24,8},{28,20},{1,17},{... | collective-permute-start | bytes 393224 | tf_op jit(solution)/shard_map/rows_first_top/ppermute | solution.py:18
  65.2 1.5 %collective-permute-start.17 = (f32[4,32,256]{2,1,0:T(8,128)S(1)}, f32[4,32,256]{2,1,0:T(8,128)S(1)}, u32[]{:S(2)}, u32[]{:S(2)}) collective-permute-start(f32[4,32,256]{2,1,0:T(8,128)S(1)} %get-tuple-element.60), channel_id=1, source_target_pairs={{0,16},{4,12},{8,24},{12,4},{16,0},{20,28},{24,8},{28,20},{1,17},{... | collective-permute-start | bytes 393224 | tf_op jit(solution)/shard_map/rows_first_low/ppermute | solution.py:18
  66.7 1.1 %collective-permute-start.19 = (f32[4,32,256]{2,1,0:T(8,128)S(1)}, f32[4,32,256]{2,1,0:T(8,128)S(1)}, u32[]{:S(2)}, u32[]{:S(2)}) collective-permute-start(f32[4,32,256]{2,1,0:T(8,128)S(1)} %get-tuple-element.61), channel_id=1, source_target_pairs={{0,8},{4,20},{8,0},{12,28},{16,24},{20,4},{24,16},{28,12},{1,9},{5... | collective-permute-start | bytes 393224 | tf_op jit(solution)/shard_map/rows_second_top/ppermute | solution.py:18
  68.0 1.8 %collective-permute-done.18 = f32[4,32,256]{2,1,0:T(8,128)S(1)} collective-permute-done((f32[4,32,256]{2,1,0:T(8,128)S(1)}, f32[4,32,256]{2,1,0:T(8,128)S(1)}, u32[]{:S(2)}, u32[]{:S(2)}) %collective-permute-start.18) | collective-permute-done | bytes 131104 | tf_op jit(solution)/shard_map/rows_first_top/ppermute | solution.py:18
  69.8 1.0 %collective-permute-start.21 = (f32[4,32,256]{2,1,0:T(8,128)S(1)}, f32[4,32,256]{2,1,0:T(8,128)S(1)}, u32[]{:S(2)}, u32[]{:S(2)}) collective-permute-start(f32[4,32,256]{2,1,0:T(8,128)S(1)} %collective-permute-done.18), channel_id=1, source_target_pairs={{0,8},{4,20},{8,0},{12,28},{16,24},{20,4},{24,16},{28,12},{1,9},{5... | collective-permute-start | bytes 393224 | tf_op jit(solution)/shard_map/rows_relay_top/ppermute | solution.py:18
  70.7 0.8 collective-permute-start.24
  71.5 1.0 %collective-permute-done.17 = f32[4,32,256]{2,1,0:T(8,128)S(1)} collective-permute-done((f32[4,32,256]{2,1,0:T(8,128)S(1)}, f32[4,32,256]{2,1,0:T(8,128)S(1)}, u32[]{:S(2)}, u32[]{:S(2)}) %collective-permute-start.17) | collective-permute-done | bytes 131104 | tf_op jit(solution)/shard_map/rows_first_low/ppermute | solution.py:18
  72.6 2.4 %collective-permute-done.21 = f32[4,32,256]{2,1,0:T(8,128)S(1)} collective-permute-done((f32[4,32,256]{2,1,0:T(8,128)S(1)}, f32[4,32,256]{2,1,0:T(8,128)S(1)}, u32[]{:S(2)}, u32[]{:S(2)}) %collective-permute-start.21) | collective-permute-done | bytes 131104 | tf_op jit(solution)/shard_map/rows_relay_top/ppermute | solution.py:18
  75.9 0.7 collective-permute-done.22
  77.4 1.3 %copy-done.3 = f32[8,256,256]{2,1,0:T(8,128)} copy-done((f32[8,256,256]{2,1,0:T(8,128)}, f32[8,256,256]{2,1,0:T(8,128)S(1)}, u32[]{:S(2)}) %copy-start.3) | copy-done | bytes 2097176
  (100 shorter events, 7.1 us)
Async XLA Ops:
  0.6 39.6 %copy-start = (f32[1,1,1,256,256]{4,3,2,1,0:T(8,128)S(1)}, f32[1,1,1,256,256]{4,3,2,1,0:T(8,128)}, u32[]{:S(2)}) copy-start(f32[1,1,1,256,256]{4,3,2,1,0:T(8,128)} %param.10) | copy-start | bytes 786436
  2.2 1.7 %collective-permute-start = (f32[8,32,256]{2,1,0:T(8,128)S(1)}, f32[8,32,256]{2,1,0:T(8,128)S(1)}, u32[]{:S(2)}, u32[]{:S(2)}) collective-permute-start(f32[8,32,256]{2,1,0:T(8,128)S(1)} %get-tuple-element.59), channel_id=1, source_target_pairs={{0,4},{4,0},{8,12},{12,8},{16,20},{20,16},{24,28},{28,24},{1,5},{5... | collective-permute-start | bytes 786440 | tf_op jit(solution)/shard_map/sum_core_across/ppermute | solution.py:18
  2.7 4.2 %collective-permute-start.2 = (f32[8,32,256]{2,1,0:T(8,128)S(1)}, f32[8,32,256]{2,1,0:T(8,128)S(1)}, u32[]{:S(2)}, u32[]{:S(2)}) collective-permute-start(f32[8,32,256]{2,1,0:T(8,128)S(1)} %get-tuple-element.56), channel_id=1, source_target_pairs={{0,4},{4,0},{8,12},{12,8},{16,20},{20,16},{24,28},{28,24},{1,5},{5... | collective-permute-start | bytes 786440 | tf_op jit(solution)/shard_map/sum_core_second/ppermute | solution.py:18
  2.8 4.1 %collective-permute-start.5 = (f32[8,32,256]{2,1,0:T(8,128)S(1)}, f32[8,32,256]{2,1,0:T(8,128)S(1)}, u32[]{:S(2)}, u32[]{:S(2)}) collective-permute-start(f32[8,32,256]{2,1,0:T(8,128)S(1)} %get-tuple-element.57), channel_id=1, source_target_pairs={{0,4},{4,0},{8,12},{12,8},{16,20},{20,16},{24,28},{28,24},{1,5},{5... | collective-permute-start | bytes 786440 | tf_op jit(solution)/shard_map/sum_core_first/ppermute | solution.py:18
  3.2 3.7 %collective-permute-start.1 = (f32[8,32,256]{2,1,0:T(8,128)S(1)}, f32[8,32,256]{2,1,0:T(8,128)S(1)}, u32[]{:S(2)}, u32[]{:S(2)}) collective-permute-start(f32[8,32,256]{2,1,0:T(8,128)S(1)} %get-tuple-element.58), channel_id=1, source_target_pairs={{0,4},{4,0},{8,12},{12,8},{16,20},{20,16},{24,28},{28,24},{1,5},{5... | collective-permute-start | bytes 786440 | tf_op jit(solution)/shard_map/sum_core_own/ppermute | solution.py:18
  4.0 5.9 %collective-permute-start.9 = (f32[8,16,256]{2,1,0:T(8,128)S(1)}, f32[8,16,256]{2,1,0:T(8,128)S(1)}, u32[]{:S(2)}, u32[]{:S(2)}) collective-permute-start(f32[8,16,256]{2,1,0:T(8,128)S(1)} %get-tuple-element.41), channel_id=1, source_target_pairs={{0,16},{4,12},{8,24},{12,4},{16,0},{20,28},{24,8},{28,20},{1,17},{... | collective-permute-start | bytes 393224 | tf_op jit(solution)/shard_map/sum_across_far/ppermute | solution.py:18
  7.1 6.4 %collective-permute-start.8 = (f32[8,16,256]{2,1,0:T(8,128)S(1)}, f32[8,16,256]{2,1,0:T(8,128)S(1)}, u32[]{:S(2)}, u32[]{:S(2)}) collective-permute-start(f32[8,16,256]{2,1,0:T(8,128)S(1)} %get-tuple-element.39), channel_id=1, source_target_pairs={{0,16},{4,12},{8,24},{12,4},{16,0},{20,28},{24,8},{28,20},{1,17},{... | collective-permute-start | bytes 393224 | tf_op jit(solution)/shard_map/sum_first_far/ppermute | solution.py:18
  8.2 6.8 %collective-permute-start.3 = (f32[8,16,256]{2,1,0:T(8,128)S(1)}, f32[8,16,256]{2,1,0:T(8,128)S(1)}, u32[]{:S(2)}, u32[]{:S(2)}) collective-permute-start(f32[8,16,256]{2,1,0:T(8,128)S(1)} %get-tuple-element.34), channel_id=1, source_target_pairs={{0,16},{4,12},{8,24},{12,4},{16,0},{20,28},{24,8},{28,20},{1,17},{... | collective-permute-start | bytes 393224 | tf_op jit(solution)/shard_map/sum_across_near/ppermute | solution.py:18
  9.9 6.4 %collective-permute-start.10 = (f32[8,16,256]{2,1,0:T(8,128)S(1)}, f32[8,16,256]{2,1,0:T(8,128)S(1)}, u32[]{:S(2)}, u32[]{:S(2)}) collective-permute-start(f32[8,16,256]{2,1,0:T(8,128)S(1)} %add.167), channel_id=1, source_target_pairs={{0,8},{4,20},{8,0},{12,28},{16,24},{20,4},{24,16},{28,12},{1,9},{5... | collective-permute-start | bytes 393224 | tf_op jit(solution)/shard_map/sum_relay_far/ppermute | solution.py:18
  12.0 8.6 %collective-permute-start.6 = (f32[8,16,256]{2,1,0:T(8,128)S(1)}, f32[8,16,256]{2,1,0:T(8,128)S(1)}, u32[]{:S(2)}, u32[]{:S(2)}) collective-permute-start(f32[8,16,256]{2,1,0:T(8,128)S(1)} %get-tuple-element.35), channel_id=1, source_target_pairs={{0,16},{4,12},{8,24},{12,4},{16,0},{20,28},{24,8},{28,20},{1,17},{... | collective-permute-start | bytes 393224 | tf_op jit(solution)/shard_map/sum_first_near/ppermute | solution.py:18
  15.0 24.8 %copy-start.4 = (f32[1,1,1,256,256]{4,3,2,1,0:T(8,128)S(1)}, f32[1,1,1,256,256]{4,3,2,1,0:T(8,128)}, u32[]{:S(2)}) copy-start(f32[1,1,1,256,256]{4,3,2,1,0:T(8,128)} %param.9) | copy-start | bytes 786436
  15.0 5.5 %collective-permute-start.4 = (f32[8,16,256]{2,1,0:T(8,128)S(1)}, f32[8,16,256]{2,1,0:T(8,128)S(1)}, u32[]{:S(2)}, u32[]{:S(2)}) collective-permute-start(f32[8,16,256]{2,1,0:T(8,128)S(1)} %add.160), channel_id=1, source_target_pairs={{0,8},{4,20},{8,0},{12,28},{16,24},{20,4},{24,16},{28,12},{1,9},{5... | collective-permute-start | bytes 393224 | tf_op jit(solution)/shard_map/sum_relay_near/ppermute | solution.py:18
  16.4 7.1 %collective-permute-start.12 = (f32[8,8,256]{2,1,0:T(8,128)S(1)}, f32[8,8,256]{2,1,0:T(8,128)S(1)}, u32[]{:S(2)}, u32[]{:S(2)}) collective-permute-start(f32[8,8,256]{2,1,0:T(8,128)S(1)} %get-tuple-element.79), channel_id=1, source_target_pairs={{0,2},{1,3},{2,0},{3,1},{4,6},{5,7},{6,4},{7,5},{8,10},{9,11},{10,... | collective-permute-start | bytes 196616 | tf_op jit(solution)/shard_map/shard_2/ppermute | solution.py:18
  19.2 6.2 %collective-permute-start.11 = (f32[8,8,256]{2,1,0:T(8,128)S(1)}, f32[8,8,256]{2,1,0:T(8,128)S(1)}, u32[]{:S(2)}, u32[]{:S(2)}) collective-permute-start(f32[8,8,256]{2,1,0:T(8,128)S(1)} %get-tuple-element.78), channel_id=1, source_target_pairs={{0,3},{1,2},{2,1},{3,0},{4,7},{5,6},{6,5},{7,4},{8,11},{9,10},{10,... | collective-permute-start | bytes 196616 | tf_op jit(solution)/shard_map/shard_3/ppermute | solution.py:18
  20.5 19.7 %copy-start.5 = (f32[1,1,1,256,256]{4,3,2,1,0:T(8,128)S(1)}, f32[1,1,1,256,256]{4,3,2,1,0:T(8,128)}, u32[]{:S(2)}) copy-start(f32[1,1,1,256,256]{4,3,2,1,0:T(8,128)} %param.11) | copy-start | bytes 786436
  20.5 19.7 %copy-start.6 = (f32[1,1,1,256,256]{4,3,2,1,0:T(8,128)S(1)}, f32[1,1,1,256,256]{4,3,2,1,0:T(8,128)}, u32[]{:S(2)}) copy-start(f32[1,1,1,256,256]{4,3,2,1,0:T(8,128)} %param.12) | copy-start | bytes 786436
  20.6 5.0 %collective-permute-start.7 = (f32[8,8,256]{2,1,0:T(8,128)S(1)}, f32[8,8,256]{2,1,0:T(8,128)S(1)}, u32[]{:S(2)}, u32[]{:S(2)}) collective-permute-start(f32[8,8,256]{2,1,0:T(8,128)S(1)} %get-tuple-element.77), channel_id=1, source_target_pairs={{0,1},{1,0},{2,3},{3,2},{4,5},{5,4},{6,7},{7,6},{8,9},{9,8},{10,11... | collective-permute-start | bytes 196616 | tf_op jit(solution)/shard_map/shard_1/ppermute | solution.py:18
  41.0 18.2 %copy-start.2 = (f32[8,32,256]{2,1,0:T(8,128)S(1)}, f32[8,32,256]{2,1,0:T(8,128)}, u32[]{:S(2)}) copy-start(f32[8,32,256]{2,1,0:T(8,128)} %param.8) | copy-start | bytes 786436
  41.0 20.4 %copy-start.1 = (f32[8,32,256]{2,1,0:T(8,128)S(1)}, f32[8,32,256]{2,1,0:T(8,128)}, u32[]{:S(2)}) copy-start(f32[8,32,256]{2,1,0:T(8,128)} %param.8) | copy-start | bytes 786436
  54.5 6.9 %collective-permute-start.13 = (f32[8,8,256]{2,1,0:T(8,128)S(1)}, f32[8,8,256]{2,1,0:T(8,128)S(1)}, u32[]{:S(2)}, u32[]{:S(2)}) collective-permute-start(f32[8,8,256]{2,1,0:T(8,128)S(1)} %copy.58), channel_id=1, source_target_pairs={{0,3},{1,2},{2,1},{3,0},{4,7},{5,6},{6,5},{7,4},{8,11},{9,10},{10,... | collective-permute-start | bytes 196616 | tf_op jit(solution)/shard_map/shard_3/ppermute | solution.py:18
  56.4 7.2 %collective-permute-start.14 = (f32[8,8,256]{2,1,0:T(8,128)S(1)}, f32[8,8,256]{2,1,0:T(8,128)S(1)}, u32[]{:S(2)}, u32[]{:S(2)}) collective-permute-start(f32[8,8,256]{2,1,0:T(8,128)S(1)} %copy.59), channel_id=1, source_target_pairs={{0,2},{1,3},{2,0},{3,1},{4,6},{5,7},{6,4},{7,5},{8,10},{9,11},{10,... | collective-permute-start | bytes 196616 | tf_op jit(solution)/shard_map/shard_2/ppermute | solution.py:18
  57.3 6.4 %collective-permute-start.15 = (f32[8,8,256]{2,1,0:T(8,128)S(1)}, f32[8,8,256]{2,1,0:T(8,128)S(1)}, u32[]{:S(2)}, u32[]{:S(2)}) collective-permute-start(f32[8,8,256]{2,1,0:T(8,128)S(1)} %copy.60), channel_id=1, source_target_pairs={{0,1},{1,0},{2,3},{3,2},{4,5},{5,4},{6,7},{7,6},{8,9},{9,8},{10,11... | collective-permute-start | bytes 196616 | tf_op jit(solution)/shard_map/shard_1/ppermute | solution.py:18
  63.7 6.1 %collective-permute-start.18 = (f32[4,32,256]{2,1,0:T(8,128)S(1)}, f32[4,32,256]{2,1,0:T(8,128)S(1)}, u32[]{:S(2)}, u32[]{:S(2)}) collective-permute-start(f32[4,32,256]{2,1,0:T(8,128)S(1)} %get-tuple-element.61), channel_id=1, source_target_pairs={{0,16},{4,12},{8,24},{12,4},{16,0},{20,28},{24,8},{28,20},{1,17},{... | collective-permute-start | bytes 393224 | tf_op jit(solution)/shard_map/rows_first_top/ppermute | solution.py:18
  64.7 6.1 %collective-permute-start.20 = (f32[4,32,256]{2,1,0:T(8,128)S(1)}, f32[4,32,256]{2,1,0:T(8,128)S(1)}, u32[]{:S(2)}, u32[]{:S(2)}) collective-permute-start(f32[4,32,256]{2,1,0:T(8,128)S(1)} %get-tuple-element.60), channel_id=1, source_target_pairs={{0,8},{4,20},{8,0},{12,28},{16,24},{20,4},{24,16},{28,12},{1,9},{5... | collective-permute-start | bytes 393224 | tf_op jit(solution)/shard_map/rows_second_low/ppermute | solution.py:18
  65.2 7.3 %collective-permute-start.17 = (f32[4,32,256]{2,1,0:T(8,128)S(1)}, f32[4,32,256]{2,1,0:T(8,128)S(1)}, u32[]{:S(2)}, u32[]{:S(2)}) collective-permute-start(f32[4,32,256]{2,1,0:T(8,128)S(1)} %get-tuple-element.60), channel_id=1, source_target_pairs={{0,16},{4,12},{8,24},{12,4},{16,0},{20,28},{24,8},{28,20},{1,17},{... | collective-permute-start | bytes 393224 | tf_op jit(solution)/shard_map/rows_first_low/ppermute | solution.py:18
  66.7 5.9 %collective-permute-start.16 = (f32[8,32,256]{2,1,0:T(8,128)S(1)}, f32[8,32,256]{2,1,0:T(8,128)S(1)}, u32[]{:S(2)}, u32[]{:S(2)}) collective-permute-start(f32[8,32,256]{2,1,0:T(8,128)S(1)} %subtract_dynamic-update-slice_fusion), channel_id=1, source_target_pairs={{0,4},{4,0},{8,12},{12,8},{16,20},{20,16},{24,28},{28,24},{1,5},{5... | collective-permute-start | bytes 786440 | tf_op jit(solution)/shard_map/rows_core_own/ppermute | solution.py:18
  66.7 5.9 %collective-permute-start.19 = (f32[4,32,256]{2,1,0:T(8,128)S(1)}, f32[4,32,256]{2,1,0:T(8,128)S(1)}, u32[]{:S(2)}, u32[]{:S(2)}) collective-permute-start(f32[4,32,256]{2,1,0:T(8,128)S(1)} %get-tuple-element.61), channel_id=1, source_target_pairs={{0,8},{4,20},{8,0},{12,28},{16,24},{20,4},{24,16},{28,12},{1,9},{5... | collective-permute-start | bytes 393224 | tf_op jit(solution)/shard_map/rows_second_top/ppermute | solution.py:18
  69.8 5.3 %collective-permute-start.21 = (f32[4,32,256]{2,1,0:T(8,128)S(1)}, f32[4,32,256]{2,1,0:T(8,128)S(1)}, u32[]{:S(2)}, u32[]{:S(2)}) collective-permute-start(f32[4,32,256]{2,1,0:T(8,128)S(1)} %collective-permute-done.18), channel_id=1, source_target_pairs={{0,8},{4,20},{8,0},{12,28},{16,24},{20,4},{24,16},{28,12},{1,9},{5... | collective-permute-start | bytes 393224 | tf_op jit(solution)/shard_map/rows_relay_top/ppermute | solution.py:18
  70.7 5.0 %collective-permute-start.24 = (f32[4,32,256]{2,1,0:T(8,128)S(1)}, f32[4,32,256]{2,1,0:T(8,128)S(1)}, u32[]{:S(2)}, u32[]{:S(2)}) collective-permute-start(f32[4,32,256]{2,1,0:T(8,128)S(1)} %collective-permute-done.20), channel_id=1, source_target_pairs={{0,16},{4,12},{8,24},{12,4},{16,0},{20,28},{24,8},{28,20},{1,17},{... | collective-permute-start | bytes 393224 | tf_op jit(solution)/shard_map/rows_relay_low/ppermute | solution.py:18
  75.0 1.5 %collective-permute-start.22 = (f32[8,32,256]{2,1,0:T(8,128)S(1)}, f32[8,32,256]{2,1,0:T(8,128)S(1)}, u32[]{:S(2)}, u32[]{:S(2)}) collective-permute-start(f32[8,32,256]{2,1,0:T(8,128)S(1)} %pad_maximum_fusion.1), channel_id=1, source_target_pairs={{0,4},{4,0},{8,12},{12,8},{16,20},{20,16},{24,28},{28,24},{1,5},{5... | collective-permute-start | bytes 786440 | tf_op jit(solution)/shard_map/rows_core_first/ppermute | solution.py:18
  75.0 1.9 %collective-permute-start.23 = (f32[8,32,256]{2,1,0:T(8,128)S(1)}, f32[8,32,256]{2,1,0:T(8,128)S(1)}, u32[]{:S(2)}, u32[]{:S(2)}) collective-permute-start(f32[8,32,256]{2,1,0:T(8,128)S(1)} %pad_maximum_fusion.2), channel_id=1, source_target_pairs={{0,4},{4,0},{8,12},{12,8},{16,20},{20,16},{24,28},{28,24},{1,5},{5... | collective-permute-start | bytes 786440 | tf_op jit(solution)/shard_map/rows_core_second/ppermute | solution.py:18
  75.7 1.6 %collective-permute-start.25 = (f32[8,32,256]{2,1,0:T(8,128)S(1)}, f32[8,32,256]{2,1,0:T(8,128)S(1)}, u32[]{:S(2)}, u32[]{:S(2)}) collective-permute-start(f32[8,32,256]{2,1,0:T(8,128)S(1)} %constant_dynamic-update-slice_fusion.6), channel_id=1, source_target_pairs={{0,4},{4,0},{8,12},{12,8},{16,20},{20,16},{24,28},{28,24},{1,5},{5... | collective-permute-start | bytes 786440 | tf_op jit(solution)/shard_map/rows_core_far/ppermute | solution.py:18
  (4 other events, 43.5 us)

commit v15 on v9

--- a/solution.py
+++ b/solution.py
@@ -80,7 +80,7 @@
     high = lax.Precision.HIGH
     core, across = 1, 6
     first_link, second_link = (2, 4), (4, 2)
-    near_order = (0, 1, 3, 2)
+    near_order = (0, 1, 2, 3)
     shard_here = lax.axis_index("shard")
     data_here = lax.axis_index("dp")
     shard_count = lax.axis_size("shard")

time: 78.9 us -> 79.4 us (level)
  transfers between devices with their start and end apart: 26 -> 26, of which waited for: 15 -> 14; matrix products, arithmetic and copies ran while one was open for 2% -> 2% of each run, Pallas kernels for 0% -> 0%
where the time goes in v15:
time: 79.4 us; the launch traced here: 79.2 us
  starting transfers between devices  27.2 us (34%)
  blocking collectives  27.1 us (34%)
  waiting for transfers between devices  17.3 us (22%)
  local copies, waits for them, and re-layouts  3.77 us (5%)
  matrix products  1.93 us (2%)
  between operations  1.29 us (2%)
    ppermute x26, starting transfers between devices, swap(): return lax.ppermute(values, name, pairs)  27.2 us
    ppermute x26, waiting for transfers between devices, swap(): return lax.ppermute(values, name, pairs)  17.3 us
    all_to_all x1, blocking collectives, routed(): lax.all_to_all(leaving.reshape((device_total,) + piece), ('dp', 'shard'),...  14.4 us
    all_to_all x1, blocking collectives, routed(): lax.all_to_all(change.reshape((device_total,) + piece), ('dp', 'shard'),...  12.7 us
  transfers between devices with their start and end apart: 26, of which 14 were waited for; matrix products, arithmetic and copies ran while one was open for 2% of the time, Pallas kernels for 0%

profile of v15, /device:TPU:0, one launch (start us, length us, event | category | flops | bytes accessed | tf_op | source)
XLA Modules:
  0.0 79.2 jit_solution(8502185459831610814)
XLA Ops:
  0.7 1.3 %dynamic-slice_bitcast_fusion = (bf16[8,4,32,256]{3,2,1,0:T(8,128)(2,1)S(1)}, bf16[8,4,32,256]{3,2,1,0:T(8,128)(2,1)S(1)}) fusion(bf16[8,4,2,32,256]{4,3,2,1,0:T(8,128)(2,1)} %bitcast.130, s32[]{:T(128)S(6)} %select_n.130, s32[]{:T(128)S(6)} %select_n.129), kind=kLoop, calls=%fused_computation.1 | loop fusion | bytes 2097160 | tf_op jit(solution)/shard_map/jit(dynamic_index_in_dim)/squeeze | solution.py:22
  3.3 0.6 collective-permute-done
  4.0 2.9 %collective-permute-start.9 = (f32[8,16,256]{2,1,0:T(8,128)S(1)}, f32[8,16,256]{2,1,0:T(8,128)S(1)}, u32[]{:S(2)}, u32[]{:S(2)}) collective-permute-start(f32[8,16,256]{2,1,0:T(8,128)S(1)} %get-tuple-element.41), channel_id=1, source_target_pairs={{0,8},{4,20},{8,0},{12,28},{16,24},{20,4},{24,16},{28,12},{1,9},{5... | collective-permute-start | bytes 393224 | tf_op jit(solution)/shard_map/sum_across_far/ppermute | solution.py:18
  7.1 1.0 %collective-permute-start.8 = (f32[8,16,256]{2,1,0:T(8,128)S(1)}, f32[8,16,256]{2,1,0:T(8,128)S(1)}, u32[]{:S(2)}, u32[]{:S(2)}) collective-permute-start(f32[8,16,256]{2,1,0:T(8,128)S(1)} %get-tuple-element.39), channel_id=1, source_target_pairs={{0,8},{4,20},{8,0},{12,28},{16,24},{20,4},{24,16},{28,12},{1,9},{5... | collective-permute-start | bytes 393224 | tf_op jit(solution)/shard_map/sum_first_far/ppermute | solution.py:18
  8.1 1.1 %collective-permute-start.3 = (f32[8,16,256]{2,1,0:T(8,128)S(1)}, f32[8,16,256]{2,1,0:T(8,128)S(1)}, u32[]{:S(2)}, u32[]{:S(2)}) collective-permute-start(f32[8,16,256]{2,1,0:T(8,128)S(1)} %get-tuple-element.34), channel_id=1, source_target_pairs={{0,8},{4,20},{8,0},{12,28},{16,24},{20,4},{24,16},{28,12},{1,9},{5... | collective-permute-start | bytes 393224 | tf_op jit(solution)/shard_map/sum_across_near/ppermute | solution.py:18
  9.2 0.6 collective-permute-done.9
  9.8 2.1 %collective-permute-start.10 = (f32[8,16,256]{2,1,0:T(8,128)S(1)}, f32[8,16,256]{2,1,0:T(8,128)S(1)}, u32[]{:S(2)}, u32[]{:S(2)}) collective-permute-start(f32[8,16,256]{2,1,0:T(8,128)S(1)} %add.167), channel_id=1, source_target_pairs={{0,16},{4,12},{8,24},{12,4},{16,0},{20,28},{24,8},{28,20},{1,17},{... | collective-permute-start | bytes 393224 | tf_op jit(solution)/shard_map/sum_relay_far/ppermute | solution.py:18
  12.0 1.6 %collective-permute-start.6 = (f32[8,16,256]{2,1,0:T(8,128)S(1)}, f32[8,16,256]{2,1,0:T(8,128)S(1)}, u32[]{:S(2)}, u32[]{:S(2)}) collective-permute-start(f32[8,16,256]{2,1,0:T(8,128)S(1)} %get-tuple-element.35), channel_id=1, source_target_pairs={{0,8},{4,20},{8,0},{12,28},{16,24},{20,4},{24,16},{28,12},{1,9},{5... | collective-permute-start | bytes 393224 | tf_op jit(solution)/shard_map/sum_first_near/ppermute | solution.py:18
  13.6 1.3 %collective-permute-done.3 = f32[8,16,256]{2,1,0:T(8,128)S(1)} collective-permute-done((f32[8,16,256]{2,1,0:T(8,128)S(1)}, f32[8,16,256]{2,1,0:T(8,128)S(1)}, u32[]{:S(2)}, u32[]{:S(2)}) %collective-permute-start.3) | collective-permute-done | bytes 131104 | tf_op jit(solution)/shard_map/sum_across_near/ppermute | solution.py:18
  14.9 1.3 %collective-permute-start.4 = (f32[8,16,256]{2,1,0:T(8,128)S(1)}, f32[8,16,256]{2,1,0:T(8,128)S(1)}, u32[]{:S(2)}, u32[]{:S(2)}) collective-permute-start(f32[8,16,256]{2,1,0:T(8,128)S(1)} %add.160), channel_id=1, source_target_pairs={{0,16},{4,12},{8,24},{12,4},{16,0},{20,28},{24,8},{28,20},{1,17},{... | collective-permute-start | bytes 393224 | tf_op jit(solution)/shard_map/sum_relay_near/ppermute | solution.py:18
  16.3 3.8 %collective-permute-start.12 = (f32[8,8,256]{2,1,0:T(8,128)S(1)}, f32[8,8,256]{2,1,0:T(8,128)S(1)}, u32[]{:S(2)}, u32[]{:S(2)}) collective-permute-start(f32[8,8,256]{2,1,0:T(8,128)S(1)} %get-tuple-element.79), channel_id=1, source_target_pairs={{0,3},{1,2},{2,1},{3,0},{4,7},{5,6},{6,5},{7,4},{8,11},{9,10},{10,... | collective-permute-start | bytes 196616 | tf_op jit(solution)/shard_map/shard_3/ppermute | solution.py:18
  20.3 1.2 %collective-permute-start.7 = (f32[8,8,256]{2,1,0:T(8,128)S(1)}, f32[8,8,256]{2,1,0:T(8,128)S(1)}, u32[]{:S(2)}, u32[]{:S(2)}) collective-permute-start(f32[8,8,256]{2,1,0:T(8,128)S(1)} %get-tuple-element.77), channel_id=1, source_target_pairs={{0,1},{1,0},{2,3},{3,2},{4,5},{5,4},{6,7},{7,6},{8,9},{9,8},{10,11... | collective-permute-start | bytes 196616 | tf_op jit(solution)/shard_map/shard_1/ppermute | solution.py:18
  21.7 0.8 %collective-permute-done.12 = f32[8,8,256]{2,1,0:T(8,128)S(1)} collective-permute-done((f32[8,8,256]{2,1,0:T(8,128)S(1)}, f32[8,8,256]{2,1,0:T(8,128)S(1)}, u32[]{:S(2)}, u32[]{:S(2)}) %collective-permute-start.12) | collective-permute-done | bytes 65568 | tf_op jit(solution)/shard_map/shard_3/ppermute | solution.py:18
  22.6 2.9 %collective-permute-done.11 = f32[8,8,256]{2,1,0:T(8,128)S(1)} collective-permute-done((f32[8,8,256]{2,1,0:T(8,128)S(1)}, f32[8,8,256]{2,1,0:T(8,128)S(1)}, u32[]{:S(2)}, u32[]{:S(2)}) %collective-permute-start.11) | collective-permute-done | bytes 65568 | tf_op jit(solution)/shard_map/shard_2/ppermute | solution.py:18
  25.9 14.4 %all_to_all.10 = f32[32,8,256]{2,1,0:T(8,128)S(1)} all-to-all(f32[32,8,256]{2,1,0:T(8,128)S(1)} %copy.56), channel_id=1, replica_groups=mesh['dp'=8,'shard'=4] {'dp','shard'}, dimensions={0} | all-to-all | bytes 524288 | tf_op jit(solution)/shard_map/all_to_all | solution.py:153
  41.8 12.7 %all_to_all.11 = f32[32,8,256]{2,1,0:T(8,128)S(1)} all-to-all(f32[32,8,256]{2,1,0:T(8,128)S(1)} %convolution_bitcast_fusion), channel_id=1, replica_groups=mesh['dp'=8,'shard'=4] {'dp','shard'}, dimensions={0} | all-to-all | bytes 524288 | tf_op jit(solution)/shard_map/all_to_all | solution.py:170
  55.0 1.8 %collective-permute-start.13 = (f32[8,8,256]{2,1,0:T(8,128)S(1)}, f32[8,8,256]{2,1,0:T(8,128)S(1)}, u32[]{:S(2)}, u32[]{:S(2)}) collective-permute-start(f32[8,8,256]{2,1,0:T(8,128)S(1)} %copy.58), channel_id=1, source_target_pairs={{0,3},{1,2},{2,1},{3,0},{4,7},{5,6},{6,5},{7,4},{8,11},{9,10},{10,... | collective-permute-start | bytes 196616 | tf_op jit(solution)/shard_map/shard_3/ppermute | solution.py:18
  56.9 0.9 %collective-permute-start.14 = (f32[8,8,256]{2,1,0:T(8,128)S(1)}, f32[8,8,256]{2,1,0:T(8,128)S(1)}, u32[]{:S(2)}, u32[]{:S(2)}) collective-permute-start(f32[8,8,256]{2,1,0:T(8,128)S(1)} %copy.59), channel_id=1, source_target_pairs={{0,2},{1,3},{2,0},{3,1},{4,6},{5,7},{6,4},{7,5},{8,10},{9,11},{10,... | collective-permute-start | bytes 196616 | tf_op jit(solution)/shard_map/shard_2/ppermute | solution.py:18
  57.8 1.9 %collective-permute-start.15 = (f32[8,8,256]{2,1,0:T(8,128)S(1)}, f32[8,8,256]{2,1,0:T(8,128)S(1)}, u32[]{:S(2)}, u32[]{:S(2)}) collective-permute-start(f32[8,8,256]{2,1,0:T(8,128)S(1)} %copy.60), channel_id=1, source_target_pairs={{0,1},{1,0},{2,3},{3,2},{4,5},{5,4},{6,7},{7,6},{8,9},{9,8},{10,11... | collective-permute-start | bytes 196616 | tf_op jit(solution)/shard_map/shard_1/ppermute | solution.py:18
  59.7 2.2 %collective-permute-done.13 = f32[8,8,256]{2,1,0:T(8,128)S(1)} collective-permute-done((f32[8,8,256]{2,1,0:T(8,128)S(1)}, f32[8,8,256]{2,1,0:T(8,128)S(1)}, u32[]{:S(2)}, u32[]{:S(2)}) %collective-permute-start.13) | collective-permute-done | bytes 65568 | tf_op jit(solution)/shard_map/shard_3/ppermute | solution.py:18
  61.9 2.2 %collective-permute-done.14 = f32[8,8,256]{2,1,0:T(8,128)S(1)} collective-permute-done((f32[8,8,256]{2,1,0:T(8,128)S(1)}, f32[8,8,256]{2,1,0:T(8,128)S(1)}, u32[]{:S(2)}, u32[]{:S(2)}) %collective-permute-start.14) | collective-permute-done | bytes 65568 | tf_op jit(solution)/shard_map/shard_2/ppermute | solution.py:18
  64.2 0.9 %collective-permute-start.18 = (f32[4,32,256]{2,1,0:T(8,128)S(1)}, f32[4,32,256]{2,1,0:T(8,128)S(1)}, u32[]{:S(2)}, u32[]{:S(2)}) collective-permute-start(f32[4,32,256]{2,1,0:T(8,128)S(1)} %get-tuple-element.61), channel_id=1, source_target_pairs={{0,8},{4,20},{8,0},{12,28},{16,24},{20,4},{24,16},{28,12},{1,9},{5... | collective-permute-start | bytes 393224 | tf_op jit(solution)/shard_map/rows_first_top/ppermute | solution.py:18
  65.1 0.6 collective-permute-start.20
  65.7 1.5 %collective-permute-start.17 = (f32[4,32,256]{2,1,0:T(8,128)S(1)}, f32[4,32,256]{2,1,0:T(8,128)S(1)}, u32[]{:S(2)}, u32[]{:S(2)}) collective-permute-start(f32[4,32,256]{2,1,0:T(8,128)S(1)} %get-tuple-element.60), channel_id=1, source_target_pairs={{0,8},{4,20},{8,0},{12,28},{16,24},{20,4},{24,16},{28,12},{1,9},{5... | collective-permute-start | bytes 393224 | tf_op jit(solution)/shard_map/rows_first_low/ppermute | solution.py:18
  67.2 1.1 %collective-permute-start.19 = (f32[4,32,256]{2,1,0:T(8,128)S(1)}, f32[4,32,256]{2,1,0:T(8,128)S(1)}, u32[]{:S(2)}, u32[]{:S(2)}) collective-permute-start(f32[4,32,256]{2,1,0:T(8,128)S(1)} %get-tuple-element.61), channel_id=1, source_target_pairs={{0,16},{4,12},{8,24},{12,4},{16,0},{20,28},{24,8},{28,20},{1,17},{... | collective-permute-start | bytes 393224 | tf_op jit(solution)/shard_map/rows_second_top/ppermute | solution.py:18
  68.5 1.8 %collective-permute-done.18 = f32[4,32,256]{2,1,0:T(8,128)S(1)} collective-permute-done((f32[4,32,256]{2,1,0:T(8,128)S(1)}, f32[4,32,256]{2,1,0:T(8,128)S(1)}, u32[]{:S(2)}, u32[]{:S(2)}) %collective-permute-start.18) | collective-permute-done | bytes 131104 | tf_op jit(solution)/shard_map/rows_first_top/ppermute | solution.py:18
  70.3 0.9 %collective-permute-start.21 = (f32[4,32,256]{2,1,0:T(8,128)S(1)}, f32[4,32,256]{2,1,0:T(8,128)S(1)}, u32[]{:S(2)}, u32[]{:S(2)}) collective-permute-start(f32[4,32,256]{2,1,0:T(8,128)S(1)} %collective-permute-done.18), channel_id=1, source_target_pairs={{0,16},{4,12},{8,24},{12,4},{16,0},{20,28},{24,8},{28,20},{1,17},{... | collective-permute-start | bytes 393224 | tf_op jit(solution)/shard_map/rows_relay_top/ppermute | solution.py:18
  71.2 0.8 %collective-permute-start.24 = (f32[4,32,256]{2,1,0:T(8,128)S(1)}, f32[4,32,256]{2,1,0:T(8,128)S(1)}, u32[]{:S(2)}, u32[]{:S(2)}) collective-permute-start(f32[4,32,256]{2,1,0:T(8,128)S(1)} %collective-permute-done.20), channel_id=1, source_target_pairs={{0,8},{4,20},{8,0},{12,28},{16,24},{20,4},{24,16},{28,12},{1,9},{5... | collective-permute-start | bytes 393224 | tf_op jit(solution)/shard_map/rows_relay_low/ppermute | solution.py:18
  72.0 1.0 %collective-permute-done.17 = f32[4,32,256]{2,1,0:T(8,128)S(1)} collective-permute-done((f32[4,32,256]{2,1,0:T(8,128)S(1)}, f32[4,32,256]{2,1,0:T(8,128)S(1)}, u32[]{:S(2)}, u32[]{:S(2)}) %collective-permute-start.17) | collective-permute-done | bytes 131104 | tf_op jit(solution)/shard_map/rows_first_low/ppermute | solution.py:18
  73.1 2.3 %collective-permute-done.21 = f32[4,32,256]{2,1,0:T(8,128)S(1)} collective-permute-done((f32[4,32,256]{2,1,0:T(8,128)S(1)}, f32[4,32,256]{2,1,0:T(8,128)S(1)}, u32[]{:S(2)}, u32[]{:S(2)}) %collective-permute-start.21) | collective-permute-done | bytes 131104 | tf_op jit(solution)/shard_map/rows_relay_top/ppermute | solution.py:18
  76.4 0.6 collective-permute-done.22
  77.9 1.3 %copy-done.3 = f32[8,256,256]{2,1,0:T(8,128)} copy-done((f32[8,256,256]{2,1,0:T(8,128)}, f32[8,256,256]{2,1,0:T(8,128)S(1)}, u32[]{:S(2)}) %copy-start.3) | copy-done | bytes 2097176
  (100 shorter events, 6.4 us)
Async XLA Ops:
  0.6 40.0 %copy-start = (f32[1,1,1,256,256]{4,3,2,1,0:T(8,128)S(1)}, f32[1,1,1,256,256]{4,3,2,1,0:T(8,128)}, u32[]{:S(2)}) copy-start(f32[1,1,1,256,256]{4,3,2,1,0:T(8,128)} %param.10) | copy-start | bytes 786436
  2.2 1.7 %collective-permute-start = (f32[8,32,256]{2,1,0:T(8,128)S(1)}, f32[8,32,256]{2,1,0:T(8,128)S(1)}, u32[]{:S(2)}, u32[]{:S(2)}) collective-permute-start(f32[8,32,256]{2,1,0:T(8,128)S(1)} %get-tuple-element.59), channel_id=1, source_target_pairs={{0,4},{4,0},{8,12},{12,8},{16,20},{20,16},{24,28},{28,24},{1,5},{5... | collective-permute-start | bytes 786440 | tf_op jit(solution)/shard_map/sum_core_across/ppermute | solution.py:18
  2.7 4.2 %collective-permute-start.2 = (f32[8,32,256]{2,1,0:T(8,128)S(1)}, f32[8,32,256]{2,1,0:T(8,128)S(1)}, u32[]{:S(2)}, u32[]{:S(2)}) collective-permute-start(f32[8,32,256]{2,1,0:T(8,128)S(1)} %get-tuple-element.56), channel_id=1, source_target_pairs={{0,4},{4,0},{8,12},{12,8},{16,20},{20,16},{24,28},{28,24},{1,5},{5... | collective-permute-start | bytes 786440 | tf_op jit(solution)/shard_map/sum_core_second/ppermute | solution.py:18
  2.8 4.1 %collective-permute-start.5 = (f32[8,32,256]{2,1,0:T(8,128)S(1)}, f32[8,32,256]{2,1,0:T(8,128)S(1)}, u32[]{:S(2)}, u32[]{:S(2)}) collective-permute-start(f32[8,32,256]{2,1,0:T(8,128)S(1)} %get-tuple-element.57), channel_id=1, source_target_pairs={{0,4},{4,0},{8,12},{12,8},{16,20},{20,16},{24,28},{28,24},{1,5},{5... | collective-permute-start | bytes 786440 | tf_op jit(solution)/shard_map/sum_core_first/ppermute | solution.py:18
  3.2 3.6 %collective-permute-start.1 = (f32[8,32,256]{2,1,0:T(8,128)S(1)}, f32[8,32,256]{2,1,0:T(8,128)S(1)}, u32[]{:S(2)}, u32[]{:S(2)}) collective-permute-start(f32[8,32,256]{2,1,0:T(8,128)S(1)} %get-tuple-element.58), channel_id=1, source_target_pairs={{0,4},{4,0},{8,12},{12,8},{16,20},{20,16},{24,28},{28,24},{1,5},{5... | collective-permute-start | bytes 786440 | tf_op jit(solution)/shard_map/sum_core_own/ppermute | solution.py:18
  4.0 5.9 %collective-permute-start.9 = (f32[8,16,256]{2,1,0:T(8,128)S(1)}, f32[8,16,256]{2,1,0:T(8,128)S(1)}, u32[]{:S(2)}, u32[]{:S(2)}) collective-permute-start(f32[8,16,256]{2,1,0:T(8,128)S(1)} %get-tuple-element.41), channel_id=1, source_target_pairs={{0,8},{4,20},{8,0},{12,28},{16,24},{20,4},{24,16},{28,12},{1,9},{5... | collective-permute-start | bytes 393224 | tf_op jit(solution)/shard_map/sum_across_far/ppermute | solution.py:18
  7.1 6.5 %collective-permute-start.8 = (f32[8,16,256]{2,1,0:T(8,128)S(1)}, f32[8,16,256]{2,1,0:T(8,128)S(1)}, u32[]{:S(2)}, u32[]{:S(2)}) collective-permute-start(f32[8,16,256]{2,1,0:T(8,128)S(1)} %get-tuple-element.39), channel_id=1, source_target_pairs={{0,8},{4,20},{8,0},{12,28},{16,24},{20,4},{24,16},{28,12},{1,9},{5... | collective-permute-start | bytes 393224 | tf_op jit(solution)/shard_map/sum_first_far/ppermute | solution.py:18
  8.1 6.8 %collective-permute-start.3 = (f32[8,16,256]{2,1,0:T(8,128)S(1)}, f32[8,16,256]{2,1,0:T(8,128)S(1)}, u32[]{:S(2)}, u32[]{:S(2)}) collective-permute-start(f32[8,16,256]{2,1,0:T(8,128)S(1)} %get-tuple-element.34), channel_id=1, source_target_pairs={{0,8},{4,20},{8,0},{12,28},{16,24},{20,4},{24,16},{28,12},{1,9},{5... | collective-permute-start | bytes 393224 | tf_op jit(solution)/shard_map/sum_across_near/ppermute | solution.py:18
  9.8 6.4 %collective-permute-start.10 = (f32[8,16,256]{2,1,0:T(8,128)S(1)}, f32[8,16,256]{2,1,0:T(8,128)S(1)}, u32[]{:S(2)}, u32[]{:S(2)}) collective-permute-start(f32[8,16,256]{2,1,0:T(8,128)S(1)} %add.167), channel_id=1, source_target_pairs={{0,16},{4,12},{8,24},{12,4},{16,0},{20,28},{24,8},{28,20},{1,17},{... | collective-permute-start | bytes 393224 | tf_op jit(solution)/shard_map/sum_relay_far/ppermute | solution.py:18
  12.0 8.2 %collective-permute-start.6 = (f32[8,16,256]{2,1,0:T(8,128)S(1)}, f32[8,16,256]{2,1,0:T(8,128)S(1)}, u32[]{:S(2)}, u32[]{:S(2)}) collective-permute-start(f32[8,16,256]{2,1,0:T(8,128)S(1)} %get-tuple-element.35), channel_id=1, source_target_pairs={{0,8},{4,20},{8,0},{12,28},{16,24},{20,4},{24,16},{28,12},{1,9},{5... | collective-permute-start | bytes 393224 | tf_op jit(solution)/shard_map/sum_first_near/ppermute | solution.py:18
  14.9 25.4 %copy-start.4 = (f32[1,1,1,256,256]{4,3,2,1,0:T(8,128)S(1)}, f32[1,1,1,256,256]{4,3,2,1,0:T(8,128)}, u32[]{:S(2)}) copy-start(f32[1,1,1,256,256]{4,3,2,1,0:T(8,128)} %param.9) | copy-start | bytes 786436
  14.9 5.2 %collective-permute-start.4 = (f32[8,16,256]{2,1,0:T(8,128)S(1)}, f32[8,16,256]{2,1,0:T(8,128)S(1)}, u32[]{:S(2)}, u32[]{:S(2)}) collective-permute-start(f32[8,16,256]{2,1,0:T(8,128)S(1)} %add.160), channel_id=1, source_target_pairs={{0,16},{4,12},{8,24},{12,4},{16,0},{20,28},{24,8},{28,20},{1,17},{... | collective-permute-start | bytes 393224 | tf_op jit(solution)/shard_map/sum_relay_near/ppermute | solution.py:18
  16.3 6.2 %collective-permute-start.12 = (f32[8,8,256]{2,1,0:T(8,128)S(1)}, f32[8,8,256]{2,1,0:T(8,128)S(1)}, u32[]{:S(2)}, u32[]{:S(2)}) collective-permute-start(f32[8,8,256]{2,1,0:T(8,128)S(1)} %get-tuple-element.79), channel_id=1, source_target_pairs={{0,3},{1,2},{2,1},{3,0},{4,7},{5,6},{6,5},{7,4},{8,11},{9,10},{10,... | collective-permute-start | bytes 196616 | tf_op jit(solution)/shard_map/shard_3/ppermute | solution.py:18
  20.1 5.3 %collective-permute-start.11 = (f32[8,8,256]{2,1,0:T(8,128)S(1)}, f32[8,8,256]{2,1,0:T(8,128)S(1)}, u32[]{:S(2)}, u32[]{:S(2)}) collective-permute-start(f32[8,8,256]{2,1,0:T(8,128)S(1)} %get-tuple-element.78), channel_id=1, source_target_pairs={{0,2},{1,3},{2,0},{3,1},{4,6},{5,7},{6,4},{7,5},{8,10},{9,11},{10,... | collective-permute-start | bytes 196616 | tf_op jit(solution)/shard_map/shard_2/ppermute | solution.py:18
  20.2 20.5 %copy-start.5 = (f32[1,1,1,256,256]{4,3,2,1,0:T(8,128)S(1)}, f32[1,1,1,256,256]{4,3,2,1,0:T(8,128)}, u32[]{:S(2)}) copy-start(f32[1,1,1,256,256]{4,3,2,1,0:T(8,128)} %param.11) | copy-start | bytes 786436
  20.2 20.5 %copy-start.6 = (f32[1,1,1,256,256]{4,3,2,1,0:T(8,128)S(1)}, f32[1,1,1,256,256]{4,3,2,1,0:T(8,128)}, u32[]{:S(2)}) copy-start(f32[1,1,1,256,256]{4,3,2,1,0:T(8,128)} %param.12) | copy-start | bytes 786436
  20.3 5.2 %collective-permute-start.7 = (f32[8,8,256]{2,1,0:T(8,128)S(1)}, f32[8,8,256]{2,1,0:T(8,128)S(1)}, u32[]{:S(2)}, u32[]{:S(2)}) collective-permute-start(f32[8,8,256]{2,1,0:T(8,128)S(1)} %get-tuple-element.77), channel_id=1, source_target_pairs={{0,1},{1,0},{2,3},{3,2},{4,5},{5,4},{6,7},{7,6},{8,9},{9,8},{10,11... | collective-permute-start | bytes 196616 | tf_op jit(solution)/shard_map/shard_1/ppermute | solution.py:18
  41.5 18.1 %copy-start.2 = (f32[8,32,256]{2,1,0:T(8,128)S(1)}, f32[8,32,256]{2,1,0:T(8,128)}, u32[]{:S(2)}) copy-start(f32[8,32,256]{2,1,0:T(8,128)} %param.8) | copy-start | bytes 786436
  41.5 20.3 %copy-start.1 = (f32[8,32,256]{2,1,0:T(8,128)S(1)}, f32[8,32,256]{2,1,0:T(8,128)}, u32[]{:S(2)}) copy-start(f32[8,32,256]{2,1,0:T(8,128)} %param.8) | copy-start | bytes 786436
  55.0 6.9 %collective-permute-start.13 = (f32[8,8,256]{2,1,0:T(8,128)S(1)}, f32[8,8,256]{2,1,0:T(8,128)S(1)}, u32[]{:S(2)}, u32[]{:S(2)}) collective-permute-start(f32[8,8,256]{2,1,0:T(8,128)S(1)} %copy.58), channel_id=1, source_target_pairs={{0,3},{1,2},{2,1},{3,0},{4,7},{5,6},{6,5},{7,4},{8,11},{9,10},{10,... | collective-permute-start | bytes 196616 | tf_op jit(solution)/shard_map/shard_3/ppermute | solution.py:18
  56.9 7.2 %collective-permute-start.14 = (f32[8,8,256]{2,1,0:T(8,128)S(1)}, f32[8,8,256]{2,1,0:T(8,128)S(1)}, u32[]{:S(2)}, u32[]{:S(2)}) collective-permute-start(f32[8,8,256]{2,1,0:T(8,128)S(1)} %copy.59), channel_id=1, source_target_pairs={{0,2},{1,3},{2,0},{3,1},{4,6},{5,7},{6,4},{7,5},{8,10},{9,11},{10,... | collective-permute-start | bytes 196616 | tf_op jit(solution)/shard_map/shard_2/ppermute | solution.py:18
  57.8 6.4 %collective-permute-start.15 = (f32[8,8,256]{2,1,0:T(8,128)S(1)}, f32[8,8,256]{2,1,0:T(8,128)S(1)}, u32[]{:S(2)}, u32[]{:S(2)}) collective-permute-start(f32[8,8,256]{2,1,0:T(8,128)S(1)} %copy.60), channel_id=1, source_target_pairs={{0,1},{1,0},{2,3},{3,2},{4,5},{5,4},{6,7},{7,6},{8,9},{9,8},{10,11... | collective-permute-start | bytes 196616 | tf_op jit(solution)/shard_map/shard_1/ppermute | solution.py:18
  64.2 6.1 %collective-permute-start.18 = (f32[4,32,256]{2,1,0:T(8,128)S(1)}, f32[4,32,256]{2,1,0:T(8,128)S(1)}, u32[]{:S(2)}, u32[]{:S(2)}) collective-permute-start(f32[4,32,256]{2,1,0:T(8,128)S(1)} %get-tuple-element.61), channel_id=1, source_target_pairs={{0,8},{4,20},{8,0},{12,28},{16,24},{20,4},{24,16},{28,12},{1,9},{5... | collective-permute-start | bytes 393224 | tf_op jit(solution)/shard_map/rows_first_top/ppermute | solution.py:18
  65.1 6.1 %collective-permute-start.20 = (f32[4,32,256]{2,1,0:T(8,128)S(1)}, f32[4,32,256]{2,1,0:T(8,128)S(1)}, u32[]{:S(2)}, u32[]{:S(2)}) collective-permute-start(f32[4,32,256]{2,1,0:T(8,128)S(1)} %get-tuple-element.60), channel_id=1, source_target_pairs={{0,16},{4,12},{8,24},{12,4},{16,0},{20,28},{24,8},{28,20},{1,17},{... | collective-permute-start | bytes 393224 | tf_op jit(solution)/shard_map/rows_second_low/ppermute | solution.py:18
  65.7 7.3 %collective-permute-start.17 = (f32[4,32,256]{2,1,0:T(8,128)S(1)}, f32[4,32,256]{2,1,0:T(8,128)S(1)}, u32[]{:S(2)}, u32[]{:S(2)}) collective-permute-start(f32[4,32,256]{2,1,0:T(8,128)S(1)} %get-tuple-element.60), channel_id=1, source_target_pairs={{0,8},{4,20},{8,0},{12,28},{16,24},{20,4},{24,16},{28,12},{1,9},{5... | collective-permute-start | bytes 393224 | tf_op jit(solution)/shard_map/rows_first_low/ppermute | solution.py:18
  67.2 5.9 %collective-permute-start.16 = (f32[8,32,256]{2,1,0:T(8,128)S(1)}, f32[8,32,256]{2,1,0:T(8,128)S(1)}, u32[]{:S(2)}, u32[]{:S(2)}) collective-permute-start(f32[8,32,256]{2,1,0:T(8,128)S(1)} %subtract_dynamic-update-slice_fusion), channel_id=1, source_target_pairs={{0,4},{4,0},{8,12},{12,8},{16,20},{20,16},{24,28},{28,24},{1,5},{5... | collective-permute-start | bytes 786440 | tf_op jit(solution)/shard_map/rows_core_own/ppermute | solution.py:18
  67.2 5.9 %collective-permute-start.19 = (f32[4,32,256]{2,1,0:T(8,128)S(1)}, f32[4,32,256]{2,1,0:T(8,128)S(1)}, u32[]{:S(2)}, u32[]{:S(2)}) collective-permute-start(f32[4,32,256]{2,1,0:T(8,128)S(1)} %get-tuple-element.61), channel_id=1, source_target_pairs={{0,16},{4,12},{8,24},{12,4},{16,0},{20,28},{24,8},{28,20},{1,17},{... | collective-permute-start | bytes 393224 | tf_op jit(solution)/shard_map/rows_second_top/ppermute | solution.py:18
  70.3 5.2 %collective-permute-start.21 = (f32[4,32,256]{2,1,0:T(8,128)S(1)}, f32[4,32,256]{2,1,0:T(8,128)S(1)}, u32[]{:S(2)}, u32[]{:S(2)}) collective-permute-start(f32[4,32,256]{2,1,0:T(8,128)S(1)} %collective-permute-done.18), channel_id=1, source_target_pairs={{0,16},{4,12},{8,24},{12,4},{16,0},{20,28},{24,8},{28,20},{1,17},{... | collective-permute-start | bytes 393224 | tf_op jit(solution)/shard_map/rows_relay_top/ppermute | solution.py:18
  71.2 5.0 %collective-permute-start.24 = (f32[4,32,256]{2,1,0:T(8,128)S(1)}, f32[4,32,256]{2,1,0:T(8,128)S(1)}, u32[]{:S(2)}, u32[]{:S(2)}) collective-permute-start(f32[4,32,256]{2,1,0:T(8,128)S(1)} %collective-permute-done.20), channel_id=1, source_target_pairs={{0,8},{4,20},{8,0},{12,28},{16,24},{20,4},{24,16},{28,12},{1,9},{5... | collective-permute-start | bytes 393224 | tf_op jit(solution)/shard_map/rows_relay_low/ppermute | solution.py:18
  75.5 1.5 %collective-permute-start.22 = (f32[8,32,256]{2,1,0:T(8,128)S(1)}, f32[8,32,256]{2,1,0:T(8,128)S(1)}, u32[]{:S(2)}, u32[]{:S(2)}) collective-permute-start(f32[8,32,256]{2,1,0:T(8,128)S(1)} %pad_maximum_fusion.1), channel_id=1, source_target_pairs={{0,4},{4,0},{8,12},{12,8},{16,20},{20,16},{24,28},{28,24},{1,5},{5... | collective-permute-start | bytes 786440 | tf_op jit(solution)/shard_map/rows_core_first/ppermute | solution.py:18
  75.5 1.9 %collective-permute-start.23 = (f32[8,32,256]{2,1,0:T(8,128)S(1)}, f32[8,32,256]{2,1,0:T(8,128)S(1)}, u32[]{:S(2)}, u32[]{:S(2)}) collective-permute-start(f32[8,32,256]{2,1,0:T(8,128)S(1)} %pad_maximum_fusion.2), channel_id=1, source_target_pairs={{0,4},{4,0},{8,12},{12,8},{16,20},{20,16},{24,28},{28,24},{1,5},{5... | collective-permute-start | bytes 786440 | tf_op jit(solution)/shard_map/rows_core_second/ppermute | solution.py:18
  76.2 1.6 %collective-permute-start.25 = (f32[8,32,256]{2,1,0:T(8,128)S(1)}, f32[8,32,256]{2,1,0:T(8,128)S(1)}, u32[]{:S(2)}, u32[]{:S(2)}) collective-permute-start(f32[8,32,256]{2,1,0:T(8,128)S(1)} %constant_dynamic-update-slice_fusion.6), channel_id=1, source_target_pairs={{0,4},{4,0},{8,12},{12,8},{16,20},{20,16},{24,28},{28,24},{1,5},{5... | collective-permute-start | bytes 786440 | tf_op jit(solution)/shard_map/rows_core_far/ppermute | solution.py:18
  (4 other events, 43.5 us)

commit v16 on v9

--- a/solution.py
+++ b/solution.py
@@ -198,28 +198,29 @@
     second_top = swap(top, "dp", second_link, "rows_second_top")
     far_top = swap(first_top, "dp", second_link, "rows_relay_top")
     far_low = swap(second_low, "dp", first_link, "rows_relay_low")
-    first_rows = jnp.concatenate([first_low, first_top], axis=0)
-    second_rows = jnp.concatenate([second_top, second_low], axis=0)
-    first_rows, second_rows, far_top, first_new, second_new = lax.optimization_barrier(
-        (first_rows, second_rows, far_top, first_new, second_new)
-    )
+
+    updated = jnp.zeros((home_count, width, width), jnp.float32)
+
+    def written(values, mask, block, rows):
+        start = (data_here ^ mask) * row_count
+        return lax.dynamic_update_slice(values, rows, (block, start, 0))
+
+    updated = written(updated, 0, 0, new_home)
+    updated = written(updated, core, 0, other)
+    for what, mask, block, rows in (
+        ("first_top", first_chip, half, first_top),
+        ("second_low", second_chip, 0, second_low),
+        ("first_low", first_chip, 0, first_low),
+        ("second_top", second_chip, half, second_top),
+    ):
+        twin = swap(rows, "dp", core, f"rows_core_{what}")
+        if what == "second_top":
+            twin, first_new, second_new = lax.optimization_barrier((twin, first_new, second_new))
+        updated = written(updated, mask, block, rows)
+        updated = written(updated, (across - mask) ^ core, block, twin)
     far_rows = jnp.concatenate([far_low, far_top], axis=0)
-    second_other = swap(second_rows, "dp", core, "rows_core_second")
-    updated = jnp.zeros((home_count, width, width), jnp.float32)
-    for mask, block, values in (
-        (0, 0, new_home),
-        (core, 0, other),
-        (first_chip, 0, first_rows),
-        (second_chip, half, second_rows[:half]),
-        (second_chip, 0, second_rows[half:]),
-        (second_chip ^ core, 0, swap(first_rows, "dp", core, "rows_core_first")),
-        (first_chip ^ core, half, second_other[:half]),
-        (first_chip ^ core, 0, second_other[half:]),
-        (across, 0, far_rows),
-        (across ^ core, 0, swap(far_rows, "dp", core, "rows_core_far")),
-    ):
-        start = (data_here ^ mask) * row_count
-        updated = lax.dynamic_update_slice(updated, values, (block, start, 0))
+    updated = written(updated, across, 0, far_rows)
+    updated = written(updated, across ^ core, 0, swap(far_rows, "dp", core, "rows_core_far"))
     return updated, first_new[None, None, None], second_new[None, None, None]
 
 

time: 78.9 us -> 79.9 us (1.013)
    ppermute x26 -> x28, starting transfers between devices: 27.2 us -> 27.9 us  [swap(): return lax.ppermute(values, name, pairs)]
    ppermute x26 -> x28, waiting for transfers between devices: 17.4 us -> 17.8 us  [swap(): return lax.ppermute(values, name, pairs)]
  transfers between devices with their start and end apart: 26 -> 28, of which waited for: 15 -> 14; matrix products, arithmetic and copies ran while one was open for 2% -> 1% of each run, Pallas kernels for 0% -> 0%
where the time goes in v16:
time: 79.9 us; the launch traced here: 79.7 us
  starting transfers between devices  27.9 us (35%)
  blocking collectives  26.5 us (33%)
  waiting for transfers between devices  17.8 us (22%)
  local copies, waits for them, and re-layouts  3.78 us (5%)
  matrix products  1.93 us (2%)
  between operations  1.3 us (2%)
    ppermute x28, starting transfers between devices, swap(): return lax.ppermute(values, name, pairs)  27.9 us
    ppermute x28, waiting for transfers between devices, swap(): return lax.ppermute(values, name, pairs)  17.8 us
    all_to_all x1, blocking collectives, routed(): lax.all_to_all(leaving.reshape((device_total,) + piece), ('dp', 'shard'),...  13.7 us
    all_to_all x1, blocking collectives, routed(): lax.all_to_all(change.reshape((device_total,) + piece), ('dp', 'shard'),...  12.7 us
  transfers between devices with their start and end apart: 28, of which 14 were waited for; matrix products, arithmetic and copies ran while one was open for 1% of the time, Pallas kernels for 0%

profile of v16, /device:TPU:0, one launch (start us, length us, event | category | flops | bytes accessed | tf_op | source)
XLA Modules:
  0.0 79.7 jit_solution(10458587835049293111)
XLA Ops:
  0.7 1.3 %dynamic-slice_bitcast_fusion = (bf16[8,4,32,256]{3,2,1,0:T(8,128)(2,1)S(1)}, bf16[8,4,32,256]{3,2,1,0:T(8,128)(2,1)S(1)}) fusion(bf16[8,4,2,32,256]{4,3,2,1,0:T(8,128)(2,1)} %bitcast.130, s32[]{:T(128)S(6)} %select_n.132, s32[]{:T(128)S(6)} %select_n.131), kind=kLoop, calls=%fused_computation.1 | loop fusion | bytes 2097160 | tf_op jit(solution)/shard_map/jit(dynamic_index_in_dim)/squeeze | solution.py:22
  3.3 0.6 collective-permute-done
  4.0 2.9 %collective-permute-start.9 = (f32[8,16,256]{2,1,0:T(8,128)S(1)}, f32[8,16,256]{2,1,0:T(8,128)S(1)}, u32[]{:S(2)}, u32[]{:S(2)}) collective-permute-start(f32[8,16,256]{2,1,0:T(8,128)S(1)} %get-tuple-element.39), channel_id=1, source_target_pairs={{0,8},{4,20},{8,0},{12,28},{16,24},{20,4},{24,16},{28,12},{1,9},{5... | collective-permute-start | bytes 393224 | tf_op jit(solution)/shard_map/sum_across_far/ppermute | solution.py:18
  7.1 1.0 %collective-permute-start.8 = (f32[8,16,256]{2,1,0:T(8,128)S(1)}, f32[8,16,256]{2,1,0:T(8,128)S(1)}, u32[]{:S(2)}, u32[]{:S(2)}) collective-permute-start(f32[8,16,256]{2,1,0:T(8,128)S(1)} %get-tuple-element.37), channel_id=1, source_target_pairs={{0,8},{4,20},{8,0},{12,28},{16,24},{20,4},{24,16},{28,12},{1,9},{5... | collective-permute-start | bytes 393224 | tf_op jit(solution)/shard_map/sum_first_far/ppermute | solution.py:18
  8.1 1.1 %collective-permute-start.3 = (f32[8,16,256]{2,1,0:T(8,128)S(1)}, f32[8,16,256]{2,1,0:T(8,128)S(1)}, u32[]{:S(2)}, u32[]{:S(2)}) collective-permute-start(f32[8,16,256]{2,1,0:T(8,128)S(1)} %get-tuple-element.32), channel_id=1, source_target_pairs={{0,8},{4,20},{8,0},{12,28},{16,24},{20,4},{24,16},{28,12},{1,9},{5... | collective-permute-start | bytes 393224 | tf_op jit(solution)/shard_map/sum_across_near/ppermute | solution.py:18
  9.2 0.6 collective-permute-done.9
  9.8 2.1 %collective-permute-start.10 = (f32[8,16,256]{2,1,0:T(8,128)S(1)}, f32[8,16,256]{2,1,0:T(8,128)S(1)}, u32[]{:S(2)}, u32[]{:S(2)}) collective-permute-start(f32[8,16,256]{2,1,0:T(8,128)S(1)} %add.169), channel_id=1, source_target_pairs={{0,16},{4,12},{8,24},{12,4},{16,0},{20,28},{24,8},{28,20},{1,17},{... | collective-permute-start | bytes 393224 | tf_op jit(solution)/shard_map/sum_relay_far/ppermute | solution.py:18
  12.0 1.6 %collective-permute-start.6 = (f32[8,16,256]{2,1,0:T(8,128)S(1)}, f32[8,16,256]{2,1,0:T(8,128)S(1)}, u32[]{:S(2)}, u32[]{:S(2)}) collective-permute-start(f32[8,16,256]{2,1,0:T(8,128)S(1)} %get-tuple-element.33), channel_id=1, source_target_pairs={{0,8},{4,20},{8,0},{12,28},{16,24},{20,4},{24,16},{28,12},{1,9},{5... | collective-permute-start | bytes 393224 | tf_op jit(solution)/shard_map/sum_first_near/ppermute | solution.py:18
  13.6 1.3 %collective-permute-done.3 = f32[8,16,256]{2,1,0:T(8,128)S(1)} collective-permute-done((f32[8,16,256]{2,1,0:T(8,128)S(1)}, f32[8,16,256]{2,1,0:T(8,128)S(1)}, u32[]{:S(2)}, u32[]{:S(2)}) %collective-permute-start.3) | collective-permute-done | bytes 131104 | tf_op jit(solution)/shard_map/sum_across_near/ppermute | solution.py:18
  14.9 1.3 %collective-permute-start.4 = (f32[8,16,256]{2,1,0:T(8,128)S(1)}, f32[8,16,256]{2,1,0:T(8,128)S(1)}, u32[]{:S(2)}, u32[]{:S(2)}) collective-permute-start(f32[8,16,256]{2,1,0:T(8,128)S(1)} %add.162), channel_id=1, source_target_pairs={{0,16},{4,12},{8,24},{12,4},{16,0},{20,28},{24,8},{28,20},{1,17},{... | collective-permute-start | bytes 393224 | tf_op jit(solution)/shard_map/sum_relay_near/ppermute | solution.py:18
  16.3 2.8 %collective-permute-start.12 = (f32[8,8,256]{2,1,0:T(8,128)S(1)}, f32[8,8,256]{2,1,0:T(8,128)S(1)}, u32[]{:S(2)}, u32[]{:S(2)}) collective-permute-start(f32[8,8,256]{2,1,0:T(8,128)S(1)} %get-tuple-element.75), channel_id=1, source_target_pairs={{0,2},{1,3},{2,0},{3,1},{4,6},{5,7},{6,4},{7,5},{8,10},{9,11},{10,... | collective-permute-start | bytes 196616 | tf_op jit(solution)/shard_map/shard_2/ppermute | solution.py:18
  19.1 1.3 %collective-permute-start.11 = (f32[8,8,256]{2,1,0:T(8,128)S(1)}, f32[8,8,256]{2,1,0:T(8,128)S(1)}, u32[]{:S(2)}, u32[]{:S(2)}) collective-permute-start(f32[8,8,256]{2,1,0:T(8,128)S(1)} %get-tuple-element.74), channel_id=1, source_target_pairs={{0,3},{1,2},{2,1},{3,0},{4,7},{5,6},{6,5},{7,4},{8,11},{9,10},{10,... | collective-permute-start | bytes 196616 | tf_op jit(solution)/shard_map/shard_3/ppermute | solution.py:18
  20.6 0.9 %collective-permute-start.7 = (f32[8,8,256]{2,1,0:T(8,128)S(1)}, f32[8,8,256]{2,1,0:T(8,128)S(1)}, u32[]{:S(2)}, u32[]{:S(2)}) collective-permute-start(f32[8,8,256]{2,1,0:T(8,128)S(1)} %get-tuple-element.73), channel_id=1, source_target_pairs={{0,1},{1,0},{2,3},{3,2},{4,5},{5,4},{6,7},{7,6},{8,9},{9,8},{10,11... | collective-permute-start | bytes 196616 | tf_op jit(solution)/shard_map/shard_1/ppermute | solution.py:18
  21.7 1.7 %collective-permute-done.12 = f32[8,8,256]{2,1,0:T(8,128)S(1)} collective-permute-done((f32[8,8,256]{2,1,0:T(8,128)S(1)}, f32[8,8,256]{2,1,0:T(8,128)S(1)}, u32[]{:S(2)}, u32[]{:S(2)}) %collective-permute-start.12) | collective-permute-done | bytes 65568 | tf_op jit(solution)/shard_map/shard_2/ppermute | solution.py:18
  23.5 1.8 %collective-permute-done.11 = f32[8,8,256]{2,1,0:T(8,128)S(1)} collective-permute-done((f32[8,8,256]{2,1,0:T(8,128)S(1)}, f32[8,8,256]{2,1,0:T(8,128)S(1)}, u32[]{:S(2)}, u32[]{:S(2)}) %collective-permute-start.11) | collective-permute-done | bytes 65568 | tf_op jit(solution)/shard_map/shard_3/ppermute | solution.py:18
  26.1 13.7 %all_to_all.10 = f32[32,8,256]{2,1,0:T(8,128)S(1)} all-to-all(f32[32,8,256]{2,1,0:T(8,128)S(1)} %copy.56), channel_id=1, replica_groups=mesh['dp'=8,'shard'=4] {'dp','shard'}, dimensions={0} | all-to-all | bytes 524288 | tf_op jit(solution)/shard_map/all_to_all | solution.py:153
  41.3 12.7 %all_to_all.11 = f32[32,8,256]{2,1,0:T(8,128)S(1)} all-to-all(f32[32,8,256]{2,1,0:T(8,128)S(1)} %convolution_bitcast_fusion), channel_id=1, replica_groups=mesh['dp'=8,'shard'=4] {'dp','shard'}, dimensions={0} | all-to-all | bytes 524288 | tf_op jit(solution)/shard_map/all_to_all | solution.py:170
  54.5 1.8 %collective-permute-start.13 = (f32[8,8,256]{2,1,0:T(8,128)S(1)}, f32[8,8,256]{2,1,0:T(8,128)S(1)}, u32[]{:S(2)}, u32[]{:S(2)}) collective-permute-start(f32[8,8,256]{2,1,0:T(8,128)S(1)} %copy.58), channel_id=1, source_target_pairs={{0,3},{1,2},{2,1},{3,0},{4,7},{5,6},{6,5},{7,4},{8,11},{9,10},{10,... | collective-permute-start | bytes 196616 | tf_op jit(solution)/shard_map/shard_3/ppermute | solution.py:18
  56.4 0.9 %collective-permute-start.14 = (f32[8,8,256]{2,1,0:T(8,128)S(1)}, f32[8,8,256]{2,1,0:T(8,128)S(1)}, u32[]{:S(2)}, u32[]{:S(2)}) collective-permute-start(f32[8,8,256]{2,1,0:T(8,128)S(1)} %copy.59), channel_id=1, source_target_pairs={{0,2},{1,3},{2,0},{3,1},{4,6},{5,7},{6,4},{7,5},{8,10},{9,11},{10,... | collective-permute-start | bytes 196616 | tf_op jit(solution)/shard_map/shard_2/ppermute | solution.py:18
  57.3 1.9 %collective-permute-start.15 = (f32[8,8,256]{2,1,0:T(8,128)S(1)}, f32[8,8,256]{2,1,0:T(8,128)S(1)}, u32[]{:S(2)}, u32[]{:S(2)}) collective-permute-start(f32[8,8,256]{2,1,0:T(8,128)S(1)} %copy.60), channel_id=1, source_target_pairs={{0,1},{1,0},{2,3},{3,2},{4,5},{5,4},{6,7},{7,6},{8,9},{9,8},{10,11... | collective-permute-start | bytes 196616 | tf_op jit(solution)/shard_map/shard_1/ppermute | solution.py:18
  59.2 2.2 %collective-permute-done.13 = f32[8,8,256]{2,1,0:T(8,128)S(1)} collective-permute-done((f32[8,8,256]{2,1,0:T(8,128)S(1)}, f32[8,8,256]{2,1,0:T(8,128)S(1)}, u32[]{:S(2)}, u32[]{:S(2)}) %collective-permute-start.13) | collective-permute-done | bytes 65568 | tf_op jit(solution)/shard_map/shard_3/ppermute | solution.py:18
  61.4 2.2 %collective-permute-done.14 = f32[8,8,256]{2,1,0:T(8,128)S(1)} collective-permute-done((f32[8,8,256]{2,1,0:T(8,128)S(1)}, f32[8,8,256]{2,1,0:T(8,128)S(1)}, u32[]{:S(2)}, u32[]{:S(2)}) %collective-permute-start.14) | collective-permute-done | bytes 65568 | tf_op jit(solution)/shard_map/shard_2/ppermute | solution.py:18
  63.8 0.9 %collective-permute-start.17 = (f32[4,32,256]{2,1,0:T(8,128)S(1)}, f32[4,32,256]{2,1,0:T(8,128)S(1)}, u32[]{:S(2)}, u32[]{:S(2)}) collective-permute-start(f32[4,32,256]{2,1,0:T(8,128)S(1)} %get-tuple-element.57), channel_id=1, source_target_pairs={{0,8},{4,20},{8,0},{12,28},{16,24},{20,4},{24,16},{28,12},{1,9},{5... | collective-permute-start | bytes 393224 | tf_op jit(solution)/shard_map/rows_first_top/ppermute | solution.py:18
  64.7 0.6 collective-permute-start.19
  65.3 1.5 %collective-permute-start.21 = (f32[4,32,256]{2,1,0:T(8,128)S(1)}, f32[4,32,256]{2,1,0:T(8,128)S(1)}, u32[]{:S(2)}, u32[]{:S(2)}) collective-permute-start(f32[4,32,256]{2,1,0:T(8,128)S(1)} %get-tuple-element.56), channel_id=1, source_target_pairs={{0,8},{4,20},{8,0},{12,28},{16,24},{20,4},{24,16},{28,12},{1,9},{5... | collective-permute-start | bytes 393224 | tf_op jit(solution)/shard_map/rows_first_low/ppermute | solution.py:18
  66.8 1.1 %collective-permute-start.23 = (f32[4,32,256]{2,1,0:T(8,128)S(1)}, f32[4,32,256]{2,1,0:T(8,128)S(1)}, u32[]{:S(2)}, u32[]{:S(2)}) collective-permute-start(f32[4,32,256]{2,1,0:T(8,128)S(1)} %get-tuple-element.57), channel_id=1, source_target_pairs={{0,16},{4,12},{8,24},{12,4},{16,0},{20,28},{24,8},{28,20},{1,17},{... | collective-permute-start | bytes 393224 | tf_op jit(solution)/shard_map/rows_second_top/ppermute | solution.py:18
  68.1 2.0 %collective-permute-done.17 = f32[4,32,256]{2,1,0:T(8,128)S(1)} collective-permute-done((f32[4,32,256]{2,1,0:T(8,128)S(1)}, f32[4,32,256]{2,1,0:T(8,128)S(1)}, u32[]{:S(2)}, u32[]{:S(2)}) %collective-permute-start.17) | collective-permute-done | bytes 131104 | tf_op jit(solution)/shard_map/rows_first_top/ppermute | solution.py:18
  70.1 1.1 %collective-permute-done.19 = f32[4,32,256]{2,1,0:T(8,128)S(1)} collective-permute-done((f32[4,32,256]{2,1,0:T(8,128)S(1)}, f32[4,32,256]{2,1,0:T(8,128)S(1)}, u32[]{:S(2)}, u32[]{:S(2)}) %collective-permute-start.19) | collective-permute-done | bytes 131104 | tf_op jit(solution)/shard_map/rows_second_low/ppermute | solution.py:18
  71.6 1.4 %collective-permute-start.25 = (f32[4,32,256]{2,1,0:T(8,128)S(1)}, f32[4,32,256]{2,1,0:T(8,128)S(1)}, u32[]{:S(2)}, u32[]{:S(2)}) collective-permute-start(f32[4,32,256]{2,1,0:T(8,128)S(1)} %collective-permute-done.19), channel_id=1, source_target_pairs={{0,8},{4,20},{8,0},{12,28},{16,24},{20,4},{24,16},{28,12},{1,9},{5... | collective-permute-start | bytes 393224 | tf_op jit(solution)/shard_map/rows_relay_low/ppermute | solution.py:18
  73.7 2.9 %collective-permute-done.25 = f32[4,32,256]{2,1,0:T(8,128)S(1)} collective-permute-done((f32[4,32,256]{2,1,0:T(8,128)S(1)}, f32[4,32,256]{2,1,0:T(8,128)S(1)}, u32[]{:S(2)}, u32[]{:S(2)}) %collective-permute-start.25) | collective-permute-done | bytes 131104 | tf_op jit(solution)/shard_map/rows_relay_low/ppermute | solution.py:18
  77.4 0.6 collective-permute-done.24
  78.4 1.3 %copy-done.3 = f32[8,256,256]{2,1,0:T(8,128)} copy-done((f32[8,256,256]{2,1,0:T(8,128)}, f32[8,256,256]{2,1,0:T(8,128)S(1)}, u32[]{:S(2)}) %copy-start.3) | copy-done | bytes 2097176
  (104 shorter events, 7.2 us)
Async XLA Ops:
  0.6 39.6 %copy-start = (f32[1,1,1,256,256]{4,3,2,1,0:T(8,128)S(1)}, f32[1,1,1,256,256]{4,3,2,1,0:T(8,128)}, u32[]{:S(2)}) copy-start(f32[1,1,1,256,256]{4,3,2,1,0:T(8,128)} %param.10) | copy-start | bytes 786436
  2.2 1.7 %collective-permute-start = (f32[8,32,256]{2,1,0:T(8,128)S(1)}, f32[8,32,256]{2,1,0:T(8,128)S(1)}, u32[]{:S(2)}, u32[]{:S(2)}) collective-permute-start(f32[8,32,256]{2,1,0:T(8,128)S(1)} %get-tuple-element.55), channel_id=1, source_target_pairs={{0,4},{4,0},{8,12},{12,8},{16,20},{20,16},{24,28},{28,24},{1,5},{5... | collective-permute-start | bytes 786440 | tf_op jit(solution)/shard_map/sum_core_across/ppermute | solution.py:18
  2.7 4.2 %collective-permute-start.2 = (f32[8,32,256]{2,1,0:T(8,128)S(1)}, f32[8,32,256]{2,1,0:T(8,128)S(1)}, u32[]{:S(2)}, u32[]{:S(2)}) collective-permute-start(f32[8,32,256]{2,1,0:T(8,128)S(1)} %get-tuple-element.52), channel_id=1, source_target_pairs={{0,4},{4,0},{8,12},{12,8},{16,20},{20,16},{24,28},{28,24},{1,5},{5... | collective-permute-start | bytes 786440 | tf_op jit(solution)/shard_map/sum_core_second/ppermute | solution.py:18
  2.8 4.1 %collective-permute-start.5 = (f32[8,32,256]{2,1,0:T(8,128)S(1)}, f32[8,32,256]{2,1,0:T(8,128)S(1)}, u32[]{:S(2)}, u32[]{:S(2)}) collective-permute-start(f32[8,32,256]{2,1,0:T(8,128)S(1)} %get-tuple-element.53), channel_id=1, source_target_pairs={{0,4},{4,0},{8,12},{12,8},{16,20},{20,16},{24,28},{28,24},{1,5},{5... | collective-permute-start | bytes 786440 | tf_op jit(solution)/shard_map/sum_core_first/ppermute | solution.py:18
  3.2 3.6 %collective-permute-start.1 = (f32[8,32,256]{2,1,0:T(8,128)S(1)}, f32[8,32,256]{2,1,0:T(8,128)S(1)}, u32[]{:S(2)}, u32[]{:S(2)}) collective-permute-start(f32[8,32,256]{2,1,0:T(8,128)S(1)} %get-tuple-element.54), channel_id=1, source_target_pairs={{0,4},{4,0},{8,12},{12,8},{16,20},{20,16},{24,28},{28,24},{1,5},{5... | collective-permute-start | bytes 786440 | tf_op jit(solution)/shard_map/sum_core_own/ppermute | solution.py:18
  4.0 5.9 %collective-permute-start.9 = (f32[8,16,256]{2,1,0:T(8,128)S(1)}, f32[8,16,256]{2,1,0:T(8,128)S(1)}, u32[]{:S(2)}, u32[]{:S(2)}) collective-permute-start(f32[8,16,256]{2,1,0:T(8,128)S(1)} %get-tuple-element.39), channel_id=1, source_target_pairs={{0,8},{4,20},{8,0},{12,28},{16,24},{20,4},{24,16},{28,12},{1,9},{5... | collective-permute-start | bytes 393224 | tf_op jit(solution)/shard_map/sum_across_far/ppermute | solution.py:18
  7.1 6.5 %collective-permute-start.8 = (f32[8,16,256]{2,1,0:T(8,128)S(1)}, f32[8,16,256]{2,1,0:T(8,128)S(1)}, u32[]{:S(2)}, u32[]{:S(2)}) collective-permute-start(f32[8,16,256]{2,1,0:T(8,128)S(1)} %get-tuple-element.37), channel_id=1, source_target_pairs={{0,8},{4,20},{8,0},{12,28},{16,24},{20,4},{24,16},{28,12},{1,9},{5... | collective-permute-start | bytes 393224 | tf_op jit(solution)/shard_map/sum_first_far/ppermute | solution.py:18
  8.1 6.8 %collective-permute-start.3 = (f32[8,16,256]{2,1,0:T(8,128)S(1)}, f32[8,16,256]{2,1,0:T(8,128)S(1)}, u32[]{:S(2)}, u32[]{:S(2)}) collective-permute-start(f32[8,16,256]{2,1,0:T(8,128)S(1)} %get-tuple-element.32), channel_id=1, source_target_pairs={{0,8},{4,20},{8,0},{12,28},{16,24},{20,4},{24,16},{28,12},{1,9},{5... | collective-permute-start | bytes 393224 | tf_op jit(solution)/shard_map/sum_across_near/ppermute | solution.py:18
  9.8 6.4 %collective-permute-start.10 = (f32[8,16,256]{2,1,0:T(8,128)S(1)}, f32[8,16,256]{2,1,0:T(8,128)S(1)}, u32[]{:S(2)}, u32[]{:S(2)}) collective-permute-start(f32[8,16,256]{2,1,0:T(8,128)S(1)} %add.169), channel_id=1, source_target_pairs={{0,16},{4,12},{8,24},{12,4},{16,0},{20,28},{24,8},{28,20},{1,17},{... | collective-permute-start | bytes 393224 | tf_op jit(solution)/shard_map/sum_relay_far/ppermute | solution.py:18
  12.0 8.5 %collective-permute-start.6 = (f32[8,16,256]{2,1,0:T(8,128)S(1)}, f32[8,16,256]{2,1,0:T(8,128)S(1)}, u32[]{:S(2)}, u32[]{:S(2)}) collective-permute-start(f32[8,16,256]{2,1,0:T(8,128)S(1)} %get-tuple-element.33), channel_id=1, source_target_pairs={{0,8},{4,20},{8,0},{12,28},{16,24},{20,4},{24,16},{28,12},{1,9},{5... | collective-permute-start | bytes 393224 | tf_op jit(solution)/shard_map/sum_first_near/ppermute | solution.py:18
  14.9 24.9 %copy-start.4 = (f32[1,1,1,256,256]{4,3,2,1,0:T(8,128)S(1)}, f32[1,1,1,256,256]{4,3,2,1,0:T(8,128)}, u32[]{:S(2)}) copy-start(f32[1,1,1,256,256]{4,3,2,1,0:T(8,128)} %param.9) | copy-start | bytes 786436
  14.9 5.6 %collective-permute-start.4 = (f32[8,16,256]{2,1,0:T(8,128)S(1)}, f32[8,16,256]{2,1,0:T(8,128)S(1)}, u32[]{:S(2)}, u32[]{:S(2)}) collective-permute-start(f32[8,16,256]{2,1,0:T(8,128)S(1)} %add.162), channel_id=1, source_target_pairs={{0,16},{4,12},{8,24},{12,4},{16,0},{20,28},{24,8},{28,20},{1,17},{... | collective-permute-start | bytes 393224 | tf_op jit(solution)/shard_map/sum_relay_near/ppermute | solution.py:18
  16.3 7.1 %collective-permute-start.12 = (f32[8,8,256]{2,1,0:T(8,128)S(1)}, f32[8,8,256]{2,1,0:T(8,128)S(1)}, u32[]{:S(2)}, u32[]{:S(2)}) collective-permute-start(f32[8,8,256]{2,1,0:T(8,128)S(1)} %get-tuple-element.75), channel_id=1, source_target_pairs={{0,2},{1,3},{2,0},{3,1},{4,6},{5,7},{6,4},{7,5},{8,10},{9,11},{10,... | collective-permute-start | bytes 196616 | tf_op jit(solution)/shard_map/shard_2/ppermute | solution.py:18
  19.1 6.2 %collective-permute-start.11 = (f32[8,8,256]{2,1,0:T(8,128)S(1)}, f32[8,8,256]{2,1,0:T(8,128)S(1)}, u32[]{:S(2)}, u32[]{:S(2)}) collective-permute-start(f32[8,8,256]{2,1,0:T(8,128)S(1)} %get-tuple-element.74), channel_id=1, source_target_pairs={{0,3},{1,2},{2,1},{3,0},{4,7},{5,6},{6,5},{7,4},{8,11},{9,10},{10,... | collective-permute-start | bytes 196616 | tf_op jit(solution)/shard_map/shard_3/ppermute | solution.py:18
  20.5 19.7 %copy-start.5 = (f32[1,1,1,256,256]{4,3,2,1,0:T(8,128)S(1)}, f32[1,1,1,256,256]{4,3,2,1,0:T(8,128)}, u32[]{:S(2)}) copy-start(f32[1,1,1,256,256]{4,3,2,1,0:T(8,128)} %param.11) | copy-start | bytes 786436
  20.6 5.0 %collective-permute-start.7 = (f32[8,8,256]{2,1,0:T(8,128)S(1)}, f32[8,8,256]{2,1,0:T(8,128)S(1)}, u32[]{:S(2)}, u32[]{:S(2)}) collective-permute-start(f32[8,8,256]{2,1,0:T(8,128)S(1)} %get-tuple-element.73), channel_id=1, source_target_pairs={{0,1},{1,0},{2,3},{3,2},{4,5},{5,4},{6,7},{7,6},{8,9},{9,8},{10,11... | collective-permute-start | bytes 196616 | tf_op jit(solution)/shard_map/shard_1/ppermute | solution.py:18
  41.0 20.3 %copy-start.1 = (f32[8,32,256]{2,1,0:T(8,128)S(1)}, f32[8,32,256]{2,1,0:T(8,128)}, u32[]{:S(2)}) copy-start(f32[8,32,256]{2,1,0:T(8,128)} %param.8) | copy-start | bytes 786436
  54.5 6.9 %collective-permute-start.13 = (f32[8,8,256]{2,1,0:T(8,128)S(1)}, f32[8,8,256]{2,1,0:T(8,128)S(1)}, u32[]{:S(2)}, u32[]{:S(2)}) collective-permute-start(f32[8,8,256]{2,1,0:T(8,128)S(1)} %copy.58), channel_id=1, source_target_pairs={{0,3},{1,2},{2,1},{3,0},{4,7},{5,6},{6,5},{7,4},{8,11},{9,10},{10,... | collective-permute-start | bytes 196616 | tf_op jit(solution)/shard_map/shard_3/ppermute | solution.py:18
  56.4 7.2 %collective-permute-start.14 = (f32[8,8,256]{2,1,0:T(8,128)S(1)}, f32[8,8,256]{2,1,0:T(8,128)S(1)}, u32[]{:S(2)}, u32[]{:S(2)}) collective-permute-start(f32[8,8,256]{2,1,0:T(8,128)S(1)} %copy.59), channel_id=1, source_target_pairs={{0,2},{1,3},{2,0},{3,1},{4,6},{5,7},{6,4},{7,5},{8,10},{9,11},{10,... | collective-permute-start | bytes 196616 | tf_op jit(solution)/shard_map/shard_2/ppermute | solution.py:18
  57.3 6.4 %collective-permute-start.15 = (f32[8,8,256]{2,1,0:T(8,128)S(1)}, f32[8,8,256]{2,1,0:T(8,128)S(1)}, u32[]{:S(2)}, u32[]{:S(2)}) collective-permute-start(f32[8,8,256]{2,1,0:T(8,128)S(1)} %copy.60), channel_id=1, source_target_pairs={{0,1},{1,0},{2,3},{3,2},{4,5},{5,4},{6,7},{7,6},{8,9},{9,8},{10,11... | collective-permute-start | bytes 196616 | tf_op jit(solution)/shard_map/shard_1/ppermute | solution.py:18
  63.7 8.0 %collective-permute-start.16 = (f32[8,32,256]{2,1,0:T(8,128)S(1)}, f32[8,32,256]{2,1,0:T(8,128)S(1)}, u32[]{:S(2)}, u32[]{:S(2)}) collective-permute-start(f32[8,32,256]{2,1,0:T(8,128)S(1)} %subtract_dynamic-update-slice_fusion), channel_id=1, source_target_pairs={{0,4},{4,0},{8,12},{12,8},{16,20},{20,16},{24,28},{28,24},{1,5},{5... | collective-permute-start | bytes 786440 | tf_op jit(solution)/shard_map/rows_core_own/ppermute | solution.py:18
  63.8 6.3 %collective-permute-start.17 = (f32[4,32,256]{2,1,0:T(8,128)S(1)}, f32[4,32,256]{2,1,0:T(8,128)S(1)}, u32[]{:S(2)}, u32[]{:S(2)}) collective-permute-start(f32[4,32,256]{2,1,0:T(8,128)S(1)} %get-tuple-element.57), channel_id=1, source_target_pairs={{0,8},{4,20},{8,0},{12,28},{16,24},{20,4},{24,16},{28,12},{1,9},{5... | collective-permute-start | bytes 393224 | tf_op jit(solution)/shard_map/rows_first_top/ppermute | solution.py:18
  64.7 6.4 %collective-permute-start.19 = (f32[4,32,256]{2,1,0:T(8,128)S(1)}, f32[4,32,256]{2,1,0:T(8,128)S(1)}, u32[]{:S(2)}, u32[]{:S(2)}) collective-permute-start(f32[4,32,256]{2,1,0:T(8,128)S(1)} %get-tuple-element.56), channel_id=1, source_target_pairs={{0,16},{4,12},{8,24},{12,4},{16,0},{20,28},{24,8},{28,20},{1,17},{... | collective-permute-start | bytes 393224 | tf_op jit(solution)/shard_map/rows_second_low/ppermute | solution.py:18
  65.3 7.8 %collective-permute-start.21 = (f32[4,32,256]{2,1,0:T(8,128)S(1)}, f32[4,32,256]{2,1,0:T(8,128)S(1)}, u32[]{:S(2)}, u32[]{:S(2)}) collective-permute-start(f32[4,32,256]{2,1,0:T(8,128)S(1)} %get-tuple-element.56), channel_id=1, source_target_pairs={{0,8},{4,20},{8,0},{12,28},{16,24},{20,4},{24,16},{28,12},{1,9},{5... | collective-permute-start | bytes 393224 | tf_op jit(solution)/shard_map/rows_first_low/ppermute | solution.py:18
  66.8 6.4 %collective-permute-start.23 = (f32[4,32,256]{2,1,0:T(8,128)S(1)}, f32[4,32,256]{2,1,0:T(8,128)S(1)}, u32[]{:S(2)}, u32[]{:S(2)}) collective-permute-start(f32[4,32,256]{2,1,0:T(8,128)S(1)} %get-tuple-element.57), channel_id=1, source_target_pairs={{0,16},{4,12},{8,24},{12,4},{16,0},{20,28},{24,8},{28,20},{1,17},{... | collective-permute-start | bytes 393224 | tf_op jit(solution)/shard_map/rows_second_top/ppermute | solution.py:18
  70.1 7.2 %collective-permute-start.18 = (f32[4,32,256]{2,1,0:T(8,128)S(1)}, f32[4,32,256]{2,1,0:T(8,128)S(1)}, u32[]{:S(2)}, u32[]{:S(2)}) collective-permute-start(f32[4,32,256]{2,1,0:T(8,128)S(1)} %collective-permute-done.17), channel_id=1, source_target_pairs={{0,4},{4,0},{8,12},{12,8},{16,20},{20,16},{24,28},{28,24},{1,5},{5... | collective-permute-start | bytes 393224 | tf_op jit(solution)/shard_map/rows_core_first_top/ppermute | solution.py:18
  71.1 5.6 %collective-permute-start.26 = (f32[4,32,256]{2,1,0:T(8,128)S(1)}, f32[4,32,256]{2,1,0:T(8,128)S(1)}, u32[]{:S(2)}, u32[]{:S(2)}) collective-permute-start(f32[4,32,256]{2,1,0:T(8,128)S(1)} %collective-permute-done.17), channel_id=1, source_target_pairs={{0,16},{4,12},{8,24},{12,4},{16,0},{20,28},{24,8},{28,20},{1,17},{... | collective-permute-start | bytes 393224 | tf_op jit(solution)/shard_map/rows_relay_top/ppermute | solution.py:18
  71.6 5.0 %collective-permute-start.25 = (f32[4,32,256]{2,1,0:T(8,128)S(1)}, f32[4,32,256]{2,1,0:T(8,128)S(1)}, u32[]{:S(2)}, u32[]{:S(2)}) collective-permute-start(f32[4,32,256]{2,1,0:T(8,128)S(1)} %collective-permute-done.19), channel_id=1, source_target_pairs={{0,8},{4,20},{8,0},{12,28},{16,24},{20,4},{24,16},{28,12},{1,9},{5... | collective-permute-start | bytes 393224 | tf_op jit(solution)/shard_map/rows_relay_low/ppermute | solution.py:18
  73.1 4.2 %collective-permute-start.20 = (f32[4,32,256]{2,1,0:T(8,128)S(1)}, f32[4,32,256]{2,1,0:T(8,128)S(1)}, u32[]{:S(2)}, u32[]{:S(2)}) collective-permute-start(f32[4,32,256]{2,1,0:T(8,128)S(1)} %collective-permute-done.19), channel_id=1, source_target_pairs={{0,4},{4,0},{8,12},{12,8},{16,20},{20,16},{24,28},{28,24},{1,5},{5... | collective-permute-start | bytes 393224 | tf_op jit(solution)/shard_map/rows_core_second_low/ppermute | solution.py:18
  73.2 4.1 %collective-permute-start.22 = (f32[4,32,256]{2,1,0:T(8,128)S(1)}, f32[4,32,256]{2,1,0:T(8,128)S(1)}, u32[]{:S(2)}, u32[]{:S(2)}) collective-permute-start(f32[4,32,256]{2,1,0:T(8,128)S(1)} %collective-permute-done.21), channel_id=1, source_target_pairs={{0,4},{4,0},{8,12},{12,8},{16,20},{20,16},{24,28},{28,24},{1,5},{5... | collective-permute-start | bytes 393224 | tf_op jit(solution)/shard_map/rows_core_first_low/ppermute | solution.py:18
  76.6 1.3 %collective-permute-start.24 = (f32[4,32,256]{2,1,0:T(8,128)S(1)}, f32[4,32,256]{2,1,0:T(8,128)S(1)}, u32[]{:S(2)}, u32[]{:S(2)}) collective-permute-start(f32[4,32,256]{2,1,0:T(8,128)S(1)} %collective-permute-done.23), channel_id=1, source_target_pairs={{0,4},{4,0},{8,12},{12,8},{16,20},{20,16},{24,28},{28,24},{1,5},{5... | collective-permute-start | bytes 393224 | tf_op jit(solution)/shard_map/rows_core_second_top/ppermute | solution.py:18
  76.7 1.7 %collective-permute-start.27 = (f32[8,32,256]{2,1,0:T(8,128)S(1)}, f32[8,32,256]{2,1,0:T(8,128)S(1)}, u32[]{:S(2)}, u32[]{:S(2)}) collective-permute-start(f32[8,32,256]{2,1,0:T(8,128)S(1)} %constant_dynamic-update-slice_fusion.12), channel_id=1, source_target_pairs={{0,4},{4,0},{8,12},{12,8},{16,20},{20,16},{24,28},{28,24},{1,5},{5... | collective-permute-start | bytes 786440 | tf_op jit(solution)/shard_map/rows_core_far/ppermute | solution.py:18
  (6 other events, 81.3 us)

commit v17 on v9

--- a/solution.py
+++ b/solution.py
@@ -204,7 +204,9 @@
         (first_rows, second_rows, far_top, first_new, second_new)
     )
     far_rows = jnp.concatenate([far_low, far_top], axis=0)
-    second_other = swap(second_rows, "dp", core, "rows_core_second")
+    first_other, second_other = swap(
+        jnp.stack([first_rows, second_rows]), "dp", core, "rows_core_direct"
+    )
     updated = jnp.zeros((home_count, width, width), jnp.float32)
     for mask, block, values in (
         (0, 0, new_home),
@@ -212,7 +214,7 @@
         (first_chip, 0, first_rows),
         (second_chip, half, second_rows[:half]),
         (second_chip, 0, second_rows[half:]),
-        (second_chip ^ core, 0, swap(first_rows, "dp", core, "rows_core_first")),
+        (second_chip ^ core, 0, first_other),
         (first_chip ^ core, half, second_other[:half]),
         (first_chip ^ core, 0, second_other[half:]),
         (across, 0, far_rows),

time: 78.9 us -> 78.9 us (level)
    ppermute x26 -> x25, starting transfers between devices: 27.2 us -> 26.8 us  [swap(): return lax.ppermute(values, name, pairs)]
    ppermute x26 -> x25, waiting for transfers between devices: 17.4 us -> 17.8 us  [swap(): return lax.ppermute(values, name, pairs)]
  transfers between devices with their start and end apart: 26 -> 25, of which waited for: 15 -> 14; matrix products, arithmetic and copies ran while one was open for 2% -> 2% of each run, Pallas kernels for 0% -> 0%
where the time goes in v17:
time: 78.9 us; the launch traced here: 78.7 us
  starting transfers between devices  26.8 us (34%)
  blocking collectives  26.5 us (34%)
  waiting for transfers between devices  17.8 us (23%)
  local copies, waits for them, and re-layouts  3.77 us (5%)
  matrix products  1.93 us (2%)
  between operations  1.29 us (2%)
    ppermute x25, starting transfers between devices, swap(): return lax.ppermute(values, name, pairs)  26.8 us
    ppermute x25, waiting for transfers between devices, swap(): return lax.ppermute(values, name, pairs)  17.8 us
    all_to_all x1, blocking collectives, routed(): lax.all_to_all(leaving.reshape((device_total,) + piece), ('dp', 'shard'),...  13.7 us
    all_to_all x1, blocking collectives, routed(): lax.all_to_all(change.reshape((device_total,) + piece), ('dp', 'shard'),...  12.7 us
  transfers between devices with their start and end apart: 25, of which 14 were waited for; matrix products, arithmetic and copies ran while one was open for 2% of the time, Pallas kernels for 0%

profile of v17, /device:TPU:0, one launch (start us, length us, event | category | flops | bytes accessed | tf_op | source)
XLA Modules:
  0.0 78.7 jit_solution(17312603780755140494)
XLA Ops:
  0.7 1.3 %dynamic-slice_bitcast_fusion = (bf16[8,4,32,256]{3,2,1,0:T(8,128)(2,1)S(1)}, bf16[8,4,32,256]{3,2,1,0:T(8,128)(2,1)S(1)}) fusion(bf16[8,4,2,32,256]{4,3,2,1,0:T(8,128)(2,1)} %bitcast.146, s32[]{:T(128)S(6)} %select_n.130, s32[]{:T(128)S(6)} %select_n.129), kind=kLoop, calls=%fused_computation.2 | loop fusion | bytes 2097160 | tf_op jit(solution)/shard_map/jit(dynamic_index_in_dim)/squeeze | solution.py:22
  4.0 2.9 %collective-permute-start.9 = (f32[8,16,256]{2,1,0:T(8,128)S(1)}, f32[8,16,256]{2,1,0:T(8,128)S(1)}, u32[]{:S(2)}, u32[]{:S(2)}) collective-permute-start(f32[8,16,256]{2,1,0:T(8,128)S(1)} %get-tuple-element.41), channel_id=1, source_target_pairs={{0,8},{4,20},{8,0},{12,28},{16,24},{20,4},{24,16},{28,12},{1,9},{5... | collective-permute-start | bytes 393224 | tf_op jit(solution)/shard_map/sum_across_far/ppermute | solution.py:18
  7.1 1.0 %collective-permute-start.8 = (f32[8,16,256]{2,1,0:T(8,128)S(1)}, f32[8,16,256]{2,1,0:T(8,128)S(1)}, u32[]{:S(2)}, u32[]{:S(2)}) collective-permute-start(f32[8,16,256]{2,1,0:T(8,128)S(1)} %get-tuple-element.39), channel_id=1, source_target_pairs={{0,8},{4,20},{8,0},{12,28},{16,24},{20,4},{24,16},{28,12},{1,9},{5... | collective-permute-start | bytes 393224 | tf_op jit(solution)/shard_map/sum_first_far/ppermute | solution.py:18
  8.1 1.1 %collective-permute-start.3 = (f32[8,16,256]{2,1,0:T(8,128)S(1)}, f32[8,16,256]{2,1,0:T(8,128)S(1)}, u32[]{:S(2)}, u32[]{:S(2)}) collective-permute-start(f32[8,16,256]{2,1,0:T(8,128)S(1)} %get-tuple-element.34), channel_id=1, source_target_pairs={{0,8},{4,20},{8,0},{12,28},{16,24},{20,4},{24,16},{28,12},{1,9},{5... | collective-permute-start | bytes 393224 | tf_op jit(solution)/shard_map/sum_across_near/ppermute | solution.py:18
  9.2 0.6 collective-permute-done.9
  9.8 2.1 %collective-permute-start.10 = (f32[8,16,256]{2,1,0:T(8,128)S(1)}, f32[8,16,256]{2,1,0:T(8,128)S(1)}, u32[]{:S(2)}, u32[]{:S(2)}) collective-permute-start(f32[8,16,256]{2,1,0:T(8,128)S(1)} %add.167), channel_id=1, source_target_pairs={{0,16},{4,12},{8,24},{12,4},{16,0},{20,28},{24,8},{28,20},{1,17},{... | collective-permute-start | bytes 393224 | tf_op jit(solution)/shard_map/sum_relay_far/ppermute | solution.py:18
  12.0 1.6 %collective-permute-start.6 = (f32[8,16,256]{2,1,0:T(8,128)S(1)}, f32[8,16,256]{2,1,0:T(8,128)S(1)}, u32[]{:S(2)}, u32[]{:S(2)}) collective-permute-start(f32[8,16,256]{2,1,0:T(8,128)S(1)} %get-tuple-element.35), channel_id=1, source_target_pairs={{0,8},{4,20},{8,0},{12,28},{16,24},{20,4},{24,16},{28,12},{1,9},{5... | collective-permute-start | bytes 393224 | tf_op jit(solution)/shard_map/sum_first_near/ppermute | solution.py:18
  13.6 1.3 %collective-permute-done.3 = f32[8,16,256]{2,1,0:T(8,128)S(1)} collective-permute-done((f32[8,16,256]{2,1,0:T(8,128)S(1)}, f32[8,16,256]{2,1,0:T(8,128)S(1)}, u32[]{:S(2)}, u32[]{:S(2)}) %collective-permute-start.3) | collective-permute-done | bytes 131104 | tf_op jit(solution)/shard_map/sum_across_near/ppermute | solution.py:18
  14.9 1.3 %collective-permute-start.4 = (f32[8,16,256]{2,1,0:T(8,128)S(1)}, f32[8,16,256]{2,1,0:T(8,128)S(1)}, u32[]{:S(2)}, u32[]{:S(2)}) collective-permute-start(f32[8,16,256]{2,1,0:T(8,128)S(1)} %add.160), channel_id=1, source_target_pairs={{0,16},{4,12},{8,24},{12,4},{16,0},{20,28},{24,8},{28,20},{1,17},{... | collective-permute-start | bytes 393224 | tf_op jit(solution)/shard_map/sum_relay_near/ppermute | solution.py:18
  16.3 2.8 %collective-permute-start.12 = (f32[8,8,256]{2,1,0:T(8,128)S(1)}, f32[8,8,256]{2,1,0:T(8,128)S(1)}, u32[]{:S(2)}, u32[]{:S(2)}) collective-permute-start(f32[8,8,256]{2,1,0:T(8,128)S(1)} %get-tuple-element.79), channel_id=1, source_target_pairs={{0,2},{1,3},{2,0},{3,1},{4,6},{5,7},{6,4},{7,5},{8,10},{9,11},{10,... | collective-permute-start | bytes 196616 | tf_op jit(solution)/shard_map/shard_2/ppermute | solution.py:18
  19.1 1.3 %collective-permute-start.11 = (f32[8,8,256]{2,1,0:T(8,128)S(1)}, f32[8,8,256]{2,1,0:T(8,128)S(1)}, u32[]{:S(2)}, u32[]{:S(2)}) collective-permute-start(f32[8,8,256]{2,1,0:T(8,128)S(1)} %get-tuple-element.78), channel_id=1, source_target_pairs={{0,3},{1,2},{2,1},{3,0},{4,7},{5,6},{6,5},{7,4},{8,11},{9,10},{10,... | collective-permute-start | bytes 196616 | tf_op jit(solution)/shard_map/shard_3/ppermute | solution.py:18
  20.6 0.9 %collective-permute-start.7 = (f32[8,8,256]{2,1,0:T(8,128)S(1)}, f32[8,8,256]{2,1,0:T(8,128)S(1)}, u32[]{:S(2)}, u32[]{:S(2)}) collective-permute-start(f32[8,8,256]{2,1,0:T(8,128)S(1)} %get-tuple-element.77), channel_id=1, source_target_pairs={{0,1},{1,0},{2,3},{3,2},{4,5},{5,4},{6,7},{7,6},{8,9},{9,8},{10,11... | collective-permute-start | bytes 196616 | tf_op jit(solution)/shard_map/shard_1/ppermute | solution.py:18
  21.7 1.7 %collective-permute-done.12 = f32[8,8,256]{2,1,0:T(8,128)S(1)} collective-permute-done((f32[8,8,256]{2,1,0:T(8,128)S(1)}, f32[8,8,256]{2,1,0:T(8,128)S(1)}, u32[]{:S(2)}, u32[]{:S(2)}) %collective-permute-start.12) | collective-permute-done | bytes 65568 | tf_op jit(solution)/shard_map/shard_2/ppermute | solution.py:18
  23.5 1.8 %collective-permute-done.11 = f32[8,8,256]{2,1,0:T(8,128)S(1)} collective-permute-done((f32[8,8,256]{2,1,0:T(8,128)S(1)}, f32[8,8,256]{2,1,0:T(8,128)S(1)}, u32[]{:S(2)}, u32[]{:S(2)}) %collective-permute-start.11) | collective-permute-done | bytes 65568 | tf_op jit(solution)/shard_map/shard_3/ppermute | solution.py:18
  26.1 13.7 %all_to_all.10 = f32[32,8,256]{2,1,0:T(8,128)S(1)} all-to-all(f32[32,8,256]{2,1,0:T(8,128)S(1)} %copy.56), channel_id=1, replica_groups=mesh['dp'=8,'shard'=4] {'dp','shard'}, dimensions={0} | all-to-all | bytes 524288 | tf_op jit(solution)/shard_map/all_to_all | solution.py:153
  41.3 12.7 %all_to_all.11 = f32[32,8,256]{2,1,0:T(8,128)S(1)} all-to-all(f32[32,8,256]{2,1,0:T(8,128)S(1)} %convolution_bitcast_fusion), channel_id=1, replica_groups=mesh['dp'=8,'shard'=4] {'dp','shard'}, dimensions={0} | all-to-all | bytes 524288 | tf_op jit(solution)/shard_map/all_to_all | solution.py:170
  54.5 1.8 %collective-permute-start.13 = (f32[8,8,256]{2,1,0:T(8,128)S(1)}, f32[8,8,256]{2,1,0:T(8,128)S(1)}, u32[]{:S(2)}, u32[]{:S(2)}) collective-permute-start(f32[8,8,256]{2,1,0:T(8,128)S(1)} %copy.58), channel_id=1, source_target_pairs={{0,3},{1,2},{2,1},{3,0},{4,7},{5,6},{6,5},{7,4},{8,11},{9,10},{10,... | collective-permute-start | bytes 196616 | tf_op jit(solution)/shard_map/shard_3/ppermute | solution.py:18
  56.4 0.9 %collective-permute-start.14 = (f32[8,8,256]{2,1,0:T(8,128)S(1)}, f32[8,8,256]{2,1,0:T(8,128)S(1)}, u32[]{:S(2)}, u32[]{:S(2)}) collective-permute-start(f32[8,8,256]{2,1,0:T(8,128)S(1)} %copy.59), channel_id=1, source_target_pairs={{0,2},{1,3},{2,0},{3,1},{4,6},{5,7},{6,4},{7,5},{8,10},{9,11},{10,... | collective-permute-start | bytes 196616 | tf_op jit(solution)/shard_map/shard_2/ppermute | solution.py:18
  57.3 1.9 %collective-permute-start.15 = (f32[8,8,256]{2,1,0:T(8,128)S(1)}, f32[8,8,256]{2,1,0:T(8,128)S(1)}, u32[]{:S(2)}, u32[]{:S(2)}) collective-permute-start(f32[8,8,256]{2,1,0:T(8,128)S(1)} %copy.60), channel_id=1, source_target_pairs={{0,1},{1,0},{2,3},{3,2},{4,5},{5,4},{6,7},{7,6},{8,9},{9,8},{10,11... | collective-permute-start | bytes 196616 | tf_op jit(solution)/shard_map/shard_1/ppermute | solution.py:18
  59.2 2.2 %collective-permute-done.13 = f32[8,8,256]{2,1,0:T(8,128)S(1)} collective-permute-done((f32[8,8,256]{2,1,0:T(8,128)S(1)}, f32[8,8,256]{2,1,0:T(8,128)S(1)}, u32[]{:S(2)}, u32[]{:S(2)}) %collective-permute-start.13) | collective-permute-done | bytes 65568 | tf_op jit(solution)/shard_map/shard_3/ppermute | solution.py:18
  61.4 2.2 %collective-permute-done.14 = f32[8,8,256]{2,1,0:T(8,128)S(1)} collective-permute-done((f32[8,8,256]{2,1,0:T(8,128)S(1)}, f32[8,8,256]{2,1,0:T(8,128)S(1)}, u32[]{:S(2)}, u32[]{:S(2)}) %collective-permute-start.14) | collective-permute-done | bytes 65568 | tf_op jit(solution)/shard_map/shard_2/ppermute | solution.py:18
  63.7 0.9 %collective-permute-start.18 = (f32[4,32,256]{2,1,0:T(8,128)S(1)}, f32[4,32,256]{2,1,0:T(8,128)S(1)}, u32[]{:S(2)}, u32[]{:S(2)}) collective-permute-start(f32[4,32,256]{2,1,0:T(8,128)S(1)} %get-tuple-element.61), channel_id=1, source_target_pairs={{0,8},{4,20},{8,0},{12,28},{16,24},{20,4},{24,16},{28,12},{1,9},{5... | collective-permute-start | bytes 393224 | tf_op jit(solution)/shard_map/rows_first_top/ppermute | solution.py:18
  65.2 1.5 %collective-permute-start.17 = (f32[4,32,256]{2,1,0:T(8,128)S(1)}, f32[4,32,256]{2,1,0:T(8,128)S(1)}, u32[]{:S(2)}, u32[]{:S(2)}) collective-permute-start(f32[4,32,256]{2,1,0:T(8,128)S(1)} %get-tuple-element.60), channel_id=1, source_target_pairs={{0,8},{4,20},{8,0},{12,28},{16,24},{20,4},{24,16},{28,12},{1,9},{5... | collective-permute-start | bytes 393224 | tf_op jit(solution)/shard_map/rows_first_low/ppermute | solution.py:18
  66.7 1.1 %collective-permute-start.19 = (f32[4,32,256]{2,1,0:T(8,128)S(1)}, f32[4,32,256]{2,1,0:T(8,128)S(1)}, u32[]{:S(2)}, u32[]{:S(2)}) collective-permute-start(f32[4,32,256]{2,1,0:T(8,128)S(1)} %get-tuple-element.61), channel_id=1, source_target_pairs={{0,16},{4,12},{8,24},{12,4},{16,0},{20,28},{24,8},{28,20},{1,17},{... | collective-permute-start | bytes 393224 | tf_op jit(solution)/shard_map/rows_second_top/ppermute | solution.py:18
  68.0 1.8 %collective-permute-done.18 = f32[4,32,256]{2,1,0:T(8,128)S(1)} collective-permute-done((f32[4,32,256]{2,1,0:T(8,128)S(1)}, f32[4,32,256]{2,1,0:T(8,128)S(1)}, u32[]{:S(2)}, u32[]{:S(2)}) %collective-permute-start.18) | collective-permute-done | bytes 131104 | tf_op jit(solution)/shard_map/rows_first_top/ppermute | solution.py:18
  69.8 0.9 %collective-permute-start.21 = (f32[4,32,256]{2,1,0:T(8,128)S(1)}, f32[4,32,256]{2,1,0:T(8,128)S(1)}, u32[]{:S(2)}, u32[]{:S(2)}) collective-permute-start(f32[4,32,256]{2,1,0:T(8,128)S(1)} %collective-permute-done.18), channel_id=1, source_target_pairs={{0,16},{4,12},{8,24},{12,4},{16,0},{20,28},{24,8},{28,20},{1,17},{... | collective-permute-start | bytes 393224 | tf_op jit(solution)/shard_map/rows_relay_top/ppermute | solution.py:18
  70.7 0.8 %collective-permute-start.23 = (f32[4,32,256]{2,1,0:T(8,128)S(1)}, f32[4,32,256]{2,1,0:T(8,128)S(1)}, u32[]{:S(2)}, u32[]{:S(2)}) collective-permute-start(f32[4,32,256]{2,1,0:T(8,128)S(1)} %collective-permute-done.20), channel_id=1, source_target_pairs={{0,8},{4,20},{8,0},{12,28},{16,24},{20,4},{24,16},{28,12},{1,9},{5... | collective-permute-start | bytes 393224 | tf_op jit(solution)/shard_map/rows_relay_low/ppermute | solution.py:18
  71.5 1.0 %collective-permute-done.17 = f32[4,32,256]{2,1,0:T(8,128)S(1)} collective-permute-done((f32[4,32,256]{2,1,0:T(8,128)S(1)}, f32[4,32,256]{2,1,0:T(8,128)S(1)}, u32[]{:S(2)}, u32[]{:S(2)}) %collective-permute-start.17) | collective-permute-done | bytes 131104 | tf_op jit(solution)/shard_map/rows_first_low/ppermute | solution.py:18
  72.6 2.3 %collective-permute-done.21 = f32[4,32,256]{2,1,0:T(8,128)S(1)} collective-permute-done((f32[4,32,256]{2,1,0:T(8,128)S(1)}, f32[4,32,256]{2,1,0:T(8,128)S(1)}, u32[]{:S(2)}, u32[]{:S(2)}) %collective-permute-start.21) | collective-permute-done | bytes 131104 | tf_op jit(solution)/shard_map/rows_relay_top/ppermute | solution.py:18
  75.1 0.6 collective-permute-done.23
  75.9 1.1 %collective-permute-done.22 = f32[2,8,32,256]{3,2,1,0:T(8,128)S(1)} collective-permute-done((f32[2,8,32,256]{3,2,1,0:T(8,128)S(1)}, f32[2,8,32,256]{3,2,1,0:T(8,128)S(1)}, u32[]{:S(2)}, u32[]{:S(2)}) %collective-permute-start.22) | collective-permute-done | bytes 524320 | tf_op jit(solution)/shard_map/rows_core_direct/ppermute | solution.py:18
  77.4 1.3 %copy-done.3 = f32[8,256,256]{2,1,0:T(8,128)} copy-done((f32[8,256,256]{2,1,0:T(8,128)}, f32[8,256,256]{2,1,0:T(8,128)S(1)}, u32[]{:S(2)}) %copy-start.3) | copy-done | bytes 2097176
  (99 shorter events, 6.7 us)
Async XLA Ops:
  0.6 39.6 %copy-start = (f32[1,1,1,256,256]{4,3,2,1,0:T(8,128)S(1)}, f32[1,1,1,256,256]{4,3,2,1,0:T(8,128)}, u32[]{:S(2)}) copy-start(f32[1,1,1,256,256]{4,3,2,1,0:T(8,128)} %param.10) | copy-start | bytes 786436
  2.2 1.7 %collective-permute-start = (f32[8,32,256]{2,1,0:T(8,128)S(1)}, f32[8,32,256]{2,1,0:T(8,128)S(1)}, u32[]{:S(2)}, u32[]{:S(2)}) collective-permute-start(f32[8,32,256]{2,1,0:T(8,128)S(1)} %get-tuple-element.59), channel_id=1, source_target_pairs={{0,4},{4,0},{8,12},{12,8},{16,20},{20,16},{24,28},{28,24},{1,5},{5... | collective-permute-start | bytes 786440 | tf_op jit(solution)/shard_map/sum_core_across/ppermute | solution.py:18
  2.7 4.2 %collective-permute-start.2 = (f32[8,32,256]{2,1,0:T(8,128)S(1)}, f32[8,32,256]{2,1,0:T(8,128)S(1)}, u32[]{:S(2)}, u32[]{:S(2)}) collective-permute-start(f32[8,32,256]{2,1,0:T(8,128)S(1)} %get-tuple-element.56), channel_id=1, source_target_pairs={{0,4},{4,0},{8,12},{12,8},{16,20},{20,16},{24,28},{28,24},{1,5},{5... | collective-permute-start | bytes 786440 | tf_op jit(solution)/shard_map/sum_core_second/ppermute | solution.py:18
  2.8 4.1 %collective-permute-start.5 = (f32[8,32,256]{2,1,0:T(8,128)S(1)}, f32[8,32,256]{2,1,0:T(8,128)S(1)}, u32[]{:S(2)}, u32[]{:S(2)}) collective-permute-start(f32[8,32,256]{2,1,0:T(8,128)S(1)} %get-tuple-element.57), channel_id=1, source_target_pairs={{0,4},{4,0},{8,12},{12,8},{16,20},{20,16},{24,28},{28,24},{1,5},{5... | collective-permute-start | bytes 786440 | tf_op jit(solution)/shard_map/sum_core_first/ppermute | solution.py:18
  3.2 3.6 %collective-permute-start.1 = (f32[8,32,256]{2,1,0:T(8,128)S(1)}, f32[8,32,256]{2,1,0:T(8,128)S(1)}, u32[]{:S(2)}, u32[]{:S(2)}) collective-permute-start(f32[8,32,256]{2,1,0:T(8,128)S(1)} %get-tuple-element.58), channel_id=1, source_target_pairs={{0,4},{4,0},{8,12},{12,8},{16,20},{20,16},{24,28},{28,24},{1,5},{5... | collective-permute-start | bytes 786440 | tf_op jit(solution)/shard_map/sum_core_own/ppermute | solution.py:18
  4.0 5.9 %collective-permute-start.9 = (f32[8,16,256]{2,1,0:T(8,128)S(1)}, f32[8,16,256]{2,1,0:T(8,128)S(1)}, u32[]{:S(2)}, u32[]{:S(2)}) collective-permute-start(f32[8,16,256]{2,1,0:T(8,128)S(1)} %get-tuple-element.41), channel_id=1, source_target_pairs={{0,8},{4,20},{8,0},{12,28},{16,24},{20,4},{24,16},{28,12},{1,9},{5... | collective-permute-start | bytes 393224 | tf_op jit(solution)/shard_map/sum_across_far/ppermute | solution.py:18
  7.0 14.5 %copy-start.9 = (s32[32]{0:T(128)S(1)}, s32[32]{0:T(128)}, u32[]{:S(2)}) copy-start(s32[32]{0:T(128)} %param.13) | copy-start | bytes 388
  7.1 6.5 %collective-permute-start.8 = (f32[8,16,256]{2,1,0:T(8,128)S(1)}, f32[8,16,256]{2,1,0:T(8,128)S(1)}, u32[]{:S(2)}, u32[]{:S(2)}) collective-permute-start(f32[8,16,256]{2,1,0:T(8,128)S(1)} %get-tuple-element.39), channel_id=1, source_target_pairs={{0,8},{4,20},{8,0},{12,28},{16,24},{20,4},{24,16},{28,12},{1,9},{5... | collective-permute-start | bytes 393224 | tf_op jit(solution)/shard_map/sum_first_far/ppermute | solution.py:18
  8.1 6.8 %collective-permute-start.3 = (f32[8,16,256]{2,1,0:T(8,128)S(1)}, f32[8,16,256]{2,1,0:T(8,128)S(1)}, u32[]{:S(2)}, u32[]{:S(2)}) collective-permute-start(f32[8,16,256]{2,1,0:T(8,128)S(1)} %get-tuple-element.34), channel_id=1, source_target_pairs={{0,8},{4,20},{8,0},{12,28},{16,24},{20,4},{24,16},{28,12},{1,9},{5... | collective-permute-start | bytes 393224 | tf_op jit(solution)/shard_map/sum_across_near/ppermute | solution.py:18
  9.8 6.4 %collective-permute-start.10 = (f32[8,16,256]{2,1,0:T(8,128)S(1)}, f32[8,16,256]{2,1,0:T(8,128)S(1)}, u32[]{:S(2)}, u32[]{:S(2)}) collective-permute-start(f32[8,16,256]{2,1,0:T(8,128)S(1)} %add.167), channel_id=1, source_target_pairs={{0,16},{4,12},{8,24},{12,4},{16,0},{20,28},{24,8},{28,20},{1,17},{... | collective-permute-start | bytes 393224 | tf_op jit(solution)/shard_map/sum_relay_far/ppermute | solution.py:18
  12.0 8.5 %collective-permute-start.6 = (f32[8,16,256]{2,1,0:T(8,128)S(1)}, f32[8,16,256]{2,1,0:T(8,128)S(1)}, u32[]{:S(2)}, u32[]{:S(2)}) collective-permute-start(f32[8,16,256]{2,1,0:T(8,128)S(1)} %get-tuple-element.35), channel_id=1, source_target_pairs={{0,8},{4,20},{8,0},{12,28},{16,24},{20,4},{24,16},{28,12},{1,9},{5... | collective-permute-start | bytes 393224 | tf_op jit(solution)/shard_map/sum_first_near/ppermute | solution.py:18
  14.9 24.9 %copy-start.4 = (f32[1,1,1,256,256]{4,3,2,1,0:T(8,128)S(1)}, f32[1,1,1,256,256]{4,3,2,1,0:T(8,128)}, u32[]{:S(2)}) copy-start(f32[1,1,1,256,256]{4,3,2,1,0:T(8,128)} %param.9) | copy-start | bytes 786436
  14.9 5.6 %collective-permute-start.4 = (f32[8,16,256]{2,1,0:T(8,128)S(1)}, f32[8,16,256]{2,1,0:T(8,128)S(1)}, u32[]{:S(2)}, u32[]{:S(2)}) collective-permute-start(f32[8,16,256]{2,1,0:T(8,128)S(1)} %add.160), channel_id=1, source_target_pairs={{0,16},{4,12},{8,24},{12,4},{16,0},{20,28},{24,8},{28,20},{1,17},{... | collective-permute-start | bytes 393224 | tf_op jit(solution)/shard_map/sum_relay_near/ppermute | solution.py:18
  16.3 7.1 %collective-permute-start.12 = (f32[8,8,256]{2,1,0:T(8,128)S(1)}, f32[8,8,256]{2,1,0:T(8,128)S(1)}, u32[]{:S(2)}, u32[]{:S(2)}) collective-permute-start(f32[8,8,256]{2,1,0:T(8,128)S(1)} %get-tuple-element.79), channel_id=1, source_target_pairs={{0,2},{1,3},{2,0},{3,1},{4,6},{5,7},{6,4},{7,5},{8,10},{9,11},{10,... | collective-permute-start | bytes 196616 | tf_op jit(solution)/shard_map/shard_2/ppermute | solution.py:18
  19.1 6.2 %collective-permute-start.11 = (f32[8,8,256]{2,1,0:T(8,128)S(1)}, f32[8,8,256]{2,1,0:T(8,128)S(1)}, u32[]{:S(2)}, u32[]{:S(2)}) collective-permute-start(f32[8,8,256]{2,1,0:T(8,128)S(1)} %get-tuple-element.78), channel_id=1, source_target_pairs={{0,3},{1,2},{2,1},{3,0},{4,7},{5,6},{6,5},{7,4},{8,11},{9,10},{10,... | collective-permute-start | bytes 196616 | tf_op jit(solution)/shard_map/shard_3/ppermute | solution.py:18
  20.5 19.7 %copy-start.5 = (f32[1,1,1,256,256]{4,3,2,1,0:T(8,128)S(1)}, f32[1,1,1,256,256]{4,3,2,1,0:T(8,128)}, u32[]{:S(2)}) copy-start(f32[1,1,1,256,256]{4,3,2,1,0:T(8,128)} %param.11) | copy-start | bytes 786436
  20.5 19.7 %copy-start.6 = (f32[1,1,1,256,256]{4,3,2,1,0:T(8,128)S(1)}, f32[1,1,1,256,256]{4,3,2,1,0:T(8,128)}, u32[]{:S(2)}) copy-start(f32[1,1,1,256,256]{4,3,2,1,0:T(8,128)} %param.12) | copy-start | bytes 786436
  20.6 5.0 %collective-permute-start.7 = (f32[8,8,256]{2,1,0:T(8,128)S(1)}, f32[8,8,256]{2,1,0:T(8,128)S(1)}, u32[]{:S(2)}, u32[]{:S(2)}) collective-permute-start(f32[8,8,256]{2,1,0:T(8,128)S(1)} %get-tuple-element.77), channel_id=1, source_target_pairs={{0,1},{1,0},{2,3},{3,2},{4,5},{5,4},{6,7},{7,6},{8,9},{9,8},{10,11... | collective-permute-start | bytes 196616 | tf_op jit(solution)/shard_map/shard_1/ppermute | solution.py:18
  41.0 18.1 %copy-start.2 = (f32[8,32,256]{2,1,0:T(8,128)S(1)}, f32[8,32,256]{2,1,0:T(8,128)}, u32[]{:S(2)}) copy-start(f32[8,32,256]{2,1,0:T(8,128)} %param.8) | copy-start | bytes 786436
  41.0 20.3 %copy-start.1 = (f32[8,32,256]{2,1,0:T(8,128)S(1)}, f32[8,32,256]{2,1,0:T(8,128)}, u32[]{:S(2)}) copy-start(f32[8,32,256]{2,1,0:T(8,128)} %param.8) | copy-start | bytes 786436
  54.5 6.9 %collective-permute-start.13 = (f32[8,8,256]{2,1,0:T(8,128)S(1)}, f32[8,8,256]{2,1,0:T(8,128)S(1)}, u32[]{:S(2)}, u32[]{:S(2)}) collective-permute-start(f32[8,8,256]{2,1,0:T(8,128)S(1)} %copy.58), channel_id=1, source_target_pairs={{0,3},{1,2},{2,1},{3,0},{4,7},{5,6},{6,5},{7,4},{8,11},{9,10},{10,... | collective-permute-start | bytes 196616 | tf_op jit(solution)/shard_map/shard_3/ppermute | solution.py:18
  56.4 7.2 %collective-permute-start.14 = (f32[8,8,256]{2,1,0:T(8,128)S(1)}, f32[8,8,256]{2,1,0:T(8,128)S(1)}, u32[]{:S(2)}, u32[]{:S(2)}) collective-permute-start(f32[8,8,256]{2,1,0:T(8,128)S(1)} %copy.59), channel_id=1, source_target_pairs={{0,2},{1,3},{2,0},{3,1},{4,6},{5,7},{6,4},{7,5},{8,10},{9,11},{10,... | collective-permute-start | bytes 196616 | tf_op jit(solution)/shard_map/shard_2/ppermute | solution.py:18
  57.3 6.4 %collective-permute-start.15 = (f32[8,8,256]{2,1,0:T(8,128)S(1)}, f32[8,8,256]{2,1,0:T(8,128)S(1)}, u32[]{:S(2)}, u32[]{:S(2)}) collective-permute-start(f32[8,8,256]{2,1,0:T(8,128)S(1)} %copy.60), channel_id=1, source_target_pairs={{0,1},{1,0},{2,3},{3,2},{4,5},{5,4},{6,7},{7,6},{8,9},{9,8},{10,11... | collective-permute-start | bytes 196616 | tf_op jit(solution)/shard_map/shard_1/ppermute | solution.py:18
  63.7 6.1 %collective-permute-start.18 = (f32[4,32,256]{2,1,0:T(8,128)S(1)}, f32[4,32,256]{2,1,0:T(8,128)S(1)}, u32[]{:S(2)}, u32[]{:S(2)}) collective-permute-start(f32[4,32,256]{2,1,0:T(8,128)S(1)} %get-tuple-element.61), channel_id=1, source_target_pairs={{0,8},{4,20},{8,0},{12,28},{16,24},{20,4},{24,16},{28,12},{1,9},{5... | collective-permute-start | bytes 393224 | tf_op jit(solution)/shard_map/rows_first_top/ppermute | solution.py:18
  64.6 6.1 %collective-permute-start.20 = (f32[4,32,256]{2,1,0:T(8,128)S(1)}, f32[4,32,256]{2,1,0:T(8,128)S(1)}, u32[]{:S(2)}, u32[]{:S(2)}) collective-permute-start(f32[4,32,256]{2,1,0:T(8,128)S(1)} %get-tuple-element.60), channel_id=1, source_target_pairs={{0,16},{4,12},{8,24},{12,4},{16,0},{20,28},{24,8},{28,20},{1,17},{... | collective-permute-start | bytes 393224 | tf_op jit(solution)/shard_map/rows_second_low/ppermute | solution.py:18
  65.2 7.3 %collective-permute-start.17 = (f32[4,32,256]{2,1,0:T(8,128)S(1)}, f32[4,32,256]{2,1,0:T(8,128)S(1)}, u32[]{:S(2)}, u32[]{:S(2)}) collective-permute-start(f32[4,32,256]{2,1,0:T(8,128)S(1)} %get-tuple-element.60), channel_id=1, source_target_pairs={{0,8},{4,20},{8,0},{12,28},{16,24},{20,4},{24,16},{28,12},{1,9},{5... | collective-permute-start | bytes 393224 | tf_op jit(solution)/shard_map/rows_first_low/ppermute | solution.py:18
  66.7 5.9 %collective-permute-start.16 = (f32[8,32,256]{2,1,0:T(8,128)S(1)}, f32[8,32,256]{2,1,0:T(8,128)S(1)}, u32[]{:S(2)}, u32[]{:S(2)}) collective-permute-start(f32[8,32,256]{2,1,0:T(8,128)S(1)} %subtract_dynamic-update-slice_fusion), channel_id=1, source_target_pairs={{0,4},{4,0},{8,12},{12,8},{16,20},{20,16},{24,28},{28,24},{1,5},{5... | collective-permute-start | bytes 786440 | tf_op jit(solution)/shard_map/rows_core_own/ppermute | solution.py:18
  66.7 5.9 %collective-permute-start.19 = (f32[4,32,256]{2,1,0:T(8,128)S(1)}, f32[4,32,256]{2,1,0:T(8,128)S(1)}, u32[]{:S(2)}, u32[]{:S(2)}) collective-permute-start(f32[4,32,256]{2,1,0:T(8,128)S(1)} %get-tuple-element.61), channel_id=1, source_target_pairs={{0,16},{4,12},{8,24},{12,4},{16,0},{20,28},{24,8},{28,20},{1,17},{... | collective-permute-start | bytes 393224 | tf_op jit(solution)/shard_map/rows_second_top/ppermute | solution.py:18
  69.8 5.2 %collective-permute-start.21 = (f32[4,32,256]{2,1,0:T(8,128)S(1)}, f32[4,32,256]{2,1,0:T(8,128)S(1)}, u32[]{:S(2)}, u32[]{:S(2)}) collective-permute-start(f32[4,32,256]{2,1,0:T(8,128)S(1)} %collective-permute-done.18), channel_id=1, source_target_pairs={{0,16},{4,12},{8,24},{12,4},{16,0},{20,28},{24,8},{28,20},{1,17},{... | collective-permute-start | bytes 393224 | tf_op jit(solution)/shard_map/rows_relay_top/ppermute | solution.py:18
  70.7 5.0 %collective-permute-start.23 = (f32[4,32,256]{2,1,0:T(8,128)S(1)}, f32[4,32,256]{2,1,0:T(8,128)S(1)}, u32[]{:S(2)}, u32[]{:S(2)}) collective-permute-start(f32[4,32,256]{2,1,0:T(8,128)S(1)} %collective-permute-done.20), channel_id=1, source_target_pairs={{0,8},{4,20},{8,0},{12,28},{16,24},{20,4},{24,16},{28,12},{1,9},{5... | collective-permute-start | bytes 393224 | tf_op jit(solution)/shard_map/rows_relay_low/ppermute | solution.py:18
  75.0 2.0 %collective-permute-start.22 = (f32[2,8,32,256]{3,2,1,0:T(8,128)S(1)}, f32[2,8,32,256]{3,2,1,0:T(8,128)S(1)}, u32[]{:S(2)}, u32[]{:S(2)}) collective-permute-start(f32[2,8,32,256]{3,2,1,0:T(8,128)S(1)} %pad_maximum_fusion), channel_id=1, source_target_pairs={{0,4},{4,0},{8,12},{12,8},{16,20},{20,16},{24,28},{28,24},{1,5},{5... | collective-permute-start | bytes 1572872 | tf_op jit(solution)/shard_map/rows_core_direct/ppermute | solution.py:18
  75.7 1.6 %collective-permute-start.24 = (f32[8,32,256]{2,1,0:T(8,128)S(1)}, f32[8,32,256]{2,1,0:T(8,128)S(1)}, u32[]{:S(2)}, u32[]{:S(2)}) collective-permute-start(f32[8,32,256]{2,1,0:T(8,128)S(1)} %constant_dynamic-update-slice_fusion.5), channel_id=1, source_target_pairs={{0,4},{4,0},{8,12},{12,8},{16,20},{20,16},{24,28},{28,24},{1,5},{5... | collective-permute-start | bytes 786440 | tf_op jit(solution)/shard_map/rows_core_far/ppermute | solution.py:18
  (3 other events, 29.0 us)

commit v18 on v9

--- a/solution.py
+++ b/solution.py
@@ -179,8 +179,13 @@
     )
     first_chip = jnp.where((data_here & core) == 0, *first_link)
     second_chip = across - first_chip
-    back = jnp.einsum("eb,en->bn", picker, coming, precision=high)
-    back = back.reshape((shard_count, home_count) + piece)
+    cut = 2 * home_count
+    far_back = jnp.einsum("eb,en->bn", picker[:, cut:], coming, precision=high)
+    coming, far_back = lax.optimization_barrier((coming, far_back))
+    near_back = jnp.einsum("eb,en->bn", picker[:, :cut], coming, precision=high)
+    near_back = near_back.reshape((2, home_count) + piece)
+    far_back = far_back.reshape((2, home_count) + piece)
+    back = [near_back[0], near_back[1], far_back[0], far_back[1]]
     returned = shard_exchange([back[near_order.index(k)] for k in range(shard_count)])
 
     new_home = params

time: 78.9 us -> 80.1 us (1.015)
  blocking collectives: 26.5 us -> 13.7 us
  waiting for transfers between devices: 17.4 us -> 27.6 us
  starting transfers between devices: 27.2 us -> 29.9 us
  matrix products: 1.93 us -> 2.9 us
    all_to_all x1 -> x0, blocking collectives: 12.7 us -> none  [routed(): lax.all_to_all(change.reshape((device_total,) + piece), ('dp', 'shard'),...]
    all_to_all x0 -> x1, waiting for transfers between devices: none -> 10.2 us  [routed(): lax.all_to_all(change.reshape((device_total,) + piece), ('dp', 'shard'),...]
    all_to_all x0 -> x1, starting transfers between devices: none -> 2.72 us  [routed(): lax.all_to_all(change.reshape((device_total,) + piece), ('dp', 'shard'),...]
  transfers between devices with their start and end apart: 26 -> 27, of which waited for: 15 -> 16; matrix products, arithmetic and copies ran while one was open for 2% -> 2% of each run, Pallas kernels for 0% -> 0%
where the time goes in v18:
time: 80.1 us; the launch traced here: 79.9 us
  starting transfers between devices  29.9 us (37%)
  waiting for transfers between devices  27.6 us (34%)
  blocking collectives  13.7 us (17%)
  local copies, waits for them, and re-layouts  3.77 us (5%)
  matrix products  2.9 us (4%)
  between operations  1.3 us (2%)
    ppermute x26, starting transfers between devices, swap(): return lax.ppermute(values, name, pairs)  27.2 us
    ppermute x26, waiting for transfers between devices, swap(): return lax.ppermute(values, name, pairs)  17.4 us
    all_to_all x1, blocking collectives, routed(): lax.all_to_all(leaving.reshape((device_total,) + piece), ('dp', 'shard'),...  13.7 us
    all_to_all x1, waiting for transfers between devices, routed(): lax.all_to_all(change.reshape((device_total,) + piece), ('dp', 'shard'),...  10.2 us
    all_to_all x1, starting transfers between devices, routed(): lax.all_to_all(change.reshape((device_total,) + piece), ('dp', 'shard'),...  2.72 us
  transfers between devices with their start and end apart: 27, of which 16 were waited for; matrix products, arithmetic and copies ran while one was open for 2% of the time, Pallas kernels for 0%

profile of v18, /device:TPU:0, one launch (start us, length us, event | category | flops | bytes accessed | tf_op | source)
XLA Modules:
  0.0 79.9 jit_solution(841410730247600302)
XLA Ops:
  0.7 1.3 %dynamic-slice_bitcast_fusion = (bf16[8,4,32,256]{3,2,1,0:T(8,128)(2,1)S(1)}, bf16[8,4,32,256]{3,2,1,0:T(8,128)(2,1)S(1)}) fusion(bf16[8,4,2,32,256]{4,3,2,1,0:T(8,128)(2,1)} %bitcast.132, s32[]{:T(128)S(6)} %select_n.130, s32[]{:T(128)S(6)} %select_n.129), kind=kLoop, calls=%fused_computation.1 | loop fusion | bytes 2097160 | tf_op jit(solution)/shard_map/jit(dynamic_index_in_dim)/squeeze | solution.py:22
  3.9 2.9 %collective-permute-start.9 = (f32[8,16,256]{2,1,0:T(8,128)S(1)}, f32[8,16,256]{2,1,0:T(8,128)S(1)}, u32[]{:S(2)}, u32[]{:S(2)}) collective-permute-start(f32[8,16,256]{2,1,0:T(8,128)S(1)} %get-tuple-element.43), channel_id=1, source_target_pairs={{0,8},{4,20},{8,0},{12,28},{16,24},{20,4},{24,16},{28,12},{1,9},{5... | collective-permute-start | bytes 393224 | tf_op jit(solution)/shard_map/sum_across_far/ppermute | solution.py:18
  7.1 1.0 %collective-permute-start.8 = (f32[8,16,256]{2,1,0:T(8,128)S(1)}, f32[8,16,256]{2,1,0:T(8,128)S(1)}, u32[]{:S(2)}, u32[]{:S(2)}) collective-permute-start(f32[8,16,256]{2,1,0:T(8,128)S(1)} %get-tuple-element.41), channel_id=1, source_target_pairs={{0,8},{4,20},{8,0},{12,28},{16,24},{20,4},{24,16},{28,12},{1,9},{5... | collective-permute-start | bytes 393224 | tf_op jit(solution)/shard_map/sum_first_far/ppermute | solution.py:18
  8.1 1.1 %collective-permute-start.3 = (f32[8,16,256]{2,1,0:T(8,128)S(1)}, f32[8,16,256]{2,1,0:T(8,128)S(1)}, u32[]{:S(2)}, u32[]{:S(2)}) collective-permute-start(f32[8,16,256]{2,1,0:T(8,128)S(1)} %get-tuple-element.36), channel_id=1, source_target_pairs={{0,8},{4,20},{8,0},{12,28},{16,24},{20,4},{24,16},{28,12},{1,9},{5... | collective-permute-start | bytes 393224 | tf_op jit(solution)/shard_map/sum_across_near/ppermute | solution.py:18
  9.2 0.6 collective-permute-done.9
  9.8 2.1 %collective-permute-start.10 = (f32[8,16,256]{2,1,0:T(8,128)S(1)}, f32[8,16,256]{2,1,0:T(8,128)S(1)}, u32[]{:S(2)}, u32[]{:S(2)}) collective-permute-start(f32[8,16,256]{2,1,0:T(8,128)S(1)} %add.167), channel_id=1, source_target_pairs={{0,16},{4,12},{8,24},{12,4},{16,0},{20,28},{24,8},{28,20},{1,17},{... | collective-permute-start | bytes 393224 | tf_op jit(solution)/shard_map/sum_relay_far/ppermute | solution.py:18
  12.0 1.6 %collective-permute-start.6 = (f32[8,16,256]{2,1,0:T(8,128)S(1)}, f32[8,16,256]{2,1,0:T(8,128)S(1)}, u32[]{:S(2)}, u32[]{:S(2)}) collective-permute-start(f32[8,16,256]{2,1,0:T(8,128)S(1)} %get-tuple-element.37), channel_id=1, source_target_pairs={{0,8},{4,20},{8,0},{12,28},{16,24},{20,4},{24,16},{28,12},{1,9},{5... | collective-permute-start | bytes 393224 | tf_op jit(solution)/shard_map/sum_first_near/ppermute | solution.py:18
  13.6 1.3 %collective-permute-done.3 = f32[8,16,256]{2,1,0:T(8,128)S(1)} collective-permute-done((f32[8,16,256]{2,1,0:T(8,128)S(1)}, f32[8,16,256]{2,1,0:T(8,128)S(1)}, u32[]{:S(2)}, u32[]{:S(2)}) %collective-permute-start.3) | collective-permute-done | bytes 131104 | tf_op jit(solution)/shard_map/sum_across_near/ppermute | solution.py:18
  14.9 1.3 %collective-permute-start.4 = (f32[8,16,256]{2,1,0:T(8,128)S(1)}, f32[8,16,256]{2,1,0:T(8,128)S(1)}, u32[]{:S(2)}, u32[]{:S(2)}) collective-permute-start(f32[8,16,256]{2,1,0:T(8,128)S(1)} %add.160), channel_id=1, source_target_pairs={{0,16},{4,12},{8,24},{12,4},{16,0},{20,28},{24,8},{28,20},{1,17},{... | collective-permute-start | bytes 393224 | tf_op jit(solution)/shard_map/sum_relay_near/ppermute | solution.py:18
  16.3 2.8 %collective-permute-start.12 = (f32[8,8,256]{2,1,0:T(8,128)S(1)}, f32[8,8,256]{2,1,0:T(8,128)S(1)}, u32[]{:S(2)}, u32[]{:S(2)}) collective-permute-start(f32[8,8,256]{2,1,0:T(8,128)S(1)} %get-tuple-element.83), channel_id=1, source_target_pairs={{0,2},{1,3},{2,0},{3,1},{4,6},{5,7},{6,4},{7,5},{8,10},{9,11},{10,... | collective-permute-start | bytes 196616 | tf_op jit(solution)/shard_map/shard_2/ppermute | solution.py:18
  19.1 1.3 %collective-permute-start.11 = (f32[8,8,256]{2,1,0:T(8,128)S(1)}, f32[8,8,256]{2,1,0:T(8,128)S(1)}, u32[]{:S(2)}, u32[]{:S(2)}) collective-permute-start(f32[8,8,256]{2,1,0:T(8,128)S(1)} %get-tuple-element.82), channel_id=1, source_target_pairs={{0,3},{1,2},{2,1},{3,0},{4,7},{5,6},{6,5},{7,4},{8,11},{9,10},{10,... | collective-permute-start | bytes 196616 | tf_op jit(solution)/shard_map/shard_3/ppermute | solution.py:18
  20.6 0.9 %collective-permute-start.7 = (f32[8,8,256]{2,1,0:T(8,128)S(1)}, f32[8,8,256]{2,1,0:T(8,128)S(1)}, u32[]{:S(2)}, u32[]{:S(2)}) collective-permute-start(f32[8,8,256]{2,1,0:T(8,128)S(1)} %get-tuple-element.81), channel_id=1, source_target_pairs={{0,1},{1,0},{2,3},{3,2},{4,5},{5,4},{6,7},{7,6},{8,9},{9,8},{10,11... | collective-permute-start | bytes 196616 | tf_op jit(solution)/shard_map/shard_1/ppermute | solution.py:18
  21.7 1.7 %collective-permute-done.12 = f32[8,8,256]{2,1,0:T(8,128)S(1)} collective-permute-done((f32[8,8,256]{2,1,0:T(8,128)S(1)}, f32[8,8,256]{2,1,0:T(8,128)S(1)}, u32[]{:S(2)}, u32[]{:S(2)}) %collective-permute-start.12) | collective-permute-done | bytes 65568 | tf_op jit(solution)/shard_map/shard_2/ppermute | solution.py:18
  23.5 1.8 %collective-permute-done.11 = f32[8,8,256]{2,1,0:T(8,128)S(1)} collective-permute-done((f32[8,8,256]{2,1,0:T(8,128)S(1)}, f32[8,8,256]{2,1,0:T(8,128)S(1)}, u32[]{:S(2)}, u32[]{:S(2)}) %collective-permute-start.11) | collective-permute-done | bytes 65568 | tf_op jit(solution)/shard_map/shard_3/ppermute | solution.py:18
  26.1 13.7 %all_to_all.10 = f32[32,8,256]{2,1,0:T(8,128)S(1)} all-to-all(f32[32,8,256]{2,1,0:T(8,128)S(1)} %copy.56), channel_id=1, replica_groups=mesh['dp'=8,'shard'=4] {'dp','shard'}, dimensions={0} | all-to-all | bytes 524288 | tf_op jit(solution)/shard_map/all_to_all | solution.py:153
  41.1 1.0 %convolution_bitcast_fusion = f32[32,8,256]{2,1,0:T(8,128)} fusion(f32[256,256]{1,0:T(8,128)S(1)} %fusion.4, f32[1,1,1,256,256]{4,3,2,1,0:T(8,128)S(1)} %copy-done.4), kind=kOutput, calls=%fused_computation | convolution fusion | flops 100663296 | bytes 786432 | tf_op jit(solution)/shard_map/ia,aj->ij/dot_general | solution.py:70
  42.0 2.7 %all-to-all-start.1 = ((f32[32,8,256]{2,1,0:T(8,128)}), f32[32,8,256]{2,1,0:T(8,128)S(1)}, u32[]{:S(2)}, u32[]{:S(2)}) async-start(f32[32,8,256]{2,1,0:T(8,128)} %convolution_bitcast_fusion), calls=%async_computation.1 | async-start | bytes 524288 | tf_op jit(solution)/shard_map/all_to_all | solution.py:170
  44.8 10.2 %all-to-all-done.1 = f32[32,8,256]{2,1,0:T(8,128)S(1)} async-done(((f32[32,8,256]{2,1,0:T(8,128)}), f32[32,8,256]{2,1,0:T(8,128)S(1)}, u32[]{:S(2)}, u32[]{:S(2)}) %all-to-all-start.1) | async-done | bytes 262176 | tf_op jit(solution)/shard_map/all_to_all | solution.py:170
  55.7 1.8 %collective-permute-start.13 = (f32[8,8,256]{2,1,0:T(8,128)S(1)}, f32[8,8,256]{2,1,0:T(8,128)S(1)}, u32[]{:S(2)}, u32[]{:S(2)}) collective-permute-start(f32[8,8,256]{2,1,0:T(8,128)S(1)} %copy.58), channel_id=1, source_target_pairs={{0,3},{1,2},{2,1},{3,0},{4,7},{5,6},{6,5},{7,4},{8,11},{9,10},{10,... | collective-permute-start | bytes 196616 | tf_op jit(solution)/shard_map/shard_3/ppermute | solution.py:18
  57.5 0.9 %collective-permute-start.14 = (f32[8,8,256]{2,1,0:T(8,128)S(1)}, f32[8,8,256]{2,1,0:T(8,128)S(1)}, u32[]{:S(2)}, u32[]{:S(2)}) collective-permute-start(f32[8,8,256]{2,1,0:T(8,128)S(1)} %copy.59), channel_id=1, source_target_pairs={{0,2},{1,3},{2,0},{3,1},{4,6},{5,7},{6,4},{7,5},{8,10},{9,11},{10,... | collective-permute-start | bytes 196616 | tf_op jit(solution)/shard_map/shard_2/ppermute | solution.py:18
  58.4 1.9 %collective-permute-start.15 = (f32[8,8,256]{2,1,0:T(8,128)S(1)}, f32[8,8,256]{2,1,0:T(8,128)S(1)}, u32[]{:S(2)}, u32[]{:S(2)}) collective-permute-start(f32[8,8,256]{2,1,0:T(8,128)S(1)} %copy.60), channel_id=1, source_target_pairs={{0,1},{1,0},{2,3},{3,2},{4,5},{5,4},{6,7},{7,6},{8,9},{9,8},{10,11... | collective-permute-start | bytes 196616 | tf_op jit(solution)/shard_map/shard_1/ppermute | solution.py:18
  60.4 2.2 %collective-permute-done.13 = f32[8,8,256]{2,1,0:T(8,128)S(1)} collective-permute-done((f32[8,8,256]{2,1,0:T(8,128)S(1)}, f32[8,8,256]{2,1,0:T(8,128)S(1)}, u32[]{:S(2)}, u32[]{:S(2)}) %collective-permute-start.13) | collective-permute-done | bytes 65568 | tf_op jit(solution)/shard_map/shard_3/ppermute | solution.py:18
  62.6 2.2 %collective-permute-done.14 = f32[8,8,256]{2,1,0:T(8,128)S(1)} collective-permute-done((f32[8,8,256]{2,1,0:T(8,128)S(1)}, f32[8,8,256]{2,1,0:T(8,128)S(1)}, u32[]{:S(2)}, u32[]{:S(2)}) %collective-permute-start.14) | collective-permute-done | bytes 65568 | tf_op jit(solution)/shard_map/shard_2/ppermute | solution.py:18
  64.9 0.9 %collective-permute-start.18 = (f32[4,32,256]{2,1,0:T(8,128)S(1)}, f32[4,32,256]{2,1,0:T(8,128)S(1)}, u32[]{:S(2)}, u32[]{:S(2)}) collective-permute-start(f32[4,32,256]{2,1,0:T(8,128)S(1)} %get-tuple-element.65), channel_id=1, source_target_pairs={{0,8},{4,20},{8,0},{12,28},{16,24},{20,4},{24,16},{28,12},{1,9},{5... | collective-permute-start | bytes 393224 | tf_op jit(solution)/shard_map/rows_first_top/ppermute | solution.py:18
  66.4 1.5 %collective-permute-start.17 = (f32[4,32,256]{2,1,0:T(8,128)S(1)}, f32[4,32,256]{2,1,0:T(8,128)S(1)}, u32[]{:S(2)}, u32[]{:S(2)}) collective-permute-start(f32[4,32,256]{2,1,0:T(8,128)S(1)} %get-tuple-element.64), channel_id=1, source_target_pairs={{0,8},{4,20},{8,0},{12,28},{16,24},{20,4},{24,16},{28,12},{1,9},{5... | collective-permute-start | bytes 393224 | tf_op jit(solution)/shard_map/rows_first_low/ppermute | solution.py:18
  67.9 1.1 %collective-permute-start.19 = (f32[4,32,256]{2,1,0:T(8,128)S(1)}, f32[4,32,256]{2,1,0:T(8,128)S(1)}, u32[]{:S(2)}, u32[]{:S(2)}) collective-permute-start(f32[4,32,256]{2,1,0:T(8,128)S(1)} %get-tuple-element.65), channel_id=1, source_target_pairs={{0,16},{4,12},{8,24},{12,4},{16,0},{20,28},{24,8},{28,20},{1,17},{... | collective-permute-start | bytes 393224 | tf_op jit(solution)/shard_map/rows_second_top/ppermute | solution.py:18
  69.2 1.8 %collective-permute-done.18 = f32[4,32,256]{2,1,0:T(8,128)S(1)} collective-permute-done((f32[4,32,256]{2,1,0:T(8,128)S(1)}, f32[4,32,256]{2,1,0:T(8,128)S(1)}, u32[]{:S(2)}, u32[]{:S(2)}) %collective-permute-start.18) | collective-permute-done | bytes 131104 | tf_op jit(solution)/shard_map/rows_first_top/ppermute | solution.py:18
  71.0 0.9 %collective-permute-start.21 = (f32[4,32,256]{2,1,0:T(8,128)S(1)}, f32[4,32,256]{2,1,0:T(8,128)S(1)}, u32[]{:S(2)}, u32[]{:S(2)}) collective-permute-start(f32[4,32,256]{2,1,0:T(8,128)S(1)} %collective-permute-done.18), channel_id=1, source_target_pairs={{0,16},{4,12},{8,24},{12,4},{16,0},{20,28},{24,8},{28,20},{1,17},{... | collective-permute-start | bytes 393224 | tf_op jit(solution)/shard_map/rows_relay_top/ppermute | solution.py:18
  71.9 0.8 %collective-permute-start.24 = (f32[4,32,256]{2,1,0:T(8,128)S(1)}, f32[4,32,256]{2,1,0:T(8,128)S(1)}, u32[]{:S(2)}, u32[]{:S(2)}) collective-permute-start(f32[4,32,256]{2,1,0:T(8,128)S(1)} %collective-permute-done.20), channel_id=1, source_target_pairs={{0,8},{4,20},{8,0},{12,28},{16,24},{20,4},{24,16},{28,12},{1,9},{5... | collective-permute-start | bytes 393224 | tf_op jit(solution)/shard_map/rows_relay_low/ppermute | solution.py:18
  72.7 1.0 %collective-permute-done.17 = f32[4,32,256]{2,1,0:T(8,128)S(1)} collective-permute-done((f32[4,32,256]{2,1,0:T(8,128)S(1)}, f32[4,32,256]{2,1,0:T(8,128)S(1)}, u32[]{:S(2)}, u32[]{:S(2)}) %collective-permute-start.17) | collective-permute-done | bytes 131104 | tf_op jit(solution)/shard_map/rows_first_low/ppermute | solution.py:18
  73.8 2.3 %collective-permute-done.21 = f32[4,32,256]{2,1,0:T(8,128)S(1)} collective-permute-done((f32[4,32,256]{2,1,0:T(8,128)S(1)}, f32[4,32,256]{2,1,0:T(8,128)S(1)}, u32[]{:S(2)}, u32[]{:S(2)}) %collective-permute-start.21) | collective-permute-done | bytes 131104 | tf_op jit(solution)/shard_map/rows_relay_top/ppermute | solution.py:18
  78.6 1.3 %copy-done.3 = f32[8,256,256]{2,1,0:T(8,128)} copy-done((f32[8,256,256]{2,1,0:T(8,128)}, f32[8,256,256]{2,1,0:T(8,128)S(1)}, u32[]{:S(2)}) %copy-start.3) | copy-done | bytes 2097176
  (104 shorter events, 8.4 us)
Async XLA Ops:
  0.6 39.6 %copy-start = (f32[1,1,1,256,256]{4,3,2,1,0:T(8,128)S(1)}, f32[1,1,1,256,256]{4,3,2,1,0:T(8,128)}, u32[]{:S(2)}) copy-start(f32[1,1,1,256,256]{4,3,2,1,0:T(8,128)} %param.10) | copy-start | bytes 786436
  2.2 1.7 %collective-permute-start = (f32[8,32,256]{2,1,0:T(8,128)S(1)}, f32[8,32,256]{2,1,0:T(8,128)S(1)}, u32[]{:S(2)}, u32[]{:S(2)}) collective-permute-start(f32[8,32,256]{2,1,0:T(8,128)S(1)} %get-tuple-element.63), channel_id=1, source_target_pairs={{0,4},{4,0},{8,12},{12,8},{16,20},{20,16},{24,28},{28,24},{1,5},{5... | collective-permute-start | bytes 786440 | tf_op jit(solution)/shard_map/sum_core_across/ppermute | solution.py:18
  2.7 4.2 %collective-permute-start.2 = (f32[8,32,256]{2,1,0:T(8,128)S(1)}, f32[8,32,256]{2,1,0:T(8,128)S(1)}, u32[]{:S(2)}, u32[]{:S(2)}) collective-permute-start(f32[8,32,256]{2,1,0:T(8,128)S(1)} %get-tuple-element.60), channel_id=1, source_target_pairs={{0,4},{4,0},{8,12},{12,8},{16,20},{20,16},{24,28},{28,24},{1,5},{5... | collective-permute-start | bytes 786440 | tf_op jit(solution)/shard_map/sum_core_second/ppermute | solution.py:18
  2.8 4.1 %collective-permute-start.5 = (f32[8,32,256]{2,1,0:T(8,128)S(1)}, f32[8,32,256]{2,1,0:T(8,128)S(1)}, u32[]{:S(2)}, u32[]{:S(2)}) collective-permute-start(f32[8,32,256]{2,1,0:T(8,128)S(1)} %get-tuple-element.61), channel_id=1, source_target_pairs={{0,4},{4,0},{8,12},{12,8},{16,20},{20,16},{24,28},{28,24},{1,5},{5... | collective-permute-start | bytes 786440 | tf_op jit(solution)/shard_map/sum_core_first/ppermute | solution.py:18
  3.2 3.6 %collective-permute-start.1 = (f32[8,32,256]{2,1,0:T(8,128)S(1)}, f32[8,32,256]{2,1,0:T(8,128)S(1)}, u32[]{:S(2)}, u32[]{:S(2)}) collective-permute-start(f32[8,32,256]{2,1,0:T(8,128)S(1)} %get-tuple-element.62), channel_id=1, source_target_pairs={{0,4},{4,0},{8,12},{12,8},{16,20},{20,16},{24,28},{28,24},{1,5},{5... | collective-permute-start | bytes 786440 | tf_op jit(solution)/shard_map/sum_core_own/ppermute | solution.py:18
  3.9 5.9 %collective-permute-start.9 = (f32[8,16,256]{2,1,0:T(8,128)S(1)}, f32[8,16,256]{2,1,0:T(8,128)S(1)}, u32[]{:S(2)}, u32[]{:S(2)}) collective-permute-start(f32[8,16,256]{2,1,0:T(8,128)S(1)} %get-tuple-element.43), channel_id=1, source_target_pairs={{0,8},{4,20},{8,0},{12,28},{16,24},{20,4},{24,16},{28,12},{1,9},{5... | collective-permute-start | bytes 393224 | tf_op jit(solution)/shard_map/sum_across_far/ppermute | solution.py:18
  7.1 6.5 %collective-permute-start.8 = (f32[8,16,256]{2,1,0:T(8,128)S(1)}, f32[8,16,256]{2,1,0:T(8,128)S(1)}, u32[]{:S(2)}, u32[]{:S(2)}) collective-permute-start(f32[8,16,256]{2,1,0:T(8,128)S(1)} %get-tuple-element.41), channel_id=1, source_target_pairs={{0,8},{4,20},{8,0},{12,28},{16,24},{20,4},{24,16},{28,12},{1,9},{5... | collective-permute-start | bytes 393224 | tf_op jit(solution)/shard_map/sum_first_far/ppermute | solution.py:18
  8.1 6.8 %collective-permute-start.3 = (f32[8,16,256]{2,1,0:T(8,128)S(1)}, f32[8,16,256]{2,1,0:T(8,128)S(1)}, u32[]{:S(2)}, u32[]{:S(2)}) collective-permute-start(f32[8,16,256]{2,1,0:T(8,128)S(1)} %get-tuple-element.36), channel_id=1, source_target_pairs={{0,8},{4,20},{8,0},{12,28},{16,24},{20,4},{24,16},{28,12},{1,9},{5... | collective-permute-start | bytes 393224 | tf_op jit(solution)/shard_map/sum_across_near/ppermute | solution.py:18
  9.8 6.4 %collective-permute-start.10 = (f32[8,16,256]{2,1,0:T(8,128)S(1)}, f32[8,16,256]{2,1,0:T(8,128)S(1)}, u32[]{:S(2)}, u32[]{:S(2)}) collective-permute-start(f32[8,16,256]{2,1,0:T(8,128)S(1)} %add.167), channel_id=1, source_target_pairs={{0,16},{4,12},{8,24},{12,4},{16,0},{20,28},{24,8},{28,20},{1,17},{... | collective-permute-start | bytes 393224 | tf_op jit(solution)/shard_map/sum_relay_far/ppermute | solution.py:18
  12.0 8.5 %collective-permute-start.6 = (f32[8,16,256]{2,1,0:T(8,128)S(1)}, f32[8,16,256]{2,1,0:T(8,128)S(1)}, u32[]{:S(2)}, u32[]{:S(2)}) collective-permute-start(f32[8,16,256]{2,1,0:T(8,128)S(1)} %get-tuple-element.37), channel_id=1, source_target_pairs={{0,8},{4,20},{8,0},{12,28},{16,24},{20,4},{24,16},{28,12},{1,9},{5... | collective-permute-start | bytes 393224 | tf_op jit(solution)/shard_map/sum_first_near/ppermute | solution.py:18
  14.9 24.9 %copy-start.4 = (f32[1,1,1,256,256]{4,3,2,1,0:T(8,128)S(1)}, f32[1,1,1,256,256]{4,3,2,1,0:T(8,128)}, u32[]{:S(2)}) copy-start(f32[1,1,1,256,256]{4,3,2,1,0:T(8,128)} %param.9) | copy-start | bytes 786436
  14.9 5.6 %collective-permute-start.4 = (f32[8,16,256]{2,1,0:T(8,128)S(1)}, f32[8,16,256]{2,1,0:T(8,128)S(1)}, u32[]{:S(2)}, u32[]{:S(2)}) collective-permute-start(f32[8,16,256]{2,1,0:T(8,128)S(1)} %add.160), channel_id=1, source_target_pairs={{0,16},{4,12},{8,24},{12,4},{16,0},{20,28},{24,8},{28,20},{1,17},{... | collective-permute-start | bytes 393224 | tf_op jit(solution)/shard_map/sum_relay_near/ppermute | solution.py:18
  16.3 7.1 %collective-permute-start.12 = (f32[8,8,256]{2,1,0:T(8,128)S(1)}, f32[8,8,256]{2,1,0:T(8,128)S(1)}, u32[]{:S(2)}, u32[]{:S(2)}) collective-permute-start(f32[8,8,256]{2,1,0:T(8,128)S(1)} %get-tuple-element.83), channel_id=1, source_target_pairs={{0,2},{1,3},{2,0},{3,1},{4,6},{5,7},{6,4},{7,5},{8,10},{9,11},{10,... | collective-permute-start | bytes 196616 | tf_op jit(solution)/shard_map/shard_2/ppermute | solution.py:18
  19.1 6.2 %collective-permute-start.11 = (f32[8,8,256]{2,1,0:T(8,128)S(1)}, f32[8,8,256]{2,1,0:T(8,128)S(1)}, u32[]{:S(2)}, u32[]{:S(2)}) collective-permute-start(f32[8,8,256]{2,1,0:T(8,128)S(1)} %get-tuple-element.82), channel_id=1, source_target_pairs={{0,3},{1,2},{2,1},{3,0},{4,7},{5,6},{6,5},{7,4},{8,11},{9,10},{10,... | collective-permute-start | bytes 196616 | tf_op jit(solution)/shard_map/shard_3/ppermute | solution.py:18
  20.5 19.7 %copy-start.5 = (f32[1,1,1,256,256]{4,3,2,1,0:T(8,128)S(1)}, f32[1,1,1,256,256]{4,3,2,1,0:T(8,128)}, u32[]{:S(2)}) copy-start(f32[1,1,1,256,256]{4,3,2,1,0:T(8,128)} %param.11) | copy-start | bytes 786436
  20.5 19.7 %copy-start.6 = (f32[1,1,1,256,256]{4,3,2,1,0:T(8,128)S(1)}, f32[1,1,1,256,256]{4,3,2,1,0:T(8,128)}, u32[]{:S(2)}) copy-start(f32[1,1,1,256,256]{4,3,2,1,0:T(8,128)} %param.12) | copy-start | bytes 786436
  20.6 5.0 %collective-permute-start.7 = (f32[8,8,256]{2,1,0:T(8,128)S(1)}, f32[8,8,256]{2,1,0:T(8,128)S(1)}, u32[]{:S(2)}, u32[]{:S(2)}) collective-permute-start(f32[8,8,256]{2,1,0:T(8,128)S(1)} %get-tuple-element.81), channel_id=1, source_target_pairs={{0,1},{1,0},{2,3},{3,2},{4,5},{5,4},{6,7},{7,6},{8,9},{9,8},{10,11... | collective-permute-start | bytes 196616 | tf_op jit(solution)/shard_map/shard_1/ppermute | solution.py:18
  41.0 21.5 %copy-start.1 = (f32[8,32,256]{2,1,0:T(8,128)S(1)}, f32[8,32,256]{2,1,0:T(8,128)}, u32[]{:S(2)}) copy-start(f32[8,32,256]{2,1,0:T(8,128)} %param.8) | copy-start | bytes 786436
  42.0 12.9 %all-to-all-start.1 = ((f32[32,8,256]{2,1,0:T(8,128)}), f32[32,8,256]{2,1,0:T(8,128)S(1)}, u32[]{:S(2)}, u32[]{:S(2)}) async-start(f32[32,8,256]{2,1,0:T(8,128)} %convolution_bitcast_fusion), calls=%async_computation.1 | async-start | bytes 524288 | tf_op jit(solution)/shard_map/all_to_all | solution.py:170
  55.7 6.9 %collective-permute-start.13 = (f32[8,8,256]{2,1,0:T(8,128)S(1)}, f32[8,8,256]{2,1,0:T(8,128)S(1)}, u32[]{:S(2)}, u32[]{:S(2)}) collective-permute-start(f32[8,8,256]{2,1,0:T(8,128)S(1)} %copy.58), channel_id=1, source_target_pairs={{0,3},{1,2},{2,1},{3,0},{4,7},{5,6},{6,5},{7,4},{8,11},{9,10},{10,... | collective-permute-start | bytes 196616 | tf_op jit(solution)/shard_map/shard_3/ppermute | solution.py:18
  57.5 7.2 %collective-permute-start.14 = (f32[8,8,256]{2,1,0:T(8,128)S(1)}, f32[8,8,256]{2,1,0:T(8,128)S(1)}, u32[]{:S(2)}, u32[]{:S(2)}) collective-permute-start(f32[8,8,256]{2,1,0:T(8,128)S(1)} %copy.59), channel_id=1, source_target_pairs={{0,2},{1,3},{2,0},{3,1},{4,6},{5,7},{6,4},{7,5},{8,10},{9,11},{10,... | collective-permute-start | bytes 196616 | tf_op jit(solution)/shard_map/shard_2/ppermute | solution.py:18
  58.4 6.4 %collective-permute-start.15 = (f32[8,8,256]{2,1,0:T(8,128)S(1)}, f32[8,8,256]{2,1,0:T(8,128)S(1)}, u32[]{:S(2)}, u32[]{:S(2)}) collective-permute-start(f32[8,8,256]{2,1,0:T(8,128)S(1)} %copy.60), channel_id=1, source_target_pairs={{0,1},{1,0},{2,3},{3,2},{4,5},{5,4},{6,7},{7,6},{8,9},{9,8},{10,11... | collective-permute-start | bytes 196616 | tf_op jit(solution)/shard_map/shard_1/ppermute | solution.py:18
  64.9 6.1 %collective-permute-start.18 = (f32[4,32,256]{2,1,0:T(8,128)S(1)}, f32[4,32,256]{2,1,0:T(8,128)S(1)}, u32[]{:S(2)}, u32[]{:S(2)}) collective-permute-start(f32[4,32,256]{2,1,0:T(8,128)S(1)} %get-tuple-element.65), channel_id=1, source_target_pairs={{0,8},{4,20},{8,0},{12,28},{16,24},{20,4},{24,16},{28,12},{1,9},{5... | collective-permute-start | bytes 393224 | tf_op jit(solution)/shard_map/rows_first_top/ppermute | solution.py:18
  65.8 6.1 %collective-permute-start.20 = (f32[4,32,256]{2,1,0:T(8,128)S(1)}, f32[4,32,256]{2,1,0:T(8,128)S(1)}, u32[]{:S(2)}, u32[]{:S(2)}) collective-permute-start(f32[4,32,256]{2,1,0:T(8,128)S(1)} %get-tuple-element.64), channel_id=1, source_target_pairs={{0,16},{4,12},{8,24},{12,4},{16,0},{20,28},{24,8},{28,20},{1,17},{... | collective-permute-start | bytes 393224 | tf_op jit(solution)/shard_map/rows_second_low/ppermute | solution.py:18
  66.4 7.4 %collective-permute-start.17 = (f32[4,32,256]{2,1,0:T(8,128)S(1)}, f32[4,32,256]{2,1,0:T(8,128)S(1)}, u32[]{:S(2)}, u32[]{:S(2)}) collective-permute-start(f32[4,32,256]{2,1,0:T(8,128)S(1)} %get-tuple-element.64), channel_id=1, source_target_pairs={{0,8},{4,20},{8,0},{12,28},{16,24},{20,4},{24,16},{28,12},{1,9},{5... | collective-permute-start | bytes 393224 | tf_op jit(solution)/shard_map/rows_first_low/ppermute | solution.py:18
  67.9 5.9 %collective-permute-start.16 = (f32[8,32,256]{2,1,0:T(8,128)S(1)}, f32[8,32,256]{2,1,0:T(8,128)S(1)}, u32[]{:S(2)}, u32[]{:S(2)}) collective-permute-start(f32[8,32,256]{2,1,0:T(8,128)S(1)} %subtract_dynamic-update-slice_fusion), channel_id=1, source_target_pairs={{0,4},{4,0},{8,12},{12,8},{16,20},{20,16},{24,28},{28,24},{1,5},{5... | collective-permute-start | bytes 786440 | tf_op jit(solution)/shard_map/rows_core_own/ppermute | solution.py:18
  67.9 5.9 %collective-permute-start.19 = (f32[4,32,256]{2,1,0:T(8,128)S(1)}, f32[4,32,256]{2,1,0:T(8,128)S(1)}, u32[]{:S(2)}, u32[]{:S(2)}) collective-permute-start(f32[4,32,256]{2,1,0:T(8,128)S(1)} %get-tuple-element.65), channel_id=1, source_target_pairs={{0,16},{4,12},{8,24},{12,4},{16,0},{20,28},{24,8},{28,20},{1,17},{... | collective-permute-start | bytes 393224 | tf_op jit(solution)/shard_map/rows_second_top/ppermute | solution.py:18
  71.0 5.2 %collective-permute-start.21 = (f32[4,32,256]{2,1,0:T(8,128)S(1)}, f32[4,32,256]{2,1,0:T(8,128)S(1)}, u32[]{:S(2)}, u32[]{:S(2)}) collective-permute-start(f32[4,32,256]{2,1,0:T(8,128)S(1)} %collective-permute-done.18), channel_id=1, source_target_pairs={{0,16},{4,12},{8,24},{12,4},{16,0},{20,28},{24,8},{28,20},{1,17},{... | collective-permute-start | bytes 393224 | tf_op jit(solution)/shard_map/rows_relay_top/ppermute | solution.py:18
  71.9 5.0 %collective-permute-start.24 = (f32[4,32,256]{2,1,0:T(8,128)S(1)}, f32[4,32,256]{2,1,0:T(8,128)S(1)}, u32[]{:S(2)}, u32[]{:S(2)}) collective-permute-start(f32[4,32,256]{2,1,0:T(8,128)S(1)} %collective-permute-done.20), channel_id=1, source_target_pairs={{0,8},{4,20},{8,0},{12,28},{16,24},{20,4},{24,16},{28,12},{1,9},{5... | collective-permute-start | bytes 393224 | tf_op jit(solution)/shard_map/rows_relay_low/ppermute | solution.py:18
  76.1 1.5 %collective-permute-start.22 = (f32[8,32,256]{2,1,0:T(8,128)S(1)}, f32[8,32,256]{2,1,0:T(8,128)S(1)}, u32[]{:S(2)}, u32[]{:S(2)}) collective-permute-start(f32[8,32,256]{2,1,0:T(8,128)S(1)} %pad_maximum_fusion.1), channel_id=1, source_target_pairs={{0,4},{4,0},{8,12},{12,8},{16,20},{20,16},{24,28},{28,24},{1,5},{5... | collective-permute-start | bytes 786440 | tf_op jit(solution)/shard_map/rows_core_first/ppermute | solution.py:18
  76.2 1.9 %collective-permute-start.23 = (f32[8,32,256]{2,1,0:T(8,128)S(1)}, f32[8,32,256]{2,1,0:T(8,128)S(1)}, u32[]{:S(2)}, u32[]{:S(2)}) collective-permute-start(f32[8,32,256]{2,1,0:T(8,128)S(1)} %pad_maximum_fusion.2), channel_id=1, source_target_pairs={{0,4},{4,0},{8,12},{12,8},{16,20},{20,16},{24,28},{28,24},{1,5},{5... | collective-permute-start | bytes 786440 | tf_op jit(solution)/shard_map/rows_core_second/ppermute | solution.py:18
  76.9 1.6 %collective-permute-start.25 = (f32[8,32,256]{2,1,0:T(8,128)S(1)}, f32[8,32,256]{2,1,0:T(8,128)S(1)}, u32[]{:S(2)}, u32[]{:S(2)}) collective-permute-start(f32[8,32,256]{2,1,0:T(8,128)S(1)} %constant_dynamic-update-slice_fusion.6), channel_id=1, source_target_pairs={{0,4},{4,0},{8,12},{12,8},{16,20},{20,16},{24,28},{28,24},{1,5},{5... | collective-permute-start | bytes 786440 | tf_op jit(solution)/shard_map/rows_core_far/ppermute | solution.py:18
  (5 other events, 65.1 us)

commit v19 on v9

--- a/solution.py
+++ b/solution.py
@@ -184,7 +184,7 @@
     returned = shard_exchange([back[near_order.index(k)] for k in range(shard_count)])
 
     new_home = params
-    for k in (0, 3, 2, 1):
+    for k in (0, 2, 3, 1):
         start = (shard_here ^ k) * piece[0]
         home = lax.dynamic_slice_in_dim(params, start, piece[0], axis=1)
         home = home - learn_rate * (returned[k] + decay_rate * home)

time: 78.9 us -> 78.6 us (level)
  starting transfers between devices: 27.2 us -> 25.8 us
  waiting for transfers between devices: 17.4 us -> 18.5 us
    ppermute x26, starting transfers between devices: 27.2 us -> 25.8 us  [swap(): return lax.ppermute(values, name, pairs)]
    ppermute x26, waiting for transfers between devices: 17.4 us -> 18.5 us  [swap(): return lax.ppermute(values, name, pairs)]
where the time goes in v19:
time: 78.6 us; the launch traced here: 78.4 us
  blocking collectives  26.5 us (34%)
  starting transfers between devices  25.8 us (33%)
  waiting for transfers between devices  18.5 us (24%)
  local copies, waits for them, and re-layouts  3.76 us (5%)
  matrix products  1.93 us (2%)
  between operations  1.28 us (2%)
    ppermute x26, starting transfers between devices, swap(): return lax.ppermute(values, name, pairs)  25.8 us
    ppermute x26, waiting for transfers between devices, swap(): return lax.ppermute(values, name, pairs)  18.5 us
    all_to_all x1, blocking collectives, routed(): lax.all_to_all(leaving.reshape((device_total,) + piece), ('dp', 'shard'),...  13.7 us
    all_to_all x1, blocking collectives, routed(): lax.all_to_all(change.reshape((device_total,) + piece), ('dp', 'shard'),...  12.7 us
    unnamed x27, local copies, waits for them, and re-layouts  1.58 us
  transfers between devices with their start and end apart: 26, of which 15 were waited for; matrix products, arithmetic and copies ran while one was open for 2% of the time, Pallas kernels for 0%

profile of v19, /device:TPU:0, one launch (start us, length us, event | category | flops | bytes accessed | tf_op | source)
XLA Modules:
  0.0 78.4 jit_solution(13558263427054308320)
XLA Ops:
  0.7 1.3 %dynamic-slice_bitcast_fusion = (bf16[8,4,32,256]{3,2,1,0:T(8,128)(2,1)S(1)}, bf16[8,4,32,256]{3,2,1,0:T(8,128)(2,1)S(1)}) fusion(bf16[8,4,2,32,256]{4,3,2,1,0:T(8,128)(2,1)} %bitcast.130, s32[]{:T(128)S(6)} %select_n.130, s32[]{:T(128)S(6)} %select_n.129), kind=kLoop, calls=%fused_computation.1 | loop fusion | bytes 2097160 | tf_op jit(solution)/shard_map/jit(dynamic_index_in_dim)/squeeze | solution.py:22
  2.2 0.5 collective-permute-start
  3.3 0.6 collective-permute-done
  4.0 2.9 %collective-permute-start.9 = (f32[8,16,256]{2,1,0:T(8,128)S(1)}, f32[8,16,256]{2,1,0:T(8,128)S(1)}, u32[]{:S(2)}, u32[]{:S(2)}) collective-permute-start(f32[8,16,256]{2,1,0:T(8,128)S(1)} %get-tuple-element.41), channel_id=1, source_target_pairs={{0,8},{4,20},{8,0},{12,28},{16,24},{20,4},{24,16},{28,12},{1,9},{5... | collective-permute-start | bytes 393224 | tf_op jit(solution)/shard_map/sum_across_far/ppermute | solution.py:18
  7.1 1.0 %collective-permute-start.8 = (f32[8,16,256]{2,1,0:T(8,128)S(1)}, f32[8,16,256]{2,1,0:T(8,128)S(1)}, u32[]{:S(2)}, u32[]{:S(2)}) collective-permute-start(f32[8,16,256]{2,1,0:T(8,128)S(1)} %get-tuple-element.39), channel_id=1, source_target_pairs={{0,8},{4,20},{8,0},{12,28},{16,24},{20,4},{24,16},{28,12},{1,9},{5... | collective-permute-start | bytes 393224 | tf_op jit(solution)/shard_map/sum_first_far/ppermute | solution.py:18
  8.1 1.1 %collective-permute-start.3 = (f32[8,16,256]{2,1,0:T(8,128)S(1)}, f32[8,16,256]{2,1,0:T(8,128)S(1)}, u32[]{:S(2)}, u32[]{:S(2)}) collective-permute-start(f32[8,16,256]{2,1,0:T(8,128)S(1)} %get-tuple-element.34), channel_id=1, source_target_pairs={{0,8},{4,20},{8,0},{12,28},{16,24},{20,4},{24,16},{28,12},{1,9},{5... | collective-permute-start | bytes 393224 | tf_op jit(solution)/shard_map/sum_across_near/ppermute | solution.py:18
  9.2 0.6 collective-permute-done.9
  9.8 2.1 %collective-permute-start.10 = (f32[8,16,256]{2,1,0:T(8,128)S(1)}, f32[8,16,256]{2,1,0:T(8,128)S(1)}, u32[]{:S(2)}, u32[]{:S(2)}) collective-permute-start(f32[8,16,256]{2,1,0:T(8,128)S(1)} %add.167), channel_id=1, source_target_pairs={{0,16},{4,12},{8,24},{12,4},{16,0},{20,28},{24,8},{28,20},{1,17},{... | collective-permute-start | bytes 393224 | tf_op jit(solution)/shard_map/sum_relay_far/ppermute | solution.py:18
  12.0 1.6 %collective-permute-start.6 = (f32[8,16,256]{2,1,0:T(8,128)S(1)}, f32[8,16,256]{2,1,0:T(8,128)S(1)}, u32[]{:S(2)}, u32[]{:S(2)}) collective-permute-start(f32[8,16,256]{2,1,0:T(8,128)S(1)} %get-tuple-element.35), channel_id=1, source_target_pairs={{0,8},{4,20},{8,0},{12,28},{16,24},{20,4},{24,16},{28,12},{1,9},{5... | collective-permute-start | bytes 393224 | tf_op jit(solution)/shard_map/sum_first_near/ppermute | solution.py:18
  13.6 1.3 %collective-permute-done.3 = f32[8,16,256]{2,1,0:T(8,128)S(1)} collective-permute-done((f32[8,16,256]{2,1,0:T(8,128)S(1)}, f32[8,16,256]{2,1,0:T(8,128)S(1)}, u32[]{:S(2)}, u32[]{:S(2)}) %collective-permute-start.3) | collective-permute-done | bytes 131104 | tf_op jit(solution)/shard_map/sum_across_near/ppermute | solution.py:18
  14.9 1.3 %collective-permute-start.4 = (f32[8,16,256]{2,1,0:T(8,128)S(1)}, f32[8,16,256]{2,1,0:T(8,128)S(1)}, u32[]{:S(2)}, u32[]{:S(2)}) collective-permute-start(f32[8,16,256]{2,1,0:T(8,128)S(1)} %add.160), channel_id=1, source_target_pairs={{0,16},{4,12},{8,24},{12,4},{16,0},{20,28},{24,8},{28,20},{1,17},{... | collective-permute-start | bytes 393224 | tf_op jit(solution)/shard_map/sum_relay_near/ppermute | solution.py:18
  16.3 2.8 %collective-permute-start.12 = (f32[8,8,256]{2,1,0:T(8,128)S(1)}, f32[8,8,256]{2,1,0:T(8,128)S(1)}, u32[]{:S(2)}, u32[]{:S(2)}) collective-permute-start(f32[8,8,256]{2,1,0:T(8,128)S(1)} %get-tuple-element.79), channel_id=1, source_target_pairs={{0,2},{1,3},{2,0},{3,1},{4,6},{5,7},{6,4},{7,5},{8,10},{9,11},{10,... | collective-permute-start | bytes 196616 | tf_op jit(solution)/shard_map/shard_2/ppermute | solution.py:18
  19.1 1.3 %collective-permute-start.11 = (f32[8,8,256]{2,1,0:T(8,128)S(1)}, f32[8,8,256]{2,1,0:T(8,128)S(1)}, u32[]{:S(2)}, u32[]{:S(2)}) collective-permute-start(f32[8,8,256]{2,1,0:T(8,128)S(1)} %get-tuple-element.78), channel_id=1, source_target_pairs={{0,3},{1,2},{2,1},{3,0},{4,7},{5,6},{6,5},{7,4},{8,11},{9,10},{10,... | collective-permute-start | bytes 196616 | tf_op jit(solution)/shard_map/shard_3/ppermute | solution.py:18
  20.6 0.9 %collective-permute-start.7 = (f32[8,8,256]{2,1,0:T(8,128)S(1)}, f32[8,8,256]{2,1,0:T(8,128)S(1)}, u32[]{:S(2)}, u32[]{:S(2)}) collective-permute-start(f32[8,8,256]{2,1,0:T(8,128)S(1)} %get-tuple-element.77), channel_id=1, source_target_pairs={{0,1},{1,0},{2,3},{3,2},{4,5},{5,4},{6,7},{7,6},{8,9},{9,8},{10,11... | collective-permute-start | bytes 196616 | tf_op jit(solution)/shard_map/shard_1/ppermute | solution.py:18
  21.7 1.7 %collective-permute-done.12 = f32[8,8,256]{2,1,0:T(8,128)S(1)} collective-permute-done((f32[8,8,256]{2,1,0:T(8,128)S(1)}, f32[8,8,256]{2,1,0:T(8,128)S(1)}, u32[]{:S(2)}, u32[]{:S(2)}) %collective-permute-start.12) | collective-permute-done | bytes 65568 | tf_op jit(solution)/shard_map/shard_2/ppermute | solution.py:18
  23.5 1.8 %collective-permute-done.11 = f32[8,8,256]{2,1,0:T(8,128)S(1)} collective-permute-done((f32[8,8,256]{2,1,0:T(8,128)S(1)}, f32[8,8,256]{2,1,0:T(8,128)S(1)}, u32[]{:S(2)}, u32[]{:S(2)}) %collective-permute-start.11) | collective-permute-done | bytes 65568 | tf_op jit(solution)/shard_map/shard_3/ppermute | solution.py:18
  26.1 13.7 %all_to_all.10 = f32[32,8,256]{2,1,0:T(8,128)S(1)} all-to-all(f32[32,8,256]{2,1,0:T(8,128)S(1)} %copy.56), channel_id=1, replica_groups=mesh['dp'=8,'shard'=4] {'dp','shard'}, dimensions={0} | all-to-all | bytes 524288 | tf_op jit(solution)/shard_map/all_to_all | solution.py:153
  41.3 12.7 %all_to_all.11 = f32[32,8,256]{2,1,0:T(8,128)S(1)} all-to-all(f32[32,8,256]{2,1,0:T(8,128)S(1)} %convolution_bitcast_fusion), channel_id=1, replica_groups=mesh['dp'=8,'shard'=4] {'dp','shard'}, dimensions={0} | all-to-all | bytes 524288 | tf_op jit(solution)/shard_map/all_to_all | solution.py:170
  54.5 0.8 %collective-permute-start.13 = (f32[8,8,256]{2,1,0:T(8,128)S(1)}, f32[8,8,256]{2,1,0:T(8,128)S(1)}, u32[]{:S(2)}, u32[]{:S(2)}) collective-permute-start(f32[8,8,256]{2,1,0:T(8,128)S(1)} %copy.58), channel_id=1, source_target_pairs={{0,2},{1,3},{2,0},{3,1},{4,6},{5,7},{6,4},{7,5},{8,10},{9,11},{10,... | collective-permute-start | bytes 196616 | tf_op jit(solution)/shard_map/shard_2/ppermute | solution.py:18
  55.4 2.8 %collective-permute-start.14 = (f32[8,8,256]{2,1,0:T(8,128)S(1)}, f32[8,8,256]{2,1,0:T(8,128)S(1)}, u32[]{:S(2)}, u32[]{:S(2)}) collective-permute-start(f32[8,8,256]{2,1,0:T(8,128)S(1)} %copy.59), channel_id=1, source_target_pairs={{0,3},{1,2},{2,1},{3,0},{4,7},{5,6},{6,5},{7,4},{8,11},{9,10},{10,... | collective-permute-start | bytes 196616 | tf_op jit(solution)/shard_map/shard_3/ppermute | solution.py:18
  58.3 4.2 %collective-permute-done.13 = f32[8,8,256]{2,1,0:T(8,128)S(1)} collective-permute-done((f32[8,8,256]{2,1,0:T(8,128)S(1)}, f32[8,8,256]{2,1,0:T(8,128)S(1)}, u32[]{:S(2)}, u32[]{:S(2)}) %collective-permute-start.13) | collective-permute-done | bytes 65568 | tf_op jit(solution)/shard_map/shard_2/ppermute | solution.py:18
  63.0 1.1 %collective-permute-start.18 = (f32[4,32,256]{2,1,0:T(8,128)S(1)}, f32[4,32,256]{2,1,0:T(8,128)S(1)}, u32[]{:S(2)}, u32[]{:S(2)}) collective-permute-start(f32[4,32,256]{2,1,0:T(8,128)S(1)} %get-tuple-element.61), channel_id=1, source_target_pairs={{0,8},{4,20},{8,0},{12,28},{16,24},{20,4},{24,16},{28,12},{1,9},{5... | collective-permute-start | bytes 393224 | tf_op jit(solution)/shard_map/rows_first_top/ppermute | solution.py:18
  64.0 1.4 %collective-permute-start.20 = (f32[4,32,256]{2,1,0:T(8,128)S(1)}, f32[4,32,256]{2,1,0:T(8,128)S(1)}, u32[]{:S(2)}, u32[]{:S(2)}) collective-permute-start(f32[4,32,256]{2,1,0:T(8,128)S(1)} %get-tuple-element.60), channel_id=1, source_target_pairs={{0,16},{4,12},{8,24},{12,4},{16,0},{20,28},{24,8},{28,20},{1,17},{... | collective-permute-start | bytes 393224 | tf_op jit(solution)/shard_map/rows_second_low/ppermute | solution.py:18
  65.5 1.1 %collective-permute-start.17 = (f32[4,32,256]{2,1,0:T(8,128)S(1)}, f32[4,32,256]{2,1,0:T(8,128)S(1)}, u32[]{:S(2)}, u32[]{:S(2)}) collective-permute-start(f32[4,32,256]{2,1,0:T(8,128)S(1)} %get-tuple-element.60), channel_id=1, source_target_pairs={{0,8},{4,20},{8,0},{12,28},{16,24},{20,4},{24,16},{28,12},{1,9},{5... | collective-permute-start | bytes 393224 | tf_op jit(solution)/shard_map/rows_first_low/ppermute | solution.py:18
  66.6 0.5 collective-permute-start.19
  67.3 2.0 %collective-permute-done.18 = f32[4,32,256]{2,1,0:T(8,128)S(1)} collective-permute-done((f32[4,32,256]{2,1,0:T(8,128)S(1)}, f32[4,32,256]{2,1,0:T(8,128)S(1)}, u32[]{:S(2)}, u32[]{:S(2)}) %collective-permute-start.18) | collective-permute-done | bytes 131104 | tf_op jit(solution)/shard_map/rows_first_top/ppermute | solution.py:18
  70.2 0.9 %collective-permute-start.24 = (f32[4,32,256]{2,1,0:T(8,128)S(1)}, f32[4,32,256]{2,1,0:T(8,128)S(1)}, u32[]{:S(2)}, u32[]{:S(2)}) collective-permute-start(f32[4,32,256]{2,1,0:T(8,128)S(1)} %collective-permute-done.20), channel_id=1, source_target_pairs={{0,8},{4,20},{8,0},{12,28},{16,24},{20,4},{24,16},{28,12},{1,9},{5... | collective-permute-start | bytes 393224 | tf_op jit(solution)/shard_map/rows_relay_low/ppermute | solution.py:18
  71.1 0.6 collective-permute-done.17
  71.8 3.0 %collective-permute-done.21 = f32[4,32,256]{2,1,0:T(8,128)S(1)} collective-permute-done((f32[4,32,256]{2,1,0:T(8,128)S(1)}, f32[4,32,256]{2,1,0:T(8,128)S(1)}, u32[]{:S(2)}, u32[]{:S(2)}) %collective-permute-start.21) | collective-permute-done | bytes 131104 | tf_op jit(solution)/shard_map/rows_relay_top/ppermute | solution.py:18
  74.8 0.5 collective-permute-start.23
  75.5 0.8 %collective-permute-done.22 = f32[8,32,256]{2,1,0:T(8,128)S(1)} collective-permute-done((f32[8,32,256]{2,1,0:T(8,128)S(1)}, f32[8,32,256]{2,1,0:T(8,128)S(1)}, u32[]{:S(2)}, u32[]{:S(2)}) %collective-permute-start.22) | collective-permute-done | bytes 262176 | tf_op jit(solution)/shard_map/rows_core_first/ppermute | solution.py:18
  77.1 1.3 %copy-done.3 = f32[8,256,256]{2,1,0:T(8,128)} copy-done((f32[8,256,256]{2,1,0:T(8,128)}, f32[8,256,256]{2,1,0:T(8,128)S(1)}, u32[]{:S(2)}) %copy-start.3) | copy-done | bytes 2097176
  (100 shorter events, 6.6 us)
Async XLA Ops:
  0.6 39.6 %copy-start = (f32[1,1,1,256,256]{4,3,2,1,0:T(8,128)S(1)}, f32[1,1,1,256,256]{4,3,2,1,0:T(8,128)}, u32[]{:S(2)}) copy-start(f32[1,1,1,256,256]{4,3,2,1,0:T(8,128)} %param.10) | copy-start | bytes 786436
  2.2 1.7 %collective-permute-start = (f32[8,32,256]{2,1,0:T(8,128)S(1)}, f32[8,32,256]{2,1,0:T(8,128)S(1)}, u32[]{:S(2)}, u32[]{:S(2)}) collective-permute-start(f32[8,32,256]{2,1,0:T(8,128)S(1)} %get-tuple-element.59), channel_id=1, source_target_pairs={{0,4},{4,0},{8,12},{12,8},{16,20},{20,16},{24,28},{28,24},{1,5},{5... | collective-permute-start | bytes 786440 | tf_op jit(solution)/shard_map/sum_core_across/ppermute | solution.py:18
  2.7 4.2 %collective-permute-start.2 = (f32[8,32,256]{2,1,0:T(8,128)S(1)}, f32[8,32,256]{2,1,0:T(8,128)S(1)}, u32[]{:S(2)}, u32[]{:S(2)}) collective-permute-start(f32[8,32,256]{2,1,0:T(8,128)S(1)} %get-tuple-element.56), channel_id=1, source_target_pairs={{0,4},{4,0},{8,12},{12,8},{16,20},{20,16},{24,28},{28,24},{1,5},{5... | collective-permute-start | bytes 786440 | tf_op jit(solution)/shard_map/sum_core_second/ppermute | solution.py:18
  2.8 4.1 %collective-permute-start.5 = (f32[8,32,256]{2,1,0:T(8,128)S(1)}, f32[8,32,256]{2,1,0:T(8,128)S(1)}, u32[]{:S(2)}, u32[]{:S(2)}) collective-permute-start(f32[8,32,256]{2,1,0:T(8,128)S(1)} %get-tuple-element.57), channel_id=1, source_target_pairs={{0,4},{4,0},{8,12},{12,8},{16,20},{20,16},{24,28},{28,24},{1,5},{5... | collective-permute-start | bytes 786440 | tf_op jit(solution)/shard_map/sum_core_first/ppermute | solution.py:18
  3.2 3.6 %collective-permute-start.1 = (f32[8,32,256]{2,1,0:T(8,128)S(1)}, f32[8,32,256]{2,1,0:T(8,128)S(1)}, u32[]{:S(2)}, u32[]{:S(2)}) collective-permute-start(f32[8,32,256]{2,1,0:T(8,128)S(1)} %get-tuple-element.58), channel_id=1, source_target_pairs={{0,4},{4,0},{8,12},{12,8},{16,20},{20,16},{24,28},{28,24},{1,5},{5... | collective-permute-start | bytes 786440 | tf_op jit(solution)/shard_map/sum_core_own/ppermute | solution.py:18
  4.0 5.9 %collective-permute-start.9 = (f32[8,16,256]{2,1,0:T(8,128)S(1)}, f32[8,16,256]{2,1,0:T(8,128)S(1)}, u32[]{:S(2)}, u32[]{:S(2)}) collective-permute-start(f32[8,16,256]{2,1,0:T(8,128)S(1)} %get-tuple-element.41), channel_id=1, source_target_pairs={{0,8},{4,20},{8,0},{12,28},{16,24},{20,4},{24,16},{28,12},{1,9},{5... | collective-permute-start | bytes 393224 | tf_op jit(solution)/shard_map/sum_across_far/ppermute | solution.py:18
  7.1 6.5 %collective-permute-start.8 = (f32[8,16,256]{2,1,0:T(8,128)S(1)}, f32[8,16,256]{2,1,0:T(8,128)S(1)}, u32[]{:S(2)}, u32[]{:S(2)}) collective-permute-start(f32[8,16,256]{2,1,0:T(8,128)S(1)} %get-tuple-element.39), channel_id=1, source_target_pairs={{0,8},{4,20},{8,0},{12,28},{16,24},{20,4},{24,16},{28,12},{1,9},{5... | collective-permute-start | bytes 393224 | tf_op jit(solution)/shard_map/sum_first_far/ppermute | solution.py:18
  8.1 6.8 %collective-permute-start.3 = (f32[8,16,256]{2,1,0:T(8,128)S(1)}, f32[8,16,256]{2,1,0:T(8,128)S(1)}, u32[]{:S(2)}, u32[]{:S(2)}) collective-permute-start(f32[8,16,256]{2,1,0:T(8,128)S(1)} %get-tuple-element.34), channel_id=1, source_target_pairs={{0,8},{4,20},{8,0},{12,28},{16,24},{20,4},{24,16},{28,12},{1,9},{5... | collective-permute-start | bytes 393224 | tf_op jit(solution)/shard_map/sum_across_near/ppermute | solution.py:18
  9.8 6.4 %collective-permute-start.10 = (f32[8,16,256]{2,1,0:T(8,128)S(1)}, f32[8,16,256]{2,1,0:T(8,128)S(1)}, u32[]{:S(2)}, u32[]{:S(2)}) collective-permute-start(f32[8,16,256]{2,1,0:T(8,128)S(1)} %add.167), channel_id=1, source_target_pairs={{0,16},{4,12},{8,24},{12,4},{16,0},{20,28},{24,8},{28,20},{1,17},{... | collective-permute-start | bytes 393224 | tf_op jit(solution)/shard_map/sum_relay_far/ppermute | solution.py:18
  12.0 8.5 %collective-permute-start.6 = (f32[8,16,256]{2,1,0:T(8,128)S(1)}, f32[8,16,256]{2,1,0:T(8,128)S(1)}, u32[]{:S(2)}, u32[]{:S(2)}) collective-permute-start(f32[8,16,256]{2,1,0:T(8,128)S(1)} %get-tuple-element.35), channel_id=1, source_target_pairs={{0,8},{4,20},{8,0},{12,28},{16,24},{20,4},{24,16},{28,12},{1,9},{5... | collective-permute-start | bytes 393224 | tf_op jit(solution)/shard_map/sum_first_near/ppermute | solution.py:18
  14.9 24.9 %copy-start.4 = (f32[1,1,1,256,256]{4,3,2,1,0:T(8,128)S(1)}, f32[1,1,1,256,256]{4,3,2,1,0:T(8,128)}, u32[]{:S(2)}) copy-start(f32[1,1,1,256,256]{4,3,2,1,0:T(8,128)} %param.9) | copy-start | bytes 786436
  14.9 5.6 %collective-permute-start.4 = (f32[8,16,256]{2,1,0:T(8,128)S(1)}, f32[8,16,256]{2,1,0:T(8,128)S(1)}, u32[]{:S(2)}, u32[]{:S(2)}) collective-permute-start(f32[8,16,256]{2,1,0:T(8,128)S(1)} %add.160), channel_id=1, source_target_pairs={{0,16},{4,12},{8,24},{12,4},{16,0},{20,28},{24,8},{28,20},{1,17},{... | collective-permute-start | bytes 393224 | tf_op jit(solution)/shard_map/sum_relay_near/ppermute | solution.py:18
  16.3 7.1 %collective-permute-start.12 = (f32[8,8,256]{2,1,0:T(8,128)S(1)}, f32[8,8,256]{2,1,0:T(8,128)S(1)}, u32[]{:S(2)}, u32[]{:S(2)}) collective-permute-start(f32[8,8,256]{2,1,0:T(8,128)S(1)} %get-tuple-element.79), channel_id=1, source_target_pairs={{0,2},{1,3},{2,0},{3,1},{4,6},{5,7},{6,4},{7,5},{8,10},{9,11},{10,... | collective-permute-start | bytes 196616 | tf_op jit(solution)/shard_map/shard_2/ppermute | solution.py:18
  19.1 6.2 %collective-permute-start.11 = (f32[8,8,256]{2,1,0:T(8,128)S(1)}, f32[8,8,256]{2,1,0:T(8,128)S(1)}, u32[]{:S(2)}, u32[]{:S(2)}) collective-permute-start(f32[8,8,256]{2,1,0:T(8,128)S(1)} %get-tuple-element.78), channel_id=1, source_target_pairs={{0,3},{1,2},{2,1},{3,0},{4,7},{5,6},{6,5},{7,4},{8,11},{9,10},{10,... | collective-permute-start | bytes 196616 | tf_op jit(solution)/shard_map/shard_3/ppermute | solution.py:18
  20.5 19.7 %copy-start.5 = (f32[1,1,1,256,256]{4,3,2,1,0:T(8,128)S(1)}, f32[1,1,1,256,256]{4,3,2,1,0:T(8,128)}, u32[]{:S(2)}) copy-start(f32[1,1,1,256,256]{4,3,2,1,0:T(8,128)} %param.11) | copy-start | bytes 786436
  20.5 19.7 %copy-start.6 = (f32[1,1,1,256,256]{4,3,2,1,0:T(8,128)S(1)}, f32[1,1,1,256,256]{4,3,2,1,0:T(8,128)}, u32[]{:S(2)}) copy-start(f32[1,1,1,256,256]{4,3,2,1,0:T(8,128)} %param.12) | copy-start | bytes 786436
  20.6 5.0 %collective-permute-start.7 = (f32[8,8,256]{2,1,0:T(8,128)S(1)}, f32[8,8,256]{2,1,0:T(8,128)S(1)}, u32[]{:S(2)}, u32[]{:S(2)}) collective-permute-start(f32[8,8,256]{2,1,0:T(8,128)S(1)} %get-tuple-element.77), channel_id=1, source_target_pairs={{0,1},{1,0},{2,3},{3,2},{4,5},{5,4},{6,7},{7,6},{8,9},{9,8},{10,11... | collective-permute-start | bytes 196616 | tf_op jit(solution)/shard_map/shard_1/ppermute | solution.py:18
  41.0 17.2 %copy-start.2 = (f32[8,32,256]{2,1,0:T(8,128)S(1)}, f32[8,32,256]{2,1,0:T(8,128)}, u32[]{:S(2)}) copy-start(f32[8,32,256]{2,1,0:T(8,128)} %param.8) | copy-start | bytes 786436
  41.0 21.4 %copy-start.1 = (f32[8,32,256]{2,1,0:T(8,128)S(1)}, f32[8,32,256]{2,1,0:T(8,128)}, u32[]{:S(2)}) copy-start(f32[8,32,256]{2,1,0:T(8,128)} %param.8) | copy-start | bytes 786436
  54.5 8.0 %collective-permute-start.13 = (f32[8,8,256]{2,1,0:T(8,128)S(1)}, f32[8,8,256]{2,1,0:T(8,128)S(1)}, u32[]{:S(2)}, u32[]{:S(2)}) collective-permute-start(f32[8,8,256]{2,1,0:T(8,128)S(1)} %copy.58), channel_id=1, source_target_pairs={{0,2},{1,3},{2,0},{3,1},{4,6},{5,7},{6,4},{7,5},{8,10},{9,11},{10,... | collective-permute-start | bytes 196616 | tf_op jit(solution)/shard_map/shard_2/ppermute | solution.py:18
  55.4 7.1 %collective-permute-start.14 = (f32[8,8,256]{2,1,0:T(8,128)S(1)}, f32[8,8,256]{2,1,0:T(8,128)S(1)}, u32[]{:S(2)}, u32[]{:S(2)}) collective-permute-start(f32[8,8,256]{2,1,0:T(8,128)S(1)} %copy.59), channel_id=1, source_target_pairs={{0,3},{1,2},{2,1},{3,0},{4,7},{5,6},{6,5},{7,4},{8,11},{9,10},{10,... | collective-permute-start | bytes 196616 | tf_op jit(solution)/shard_map/shard_3/ppermute | solution.py:18
  58.2 4.8 %collective-permute-start.15 = (f32[8,8,256]{2,1,0:T(8,128)S(1)}, f32[8,8,256]{2,1,0:T(8,128)S(1)}, u32[]{:S(2)}, u32[]{:S(2)}) collective-permute-start(f32[8,8,256]{2,1,0:T(8,128)S(1)} %copy.60), channel_id=1, source_target_pairs={{0,1},{1,0},{2,3},{3,2},{4,5},{5,4},{6,7},{7,6},{8,9},{9,8},{10,11... | collective-permute-start | bytes 196616 | tf_op jit(solution)/shard_map/shard_1/ppermute | solution.py:18
  63.0 6.4 %collective-permute-start.18 = (f32[4,32,256]{2,1,0:T(8,128)S(1)}, f32[4,32,256]{2,1,0:T(8,128)S(1)}, u32[]{:S(2)}, u32[]{:S(2)}) collective-permute-start(f32[4,32,256]{2,1,0:T(8,128)S(1)} %get-tuple-element.61), channel_id=1, source_target_pairs={{0,8},{4,20},{8,0},{12,28},{16,24},{20,4},{24,16},{28,12},{1,9},{5... | collective-permute-start | bytes 393224 | tf_op jit(solution)/shard_map/rows_first_top/ppermute | solution.py:18
  64.0 6.1 %collective-permute-start.20 = (f32[4,32,256]{2,1,0:T(8,128)S(1)}, f32[4,32,256]{2,1,0:T(8,128)S(1)}, u32[]{:S(2)}, u32[]{:S(2)}) collective-permute-start(f32[4,32,256]{2,1,0:T(8,128)S(1)} %get-tuple-element.60), channel_id=1, source_target_pairs={{0,16},{4,12},{8,24},{12,4},{16,0},{20,28},{24,8},{28,20},{1,17},{... | collective-permute-start | bytes 393224 | tf_op jit(solution)/shard_map/rows_second_low/ppermute | solution.py:18
  65.5 6.2 %collective-permute-start.17 = (f32[4,32,256]{2,1,0:T(8,128)S(1)}, f32[4,32,256]{2,1,0:T(8,128)S(1)}, u32[]{:S(2)}, u32[]{:S(2)}) collective-permute-start(f32[4,32,256]{2,1,0:T(8,128)S(1)} %get-tuple-element.60), channel_id=1, source_target_pairs={{0,8},{4,20},{8,0},{12,28},{16,24},{20,4},{24,16},{28,12},{1,9},{5... | collective-permute-start | bytes 393224 | tf_op jit(solution)/shard_map/rows_first_low/ppermute | solution.py:18
  66.6 5.2 %collective-permute-start.16 = (f32[8,32,256]{2,1,0:T(8,128)S(1)}, f32[8,32,256]{2,1,0:T(8,128)S(1)}, u32[]{:S(2)}, u32[]{:S(2)}) collective-permute-start(f32[8,32,256]{2,1,0:T(8,128)S(1)} %subtract_dynamic-update-slice_fusion), channel_id=1, source_target_pairs={{0,4},{4,0},{8,12},{12,8},{16,20},{20,16},{24,28},{28,24},{1,5},{5... | collective-permute-start | bytes 786440 | tf_op jit(solution)/shard_map/rows_core_own/ppermute | solution.py:18
  66.6 5.1 %collective-permute-start.19 = (f32[4,32,256]{2,1,0:T(8,128)S(1)}, f32[4,32,256]{2,1,0:T(8,128)S(1)}, u32[]{:S(2)}, u32[]{:S(2)}) collective-permute-start(f32[4,32,256]{2,1,0:T(8,128)S(1)} %get-tuple-element.61), channel_id=1, source_target_pairs={{0,16},{4,12},{8,24},{12,4},{16,0},{20,28},{24,8},{28,20},{1,17},{... | collective-permute-start | bytes 393224 | tf_op jit(solution)/shard_map/rows_second_top/ppermute | solution.py:18
  69.3 5.4 %collective-permute-start.21 = (f32[4,32,256]{2,1,0:T(8,128)S(1)}, f32[4,32,256]{2,1,0:T(8,128)S(1)}, u32[]{:S(2)}, u32[]{:S(2)}) collective-permute-start(f32[4,32,256]{2,1,0:T(8,128)S(1)} %collective-permute-done.18), channel_id=1, source_target_pairs={{0,16},{4,12},{8,24},{12,4},{16,0},{20,28},{24,8},{28,20},{1,17},{... | collective-permute-start | bytes 393224 | tf_op jit(solution)/shard_map/rows_relay_top/ppermute | solution.py:18
  70.2 5.1 %collective-permute-start.24 = (f32[4,32,256]{2,1,0:T(8,128)S(1)}, f32[4,32,256]{2,1,0:T(8,128)S(1)}, u32[]{:S(2)}, u32[]{:S(2)}) collective-permute-start(f32[4,32,256]{2,1,0:T(8,128)S(1)} %collective-permute-done.20), channel_id=1, source_target_pairs={{0,8},{4,20},{8,0},{12,28},{16,24},{20,4},{24,16},{28,12},{1,9},{5... | collective-permute-start | bytes 393224 | tf_op jit(solution)/shard_map/rows_relay_low/ppermute | solution.py:18
  74.8 1.5 %collective-permute-start.22 = (f32[8,32,256]{2,1,0:T(8,128)S(1)}, f32[8,32,256]{2,1,0:T(8,128)S(1)}, u32[]{:S(2)}, u32[]{:S(2)}) collective-permute-start(f32[8,32,256]{2,1,0:T(8,128)S(1)} %pad_maximum_fusion.1), channel_id=1, source_target_pairs={{0,4},{4,0},{8,12},{12,8},{16,20},{20,16},{24,28},{28,24},{1,5},{5... | collective-permute-start | bytes 786440 | tf_op jit(solution)/shard_map/rows_core_first/ppermute | solution.py:18
  74.8 1.9 %collective-permute-start.23 = (f32[8,32,256]{2,1,0:T(8,128)S(1)}, f32[8,32,256]{2,1,0:T(8,128)S(1)}, u32[]{:S(2)}, u32[]{:S(2)}) collective-permute-start(f32[8,32,256]{2,1,0:T(8,128)S(1)} %pad_maximum_fusion.2), channel_id=1, source_target_pairs={{0,4},{4,0},{8,12},{12,8},{16,20},{20,16},{24,28},{28,24},{1,5},{5... | collective-permute-start | bytes 786440 | tf_op jit(solution)/shard_map/rows_core_second/ppermute | solution.py:18
  75.3 1.7 %collective-permute-start.25 = (f32[8,32,256]{2,1,0:T(8,128)S(1)}, f32[8,32,256]{2,1,0:T(8,128)S(1)}, u32[]{:S(2)}, u32[]{:S(2)}) collective-permute-start(f32[8,32,256]{2,1,0:T(8,128)S(1)} %constant_dynamic-update-slice_fusion.6), channel_id=1, source_target_pairs={{0,4},{4,0},{8,12},{12,8},{16,20},{20,16},{24,28},{28,24},{1,5},{5... | collective-permute-start | bytes 786440 | tf_op jit(solution)/shard_map/rows_core_far/ppermute | solution.py:18
  (4 other events, 43.5 us)

commit v20 on v17

--- a/solution.py
+++ b/solution.py
@@ -184,7 +184,7 @@
     returned = shard_exchange([back[near_order.index(k)] for k in range(shard_count)])
 
     new_home = params
-    for k in (0, 3, 2, 1):
+    for k in (0, 2, 3, 1):
         start = (shard_here ^ k) * piece[0]
         home = lax.dynamic_slice_in_dim(params, start, piece[0], axis=1)
         home = home - learn_rate * (returned[k] + decay_rate * home)

time: 78.9 us -> 78.7 us (level)
  starting transfers between devices: 26.8 us -> 25.7 us
  waiting for transfers between devices: 17.8 us -> 18.8 us
    ppermute x25, starting transfers between devices: 26.8 us -> 25.7 us  [swap(): return lax.ppermute(values, name, pairs)]
    ppermute x25, waiting for transfers between devices: 17.8 us -> 18.8 us  [swap(): return lax.ppermute(values, name, pairs)]
  transfers between devices with their start and end apart: 25 -> 25, of which waited for: 14 -> 15; matrix products, arithmetic and copies ran while one was open for 2% -> 2% of each run, Pallas kernels for 0% -> 0%
where the time goes in v20:
time: 78.7 us; the launch traced here: 78.5 us
  blocking collectives  26.5 us (34%)
  starting transfers between devices  25.7 us (33%)
  waiting for transfers between devices  18.8 us (24%)
  local copies, waits for them, and re-layouts  3.76 us (5%)
  matrix products  1.93 us (2%)
  between operations  1.28 us (2%)
    ppermute x25, starting transfers between devices, swap(): return lax.ppermute(values, name, pairs)  25.7 us
    ppermute x25, waiting for transfers between devices, swap(): return lax.ppermute(values, name, pairs)  18.8 us
    all_to_all x1, blocking collectives, routed(): lax.all_to_all(leaving.reshape((device_total,) + piece), ('dp', 'shard'),...  13.7 us
    all_to_all x1, blocking collectives, routed(): lax.all_to_all(change.reshape((device_total,) + piece), ('dp', 'shard'),...  12.7 us
    unnamed x27, local copies, waits for them, and re-layouts  1.58 us
  transfers between devices with their start and end apart: 25, of which 15 were waited for; matrix products, arithmetic and copies ran while one was open for 2% of the time, Pallas kernels for 0%

profile of v20, /device:TPU:0, one launch (start us, length us, event | category | flops | bytes accessed | tf_op | source)
XLA Modules:
  0.0 78.5 jit_solution(13962381145794040882)
XLA Ops:
  0.7 1.3 %dynamic-slice_bitcast_fusion = (bf16[8,4,32,256]{3,2,1,0:T(8,128)(2,1)S(1)}, bf16[8,4,32,256]{3,2,1,0:T(8,128)(2,1)S(1)}) fusion(bf16[8,4,2,32,256]{4,3,2,1,0:T(8,128)(2,1)} %bitcast.146, s32[]{:T(128)S(6)} %select_n.130, s32[]{:T(128)S(6)} %select_n.129), kind=kLoop, calls=%fused_computation.2 | loop fusion | bytes 2097160 | tf_op jit(solution)/shard_map/jit(dynamic_index_in_dim)/squeeze | solution.py:22
  2.2 0.5 collective-permute-start
  3.3 0.6 collective-permute-done
  4.0 2.9 %collective-permute-start.9 = (f32[8,16,256]{2,1,0:T(8,128)S(1)}, f32[8,16,256]{2,1,0:T(8,128)S(1)}, u32[]{:S(2)}, u32[]{:S(2)}) collective-permute-start(f32[8,16,256]{2,1,0:T(8,128)S(1)} %get-tuple-element.41), channel_id=1, source_target_pairs={{0,8},{4,20},{8,0},{12,28},{16,24},{20,4},{24,16},{28,12},{1,9},{5... | collective-permute-start | bytes 393224 | tf_op jit(solution)/shard_map/sum_across_far/ppermute | solution.py:18
  7.1 1.0 %collective-permute-start.8 = (f32[8,16,256]{2,1,0:T(8,128)S(1)}, f32[8,16,256]{2,1,0:T(8,128)S(1)}, u32[]{:S(2)}, u32[]{:S(2)}) collective-permute-start(f32[8,16,256]{2,1,0:T(8,128)S(1)} %get-tuple-element.39), channel_id=1, source_target_pairs={{0,8},{4,20},{8,0},{12,28},{16,24},{20,4},{24,16},{28,12},{1,9},{5... | collective-permute-start | bytes 393224 | tf_op jit(solution)/shard_map/sum_first_far/ppermute | solution.py:18
  8.1 1.1 %collective-permute-start.3 = (f32[8,16,256]{2,1,0:T(8,128)S(1)}, f32[8,16,256]{2,1,0:T(8,128)S(1)}, u32[]{:S(2)}, u32[]{:S(2)}) collective-permute-start(f32[8,16,256]{2,1,0:T(8,128)S(1)} %get-tuple-element.34), channel_id=1, source_target_pairs={{0,8},{4,20},{8,0},{12,28},{16,24},{20,4},{24,16},{28,12},{1,9},{5... | collective-permute-start | bytes 393224 | tf_op jit(solution)/shard_map/sum_across_near/ppermute | solution.py:18
  9.2 0.6 collective-permute-done.9
  9.8 2.1 %collective-permute-start.10 = (f32[8,16,256]{2,1,0:T(8,128)S(1)}, f32[8,16,256]{2,1,0:T(8,128)S(1)}, u32[]{:S(2)}, u32[]{:S(2)}) collective-permute-start(f32[8,16,256]{2,1,0:T(8,128)S(1)} %add.167), channel_id=1, source_target_pairs={{0,16},{4,12},{8,24},{12,4},{16,0},{20,28},{24,8},{28,20},{1,17},{... | collective-permute-start | bytes 393224 | tf_op jit(solution)/shard_map/sum_relay_far/ppermute | solution.py:18
  12.0 1.6 %collective-permute-start.6 = (f32[8,16,256]{2,1,0:T(8,128)S(1)}, f32[8,16,256]{2,1,0:T(8,128)S(1)}, u32[]{:S(2)}, u32[]{:S(2)}) collective-permute-start(f32[8,16,256]{2,1,0:T(8,128)S(1)} %get-tuple-element.35), channel_id=1, source_target_pairs={{0,8},{4,20},{8,0},{12,28},{16,24},{20,4},{24,16},{28,12},{1,9},{5... | collective-permute-start | bytes 393224 | tf_op jit(solution)/shard_map/sum_first_near/ppermute | solution.py:18
  13.6 1.3 %collective-permute-done.3 = f32[8,16,256]{2,1,0:T(8,128)S(1)} collective-permute-done((f32[8,16,256]{2,1,0:T(8,128)S(1)}, f32[8,16,256]{2,1,0:T(8,128)S(1)}, u32[]{:S(2)}, u32[]{:S(2)}) %collective-permute-start.3) | collective-permute-done | bytes 131104 | tf_op jit(solution)/shard_map/sum_across_near/ppermute | solution.py:18
  14.9 1.3 %collective-permute-start.4 = (f32[8,16,256]{2,1,0:T(8,128)S(1)}, f32[8,16,256]{2,1,0:T(8,128)S(1)}, u32[]{:S(2)}, u32[]{:S(2)}) collective-permute-start(f32[8,16,256]{2,1,0:T(8,128)S(1)} %add.160), channel_id=1, source_target_pairs={{0,16},{4,12},{8,24},{12,4},{16,0},{20,28},{24,8},{28,20},{1,17},{... | collective-permute-start | bytes 393224 | tf_op jit(solution)/shard_map/sum_relay_near/ppermute | solution.py:18
  16.3 2.8 %collective-permute-start.12 = (f32[8,8,256]{2,1,0:T(8,128)S(1)}, f32[8,8,256]{2,1,0:T(8,128)S(1)}, u32[]{:S(2)}, u32[]{:S(2)}) collective-permute-start(f32[8,8,256]{2,1,0:T(8,128)S(1)} %get-tuple-element.79), channel_id=1, source_target_pairs={{0,2},{1,3},{2,0},{3,1},{4,6},{5,7},{6,4},{7,5},{8,10},{9,11},{10,... | collective-permute-start | bytes 196616 | tf_op jit(solution)/shard_map/shard_2/ppermute | solution.py:18
  19.1 1.3 %collective-permute-start.11 = (f32[8,8,256]{2,1,0:T(8,128)S(1)}, f32[8,8,256]{2,1,0:T(8,128)S(1)}, u32[]{:S(2)}, u32[]{:S(2)}) collective-permute-start(f32[8,8,256]{2,1,0:T(8,128)S(1)} %get-tuple-element.78), channel_id=1, source_target_pairs={{0,3},{1,2},{2,1},{3,0},{4,7},{5,6},{6,5},{7,4},{8,11},{9,10},{10,... | collective-permute-start | bytes 196616 | tf_op jit(solution)/shard_map/shard_3/ppermute | solution.py:18
  20.6 0.9 %collective-permute-start.7 = (f32[8,8,256]{2,1,0:T(8,128)S(1)}, f32[8,8,256]{2,1,0:T(8,128)S(1)}, u32[]{:S(2)}, u32[]{:S(2)}) collective-permute-start(f32[8,8,256]{2,1,0:T(8,128)S(1)} %get-tuple-element.77), channel_id=1, source_target_pairs={{0,1},{1,0},{2,3},{3,2},{4,5},{5,4},{6,7},{7,6},{8,9},{9,8},{10,11... | collective-permute-start | bytes 196616 | tf_op jit(solution)/shard_map/shard_1/ppermute | solution.py:18
  21.7 1.7 %collective-permute-done.12 = f32[8,8,256]{2,1,0:T(8,128)S(1)} collective-permute-done((f32[8,8,256]{2,1,0:T(8,128)S(1)}, f32[8,8,256]{2,1,0:T(8,128)S(1)}, u32[]{:S(2)}, u32[]{:S(2)}) %collective-permute-start.12) | collective-permute-done | bytes 65568 | tf_op jit(solution)/shard_map/shard_2/ppermute | solution.py:18
  23.5 1.8 %collective-permute-done.11 = f32[8,8,256]{2,1,0:T(8,128)S(1)} collective-permute-done((f32[8,8,256]{2,1,0:T(8,128)S(1)}, f32[8,8,256]{2,1,0:T(8,128)S(1)}, u32[]{:S(2)}, u32[]{:S(2)}) %collective-permute-start.11) | collective-permute-done | bytes 65568 | tf_op jit(solution)/shard_map/shard_3/ppermute | solution.py:18
  26.1 13.7 %all_to_all.10 = f32[32,8,256]{2,1,0:T(8,128)S(1)} all-to-all(f32[32,8,256]{2,1,0:T(8,128)S(1)} %copy.56), channel_id=1, replica_groups=mesh['dp'=8,'shard'=4] {'dp','shard'}, dimensions={0} | all-to-all | bytes 524288 | tf_op jit(solution)/shard_map/all_to_all | solution.py:153
  41.3 12.7 %all_to_all.11 = f32[32,8,256]{2,1,0:T(8,128)S(1)} all-to-all(f32[32,8,256]{2,1,0:T(8,128)S(1)} %convolution_bitcast_fusion), channel_id=1, replica_groups=mesh['dp'=8,'shard'=4] {'dp','shard'}, dimensions={0} | all-to-all | bytes 524288 | tf_op jit(solution)/shard_map/all_to_all | solution.py:170
  54.5 0.8 %collective-permute-start.13 = (f32[8,8,256]{2,1,0:T(8,128)S(1)}, f32[8,8,256]{2,1,0:T(8,128)S(1)}, u32[]{:S(2)}, u32[]{:S(2)}) collective-permute-start(f32[8,8,256]{2,1,0:T(8,128)S(1)} %copy.58), channel_id=1, source_target_pairs={{0,2},{1,3},{2,0},{3,1},{4,6},{5,7},{6,4},{7,5},{8,10},{9,11},{10,... | collective-permute-start | bytes 196616 | tf_op jit(solution)/shard_map/shard_2/ppermute | solution.py:18
  55.4 2.8 %collective-permute-start.14 = (f32[8,8,256]{2,1,0:T(8,128)S(1)}, f32[8,8,256]{2,1,0:T(8,128)S(1)}, u32[]{:S(2)}, u32[]{:S(2)}) collective-permute-start(f32[8,8,256]{2,1,0:T(8,128)S(1)} %copy.59), channel_id=1, source_target_pairs={{0,3},{1,2},{2,1},{3,0},{4,7},{5,6},{6,5},{7,4},{8,11},{9,10},{10,... | collective-permute-start | bytes 196616 | tf_op jit(solution)/shard_map/shard_3/ppermute | solution.py:18
  58.3 4.2 %collective-permute-done.13 = f32[8,8,256]{2,1,0:T(8,128)S(1)} collective-permute-done((f32[8,8,256]{2,1,0:T(8,128)S(1)}, f32[8,8,256]{2,1,0:T(8,128)S(1)}, u32[]{:S(2)}, u32[]{:S(2)}) %collective-permute-start.13) | collective-permute-done | bytes 65568 | tf_op jit(solution)/shard_map/shard_2/ppermute | solution.py:18
  63.0 1.1 %collective-permute-start.18 = (f32[4,32,256]{2,1,0:T(8,128)S(1)}, f32[4,32,256]{2,1,0:T(8,128)S(1)}, u32[]{:S(2)}, u32[]{:S(2)}) collective-permute-start(f32[4,32,256]{2,1,0:T(8,128)S(1)} %get-tuple-element.61), channel_id=1, source_target_pairs={{0,8},{4,20},{8,0},{12,28},{16,24},{20,4},{24,16},{28,12},{1,9},{5... | collective-permute-start | bytes 393224 | tf_op jit(solution)/shard_map/rows_first_top/ppermute | solution.py:18
  64.0 1.4 %collective-permute-start.20 = (f32[4,32,256]{2,1,0:T(8,128)S(1)}, f32[4,32,256]{2,1,0:T(8,128)S(1)}, u32[]{:S(2)}, u32[]{:S(2)}) collective-permute-start(f32[4,32,256]{2,1,0:T(8,128)S(1)} %get-tuple-element.60), channel_id=1, source_target_pairs={{0,16},{4,12},{8,24},{12,4},{16,0},{20,28},{24,8},{28,20},{1,17},{... | collective-permute-start | bytes 393224 | tf_op jit(solution)/shard_map/rows_second_low/ppermute | solution.py:18
  65.5 1.1 %collective-permute-start.17 = (f32[4,32,256]{2,1,0:T(8,128)S(1)}, f32[4,32,256]{2,1,0:T(8,128)S(1)}, u32[]{:S(2)}, u32[]{:S(2)}) collective-permute-start(f32[4,32,256]{2,1,0:T(8,128)S(1)} %get-tuple-element.60), channel_id=1, source_target_pairs={{0,8},{4,20},{8,0},{12,28},{16,24},{20,4},{24,16},{28,12},{1,9},{5... | collective-permute-start | bytes 393224 | tf_op jit(solution)/shard_map/rows_first_low/ppermute | solution.py:18
  66.6 0.5 collective-permute-start.19
  67.3 2.0 %collective-permute-done.18 = f32[4,32,256]{2,1,0:T(8,128)S(1)} collective-permute-done((f32[4,32,256]{2,1,0:T(8,128)S(1)}, f32[4,32,256]{2,1,0:T(8,128)S(1)}, u32[]{:S(2)}, u32[]{:S(2)}) %collective-permute-start.18) | collective-permute-done | bytes 131104 | tf_op jit(solution)/shard_map/rows_first_top/ppermute | solution.py:18
  69.7 0.5 collective-permute-done.20
  70.2 0.9 %collective-permute-start.23 = (f32[4,32,256]{2,1,0:T(8,128)S(1)}, f32[4,32,256]{2,1,0:T(8,128)S(1)}, u32[]{:S(2)}, u32[]{:S(2)}) collective-permute-start(f32[4,32,256]{2,1,0:T(8,128)S(1)} %collective-permute-done.20), channel_id=1, source_target_pairs={{0,8},{4,20},{8,0},{12,28},{16,24},{20,4},{24,16},{28,12},{1,9},{5... | collective-permute-start | bytes 393224 | tf_op jit(solution)/shard_map/rows_relay_low/ppermute | solution.py:18
  71.1 0.6 collective-permute-done.17
  71.8 3.0 %collective-permute-done.21 = f32[4,32,256]{2,1,0:T(8,128)S(1)} collective-permute-done((f32[4,32,256]{2,1,0:T(8,128)S(1)}, f32[4,32,256]{2,1,0:T(8,128)S(1)}, u32[]{:S(2)}, u32[]{:S(2)}) %collective-permute-start.21) | collective-permute-done | bytes 131104 | tf_op jit(solution)/shard_map/rows_relay_top/ppermute | solution.py:18
  75.6 1.2 %collective-permute-done.22 = f32[2,8,32,256]{3,2,1,0:T(8,128)S(1)} collective-permute-done((f32[2,8,32,256]{3,2,1,0:T(8,128)S(1)}, f32[2,8,32,256]{3,2,1,0:T(8,128)S(1)}, u32[]{:S(2)}, u32[]{:S(2)}) %collective-permute-start.22) | collective-permute-done | bytes 524320 | tf_op jit(solution)/shard_map/rows_core_direct/ppermute | solution.py:18
  77.2 1.3 %copy-done.3 = f32[8,256,256]{2,1,0:T(8,128)} copy-done((f32[8,256,256]{2,1,0:T(8,128)}, f32[8,256,256]{2,1,0:T(8,128)S(1)}, u32[]{:S(2)}) %copy-start.3) | copy-done | bytes 2097176
  (99 shorter events, 6.4 us)
Async XLA Ops:
  0.6 39.6 %copy-start = (f32[1,1,1,256,256]{4,3,2,1,0:T(8,128)S(1)}, f32[1,1,1,256,256]{4,3,2,1,0:T(8,128)}, u32[]{:S(2)}) copy-start(f32[1,1,1,256,256]{4,3,2,1,0:T(8,128)} %param.10) | copy-start | bytes 786436
  2.2 1.7 %collective-permute-start = (f32[8,32,256]{2,1,0:T(8,128)S(1)}, f32[8,32,256]{2,1,0:T(8,128)S(1)}, u32[]{:S(2)}, u32[]{:S(2)}) collective-permute-start(f32[8,32,256]{2,1,0:T(8,128)S(1)} %get-tuple-element.59), channel_id=1, source_target_pairs={{0,4},{4,0},{8,12},{12,8},{16,20},{20,16},{24,28},{28,24},{1,5},{5... | collective-permute-start | bytes 786440 | tf_op jit(solution)/shard_map/sum_core_across/ppermute | solution.py:18
  2.7 4.2 %collective-permute-start.2 = (f32[8,32,256]{2,1,0:T(8,128)S(1)}, f32[8,32,256]{2,1,0:T(8,128)S(1)}, u32[]{:S(2)}, u32[]{:S(2)}) collective-permute-start(f32[8,32,256]{2,1,0:T(8,128)S(1)} %get-tuple-element.56), channel_id=1, source_target_pairs={{0,4},{4,0},{8,12},{12,8},{16,20},{20,16},{24,28},{28,24},{1,5},{5... | collective-permute-start | bytes 786440 | tf_op jit(solution)/shard_map/sum_core_second/ppermute | solution.py:18
  2.8 4.1 %collective-permute-start.5 = (f32[8,32,256]{2,1,0:T(8,128)S(1)}, f32[8,32,256]{2,1,0:T(8,128)S(1)}, u32[]{:S(2)}, u32[]{:S(2)}) collective-permute-start(f32[8,32,256]{2,1,0:T(8,128)S(1)} %get-tuple-element.57), channel_id=1, source_target_pairs={{0,4},{4,0},{8,12},{12,8},{16,20},{20,16},{24,28},{28,24},{1,5},{5... | collective-permute-start | bytes 786440 | tf_op jit(solution)/shard_map/sum_core_first/ppermute | solution.py:18
  3.2 3.6 %collective-permute-start.1 = (f32[8,32,256]{2,1,0:T(8,128)S(1)}, f32[8,32,256]{2,1,0:T(8,128)S(1)}, u32[]{:S(2)}, u32[]{:S(2)}) collective-permute-start(f32[8,32,256]{2,1,0:T(8,128)S(1)} %get-tuple-element.58), channel_id=1, source_target_pairs={{0,4},{4,0},{8,12},{12,8},{16,20},{20,16},{24,28},{28,24},{1,5},{5... | collective-permute-start | bytes 786440 | tf_op jit(solution)/shard_map/sum_core_own/ppermute | solution.py:18
  4.0 5.9 %collective-permute-start.9 = (f32[8,16,256]{2,1,0:T(8,128)S(1)}, f32[8,16,256]{2,1,0:T(8,128)S(1)}, u32[]{:S(2)}, u32[]{:S(2)}) collective-permute-start(f32[8,16,256]{2,1,0:T(8,128)S(1)} %get-tuple-element.41), channel_id=1, source_target_pairs={{0,8},{4,20},{8,0},{12,28},{16,24},{20,4},{24,16},{28,12},{1,9},{5... | collective-permute-start | bytes 393224 | tf_op jit(solution)/shard_map/sum_across_far/ppermute | solution.py:18
  7.0 14.5 %copy-start.9 = (s32[32]{0:T(128)S(1)}, s32[32]{0:T(128)}, u32[]{:S(2)}) copy-start(s32[32]{0:T(128)} %param.13) | copy-start | bytes 388
  7.1 6.5 %collective-permute-start.8 = (f32[8,16,256]{2,1,0:T(8,128)S(1)}, f32[8,16,256]{2,1,0:T(8,128)S(1)}, u32[]{:S(2)}, u32[]{:S(2)}) collective-permute-start(f32[8,16,256]{2,1,0:T(8,128)S(1)} %get-tuple-element.39), channel_id=1, source_target_pairs={{0,8},{4,20},{8,0},{12,28},{16,24},{20,4},{24,16},{28,12},{1,9},{5... | collective-permute-start | bytes 393224 | tf_op jit(solution)/shard_map/sum_first_far/ppermute | solution.py:18
  8.1 6.8 %collective-permute-start.3 = (f32[8,16,256]{2,1,0:T(8,128)S(1)}, f32[8,16,256]{2,1,0:T(8,128)S(1)}, u32[]{:S(2)}, u32[]{:S(2)}) collective-permute-start(f32[8,16,256]{2,1,0:T(8,128)S(1)} %get-tuple-element.34), channel_id=1, source_target_pairs={{0,8},{4,20},{8,0},{12,28},{16,24},{20,4},{24,16},{28,12},{1,9},{5... | collective-permute-start | bytes 393224 | tf_op jit(solution)/shard_map/sum_across_near/ppermute | solution.py:18
  9.8 6.4 %collective-permute-start.10 = (f32[8,16,256]{2,1,0:T(8,128)S(1)}, f32[8,16,256]{2,1,0:T(8,128)S(1)}, u32[]{:S(2)}, u32[]{:S(2)}) collective-permute-start(f32[8,16,256]{2,1,0:T(8,128)S(1)} %add.167), channel_id=1, source_target_pairs={{0,16},{4,12},{8,24},{12,4},{16,0},{20,28},{24,8},{28,20},{1,17},{... | collective-permute-start | bytes 393224 | tf_op jit(solution)/shard_map/sum_relay_far/ppermute | solution.py:18
  12.0 8.5 %collective-permute-start.6 = (f32[8,16,256]{2,1,0:T(8,128)S(1)}, f32[8,16,256]{2,1,0:T(8,128)S(1)}, u32[]{:S(2)}, u32[]{:S(2)}) collective-permute-start(f32[8,16,256]{2,1,0:T(8,128)S(1)} %get-tuple-element.35), channel_id=1, source_target_pairs={{0,8},{4,20},{8,0},{12,28},{16,24},{20,4},{24,16},{28,12},{1,9},{5... | collective-permute-start | bytes 393224 | tf_op jit(solution)/shard_map/sum_first_near/ppermute | solution.py:18
  14.9 24.9 %copy-start.4 = (f32[1,1,1,256,256]{4,3,2,1,0:T(8,128)S(1)}, f32[1,1,1,256,256]{4,3,2,1,0:T(8,128)}, u32[]{:S(2)}) copy-start(f32[1,1,1,256,256]{4,3,2,1,0:T(8,128)} %param.9) | copy-start | bytes 786436
  14.9 5.6 %collective-permute-start.4 = (f32[8,16,256]{2,1,0:T(8,128)S(1)}, f32[8,16,256]{2,1,0:T(8,128)S(1)}, u32[]{:S(2)}, u32[]{:S(2)}) collective-permute-start(f32[8,16,256]{2,1,0:T(8,128)S(1)} %add.160), channel_id=1, source_target_pairs={{0,16},{4,12},{8,24},{12,4},{16,0},{20,28},{24,8},{28,20},{1,17},{... | collective-permute-start | bytes 393224 | tf_op jit(solution)/shard_map/sum_relay_near/ppermute | solution.py:18
  16.3 7.1 %collective-permute-start.12 = (f32[8,8,256]{2,1,0:T(8,128)S(1)}, f32[8,8,256]{2,1,0:T(8,128)S(1)}, u32[]{:S(2)}, u32[]{:S(2)}) collective-permute-start(f32[8,8,256]{2,1,0:T(8,128)S(1)} %get-tuple-element.79), channel_id=1, source_target_pairs={{0,2},{1,3},{2,0},{3,1},{4,6},{5,7},{6,4},{7,5},{8,10},{9,11},{10,... | collective-permute-start | bytes 196616 | tf_op jit(solution)/shard_map/shard_2/ppermute | solution.py:18
  19.1 6.2 %collective-permute-start.11 = (f32[8,8,256]{2,1,0:T(8,128)S(1)}, f32[8,8,256]{2,1,0:T(8,128)S(1)}, u32[]{:S(2)}, u32[]{:S(2)}) collective-permute-start(f32[8,8,256]{2,1,0:T(8,128)S(1)} %get-tuple-element.78), channel_id=1, source_target_pairs={{0,3},{1,2},{2,1},{3,0},{4,7},{5,6},{6,5},{7,4},{8,11},{9,10},{10,... | collective-permute-start | bytes 196616 | tf_op jit(solution)/shard_map/shard_3/ppermute | solution.py:18
  20.5 19.7 %copy-start.5 = (f32[1,1,1,256,256]{4,3,2,1,0:T(8,128)S(1)}, f32[1,1,1,256,256]{4,3,2,1,0:T(8,128)}, u32[]{:S(2)}) copy-start(f32[1,1,1,256,256]{4,3,2,1,0:T(8,128)} %param.11) | copy-start | bytes 786436
  20.5 19.7 %copy-start.6 = (f32[1,1,1,256,256]{4,3,2,1,0:T(8,128)S(1)}, f32[1,1,1,256,256]{4,3,2,1,0:T(8,128)}, u32[]{:S(2)}) copy-start(f32[1,1,1,256,256]{4,3,2,1,0:T(8,128)} %param.12) | copy-start | bytes 786436
  20.6 5.0 %collective-permute-start.7 = (f32[8,8,256]{2,1,0:T(8,128)S(1)}, f32[8,8,256]{2,1,0:T(8,128)S(1)}, u32[]{:S(2)}, u32[]{:S(2)}) collective-permute-start(f32[8,8,256]{2,1,0:T(8,128)S(1)} %get-tuple-element.77), channel_id=1, source_target_pairs={{0,1},{1,0},{2,3},{3,2},{4,5},{5,4},{6,7},{7,6},{8,9},{9,8},{10,11... | collective-permute-start | bytes 196616 | tf_op jit(solution)/shard_map/shard_1/ppermute | solution.py:18
  41.0 17.2 %copy-start.2 = (f32[8,32,256]{2,1,0:T(8,128)S(1)}, f32[8,32,256]{2,1,0:T(8,128)}, u32[]{:S(2)}) copy-start(f32[8,32,256]{2,1,0:T(8,128)} %param.8) | copy-start | bytes 786436
  41.0 21.4 %copy-start.1 = (f32[8,32,256]{2,1,0:T(8,128)S(1)}, f32[8,32,256]{2,1,0:T(8,128)}, u32[]{:S(2)}) copy-start(f32[8,32,256]{2,1,0:T(8,128)} %param.8) | copy-start | bytes 786436
  54.5 8.0 %collective-permute-start.13 = (f32[8,8,256]{2,1,0:T(8,128)S(1)}, f32[8,8,256]{2,1,0:T(8,128)S(1)}, u32[]{:S(2)}, u32[]{:S(2)}) collective-permute-start(f32[8,8,256]{2,1,0:T(8,128)S(1)} %copy.58), channel_id=1, source_target_pairs={{0,2},{1,3},{2,0},{3,1},{4,6},{5,7},{6,4},{7,5},{8,10},{9,11},{10,... | collective-permute-start | bytes 196616 | tf_op jit(solution)/shard_map/shard_2/ppermute | solution.py:18
  55.4 7.1 %collective-permute-start.14 = (f32[8,8,256]{2,1,0:T(8,128)S(1)}, f32[8,8,256]{2,1,0:T(8,128)S(1)}, u32[]{:S(2)}, u32[]{:S(2)}) collective-permute-start(f32[8,8,256]{2,1,0:T(8,128)S(1)} %copy.59), channel_id=1, source_target_pairs={{0,3},{1,2},{2,1},{3,0},{4,7},{5,6},{6,5},{7,4},{8,11},{9,10},{10,... | collective-permute-start | bytes 196616 | tf_op jit(solution)/shard_map/shard_3/ppermute | solution.py:18
  58.2 4.8 %collective-permute-start.15 = (f32[8,8,256]{2,1,0:T(8,128)S(1)}, f32[8,8,256]{2,1,0:T(8,128)S(1)}, u32[]{:S(2)}, u32[]{:S(2)}) collective-permute-start(f32[8,8,256]{2,1,0:T(8,128)S(1)} %copy.60), channel_id=1, source_target_pairs={{0,1},{1,0},{2,3},{3,2},{4,5},{5,4},{6,7},{7,6},{8,9},{9,8},{10,11... | collective-permute-start | bytes 196616 | tf_op jit(solution)/shard_map/shard_1/ppermute | solution.py:18
  63.0 6.4 %collective-permute-start.18 = (f32[4,32,256]{2,1,0:T(8,128)S(1)}, f32[4,32,256]{2,1,0:T(8,128)S(1)}, u32[]{:S(2)}, u32[]{:S(2)}) collective-permute-start(f32[4,32,256]{2,1,0:T(8,128)S(1)} %get-tuple-element.61), channel_id=1, source_target_pairs={{0,8},{4,20},{8,0},{12,28},{16,24},{20,4},{24,16},{28,12},{1,9},{5... | collective-permute-start | bytes 393224 | tf_op jit(solution)/shard_map/rows_first_top/ppermute | solution.py:18
  64.0 6.1 %collective-permute-start.20 = (f32[4,32,256]{2,1,0:T(8,128)S(1)}, f32[4,32,256]{2,1,0:T(8,128)S(1)}, u32[]{:S(2)}, u32[]{:S(2)}) collective-permute-start(f32[4,32,256]{2,1,0:T(8,128)S(1)} %get-tuple-element.60), channel_id=1, source_target_pairs={{0,16},{4,12},{8,24},{12,4},{16,0},{20,28},{24,8},{28,20},{1,17},{... | collective-permute-start | bytes 393224 | tf_op jit(solution)/shard_map/rows_second_low/ppermute | solution.py:18
  65.5 6.2 %collective-permute-start.17 = (f32[4,32,256]{2,1,0:T(8,128)S(1)}, f32[4,32,256]{2,1,0:T(8,128)S(1)}, u32[]{:S(2)}, u32[]{:S(2)}) collective-permute-start(f32[4,32,256]{2,1,0:T(8,128)S(1)} %get-tuple-element.60), channel_id=1, source_target_pairs={{0,8},{4,20},{8,0},{12,28},{16,24},{20,4},{24,16},{28,12},{1,9},{5... | collective-permute-start | bytes 393224 | tf_op jit(solution)/shard_map/rows_first_low/ppermute | solution.py:18
  66.6 5.2 %collective-permute-start.16 = (f32[8,32,256]{2,1,0:T(8,128)S(1)}, f32[8,32,256]{2,1,0:T(8,128)S(1)}, u32[]{:S(2)}, u32[]{:S(2)}) collective-permute-start(f32[8,32,256]{2,1,0:T(8,128)S(1)} %subtract_dynamic-update-slice_fusion), channel_id=1, source_target_pairs={{0,4},{4,0},{8,12},{12,8},{16,20},{20,16},{24,28},{28,24},{1,5},{5... | collective-permute-start | bytes 786440 | tf_op jit(solution)/shard_map/rows_core_own/ppermute | solution.py:18
  66.6 5.1 %collective-permute-start.19 = (f32[4,32,256]{2,1,0:T(8,128)S(1)}, f32[4,32,256]{2,1,0:T(8,128)S(1)}, u32[]{:S(2)}, u32[]{:S(2)}) collective-permute-start(f32[4,32,256]{2,1,0:T(8,128)S(1)} %get-tuple-element.61), channel_id=1, source_target_pairs={{0,16},{4,12},{8,24},{12,4},{16,0},{20,28},{24,8},{28,20},{1,17},{... | collective-permute-start | bytes 393224 | tf_op jit(solution)/shard_map/rows_second_top/ppermute | solution.py:18
  69.3 5.4 %collective-permute-start.21 = (f32[4,32,256]{2,1,0:T(8,128)S(1)}, f32[4,32,256]{2,1,0:T(8,128)S(1)}, u32[]{:S(2)}, u32[]{:S(2)}) collective-permute-start(f32[4,32,256]{2,1,0:T(8,128)S(1)} %collective-permute-done.18), channel_id=1, source_target_pairs={{0,16},{4,12},{8,24},{12,4},{16,0},{20,28},{24,8},{28,20},{1,17},{... | collective-permute-start | bytes 393224 | tf_op jit(solution)/shard_map/rows_relay_top/ppermute | solution.py:18
  70.2 5.0 %collective-permute-start.23 = (f32[4,32,256]{2,1,0:T(8,128)S(1)}, f32[4,32,256]{2,1,0:T(8,128)S(1)}, u32[]{:S(2)}, u32[]{:S(2)}) collective-permute-start(f32[4,32,256]{2,1,0:T(8,128)S(1)} %collective-permute-done.20), channel_id=1, source_target_pairs={{0,8},{4,20},{8,0},{12,28},{16,24},{20,4},{24,16},{28,12},{1,9},{5... | collective-permute-start | bytes 393224 | tf_op jit(solution)/shard_map/rows_relay_low/ppermute | solution.py:18
  74.8 2.0 %collective-permute-start.22 = (f32[2,8,32,256]{3,2,1,0:T(8,128)S(1)}, f32[2,8,32,256]{3,2,1,0:T(8,128)S(1)}, u32[]{:S(2)}, u32[]{:S(2)}) collective-permute-start(f32[2,8,32,256]{3,2,1,0:T(8,128)S(1)} %pad_maximum_fusion), channel_id=1, source_target_pairs={{0,4},{4,0},{8,12},{12,8},{16,20},{20,16},{24,28},{28,24},{1,5},{5... | collective-permute-start | bytes 1572872 | tf_op jit(solution)/shard_map/rows_core_direct/ppermute | solution.py:18
  75.2 2.0 %collective-permute-start.24 = (f32[8,32,256]{2,1,0:T(8,128)S(1)}, f32[8,32,256]{2,1,0:T(8,128)S(1)}, u32[]{:S(2)}, u32[]{:S(2)}) collective-permute-start(f32[8,32,256]{2,1,0:T(8,128)S(1)} %constant_dynamic-update-slice_fusion.5), channel_id=1, source_target_pairs={{0,4},{4,0},{8,12},{12,8},{16,20},{20,16},{24,28},{28,24},{1,5},{5... | collective-permute-start | bytes 786440 | tf_op jit(solution)/shard_map/rows_core_far/ppermute | solution.py:18
  (3 other events, 29.0 us)
